TPU v7x, 32 devices: a whole 2x2x4 slice. The times are simulated.
32 devices in a mesh: dp: 8 (over z, x), tensor: 4 (over y, core).
Axes of the slice: x: 2, y: 2, z: 4, core: 2. Of those that a mesh axis runs over, the one named last changes fastest.
Arguments:
- token_ids: int32 [8, 2048], P('dp'), may hold values from 0 to 30527
- seq_lengths: int32 [8], replicated, may hold values from 1024 to 2048, as said below
- mask_slots: int32 [8, 4, 40], replicated, may hold values from 0 to 511, as said below
- mask_targets: int32 [8, 4, 40], P('dp'), may hold values from 0 to 30527
- positive_rows: int32 [8], replicated, may hold values from 0 to 1023
- doc_ids: int32 [8], replicated, may hold values from 0 to 255
- false_pairs: int32 [8, 4], replicated, may hold values from 0 to 1023
- queue_docs: int32 [1024], replicated, may hold values from 0 to 255
- queue_embed: bfloat16 [1024, 768], P('dp'), may hold values from -6 to 6
- attend_weight: float32 [768, 3072], P('dp')
- attend_moment: float32 [768, 3072], P('dp'), may hold values from -5.340576e-05 to 5.340576e-05
- gate_up: float32 [768, 2, 3072], P('dp', None, 'tensor'), may hold values from -0.21875 to 0.21875
- gate_up_moment: float32 [768, 2, 3072], P('dp', None, 'tensor'), may hold values from -5.340576e-05 to 5.340576e-05
- down_weight: float32 [768, 3072], P('dp', 'tensor'), may hold values from -0.109375 to 0.109375
- down_moment: float32 [768, 3072], P('dp', 'tensor'), may hold values from -5.340576e-05 to 5.340576e-05
- embed_table: float32 [768, 30528], P('dp', 'tensor')
- embed_moment: float32 [768, 30528], P('dp', 'tensor'), may hold values from -5.340576e-05 to 5.340576e-05
- gains: float32 [3, 768], replicated, may hold values from 0.5 to 1.5
- gains_moment: float32 [3, 768], replicated, may hold values from -0.00024414062 to 0.00024414062
- attend_error: float32 [8, 768, 3072], P('dp', None, 'tensor'), may hold values from -0.00024414062 to 0.00024414062
- gate_up_error: float32 [8, 768, 2, 3072], P('dp', None, None, 'tensor'), may hold values from -0.00024414062 to 0.00024414062
- down_error: float32 [8, 768, 3072], P('dp', None, 'tensor'), may hold values from -0.00024414062 to 0.00024414062
- embed_error: float32 [8, 768, 30528], P('dp', None, 'tensor'), may hold values from -0.00024414062 to 0.00024414062
- factors: float32 [5, 768, 32], P(None, None, 'tensor'), may hold values from -6 to 6
Outputs:
- new_attend: float32 [768, 3072], P('dp')
- new_attend_moment: float32 [768, 3072], P('dp')
- new_gate_up: float32 [768, 2, 3072], P('dp', None, 'tensor')
- new_gate_up_moment: float32 [768, 2, 3072], P('dp', None, 'tensor')
- new_down: float32 [768, 3072], P('dp', 'tensor')
- new_down_moment: float32 [768, 3072], P('dp', 'tensor')
- new_table: float32 [768, 30528], P('dp', 'tensor')
- new_table_moment: float32 [768, 30528], P('dp', 'tensor')
- new_gains: float32 [3, 768], replicated
- new_gains_moment: float32 [3, 768], replicated
- new_attend_error: float32 [8, 768, 3072], P('dp', None, 'tensor')
- new_gate_up_error: float32 [8, 768, 2, 3072], P('dp', None, None, 'tensor')
- new_down_error: float32 [8, 768, 3072], P('dp', None, 'tensor')
- new_table_error: float32 [8, 768, 30528], P('dp', None, 'tensor')
- new_factors: float32 [5, 768, 32], P(None, None, 'tensor')
- clip_norm: float32 [], replicated
- masked_sum: float32 [], replicated
- mask_count: float32 [], replicated
- contrast_loss: float32 [], replicated
Inputs may be any that keep to these rules, and one draw needn't show every extreme that they name: `seq_lengths`: the first sequence is full: its length is 2048. `mask_slots`: the 40 slots of one device of one group are distinct.
All inputs are finite; a program needn't handle non-finite values.
Results may differ from a plain program's by a relative error of at most 0.01405.
The roundings to bfloat16 on the way count: a program that leaves them out, or rounds other values in their place, can miss the bound.
Values may be sent and summed in bfloat16 or wider, within the bound.
No kernel may reach another device: no remote copies, remote signals or barrier semaphores. Data moves between devices by JAX's collectives and lax.ppermute only.
A program may use at most 448 MiB of HBM per device.

v0:
```python
import jax
import jax.numpy as jnp
from jax import lax
from jax.sharding import PartitionSpec as P

HEADS = 12
HEAD_DIM = 64
RANK = 8


EPS = 1e-05
ROPE_BASE = 1000.0
TAU = 0.02
LAMBDA = 1.0
CLIP = 0.02
LRATE = 5000.0
MOMENTUM = 0.9
WIDE = jnp.float32
NARROW = jnp.bfloat16
HIGH = lax.Precision.HIGHEST
NEGATIVE = -1e30


def combined_all(value, axis, combine):
    everything = jax.tree.map(lambda part: lax.all_gather(part, axis), value)
    initial = jax.tree.map(lambda part: part[0], everything)

    def hop(k, so_far):
        return combine(so_far, jax.tree.map(lambda part: part[k], everything))

    return lax.fori_loop(1, lax.axis_size(axis), hop, initial)


def layer_norm(values, gain):
    mean = jnp.mean(values, axis=-1, keepdims=True)
    centred = values - mean
    spread = jnp.mean(centred * centred, axis=-1, keepdims=True)
    return centred * lax.rsqrt(spread + EPS) * gain


def rotary_tables(total_rows, seq_len):
    half = HEAD_DIM // 2
    column = (jnp.arange(HEADS * HEAD_DIM) % HEAD_DIM % half).astype(WIDE)
    freq = ROPE_BASE ** (-2.0 * column / HEAD_DIM)
    places = (jnp.arange(total_rows) % seq_len).astype(WIDE)
    angle = places[:, None] * freq[None, :]
    return (jnp.cos(angle), jnp.sin(angle))


def rotate(flat, cosine, sine):
    count_rows = flat.shape[0]
    split = flat.reshape(count_rows, HEADS, 2, HEAD_DIM // 2)
    swapped = jnp.stack([-split[:, :, 1], split[:, :, 0]], axis=2).reshape(count_rows, -1)
    return flat * cosine + swapped * sine


def swiglu(gate_val):
    return jax.nn.silu(gate_val[:, 0]) * gate_val[:, 1]


def contract_rows(left, right):
    return lax.dot_general(left, right, (((0,), (0,)), ((), ())), preferred_element_type=WIDE)


def contract_cols(left, right):
    return lax.dot_general(left, right, (((1,), (1,)), ((), ())), preferred_element_type=WIDE)


def exact(left, right):
    return jnp.dot(left, right, precision=HIGH, preferred_element_type=WIDE)


def exact_rows(left, right):
    return lax.dot_general(
        left, right, (((0,), (0,)), ((), ())), precision=HIGH, preferred_element_type=WIDE
    )


def orthonormal(matrix):
    finished = []
    for index in range(RANK):
        column = matrix[:, index]
        for earlier in finished:
            column = column - jnp.sum(earlier * column) * earlier
        column = column * lax.rsqrt(jnp.sum(column * column))
        finished.append(column)
    return jnp.stack(finished, axis=1)


def merge_stats(first, second):
    top = jnp.maximum(first[0], second[0])
    total = first[1] * jnp.exp(first[0] - top) + second[1] * jnp.exp(second[0] - top)
    return (top, total) + tuple((left + right for left, right in zip(first[2:], second[2:])))


def block_scores(query_block, key_heads, keep_seq):
    scores = jnp.einsum(
        "qhd,khd->hqk", query_block, key_heads, preferred_element_type=WIDE
    ) * HEAD_DIM ** (-0.5)
    return jnp.where(keep_seq[None, None, :], scores, NEGATIVE)


def attention_forward(queries, keys, values, keep):

    def one_sequence(item):
        query_seq, key_seq, value_seq, keep_seq = item
        length = query_seq.shape[0]
        block = min(512, length)
        key_heads = key_seq.reshape(length, HEADS, HEAD_DIM)
        value_heads = value_seq.reshape(length, HEADS, HEAD_DIM)

        def one_block(query_block):
            scores = block_scores(query_block, key_heads, keep_seq)
            top = jnp.max(scores, axis=-1, keepdims=True)
            powers = jnp.exp(scores - top)
            total = jnp.sum(powers, axis=-1, keepdims=True)
            probs = (powers / total).astype(NARROW)
            output = jnp.einsum("hqk,khd->qhd", probs, value_heads, preferred_element_type=WIDE)
            return (output.reshape(block, -1), (top + jnp.log(total))[..., 0])

        outputs, log_total = lax.map(
            one_block, query_seq.reshape(length // block, block, HEADS, HEAD_DIM)
        )
        return (outputs.reshape(length, -1), log_total)

    return lax.map(one_sequence, (queries, keys, values, keep))


def attention_backward(queries, keys, values, keep, log_total, grad_out):
    scale = HEAD_DIM ** (-0.5)

    def one_sequence(item):
        query_seq, key_seq, value_seq, keep_seq, log_seq, grad_seq = item
        length = query_seq.shape[0]
        block = min(512, length)
        key_heads = key_seq.reshape(length, HEADS, HEAD_DIM)
        value_heads = value_seq.reshape(length, HEADS, HEAD_DIM)

        def one_block(carry, piece):
            key_acc, value_acc = carry
            query_block, log_block, grad_block = piece
            scores = block_scores(query_block, key_heads, keep_seq)
            probs = jnp.exp(scores - log_block[..., None])
            value_acc = value_acc + jnp.einsum(
                "hqk,qhd->khd", probs.astype(NARROW), grad_block, preferred_element_type=WIDE
            )
            dprobs = jnp.einsum(
                "qhd,khd->hqk", grad_block, value_heads, preferred_element_type=WIDE
            )
            dscores = (probs * (dprobs - jnp.sum(probs * dprobs, axis=-1, keepdims=True))).astype(
                NARROW
            )
            query_grad = (
                jnp.einsum("hqk,khd->qhd", dscores, key_heads, preferred_element_type=WIDE) * scale
            )
            key_acc = (
                key_acc
                + jnp.einsum("hqk,qhd->khd", dscores, query_block, preferred_element_type=WIDE)
                * scale
            )
            return ((key_acc, value_acc), query_grad.reshape(block, -1))

        zeros = jnp.zeros((length, HEADS, HEAD_DIM), WIDE)
        pieces = (
            query_seq.reshape(length // block, block, HEADS, HEAD_DIM),
            log_seq,
            grad_seq.reshape(length // block, block, HEADS, HEAD_DIM),
        )
        (key_acc, value_acc), query_grad = lax.scan(one_block, (zeros, zeros), pieces)
        return (
            query_grad.reshape(length, -1),
            key_acc.reshape(length, -1),
            value_acc.reshape(length, -1),
        )

    return lax.map(one_sequence, (queries, keys, values, keep, log_total, grad_out))


def normalize_keys(raw_keys):
    wide_keys = raw_keys.astype(WIDE)
    return (
        wide_keys * lax.rsqrt(jnp.sum(wide_keys * wide_keys, axis=-1, keepdims=True) + EPS)
    ).astype(NARROW)


def contrast_terms(
    queries, keys_hat, seq_index, column_ids, doc_ids, queue_docs, false_pairs, positive_rows
):
    scores = contract_cols(queries, keys_hat) / TAU
    seq_docs = jnp.take(doc_ids, seq_index)
    pairs = jnp.take(false_pairs, seq_index, axis=0)
    chosen = jnp.take(positive_rows, seq_index)
    column_docs = jnp.take(queue_docs, column_ids)
    target = column_ids[None, :] == chosen[:, None]
    blocked = (column_docs[None, :] == seq_docs[:, None]) | jnp.any(
        pairs[:, :, None] == column_ids[None, None, :], axis=1
    )
    blocked = blocked & jnp.logical_not(target)
    masked = jnp.where(blocked, NEGATIVE, scores)
    top = jnp.max(masked, axis=-1)
    total = jnp.sum(jnp.exp(masked - top[:, None]), axis=-1)
    chosen_score = jnp.sum(jnp.where(target, scores, 0.0), axis=-1)
    return (masked, target.astype(WIDE), top, total, chosen_score)


def per_device(
    token_ids,
    seq_lengths,
    mask_slots,
    mask_targets,
    positive_rows,
    doc_ids,
    false_pairs,
    queue_docs,
    queue_embed,
    attend_weight,
    attend_moment,
    gate_up,
    gate_up_moment,
    down_weight,
    down_moment,
    embed_table,
    embed_moment,
    gains,
    gains_moment,
    attend_error,
    gate_up_error,
    down_error,
    embed_error,
    factors,
):
    tensor_count = lax.axis_size("tensor")
    tensor_rank = lax.axis_index("tensor")
    data_count = lax.axis_size("dp")
    data_rank = lax.axis_index("dp")
    groups, seq_len = token_ids.shape
    width = gains.shape[1]
    total_rows = groups * seq_len
    own_rows = total_rows // tensor_count
    own_start = tensor_rank * own_rows
    slot_count = mask_slots.shape[2]
    seq_total = groups * data_count
    attend_b, gate_b, down_b, table_b = (
        lax.all_gather(attend_weight.astype(NARROW), "dp", axis=0, tiled=True),
        lax.all_gather(gate_up.astype(NARROW), "dp", axis=0, tiled=True),
        lax.all_gather(down_weight.astype(NARROW), "dp", axis=0, tiled=True),
        lax.all_gather(embed_table.astype(NARROW), "dp", axis=0, tiled=True),
    )
    queue_all = lax.all_gather(queue_embed, "dp", axis=0, tiled=True)
    every_rows = mask_slots + own_rows * jnp.arange(tensor_count)[None, :, None]
    every_len = jnp.take(
        seq_lengths, jnp.arange(mask_slots.shape[0])[:, None, None] * groups + every_rows // seq_len
    )
    count = jnp.sum((every_rows % seq_len < every_len).astype(WIDE))
    my_lengths = lax.dynamic_slice_in_dim(seq_lengths, data_rank * groups, groups, 0)
    group_valid = lax.dynamic_index_in_dim(
        every_rows % seq_len < every_len, data_rank, 0, keepdims=False
    )
    own_slots = lax.dynamic_index_in_dim(
        lax.dynamic_index_in_dim(mask_slots, data_rank, 0, keepdims=False),
        tensor_rank,
        0,
        keepdims=False,
    )
    vocab_own = table_b.shape[1]
    vocab_start = tensor_rank * vocab_own
    shifted = token_ids.reshape(-1) - vocab_start
    inside = (shifted >= 0) & (shifted < vocab_own)
    safe_ids = jnp.clip(shifted, 0, vocab_own - 1)
    looked = jnp.take(table_b, safe_ids, axis=1).T
    looked = jnp.where(inside[:, None], looked, jnp.zeros((), NARROW))
    embedded = lax.psum(looked, "tensor").astype(jnp.float32)
    x_zero, norm_zero = jax.vjp(lambda v: layer_norm(v, gains[0]), embedded)
    x_zero_b = x_zero.astype(NARROW)
    projected = jnp.dot(x_zero_b, attend_b[:, : 3 * width], preferred_element_type=WIDE)
    cosine, sine = rotary_tables(total_rows, seq_len)
    (query_rot, key_rot), turn_back = jax.vjp(
        lambda a, b: (rotate(a, cosine, sine), rotate(b, cosine, sine)),
        projected[:, :width],
        projected[:, width : 2 * width],
    )
    queries = query_rot.astype(NARROW).reshape(groups, seq_len, width)
    keys = key_rot.astype(NARROW).reshape(groups, seq_len, width)
    values = projected[:, 2 * width :].astype(NARROW).reshape(groups, seq_len, width)
    keep = jnp.arange(seq_len)[None, :] < my_lengths[:, None]
    attended, log_total = attention_forward(queries, keys, values, keep)
    attended_b = attended.reshape(total_rows, width).astype(NARROW)
    branch = jnp.dot(attended_b, attend_b[:, 3 * width :], preferred_element_type=WIDE)
    pre_one = x_zero + branch
    hidden_in, norm_one = jax.vjp(lambda v: layer_norm(v, gains[1]), pre_one)
    hidden_b = hidden_in.astype(NARROW)
    gate_val = jnp.einsum("rd,dgf->rgf", hidden_b, gate_b, preferred_element_type=WIDE)
    activated, act_back = jax.vjp(swiglu, gate_val)
    activated_b = activated.astype(NARROW)
    ffn_own = lax.psum_scatter(
        contract_cols(activated_b, down_b), "tensor", scatter_dimension=0, tiled=True
    )
    pre_out = lax.dynamic_slice_in_dim(hidden_in, own_start, own_rows, 0) + ffn_own
    final, norm_two = jax.vjp(lambda v: layer_norm(v, gains[2]), pre_out)
    row_index = own_start + jnp.arange(own_rows)
    seq_own = row_index // seq_len
    keep_own = row_index % seq_len < jnp.take(my_lengths, seq_own)
    member = (jnp.arange(groups)[:, None] == seq_own[None, :]) & keep_own[None, :]
    pool_part = jnp.sum(jnp.where(member[:, :, None], final[None], 0.0), axis=1)
    picked = jnp.take(final.astype(NARROW), own_slots, axis=0)
    rows_all = lax.all_gather(picked, "tensor", axis=0, tiled=True)
    logits = jnp.dot(rows_all, table_b, preferred_element_type=WIDE)
    targets = mask_targets.reshape(-1) - vocab_start
    hits = (jnp.arange(vocab_own)[None, :] == targets[:, None]).astype(WIDE)
    target_logit = jnp.sum(hits * logits, axis=-1)
    top = jnp.max(logits, axis=-1)
    total = jnp.sum(jnp.exp(logits - top[:, None]), axis=-1)
    top_all, total_all, target_all, pooled_sum = combined_all(
        (top, total, target_logit, pool_part), "tensor", merge_stats
    )
    log_all = top_all + jnp.log(total_all)
    valid_rows = group_valid.reshape(-1).astype(WIDE)
    row_weight = valid_rows / count
    cross = valid_rows * (log_all - target_all)
    masked_part = jnp.sum(lax.dynamic_slice_in_dim(cross, tensor_rank * slot_count, slot_count, 0))
    dlogits = ((jnp.exp(logits - log_all[:, None]) - hits) * row_weight[:, None]).astype(NARROW)
    row_grad = lax.psum_scatter(
        contract_cols(dlogits, table_b).astype(jnp.bfloat16),
        "tensor",
        scatter_dimension=0,
        tiled=True,
    ).astype(jnp.float32)
    table_grad = contract_rows(rows_all, dlogits)
    pooled = pooled_sum / my_lengths[:, None].astype(WIDE)
    embedding, embed_back = jax.vjp(
        lambda v: v * lax.rsqrt(jnp.sum(v * v, axis=-1, keepdims=True) + EPS), pooled
    )
    embedding_b = embedding.astype(NARROW)
    weight_c = LAMBDA / seq_total
    first_rank = jnp.where(tensor_rank == 0, 1.0, 0.0)
    keys_hat = normalize_keys(queue_all)
    seq_index = data_rank * groups + jnp.arange(groups)
    masked, target, top_c, total_c, chosen_c = contrast_terms(
        embedding_b,
        keys_hat,
        seq_index,
        jnp.arange(keys_hat.shape[0]),
        doc_ids,
        queue_docs,
        false_pairs,
        positive_rows,
    )
    log_c = top_c + jnp.log(total_c)
    contrast_part = jnp.sum(log_c - chosen_c) * weight_c * first_rank
    dscores = ((jnp.exp(masked - log_c[:, None]) - target) * (weight_c / TAU)).astype(NARROW)
    embed_grad = jnp.dot(dscores, keys_hat, preferred_element_type=WIDE)
    pooled_grad = embed_back(embed_grad)[0] / my_lengths[:, None].astype(WIDE)
    final_grad = jnp.sum(jnp.where(member[:, :, None], pooled_grad[:, None, :], 0.0), axis=0)
    final_grad = final_grad.at[own_slots].add(row_grad)
    pre_grad = norm_two(final_grad)[0]
    gain_two = jnp.sum(final_grad * layer_norm(pre_out, 1.0), axis=0)
    ffn_grad = lax.all_gather(pre_grad.astype(NARROW), "tensor", axis=0, tiled=True)
    down_grad = contract_rows(ffn_grad, activated_b)
    act_grad = jnp.dot(ffn_grad, down_b, preferred_element_type=WIDE)
    gate_grad = act_back(act_grad)[0].astype(NARROW)
    gate_up_grad = jnp.einsum("rd,rgf->dgf", hidden_b, gate_grad, preferred_element_type=WIDE)
    hidden_part = jnp.einsum("rgf,dgf->rd", gate_grad, gate_b, preferred_element_type=WIDE)
    own_part = lax.dynamic_slice_in_dim(hidden_part, own_start, own_rows, 0) + pre_grad
    hidden_part = lax.dynamic_update_slice_in_dim(hidden_part, own_part, own_start, 0)
    hidden_grad = lax.psum(hidden_part, "tensor")
    pre_one_grad = norm_one(hidden_grad)[0]
    gain_one = jnp.sum(
        lax.dynamic_slice_in_dim(hidden_grad * layer_norm(pre_one, 1.0), own_start, own_rows, 0),
        axis=0,
    )
    branch_grad = pre_one_grad.astype(NARROW)
    output_grad = contract_rows(attended_b, branch_grad)
    attended_grad = contract_cols(branch_grad, attend_b[:, 3 * width :]).astype(NARROW)
    query_grad, key_grad, value_grad = attention_backward(
        queries, keys, values, keep, log_total, attended_grad.reshape(groups, seq_len, width)
    )
    query_back, key_back = turn_back(
        (query_grad.reshape(total_rows, width), key_grad.reshape(total_rows, width))
    )
    projected_grad = jnp.concatenate(
        [query_back, key_back, value_grad.reshape(total_rows, width)], axis=1
    ).astype(NARROW)
    input_grad = contract_rows(x_zero_b, projected_grad)
    x_zero_grad = pre_one_grad + contract_cols(projected_grad, attend_b[:, : 3 * width])
    embedded_grad = norm_zero(x_zero_grad)[0]
    gain_zero = jnp.sum(
        lax.dynamic_slice_in_dim(x_zero_grad * layer_norm(embedded, 1.0), own_start, own_rows, 0),
        axis=0,
    )
    lookup_grad = (
        jnp.zeros((vocab_own, width), WIDE)
        .at[safe_ids]
        .add(jnp.where(inside[:, None], embedded_grad, 0.0))
    )
    table_grad = table_grad + lookup_grad.T
    attend_cols = attend_error.shape[2]
    attend_full = jnp.concatenate([input_grad, output_grad], axis=1)
    matrices = (
        lax.dynamic_slice_in_dim(attend_full, tensor_rank * attend_cols, attend_cols, 1)
        + attend_error[0],
        gate_up_grad[:, 0] + gate_up_error[0, :, 0],
        gate_up_grad[:, 1] + gate_up_error[0, :, 1],
        down_grad + down_error[0],
        table_grad + embed_error[0],
    )
    projections = [exact_rows(matrices[index], factors[index]) for index in range(5)]

    def slotted(piece):
        empty = jnp.zeros((tensor_count,) + piece.shape, WIDE)
        return lax.dynamic_update_index_in_dim(empty, piece, tensor_rank, 0)

    attend_sums, ffn_sums, table_sums = lax.psum(
        (slotted(projections[0]), slotted(jnp.stack(projections[1:4])), slotted(projections[4])),
        ("dp", "tensor"),
    )
    attend_basis_all = jax.vmap(orthonormal)(attend_sums)
    ffn_basis = jax.vmap(orthonormal)(
        lax.dynamic_index_in_dim(ffn_sums, tensor_rank, 0, keepdims=False)
    )
    table_basis = orthonormal(lax.dynamic_index_in_dim(table_sums, tensor_rank, 0, keepdims=False))
    bases = (
        lax.dynamic_index_in_dim(attend_basis_all, tensor_rank, 0, keepdims=False),
        ffn_basis[0],
        ffn_basis[1],
        ffn_basis[2],
        table_basis,
    )
    backs = [exact(matrices[index], bases[index]) for index in range(5)]
    errors = [matrices[index] - exact(backs[index], bases[index].T) for index in range(5)]
    gain_terms = jnp.stack([gain_zero, gain_one, gain_two])
    loss_terms = jnp.stack([masked_part, contrast_part])
    factor_sums, gains_grad, loss_sums = lax.psum(
        (slotted(jnp.stack(backs)), gain_terms, loss_terms), ("dp", "tensor")
    )
    clip_norm = jnp.sqrt(jnp.sum(factor_sums * factor_sums) + jnp.sum(gains_grad * gains_grad))
    shrink = CLIP / jnp.maximum(clip_norm, CLIP)
    row_count = attend_weight.shape[0]
    row_start = data_rank * row_count
    own_factors = lax.dynamic_index_in_dim(factor_sums, tensor_rank, 0, keepdims=False)

    def rows_of(matrix):
        return lax.dynamic_slice_in_dim(matrix, row_start, row_count, 0)

    attend_rows = lax.dynamic_slice_in_dim(factor_sums[:, 0], row_start, row_count, 1)
    reduced_attend = jnp.einsum(
        "tdk,tnk->dtn", attend_rows, attend_basis_all, precision=HIGH
    ).reshape(row_count, -1)
    reduced_gate_up = jnp.stack(
        [exact(rows_of(own_factors[1]), bases[1].T), exact(rows_of(own_factors[2]), bases[2].T)],
        axis=1,
    )
    reduced_down = exact(rows_of(own_factors[3]), bases[3].T)
    reduced_table = exact(rows_of(own_factors[4]), bases[4].T)

    def advance(weight, moment, grad):
        fresh = MOMENTUM * moment + shrink * grad
        return (weight - LRATE * fresh, fresh)

    new_attend, new_attend_moment = advance(attend_weight, attend_moment, reduced_attend)
    new_gate_up, new_gate_up_moment = advance(gate_up, gate_up_moment, reduced_gate_up)
    new_down, new_down_moment = advance(down_weight, down_moment, reduced_down)
    new_table, new_table_moment = advance(embed_table, embed_moment, reduced_table)
    new_gains, new_gains_moment = advance(gains, gains_moment, gains_grad)
    return (
        new_attend,
        new_attend_moment,
        new_gate_up,
        new_gate_up_moment,
        new_down,
        new_down_moment,
        new_table,
        new_table_moment,
        new_gains,
        new_gains_moment,
        errors[0][None],
        jnp.stack([errors[1], errors[2]], axis=1)[None],
        errors[3][None],
        errors[4][None],
        own_factors,
        clip_norm,
        loss_sums[0],
        count,
        loss_sums[1],
    )


def solution(mesh):
    in_specs = (
        P("dp", None),
        P(),
        P(),
        P("dp", None, None),
        P(),
        P(),
        P(),
        P(),
        P("dp", None),
        P("dp", None),
        P("dp", None),
        P("dp", None, "tensor"),
        P("dp", None, "tensor"),
        P("dp", "tensor"),
        P("dp", "tensor"),
        P("dp", "tensor"),
        P("dp", "tensor"),
        P(),
        P(),
        P("dp", None, "tensor"),
        P("dp", None, None, "tensor"),
        P("dp", None, "tensor"),
        P("dp", None, "tensor"),
        P(None, None, "tensor"),
    )
    out_specs = (
        P("dp", None),
        P("dp", None),
        P("dp", None, "tensor"),
        P("dp", None, "tensor"),
        P("dp", "tensor"),
        P("dp", "tensor"),
        P("dp", "tensor"),
        P("dp", "tensor"),
        P(),
        P(),
        P("dp", None, "tensor"),
        P("dp", None, None, "tensor"),
        P("dp", None, "tensor"),
        P("dp", None, "tensor"),
        P(None, None, "tensor"),
        P(),
        P(),
        P(),
        P(),
    )
    return jax.shard_map(
        per_device, mesh=mesh, in_specs=in_specs, out_specs=out_specs, check_vma=False
    )
```

profile of v0, /device:TPU:0, one launch (start us, length us, event | category | flops | bytes accessed | tf_op | source)
XLA Modules:
  0.0 2416.2 jit_solution(11815283596554996811)
XLA Ops:
  11.1 169.3 %all-gather.12.cloned.1.call-done = bf16[768,7632]{1,0:T(8,128)(2,1)} async-done(((bf16[96,7632]{1,0:T(8,128)(2,1)}), bf16[768,7632]{1,0:T(8,128)(2,1)}) %all-gather.12.cloned.1.call-update) | async-done | bytes 11722768 | tf_op jit(solution)/shard_map/all_gather | solution.py:247
  223.9 60.7 %all-reduce.17.cloned.1.call-done = bf16[2048,768]{0,1:T(8,128)(2,1)} async-done(((bf16[2048,768]{0,1:T(8,128)(2,1)}), bf16[2048,768]{0,1:T(8,128)(2,1)}) %all-reduce.17.cloned.1.call-update) | async-done | bytes 3145744 | tf_op jit(solution)/shard_map/psum | solution.py:272
  288.8 78.5 %all-gather.14.cloned.1.call-done = bf16[768,3072]{1,0:T(8,128)(2,1)} async-done(((bf16[96,3072]{1,0:T(8,128)(2,1)}), bf16[768,3072]{1,0:T(8,128)(2,1)}) %all-gather.14.cloned.1.call-update) | async-done | bytes 4718608 | tf_op jit(solution)/shard_map/all_gather | solution.py:244
  437.1 28.8 %fusion.54 = (bf16[2048,768]{1,0:T(8,128)(2,1)}, bf16[2048,768]{1,0:T(8,128)(2,1)}) fusion(f32[2048,768]{1,0:T(8,128)} %copy.374, f32[768]{0:T(1024)S(1)} %fusion.196, f32[2048]{0:T(1024)S(1)} %fusion.178, f32[2048,2304]{1,0:T(8,128)} %copy-done.10, f32[2048,768]{1,0:T(8,128)} %copy.371), kind=kLoop, calls=%fused_computation.91 | loop fusion | flops 14155776 | bytes 31468544 | tf_op jit(solution)/shard_map/convert_element_type | solution.py:283
  484.3 270.7 %while.73 = (s32[]{:T(128)}, bf16[4,512,768]{2,1,0:T(8,128)(2,1)}, f32[4,12,512]{2,1,0:T(8,128)}, bf16[4,512,12,64]{1,3,2,0:T(8,128)(2,1)}, bf16[2048,12,64]{0,2...) while((s32[]{:T(128)}, bf16[4,512,768]{2,1,0:T(8,128)(2,1)}, ...), condition=%wide.region_6.7_spmd.clone, body=%wide.region_3.6_spmd.clone.sunk | while | flops 3372216320 | bytes 174801040 | solution.py:121
  485.1 20.8 fusion.289
  505.9 21.3 fusion.290
  527.2 20.0 fusion.291
  552.7 20.7 fusion.289
  573.4 21.3 fusion.290
  594.7 20.0 fusion.291
  620.3 20.7 fusion.289
  641.0 21.3 fusion.290
  662.3 20.0 fusion.291
  687.9 20.7 fusion.289
  708.5 21.3 fusion.290
  729.8 19.9 fusion.291
  815.4 34.9 %reduce-scatter.3.cloned.1.call-done = f32[512,768]{0,1:T(8,128)} async-done(((f32[2048,768]{0,1:T(8,128)}), f32[512,768]{0,1:T(8,128)}) %reduce-scatter.3.cloned.1.call-update) | async-done | bytes 1572880 | tf_op jit(solution)/shard_map/reduce_scatter | solution.py:295
  933.4 28.6 %all-gather.22.cloned.1.call-done = bf16[2048,768]{0,1:T(8,128)(2,1)} async-done(((bf16[512,768]{0,1:T(8,128)(2,1)}), bf16[2048,768]{0,1:T(8,128)(2,1)}) %all-gather.22.cloned.1.call-update) | async-done | bytes 3145744 | tf_op jit(solution)/shard_map/all_gather | solution.py:357
  1017.2 83.7 %all-reduce.19.cloned.1.call-done = f32[2048,768]{0,1:T(8,128)} async-done(((f32[2048,768]{0,1:T(8,128)}), f32[2048,768]{0,1:T(8,128)}) %all-reduce.19.cloned.1.call-update) | async-done | bytes 6291472 | tf_op jit(solution)/shard_map/psum | solution.py:365
  1133.2 615.3 %while.74 = (s32[]{:T(128)}, f32[2048,12,64]{0,2,1:T(8,128)}, f32[2048,12,64]{0,2,1:T(8,128)}, f32[4,512,768]{1,2,0:T(8,128)}, bf16[4,512,12,64]{1,3,2,0:T(8,128...) while((s32[]{:T(128)}, f32[2048,12,64]{0,2,1:T(8,128)}, ...), condition=%wide.region_34.35_spmd.clone, body=%wide.region_32.34_spmd.clone.sunk | while | flops 8250060800 | bytes 426426528 | solution.py:169
  1134.8 20.5 fusion.301
  1155.3 22.3 bitcast_add_fusion.19
  1177.6 35.8 %multiply_reduce_fusion.103 = (f32[12,512]{1,0:T(8,128)S(1)}, f32[12,512,2048]{2,1,0:T(8,128)}) fusion(f32[12,512,2048]{2,1,0:T(8,128)} %fusion.301, f32[12,512]{1,0:T(8,128)S(1)} %dynamic-slice_bitcast_fusion.5, pred[2048]{0:T(1024)(128)(4,1)S(1)} %iota_compare_fusion.9, bf16[2048,12,64]{0,2,1:T(8,128)(2,1)} %get-tuple-element.1257, ...), kind=kOutput, calls=%fused_computation.29.clone.1 | convolution fusion | flops 1673521152 | bytes 104646656 | tf_op jit(solution)/shard_map/while/body/eval_jaxpr/while/body/eval_jaxpr/qhd,khd->hqk/dot_general | solution.py:147
  1213.3 40.3 %multiply_convert_fusion.11 = bf16[12,512,2048]{2,1,0:T(8,128)(2,1)} fusion(f32[12,512,2048]{2,1,0:T(8,128)} %get-tuple-element.1163, f32[12,512,2048]{2,1,0:T(8,128)} %fusion.301, f32[12,512]{1,0:T(8,128)S(1)} %get-tuple-element.1164, f32[12,512]{1,0:T(8,128)S(1)} %dynamic-slice_bitcast_fusion.5, pred[2048]{0:T(1024)(128)(4,1)S(1)} %iota_compare_fusion.9), kind=kLoop, calls=%fused_computation.28.clone.1 | loop fusion | flops 75497472 | bytes 125880320 | tf_op jit(solution)/shard_map/while/body/eval_jaxpr/while/body/eval_jaxpr/convert_element_type | solution.py:150
  1285.8 20.5 fusion.301
  1306.3 24.1 bitcast_add_fusion.19
  1330.4 35.8 %multiply_reduce_fusion.103 = (f32[12,512]{1,0:T(8,128)S(1)}, f32[12,512,2048]{2,1,0:T(8,128)}) fusion(f32[12,512,2048]{2,1,0:T(8,128)} %fusion.301, f32[12,512]{1,0:T(8,128)S(1)} %dynamic-slice_bitcast_fusion.5, pred[2048]{0:T(1024)(128)(4,1)S(1)} %iota_compare_fusion.9, bf16[2048,12,64]{0,2,1:T(8,128)(2,1)} %get-tuple-element.1257, ...), kind=kOutput, calls=%fused_computation.29.clone.1 | convolution fusion | flops 1673521152 | bytes 104646656 | tf_op jit(solution)/shard_map/while/body/eval_jaxpr/while/body/eval_jaxpr/qhd,khd->hqk/dot_general | solution.py:147
  1366.1 40.3 %multiply_convert_fusion.11 = bf16[12,512,2048]{2,1,0:T(8,128)(2,1)} fusion(f32[12,512,2048]{2,1,0:T(8,128)} %get-tuple-element.1163, f32[12,512,2048]{2,1,0:T(8,128)} %fusion.301, f32[12,512]{1,0:T(8,128)S(1)} %get-tuple-element.1164, f32[12,512]{1,0:T(8,128)S(1)} %dynamic-slice_bitcast_fusion.5, pred[2048]{0:T(1024)(128)(4,1)S(1)} %iota_compare_fusion.9), kind=kLoop, calls=%fused_computation.28.clone.1 | loop fusion | flops 75497472 | bytes 125880320 | tf_op jit(solution)/shard_map/while/body/eval_jaxpr/while/body/eval_jaxpr/convert_element_type | solution.py:150
  1420.2 17.5 bitcast_add_fusion.18
  1440.4 20.5 fusion.301
  1460.9 24.1 bitcast_add_fusion.19
  1484.9 35.8 %multiply_reduce_fusion.103 = (f32[12,512]{1,0:T(8,128)S(1)}, f32[12,512,2048]{2,1,0:T(8,128)}) fusion(f32[12,512,2048]{2,1,0:T(8,128)} %fusion.301, f32[12,512]{1,0:T(8,128)S(1)} %dynamic-slice_bitcast_fusion.5, pred[2048]{0:T(1024)(128)(4,1)S(1)} %iota_compare_fusion.9, bf16[2048,12,64]{0,2,1:T(8,128)(2,1)} %get-tuple-element.1257, ...), kind=kOutput, calls=%fused_computation.29.clone.1 | convolution fusion | flops 1673521152 | bytes 104646656 | tf_op jit(solution)/shard_map/while/body/eval_jaxpr/while/body/eval_jaxpr/qhd,khd->hqk/dot_general | solution.py:147
  1520.7 40.3 %multiply_convert_fusion.11 = bf16[12,512,2048]{2,1,0:T(8,128)(2,1)} fusion(f32[12,512,2048]{2,1,0:T(8,128)} %get-tuple-element.1163, f32[12,512,2048]{2,1,0:T(8,128)} %fusion.301, f32[12,512]{1,0:T(8,128)S(1)} %get-tuple-element.1164, f32[12,512]{1,0:T(8,128)S(1)} %dynamic-slice_bitcast_fusion.5, pred[2048]{0:T(1024)(128)(4,1)S(1)} %iota_compare_fusion.9), kind=kLoop, calls=%fused_computation.28.clone.1 | loop fusion | flops 75497472 | bytes 125880320 | tf_op jit(solution)/shard_map/while/body/eval_jaxpr/while/body/eval_jaxpr/convert_element_type | solution.py:150
  1595.0 20.5 fusion.301
  1615.4 24.1 bitcast_add_fusion.19
  1639.5 35.8 %multiply_reduce_fusion.103 = (f32[12,512]{1,0:T(8,128)S(1)}, f32[12,512,2048]{2,1,0:T(8,128)}) fusion(f32[12,512,2048]{2,1,0:T(8,128)} %fusion.301, f32[12,512]{1,0:T(8,128)S(1)} %dynamic-slice_bitcast_fusion.5, pred[2048]{0:T(1024)(128)(4,1)S(1)} %iota_compare_fusion.9, bf16[2048,12,64]{0,2,1:T(8,128)(2,1)} %get-tuple-element.1257, ...), kind=kOutput, calls=%fused_computation.29.clone.1 | convolution fusion | flops 1673521152 | bytes 104646656 | tf_op jit(solution)/shard_map/while/body/eval_jaxpr/while/body/eval_jaxpr/qhd,khd->hqk/dot_general | solution.py:147
  1675.3 40.3 %multiply_convert_fusion.11 = bf16[12,512,2048]{2,1,0:T(8,128)(2,1)} fusion(f32[12,512,2048]{2,1,0:T(8,128)} %get-tuple-element.1163, f32[12,512,2048]{2,1,0:T(8,128)} %fusion.301, f32[12,512]{1,0:T(8,128)S(1)} %get-tuple-element.1164, f32[12,512]{1,0:T(8,128)S(1)} %dynamic-slice_bitcast_fusion.5, pred[2048]{0:T(1024)(128)(4,1)S(1)} %iota_compare_fusion.9), kind=kLoop, calls=%fused_computation.28.clone.1 | loop fusion | flops 75497472 | bytes 125880320 | tf_op jit(solution)/shard_map/while/body/eval_jaxpr/while/body/eval_jaxpr/convert_element_type | solution.py:150
  1783.1 24.1 fusion.63
  1830.8 25.3 %fusion.56 = (bf16[2048,768]{1,0:T(8,128)(2,1)S(1)}, bf16[2048,768]{1,0:T(8,128)(2,1)}) fusion(f32[2048,768]{1,0:T(8,128)} %copy.392, f32[4,512,768]{2,1,0:T(8,128)} %copy.390, f32[768]{0:T(1024)S(1)} %copy-done.66, f32[2048]{0:T(1024)S(1)} %copy-done.46, f32[2048,768]{1,0:T(8,128)} %copy.394, f32[2048,768]{1,0:T(8,128)} %copy.393), kind=kLoop, calls=%fused_computation.93 | loop fusion | flops 11010048 | bytes 31468544 | tf_op jit(solution)/shard_map/convert
  1906.3 24.4 %scatter_custom_fusion.1 = f32[7632,768]{1,0:T(8,128)} fusion(s32[2048]{0:T(1024)} %bitcast.635, f32[2048,768]{1,0:T(8,128)} %copy.421, f32[]{:T(128)} %constant.426.clone.1), kind=kCustom, calls=%fused_computation.60 | custom fusion | flops 1572864 | bytes 23446016 | tf_op jit(solution)/shard_map/scatter-add | solution.py:393
  1930.7 27.7 %bitcast_add_fusion.3 = f32[768,7632]{0,1:T(8,128)} fusion(f32[1,768,7632]{1,2,0:T(8,128)} %param.52, f32[7632,768]{1,0:T(8,128)} %scatter_custom_fusion.1, bf16[160,768]{1,0:T(8,128)(2,1)S(1)} %copy-done.34, f32[160,7632]{1,0:T(8,128)} %get-tuple-element.971, f32[160]{0:T(256)S(1)} %copy-done.83, f32[160]{0:T(256)S(1)} %copy-done.81, s32[160]{0:T(256)S(1)} %copy-done.77), kind=kOutput, calls=%fused_computation.56 | convolution fusion | flops 1894689792 | bytes 75468672 | tf_op jit(solution)/shard_map/dot_general | solution.py:62
  1959.4 23.5 fusion.42
  1988.3 40.1 %all-reduce.9 = (f32[3,768]{1,0:T(4,128)S(1)}, f32[2]{0:T(128)S(1)}) all-reduce(f32[3,768]{1,0:T(4,128)S(1)} %pad_maximum_fusion.7, f32[2]{0:T(128)S(1)} %pad_maximum_fusion.8), channel_id=1, replica_groups=mesh['dp'=8,'tensor'=4] {'dp','tensor'}, use_global_device_ids=true, to_apply=%region_154.155 | all-reduce | flops 2306 | bytes 18448 | tf_op jit(solution)/shard_map/psum | solution.py:432
  2029.6 86.0 %all-reduce.23.cloned.1.call-done = (f32[4,768,8]{1,0,2:T(4,128)}, f32[4,3,768,8]{2,3,1,0:T(8,128)}, f32[4,7632,8]{1,2,0:T(8,128)}) async-done(((f32[4,768,8]{1,0,2:T(4,128)}, f32[4,3,768,8]{2,3,1,0:T(8,128)}, f32[4,7632,8]{1,2,0:T(8,128)}), (f32[4,768,8]{1,0,2:T(4,128)}, f32[4,3,768,8]{2,3,1,0:T(8,128)}, f32[4,7632,8]{1,2,0:T(8,128)})) %all-reduce.23.cloned.1.call-update) | async-done | bytes 1370128 | tf_op jit(solution)/shard_map/psum | solution.py:412
  2200.6 18.2 subtract_multiply_fusion.2
  2235.4 24.5 %subtract_bitcast_fusion = f32[1,768,7632]{1,2,0:T(8,128)} fusion(f32[768,7632]{0,1:T(8,128)} %bitcast_add_fusion.3, f32[768,8]{0,1:T(8,128)S(1)} %get-tuple-element.983, f32[7632,8]{0,1:T(8,128)S(1)} %stack.122), kind=kOutput, calls=%fused_computation.58 | convolution fusion | flops 568553472 | bytes 47159808 | tf_op jit(solution)/shard_map/dot_general | solution.py:70
  2277.5 110.7 %all-reduce.21.cloned.1.call-done = f32[4,5,768,8]{2,3,1,0:T(8,128)} async-done(((f32[4,5,768,8]{2,3,1,0:T(8,128)}), f32[4,5,768,8]{2,3,1,0:T(8,128)}) %all-reduce.21.cloned.1.call-update) | async-done | bytes 491536 | tf_op jit(solution)/shard_map/psum | solution.py:432
  (577 shorter events, 749.8 us)
Async XLA Ops:
  7.2 799.9 %copy-start = (s32[1024]{0:T(1024)S(1)}, s32[1024]{0:T(1024)}, u32[]{:S(2)}) copy-start(s32[1024]{0:T(1024)} %param.37) | copy-start | bytes 12292
  7.2 173.2 %all-gather.12.cloned.1.call-start = ((), (), s32[]{:S(2)}) async-start(), calls=%async_computation.2 | async-start | bytes 13271040 | tf_op jit(solution)/shard_map/all_gather | solution.py:247
  10.4 274.2 %all-reduce.17.cloned.1.call-start = ((), (), s32[]{:S(2)}) async-start(), calls=%async_computation.3 | async-start | bytes 6291456 | tf_op jit(solution)/shard_map/psum | solution.py:272
  10.5 205.2 %copy-start.72 = (pred[2048]{0:T(1024)(128)(4,1)}, pred[2048]{0:T(1024)(128)(4,1)S(1)}, u32[]{:S(2)}) copy-start(pred[2048]{0:T(1024)(128)(4,1)S(1)} %and_reduce_fusion) | copy-start | bytes 6148
  217.8 149.6 %all-gather.14.cloned.1.call-start = ((), (), s32[]{:S(2)}) async-start(), calls=%async_computation.4 | async-start | bytes 5308416 | tf_op jit(solution)/shard_map/all_gather | solution.py:244
  220.1 551.0 %all-gather.16.cloned.1.call-start = ((), (), s32[]{:S(2)}) async-start(), calls=%async_computation.5 | async-start | bytes 2654208 | tf_op jit(solution)/shard_map/all_gather | solution.py:245
  220.9 564.9 %all-gather.18.cloned.1.call-start = ((), (), s32[]{:S(2)}) async-start(), calls=%async_computation.6 | async-start | bytes 1327104 | tf_op jit(solution)/shard_map/all_gather | solution.py:246
  221.7 591.7 %all-gather.20.cloned.1.call-start = ((), (), s32[]{:S(2)}) async-start(), calls=%async_computation.8 | async-start | bytes 1769472 | tf_op jit(solution)/shard_map/all_gather | solution.py:249
  222.2 628.2 %reduce-scatter.3.cloned.1.call-start = ((), (), s32[]{:S(2)}) async-start(), calls=%async_computation.7 | async-start | bytes 7864320 | tf_op jit(solution)/shard_map/reduce_scatter | solution.py:295
  222.6 214.6 %copy-start.65 = (f32[768]{0:T(1024)}, f32[768]{0:T(1024)S(1)}, u32[]{:S(2)}) copy-start(f32[768]{0:T(1024)S(1)} %fusion.196) | copy-start | bytes 9220
  222.6 214.5 %copy-start.45 = (f32[2048]{0:T(1024)}, f32[2048]{0:T(1024)S(1)}, u32[]{:S(2)}) copy-start(f32[2048]{0:T(1024)S(1)} %fusion.178) | copy-start | bytes 24580
  223.3 154.2 %copy-start.67 = (f32[768]{0:T(1024)}, f32[768]{0:T(1024)S(1)}, u32[]{:S(2)}) copy-start(f32[768]{0:T(1024)S(1)} %get-tuple-element.748) | copy-start | bytes 9220
  287.4 90.1 %copy-start.47 = (f32[2048]{0:T(1024)}, f32[2048]{0:T(1024)S(1)}, u32[]{:S(2)}) copy-start(f32[2048]{0:T(1024)S(1)} %broadcast_multiply_fusion.13) | copy-start | bytes 24580
  288.8 88.6 %copy-start.54 = (f32[2048]{0:T(1024)}, f32[2048]{0:T(1024)S(1)}, u32[]{:S(2)}) copy-start(f32[2048]{0:T(1024)S(1)} %fusion.182) | copy-start | bytes 24580
  484.2 270.7 %copy-start.48 = (f32[2048]{0:T(1024)S(1)}, f32[2048]{0:T(1024)}, u32[]{:S(2)}) copy-start(f32[2048]{0:T(1024)} %copy-done.47) | copy-start | bytes 24580
  484.3 270.7 %copy-start.55 = (f32[2048]{0:T(1024)S(1)}, f32[2048]{0:T(1024)}, u32[]{:S(2)}) copy-start(f32[2048]{0:T(1024)} %copy-done.54) | copy-start | bytes 24580
  484.3 270.8 %copy-start.68 = (f32[768]{0:T(1024)S(1)}, f32[768]{0:T(1024)}, u32[]{:S(2)}) copy-start(f32[768]{0:T(1024)} %copy-done.67) | copy-start | bytes 9220
  505.9 21.3 copy-start.6
  573.4 21.3 copy-start.6
  641.0 21.3 copy-start.6
  793.3 130.6 %reduce-scatter.5.cloned.1.call-start = ((), (), s32[]{:S(2)}) async-start(), calls=%async_computation.9 | async-start | bytes 307200 | tf_op jit(solution)/shard_map/reduce_scatter | solution.py:322
  796.6 94.9 %copy-start.76 = (s32[160]{0:T(256)}, s32[160]{0:T(256)S(1)}, u32[]{:S(2)}) copy-start(s32[160]{0:T(256)S(1)} %sub.894) | copy-start | bytes 1924
  811.6 41.4 %copy-start.58 = (f32[768]{0:T(1024)S(1)}, f32[768]{0:T(1024)}, u32[]{:S(2)}) copy-start(f32[768]{0:T(1024)} %get-tuple-element.746) | copy-start | bytes 9220
  902.8 59.2 %all-gather.22.cloned.1.call-start = ((), (), s32[]{:S(2)}) async-start(), calls=%async_computation.10 | async-start | bytes 3932160 | tf_op jit(solution)/shard_map/all_gather | solution.py:357
  933.3 38.1 %copy-start.88 = (bf16[768,2,768]{2,0,1:T(8,128)(2,1)S(1)}, bf16[768,2,768]{2,0,1:T(8,128)(2,1)}, u32[]{:S(2)}) copy-start(bf16[768,2,768]{2,0,1:T(8,128)(2,1)} %all-gather.16.cloned.1.call-done) | copy-start | bytes 7077892
  933.3 167.7 %all-reduce.19.cloned.1.call-start = ((), (), s32[]{:S(2)}) async-start(), calls=%async_computation.11 | async-start | bytes 12582912 | tf_op jit(solution)/shard_map/psum | solution.py:365
  981.2 1134.4 %all-reduce.23.cloned.1.call-start = ((), (), s32[]{:S(2)}) async-start(), calls=%async_computation.13 | async-start | bytes 2752512 | tf_op jit(solution)/shard_map/psum | solution.py:412
  1830.8 25.3 %copy-start.9 = (bf16[2048,768]{0,1:T(8,128)(2,1)S(1)}, bf16[2048,768]{0,1:T(8,128)(2,1)}, u32[]{:S(2)}) copy-start(bf16[2048,768]{0,1:T(8,128)(2,1)} %all-reduce.17.cloned.1.call-done) | copy-start | bytes 9437188
  1830.8 25.4 %copy-start.49 = (f32[2048]{0:T(1024)S(1)}, f32[2048]{0:T(1024)}, u32[]{:S(2)}) copy-start(f32[2048]{0:T(1024)} %copy-done.47) | copy-start | bytes 24580
  1830.8 25.4 %copy-start.69 = (f32[768]{0:T(1024)S(1)}, f32[768]{0:T(1024)}, u32[]{:S(2)}) copy-start(f32[768]{0:T(1024)} %copy-done.67) | copy-start | bytes 9220
  1830.8 25.4 %copy-start.79 = (f32[2048]{0:T(1024)S(1)}, f32[2048]{0:T(1024)}, u32[]{:S(2)}) copy-start(f32[2048]{0:T(1024)} %copy-done.78) | copy-start | bytes 24580
  1870.0 23.3 slice-start.2
  1906.3 24.4 %copy-start.41 = (f32[4,768,8]{1,0,2:T(4,128)}, f32[4,768,8]{1,0,2:T(4,128)S(1)}, u32[]{:S(2)}) copy-start(f32[4,768,8]{1,0,2:T(4,128)S(1)} %dynamic_update_slice.43) | copy-start | bytes 294916
  1906.3 24.4 %copy-start.34 = (bf16[160,768]{1,0:T(8,128)(2,1)S(1)}, bf16[160,768]{1,0:T(8,128)(2,1)}, u32[]{:S(2)}) copy-start(bf16[160,768]{1,0:T(8,128)(2,1)} %copy-done.33) | copy-start | bytes 737284
  1906.3 24.4 %copy-start.77 = (s32[160]{0:T(256)S(1)}, s32[160]{0:T(256)}, u32[]{:S(2)}) copy-start(s32[160]{0:T(256)} %copy-done.76) | copy-start | bytes 1924
  1906.3 24.4 %copy-start.81 = (f32[160]{0:T(256)S(1)}, f32[160]{0:T(256)}, u32[]{:S(2)}) copy-start(f32[160]{0:T(256)} %copy-done.80) | copy-start | bytes 1924
  1906.3 24.4 %copy-start.83 = (f32[160]{0:T(256)S(1)}, f32[160]{0:T(256)}, u32[]{:S(2)}) copy-start(f32[160]{0:T(256)} %copy-done.82) | copy-start | bytes 1924
  1959.4 24.2 %copy-start.86 = (f32[160]{0:T(256)S(1)}, f32[160]{0:T(256)}, u32[]{:S(2)}) copy-start(f32[160]{0:T(256)} %get-tuple-element.826) | copy-start | bytes 1924
  1959.4 25.6 %copy-start.74 = (f32[768]{0:T(1024)S(1)}, f32[768]{0:T(1024)}, u32[]{:S(2)}) copy-start(f32[768]{0:T(1024)} %get-tuple-element.662) | copy-start | bytes 9220
  1982.9 405.2 %all-reduce.21.cloned.1.call-start = ((), (), s32[]{:S(2)}) async-start(), calls=%async_computation.12 | async-start | bytes 983040 | tf_op jit(solution)/shard_map/psum | solution.py:432
  2028.4 95.3 %copy-start.61 = (f32[3,768]{1,0:T(4,128)}, f32[3,768]{1,0:T(4,128)S(1)}, u32[]{:S(2)}) copy-start(f32[3,768]{1,0:T(4,128)S(1)} %get-tuple-element.810) | copy-start | bytes 27652
  2123.7 25.6 %slice-start = ((s8[4718592]{0:T(1024)(128)(4,1)}), s8[524288]{0:T(1024)(128)(4,1)S(1)}, s32[]{:S(2)}) async-start(s8[4718592]{0:T(1024)(128)(4,1)} %bitcast.616), calls=%async_computation.14 | async-start | bytes 1048576
  2273.8 117.6 %copy-start.62 = (f32[3,768]{1,0:T(4,128)S(1)}, f32[3,768]{1,0:T(4,128)}, u32[]{:S(2)}) copy-start(f32[3,768]{1,0:T(4,128)} %copy-done.61) | copy-start | bytes 27652
  2273.8 117.6 %copy-start.64 = (f32[3,768]{1,0:T(4,128)S(1)}, f32[3,768]{1,0:T(4,128)}, u32[]{:S(2)}) copy-start(f32[3,768]{1,0:T(4,128)} %param.47) | copy-start | bytes 27652
  2273.8 117.6 %copy-start.75 = (f32[3,768]{1,0:T(4,128)S(1)}, f32[3,768]{1,0:T(4,128)}, u32[]{:S(2)}) copy-start(f32[3,768]{1,0:T(4,128)} %param.48) | copy-start | bytes 27652
  2273.8 120.8 %copy-start.32 = (f32[96,2,768]{2,1,0:T(2,128)S(1)}, f32[96,2,768]{2,1,0:T(2,128)}, u32[]{:S(2)}) copy-start(f32[96,2,768]{2,1,0:T(2,128)} %param.41) | copy-start | bytes 1769476
  2273.8 120.8 %copy-start.40 = (f32[96,2,768]{2,1,0:T(2,128)S(1)}, f32[96,2,768]{2,1,0:T(2,128)}, u32[]{:S(2)}) copy-start(f32[96,2,768]{2,1,0:T(2,128)} %param.42) | copy-start | bytes 1769476
  2273.8 123.5 %copy-start.44 = (f32[4,768,8]{1,0,2:T(4,128)S(1)}, f32[4,768,8]{1,0,2:T(4,128)}, u32[]{:S(2)}) copy-start(f32[4,768,8]{1,0,2:T(4,128)} %copy-done.43) | copy-start | bytes 294916
  (69 other events, 475.6 us)
Sparse Core Ops, SparseCore 0:
  10.8 169.5 all-gather.11
  217.9 66.6 all-reduce.16
  287.3 79.9 all-gather.13
  370.0 50.2 all-gather.15
  422.8 39.6 all-gather.17
  464.5 42.9 all-gather.19
  793.4 56.8 reduce-scatter.2
  902.9 20.9 reduce-scatter.4
  933.4 28.5 all-gather.21
  981.4 119.5 all-reduce.18
  1983.1 132.4 all-reduce.22
  2261.8 126.2 all-reduce.20
where the time goes:
time: 2430 us; the launch traced here: 2420 us
  matrix products  866 us (36%)
  waiting for transfers between devices  667 us (27%)
  other arithmetic  532 us (22%)
  local copies, waits for them, and re-layouts  257 us (11%)
  blocking collectives  61.3 us (3%)
  between operations  30.7 us (1%)
    all_gather x1, waiting for transfers between devices, per_device(): lax.all_gather(embed_table.astype(NARROW), 'dp', axis=0, tiled=True)  169 us
    dot_general x8, matrix products, block_scores(): jnp.einsum('qhd,khd->hqk', query_block, key_heads, preferred_element_type...  165 us
    convert_element_type x4, other arithmetic, one_block(): (probs * (dprobs - jnp.sum(probs * dprobs, axis=-1, keepdims=True))).asty...  161 us
    dot_general x4, matrix products, one_block(): jnp.einsum('qhd,khd->hqk', grad_block, value_heads, preferred_element_typ...  143 us
    psum x1, waiting for transfers between devices, per_device(): lax.psum((slotted(jnp.stack(backs)), gain_terms, loss_terms), ('dp', 'ten...  111 us
    dot_general x4, matrix products, one_block(): jnp.einsum('hqk,qhd->khd', probs.astype(NARROW), grad_block, preferred_el...  94.6 us
    psum x1, waiting for transfers between devices, per_device(): lax.psum((slotted(projections[0]), slotted(jnp.stack(projections[1:4])),...  86 us
    reduce_sum x4, other arithmetic, one_block(): total = jnp.sum(powers, axis=-1, keepdims=True)  85.1 us
  transfers between devices with their start and end apart: 12, of which 9 were waited for; matrix products, arithmetic and copies ran while one was open for 21% of the time, Pallas kernels for 0%

commit v1 on v0

v1 whole, which is shorter than its diff:
```python
import functools

import jax
import jax.numpy as jnp
from jax import lax
from jax.experimental import pallas as pl
from jax.experimental.pallas import tpu as pltpu
from jax.sharding import PartitionSpec as P

HEADS = 12
HEAD_DIM = 64
RANK = 8
PAIR = 2 * HEAD_DIM
TILE = 512

EPS = 1e-05
ROPE_BASE = 1000.0
TAU = 0.02
LAMBDA = 1.0
CLIP = 0.02
LRATE = 5000.0
MOMENTUM = 0.9
WIDE = jnp.float32
NARROW = jnp.bfloat16
HIGH = lax.Precision.HIGHEST
NEGATIVE = -1e30
VMEM_BYTES = 56 * 1024 * 1024


def params():
    return pltpu.CompilerParams(vmem_limit_bytes=VMEM_BYTES)


def axis_bits(axis):
    size = lax.axis_size(axis)
    return [1 << place for place in range(size.bit_length() - 1)]


def swap(value, axis, bit):
    size = lax.axis_size(axis)
    return lax.ppermute(value, axis, [(index, index ^ bit) for index in range(size)])


def spread_blocks(value, axis):
    held = {0: value}
    for bit in reversed(axis_bits(axis)):
        for key in sorted(held):
            held[key ^ bit] = swap(held[key], axis, bit)
    return [held[key] for key in range(len(held))]


def summed_block(blocks, axis, kind):
    held = dict(enumerate(blocks))
    for bit in axis_bits(axis):
        for key in sorted((k for k in held if not k & bit), reverse=True):
            if key in held:
                got = swap(held.pop(key ^ bit).astype(kind), axis, bit)
                held[key] = held[key].astype(WIDE) + got.astype(WIDE)
    return held[0]


def summed_all(value, axis):
    for bit in axis_bits(axis):
        value = value + swap(value, axis, bit)
    return value


def picked_blocks(blocks, order):
    stacked = blocks if isinstance(blocks, jax.Array) else jnp.stack(blocks)
    return jnp.stack(
        [
            lax.dynamic_index_in_dim(stacked, order[k], 0, keepdims=False)
            for k in range(stacked.shape[0])
        ]
    )


def row_blocks(value, count):
    rows = value.shape[0] // count
    return [value[k * rows : (k + 1) * rows] for k in range(count)]


def layer_norm(values, gain):
    mean = jnp.mean(values, axis=-1, keepdims=True)
    centred = values - mean
    spread = jnp.mean(centred * centred, axis=-1, keepdims=True)
    return centred * lax.rsqrt(spread + EPS) * gain


def swiglu(gate, up):
    return jax.nn.silu(gate) * up


def dot_in(left, right, axes, precision=None):
    return lax.dot_general(
        left, right, (axes, ((), ())), precision=precision, preferred_element_type=WIDE
    )


def contract_rows(left, right):
    return dot_in(left, right, ((0,), (0,)))


def contract_cols(left, right):
    return dot_in(left, right, ((1,), (1,)))


def halves(value):
    high = value.astype(NARROW)
    return high, (value - high.astype(WIDE)).astype(NARROW)


def turn(piece, cosine, sine):
    lane = lax.broadcasted_iota(jnp.int32, piece.shape, 1) % HEAD_DIM
    half = HEAD_DIM // 2
    ahead = pltpu.roll(piece, PAIR - half, 1)
    behind = pltpu.roll(piece, half, 1)
    return piece * cosine + jnp.where(lane < half, -ahead, behind) * sine


def rotary_tables(places):
    half = HEAD_DIM // 2
    column = (jnp.arange(PAIR) % half).astype(WIDE)
    freq = ROPE_BASE ** (-2.0 * column / HEAD_DIM)
    angle = places.astype(WIDE)[:, None] * freq[None, :]
    return (jnp.cos(angle), jnp.sin(angle))


def project_kernel(scale, x_ref, w_ref, cos_ref, sin_ref, out_ref):
    flat = jnp.dot(x_ref[...], w_ref[...], preferred_element_type=WIDE)
    cosine, sine = cos_ref[...], sin_ref[...]
    for start in range(0, flat.shape[1], PAIR):
        piece = turn(flat[:, start : start + PAIR], cosine, sine).astype(NARROW)
        if scale != 1.0:
            piece = (piece.astype(WIDE) * scale).astype(NARROW)
        out_ref[:, start : start + PAIR] = piece


def project(x, weight, cosine, sine, scale):
    rows, width = x.shape
    columns = weight.shape[1]
    block, span = min(512, rows), 256
    return pl.pallas_call(
        functools.partial(project_kernel, scale),
        grid=(rows // block, columns // span),
        in_specs=[
            pl.BlockSpec((block, width), lambda i, j: (i, 0)),
            pl.BlockSpec((width, span), lambda i, j: (0, j)),
            pl.BlockSpec((block, PAIR), lambda i, j: (i, 0)),
            pl.BlockSpec((block, PAIR), lambda i, j: (i, 0)),
        ],
        out_specs=pl.BlockSpec((block, span), lambda i, j: (i, j)),
        out_shape=jax.ShapeDtypeStruct((rows, columns), NARROW),
        compiler_params=params(),
        cost_estimate=pl.CostEstimate(
            flops=2 * rows * width * columns,
            bytes_accessed=2 * (rows * width + width * columns + rows * columns),
            transcendentals=0,
        ),
    )(x, weight, cosine, sine)


def head_lanes(head):
    lane = lax.broadcasted_iota(jnp.int32, (1, PAIR), 1)
    return (lane // HEAD_DIM) == head, lane == HEAD_DIM * (1 - head)


def attend_kernel(q_ref, k_ref, v_ref, bias_ref, out_ref, log_ref, s_ref):
    head = pl.program_id(1)
    mine, spare = head_lanes(head)
    length = k_ref.shape[0]
    step = min(TILE, length)
    query = jnp.where(spare, 1.0, jnp.where(mine, q_ref[...].astype(WIDE), 0.0)).astype(NARROW)
    top = None
    for start in range(0, length, step):
        rows = pl.ds(start, step)
        key = jnp.where(spare, bias_ref[rows, :].astype(WIDE), k_ref[rows, :].astype(WIDE))
        scores = contract_cols(key.astype(NARROW), query)
        s_ref[rows, :] = scores
        peak = jnp.max(scores, axis=0, keepdims=True)
        top = peak if top is None else jnp.maximum(top, peak)
    total = None
    for start in range(0, length, step):
        rows = pl.ds(start, step)
        powers = jnp.exp(s_ref[rows, :] - top)
        s_ref[rows, :] = powers
        part = jnp.sum(powers, axis=0, keepdims=True)
        total = part if total is None else total + part
    share = 1.0 / total
    result = None
    for start in range(0, length, step):
        rows = pl.ds(start, step)
        probs = (s_ref[rows, :] * share).astype(NARROW)
        part = dot_in(v_ref[rows, :], probs, ((0,), (0,)))
        result = part if result is None else result + part
    log_ref[0, pl.ds(head, 1), :] = top + jnp.log(total)

    @pl.when(head == 0)
    def _():
        out_ref[...] = result

    @pl.when(head == 1)
    def _():
        out_ref[HEAD_DIM:, :] = result[HEAD_DIM:, :]


def attention_forward(queries, keys, values, bias):
    rows, width = queries.shape
    length = keys.shape[0]
    pairs = width // PAIR
    lanes = lambda i, h: (0, i)
    return pl.pallas_call(
        attend_kernel,
        grid=(pairs, 2),
        in_specs=[
            pl.BlockSpec((rows, PAIR), lanes),
            pl.BlockSpec((length, PAIR), lanes),
            pl.BlockSpec((length, PAIR), lanes),
            pl.BlockSpec((length, PAIR), lambda i, h: (0, 0)),
        ],
        out_specs=[
            pl.BlockSpec((PAIR, rows), lambda i, h: (i, 0)),
            pl.BlockSpec((1, 2, rows), lambda i, h: (i, 0, 0)),
        ],
        out_shape=[
            jax.ShapeDtypeStruct((width, rows), WIDE),
            jax.ShapeDtypeStruct((pairs, 2, rows), WIDE),
        ],
        scratch_shapes=[pltpu.VMEM((length, rows), WIDE)],
        compiler_params=params(),
        cost_estimate=pl.CostEstimate(
            flops=4 * rows * length * width,
            bytes_accessed=4 * length * width + 8 * rows * width,
            transcendentals=rows * length * HEADS,
        ),
    )(queries, keys, values, bias)


def attend_back_kernel(
    q_ref, k_ref, v_ref, bias_ref, grad_ref, out_ref, log_ref, cos_ref, sin_ref, cos_q_ref, sin_q_ref,
    dq_ref, dk_ref, dv_ref, dk_sum, dv_sum, dq_sum,
):
    head = pl.program_id(1)
    mine, spare = head_lanes(head)
    length, scale = k_ref.shape[0], HEAD_DIM ** (-0.5)
    step = min(TILE, length)
    own = jnp.where(mine, q_ref[...].astype(WIDE), 0.0)
    query = own.astype(NARROW)
    asked = jnp.where(spare, 1.0, own).astype(NARROW)
    grad_wide = jnp.where(mine, grad_ref[...].astype(WIDE), 0.0)
    grad = grad_wide.astype(NARROW)
    delta = jnp.sum(grad_wide.T * out_ref[...], axis=0, keepdims=True)
    log_total = log_ref[0, pl.ds(head, 1), :]
    dq = None
    for start in range(0, length, step):
        rows = pl.ds(start, step)
        key_block = k_ref[rows, :]
        key = jnp.where(spare, bias_ref[rows, :].astype(WIDE), key_block.astype(WIDE))
        scores = contract_cols(key.astype(NARROW), asked)
        probs = jnp.exp(scores - log_total)
        dprobs = contract_cols(v_ref[rows, :], grad)
        dv = jnp.dot(probs.astype(NARROW), grad, preferred_element_type=WIDE)
        dscores = (probs * (dprobs - delta)).astype(NARROW)
        dk = jnp.dot(dscores, query, preferred_element_type=WIDE)
        part = dot_in(key_block, dscores, ((0,), (0,)))
        dq = part if dq is None else dq + part

        @pl.when(head == 0)
        def _():
            dk_sum[rows, :] = dk
            dv_sum[rows, :] = dv

        @pl.when(head == 1)
        def _():
            total = dk_sum[rows, :] + dk
            dk_ref[rows, :] = turn(total, cos_ref[rows, :], -sin_ref[rows, :]).astype(NARROW)
            dv_ref[rows, :] = (dv_sum[rows, :] + dv).astype(NARROW)

    @pl.when(head == 0)
    def _():
        dq_sum[...] = dq

    @pl.when(head == 1)
    def _():
        dq_sum[HEAD_DIM:, :] = dq[HEAD_DIM:, :]
        total = dq_sum[...].T * scale
        dq_ref[...] = turn(total, cos_q_ref[...], -sin_q_ref[...]).astype(NARROW)


def attention_backward(queries, keys, values, bias, grad, out_t, log_total, tables, own_tables):
    rows, width = queries.shape
    length = keys.shape[0]
    pairs = width // PAIR
    lanes = lambda i, h: (0, i)
    still = lambda i, h: (0, 0)
    own_block = pl.BlockSpec((rows, PAIR), lanes)
    all_block = pl.BlockSpec((length, PAIR), lanes)
    return pl.pallas_call(
        attend_back_kernel,
        grid=(pairs, 2),
        in_specs=[
            own_block,
            all_block,
            all_block,
            pl.BlockSpec((length, PAIR), still),
            own_block,
            pl.BlockSpec((PAIR, rows), lambda i, h: (i, 0)),
            pl.BlockSpec((1, 2, rows), lambda i, h: (i, 0, 0)),
            pl.BlockSpec((length, PAIR), still),
            pl.BlockSpec((length, PAIR), still),
            pl.BlockSpec((rows, PAIR), still),
            pl.BlockSpec((rows, PAIR), still),
        ],
        out_specs=[own_block, all_block, all_block],
        out_shape=[
            jax.ShapeDtypeStruct((rows, width), NARROW),
            jax.ShapeDtypeStruct((length, width), NARROW),
            jax.ShapeDtypeStruct((length, width), NARROW),
        ],
        scratch_shapes=[
            pltpu.VMEM((length, PAIR), WIDE),
            pltpu.VMEM((length, PAIR), WIDE),
            pltpu.VMEM((PAIR, rows), WIDE),
        ],
        compiler_params=params(),
        cost_estimate=pl.CostEstimate(
            flops=10 * rows * length * width,
            bytes_accessed=8 * length * width + 8 * rows * width,
            transcendentals=rows * length * HEADS,
        ),
    )(queries, keys, values, bias, grad, out_t, log_total, *tables, *own_tables)


def project_down(matrix, factor_t):
    high, low = halves(matrix)
    factor_high, factor_low = halves(factor_t)
    both = jnp.concatenate([factor_high, factor_low], axis=0)
    first = jnp.dot(both, high, preferred_element_type=WIDE)
    second = jnp.dot(factor_high, low, preferred_element_type=WIDE)
    return first[:RANK] + first[RANK:] + second


def project_back(matrix, basis_t):
    high, low = halves(matrix)
    basis_high, basis_low = halves(basis_t)
    both = jnp.concatenate([basis_high, basis_low], axis=0)
    first = contract_cols(both, high)
    second = contract_cols(basis_high, low)
    return first[:RANK] + first[RANK:] + second


def expand(back_t, basis_t):
    back_high, back_low = halves(back_t)
    basis_high, basis_low = halves(basis_t)
    left = jnp.concatenate([back_high, back_low, back_high], axis=0)
    right = jnp.concatenate([basis_high, basis_high, basis_low], axis=0)
    return contract_rows(left, right)


def table_kernel(columns, left_ref, tokens_ref, rows_ref, dlogits_ref, error_ref, factor_ref, high_ref, low_ref, p_ref):
    start = pl.program_id(0) * TILE
    place = start + lax.broadcasted_iota(jnp.int32, (TILE, 1), 0)
    hot = (tokens_ref[...] == place).astype(WIDE).astype(NARROW)
    total = jnp.dot(hot, left_ref[...], preferred_element_type=WIDE)
    total = total + contract_rows(dlogits_ref[...], rows_ref[...])
    total = jnp.where(place < columns, total + error_ref[...], 0.0)
    high, low = halves(total)
    high_ref[...] = high
    low_ref[...] = low
    factor_high, factor_low = halves(factor_ref[...])
    both = jnp.concatenate([factor_high, factor_low], axis=0)
    first = contract_cols(both, high)
    p_ref[...] = first[:RANK] + first[RANK:] + contract_cols(factor_high, low)


def table_matrix(left, tokens, rows, dlogits, error, factor_t):
    columns, width = error.shape
    slots = left.shape[0]
    picks = rows.shape[0]
    tiles = -(-columns // TILE)
    still = lambda j: (0, 0)
    down = lambda j: (j, 0)
    along = lambda j: (0, j)
    return pl.pallas_call(
        functools.partial(table_kernel, columns),
        grid=(tiles,),
        in_specs=[
            pl.BlockSpec((slots, width), still),
            pl.BlockSpec((1, slots), still),
            pl.BlockSpec((picks, width), still),
            pl.BlockSpec((picks, TILE), along),
            pl.BlockSpec((TILE, width), down),
            pl.BlockSpec((RANK, width), still),
        ],
        out_specs=[
            pl.BlockSpec((TILE, width), down),
            pl.BlockSpec((TILE, width), down),
            pl.BlockSpec((RANK, TILE), along),
        ],
        out_shape=[
            jax.ShapeDtypeStruct((tiles * TILE, width), NARROW),
            jax.ShapeDtypeStruct((tiles * TILE, width), NARROW),
            jax.ShapeDtypeStruct((RANK, tiles * TILE), WIDE),
        ],
        compiler_params=params(),
        cost_estimate=pl.CostEstimate(
            flops=2 * width * columns * (slots + picks + 24),
            bytes_accessed=8 * width * columns,
            transcendentals=0,
        ),
    )(left, tokens, rows, dlogits, error, factor_t)


def small_kernel(count, *refs):
    grads, errors, factor_ref = refs[:count], refs[count : 2 * count], refs[2 * count]
    m_ref, p_ref = refs[2 * count + 1 :]
    for index in range(count):
        total = grads[index][...] + errors[index][...]
        m_ref[index] = total
        p_ref[index] = project_down(total, factor_ref[index])


def small_matrices(grads, errors, factor_t):
    count, (width, columns) = len(grads), grads[0].shape
    return pl.pallas_call(
        functools.partial(small_kernel, count),
        out_shape=[
            jax.ShapeDtypeStruct((count, width, columns), WIDE),
            jax.ShapeDtypeStruct((count, RANK, columns), WIDE),
        ],
        compiler_params=params(),
        cost_estimate=pl.CostEstimate(
            flops=48 * count * width * columns,
            bytes_accessed=12 * count * width * columns,
            transcendentals=0,
        ),
    )(*grads, *errors, factor_t)


def basis_kernel(spans, p_ref, out_ref):
    index = lax.broadcasted_iota(jnp.int32, (RANK, 1), 0)
    for start, size in spans:
        rows = p_ref[:, pl.ds(start, size)]
        for place in range(RANK):
            row = rows[place : place + 1, :]
            row = row * lax.rsqrt(jnp.sum(row * row, axis=1, keepdims=True))
            inner = jnp.sum(rows * row, axis=1, keepdims=True)
            rows = jnp.where(index == place, row, rows - jnp.where(index > place, inner, 0.0) * row)
        out_ref[:, pl.ds(start, size)] = rows


def bases_of(sums, spans):
    return pl.pallas_call(
        functools.partial(basis_kernel, spans),
        out_shape=jax.ShapeDtypeStruct(sums.shape, WIDE),
        compiler_params=params(),
        cost_estimate=pl.CostEstimate(
            flops=64 * sums.size, bytes_accessed=8 * sums.size, transcendentals=40
        ),
    )(sums)


def small_back_kernel(m_ref, basis_ref, back_ref):
    for index in range(m_ref.shape[0]):
        back_ref[index] = project_back(m_ref[index], basis_ref[index])


def small_backs(matrices, basis):
    count, width, columns = matrices.shape
    return pl.pallas_call(
        small_back_kernel,
        out_shape=jax.ShapeDtypeStruct((count, RANK, width), WIDE),
        compiler_params=params(),
        cost_estimate=pl.CostEstimate(
            flops=48 * count * width * columns,
            bytes_accessed=4 * count * width * columns,
            transcendentals=0,
        ),
    )(matrices, basis)


def table_back_kernel(high_ref, low_ref, basis_ref, back_ref):
    basis_high, basis_low = halves(basis_ref[...])
    both = jnp.concatenate([basis_high, basis_low], axis=0)
    first = jnp.dot(both, high_ref[...], preferred_element_type=WIDE)
    second = jnp.dot(basis_high, low_ref[...], preferred_element_type=WIDE)
    part = first[:RANK] + first[RANK:] + second

    @pl.when(pl.program_id(0) == 0)
    def _():
        back_ref[...] = part

    @pl.when(pl.program_id(0) > 0)
    def _():
        back_ref[...] += part


def table_back(high, low, basis):
    columns, width = high.shape
    down = pl.BlockSpec((TILE, width), lambda j: (j, 0))
    return pl.pallas_call(
        table_back_kernel,
        grid=(columns // TILE,),
        in_specs=[down, down, pl.BlockSpec((RANK, TILE), lambda j: (0, j))],
        out_specs=pl.BlockSpec((RANK, width), lambda j: (0, 0)),
        out_shape=jax.ShapeDtypeStruct((RANK, width), WIDE),
        compiler_params=params(),
        cost_estimate=pl.CostEstimate(
            flops=48 * width * columns, bytes_accessed=4 * width * columns, transcendentals=0
        ),
    )(high, low, basis)


def small_error_kernel(m_ref, back_ref, basis_ref, *out_refs):
    for index, out_ref in enumerate(out_refs):
        out_ref[...] = m_ref[index] - expand(back_ref[index], basis_ref[index])


def small_errors(matrices, backs, basis):
    count, width, columns = matrices.shape
    return pl.pallas_call(
        small_error_kernel,
        out_shape=[jax.ShapeDtypeStruct((width, columns), WIDE)] * count,
        compiler_params=params(),
        cost_estimate=pl.CostEstimate(
            flops=48 * count * width * columns,
            bytes_accessed=8 * count * width * columns,
            transcendentals=0,
        ),
    )(matrices, backs, basis)


def table_error_kernel(high_ref, low_ref, back_ref, basis_ref, out_ref):
    whole = high_ref[...].astype(WIDE) + low_ref[...].astype(WIDE)
    out_ref[...] = whole - expand(basis_ref[...], back_ref[...])


def table_error(high, low, back, basis, columns):
    width = high.shape[1]
    down = pl.BlockSpec((TILE, width), lambda j: (j, 0))
    return pl.pallas_call(
        table_error_kernel,
        grid=(-(-columns // TILE),),
        in_specs=[
            down,
            down,
            pl.BlockSpec((RANK, width), lambda j: (0, 0)),
            pl.BlockSpec((RANK, TILE), lambda j: (0, j)),
        ],
        out_specs=down,
        out_shape=jax.ShapeDtypeStruct((columns, width), WIDE),
        compiler_params=params(),
        cost_estimate=pl.CostEstimate(
            flops=48 * width * columns, bytes_accessed=8 * width * columns, transcendentals=0
        ),
    )(high, low, back, basis)


def normalize_keys(raw_keys):
    wide_keys = raw_keys.astype(WIDE)
    return (
        wide_keys * lax.rsqrt(jnp.sum(wide_keys * wide_keys, axis=-1, keepdims=True) + EPS)
    ).astype(NARROW)


def contrast_terms(
    queries, keys_hat, seq_index, column_ids, doc_ids, queue_docs, false_pairs, positive_rows
):
    scores = contract_cols(queries, keys_hat) / TAU
    seq_docs = lax.dynamic_slice_in_dim(doc_ids, seq_index, 1, 0)
    pairs = lax.dynamic_slice_in_dim(false_pairs, seq_index, 1, 0)
    chosen = lax.dynamic_slice_in_dim(positive_rows, seq_index, 1, 0)
    column_docs = queue_docs
    target = column_ids[None, :] == chosen[:, None]
    blocked = (column_docs[None, :] == seq_docs[:, None]) | jnp.any(
        pairs[:, :, None] == column_ids[None, None, :], axis=1
    )
    blocked = blocked & jnp.logical_not(target)
    masked = jnp.where(blocked, NEGATIVE, scores)
    top = jnp.max(masked, axis=-1)
    total = jnp.sum(jnp.exp(masked - top[:, None]), axis=-1)
    chosen_score = jnp.sum(jnp.where(target, scores, 0.0), axis=-1)
    return (masked, target.astype(WIDE), top, total, chosen_score)


def per_device(
    token_ids,
    seq_lengths,
    mask_slots,
    mask_targets,
    positive_rows,
    doc_ids,
    false_pairs,
    queue_docs,
    queue_embed,
    attend_weight,
    attend_moment,
    gate_up,
    gate_up_moment,
    down_weight,
    down_moment,
    embed_table,
    embed_moment,
    gains,
    gains_moment,
    attend_error,
    gate_up_error,
    down_error,
    embed_error,
    factors,
):
    tensor_count = lax.axis_size("tensor")
    tensor_rank = lax.axis_index("tensor")
    data_count = lax.axis_size("dp")
    data_rank = lax.axis_index("dp")
    groups, seq_len = token_ids.shape
    width = gains.shape[1]
    total_rows = groups * seq_len
    own_rows = total_rows // tensor_count
    slot_count = mask_slots.shape[2]
    seq_total = groups * data_count
    near = jnp.arange(tensor_count) ^ tensor_rank
    row_count = attend_weight.shape[0]

    attend_cols = attend_error.shape[2]
    quarter = lax.dynamic_slice_in_dim(attend_weight, tensor_rank * attend_cols, attend_cols, 1)
    table_b = lax.all_gather(embed_table.astype(NARROW), "dp", axis=0, tiled=True)
    quarter_b = lax.all_gather(quarter.astype(NARROW), "dp", axis=0, tiled=True)
    attend_near = picked_blocks(spread_blocks(quarter_b, "tensor"), near)
    attend_b = jnp.concatenate([attend_near[k] for k in range(tensor_count)], axis=1)
    ff_own = gate_up.shape[2]
    gate_b = lax.all_gather(
        gate_up.astype(NARROW).reshape(row_count, -1), "dp", axis=0, tiled=True
    )
    down_b = lax.all_gather(down_weight.astype(NARROW), "dp", axis=0, tiled=True)
    queue_all = lax.all_gather(queue_embed, "dp", axis=0, tiled=True)

    every_rows = mask_slots + own_rows * jnp.arange(tensor_count)[None, :, None]
    every_len = seq_lengths[:, None, None]
    count = jnp.sum((every_rows < every_len).astype(WIDE))
    my_length = lax.dynamic_index_in_dim(seq_lengths, data_rank, 0, keepdims=False)
    group_valid = lax.dynamic_index_in_dim(
        every_rows < every_len, data_rank, 0, keepdims=False
    )
    own_slots = lax.dynamic_index_in_dim(
        lax.dynamic_index_in_dim(mask_slots, data_rank, 0, keepdims=False),
        tensor_rank,
        0,
        keepdims=False,
    )
    valid_rows = picked_blocks(group_valid, near).reshape(-1).astype(WIDE)
    near_targets = picked_blocks(mask_targets[0], near).reshape(-1)
    near_tokens = picked_blocks(token_ids.reshape(tensor_count, own_rows), near).reshape(-1)
    places = (near[:, None] * own_rows + jnp.arange(own_rows)[None, :]).reshape(-1)
    tables = rotary_tables(places)
    own_tables = tuple(table[:own_rows] for table in tables)
    bias = jnp.broadcast_to(
        jnp.where(places < my_length, 0.0, NEGATIVE).astype(NARROW)[:, None], (total_rows, PAIR)
    )
    keep_own = (places[:own_rows] < my_length)[:, None]

    vocab_own = table_b.shape[1]
    vocab_start = tensor_rank * vocab_own
    shifted = near_tokens - vocab_start
    inside = (shifted >= 0) & (shifted < vocab_own)
    safe_ids = jnp.clip(shifted, 0, vocab_own - 1)
    looked = jnp.take(table_b, safe_ids, axis=1).T
    looked = jnp.where(inside[:, None], looked, jnp.zeros((), NARROW))
    embedded = summed_block(row_blocks(looked, tensor_count), "tensor", NARROW)

    x_zero, norm_zero = jax.vjp(lambda v: layer_norm(v, gains[0]), embedded)
    x_zero_b = x_zero.astype(NARROW)
    x_all_b = jnp.concatenate(spread_blocks(x_zero_b, "tensor"), axis=0)
    scale = HEAD_DIM ** (-0.5)
    queries = project(x_zero_b, attend_b[:, :width], *own_tables, scale)
    keys = project(x_all_b, attend_b[:, width : 2 * width], *tables, 1.0)
    values = jnp.dot(
        x_all_b, attend_b[:, 2 * width : 3 * width], preferred_element_type=WIDE
    ).astype(NARROW)
    attended_t, log_total = attention_forward(queries, keys, values, bias)
    attended_b = attended_t.astype(NARROW)
    branch = contract_rows(attended_b, attend_b[:, 3 * width :])
    pre_one = x_zero + branch
    hidden_in, norm_one = jax.vjp(lambda v: layer_norm(v, gains[1]), pre_one)
    hidden_b = jnp.concatenate(spread_blocks(hidden_in.astype(NARROW), "tensor"), axis=0)
    gate = jnp.dot(hidden_b, gate_b[:, :ff_own], preferred_element_type=WIDE)
    up = jnp.dot(hidden_b, gate_b[:, ff_own:], preferred_element_type=WIDE)
    activated, act_back = jax.vjp(swiglu, gate, up)
    activated_b = activated.astype(NARROW)
    ffn_part = contract_cols(activated_b, down_b)
    ffn_own = summed_block(row_blocks(ffn_part, tensor_count), "tensor", NARROW)
    pre_out = hidden_in + ffn_own
    final, norm_two = jax.vjp(lambda v: layer_norm(v, gains[2]), pre_out)

    pool_part = jnp.sum(jnp.where(keep_own, final, 0.0), axis=0)
    picked = jnp.take(final, own_slots, axis=0).astype(NARROW)
    rows_all = jnp.concatenate(spread_blocks(picked, "tensor"), axis=0)
    logits = jnp.dot(rows_all, table_b, preferred_element_type=WIDE)
    targets = near_targets - vocab_start
    hits = jnp.arange(vocab_own)[None, :] == targets[:, None]
    target_logit = jnp.sum(jnp.where(hits, logits, 0.0), axis=-1)
    top = jnp.max(logits, axis=-1)
    total = jnp.sum(jnp.exp(logits - top[:, None]), axis=-1)
    picks = rows_all.shape[0]
    stats = jnp.stack([top, total, target_logit]).reshape(3, tensor_count, slot_count)
    pooled_sum = pool_part
    for bit in axis_bits("tensor"):
        flat = jnp.concatenate([stats.reshape(-1), pooled_sum])
        other = swap(flat, "tensor", bit)
        theirs = other[: 3 * picks].reshape(3, tensor_count, slot_count)
        theirs = jnp.stack([theirs[:, k ^ bit] for k in range(tensor_count)], axis=1)
        peak = jnp.maximum(stats[0], theirs[0])
        stats = jnp.stack(
            [
                peak,
                stats[1] * jnp.exp(stats[0] - peak) + theirs[1] * jnp.exp(theirs[0] - peak),
                stats[2] + theirs[2],
            ]
        )
        pooled_sum = pooled_sum + other[3 * picks :]
    top_all, total_all, target_all = stats.reshape(3, picks)
    log_all = top_all + jnp.log(total_all)
    row_weight = valid_rows / count
    cross = valid_rows * (log_all - target_all)
    masked_part = jnp.sum(cross[:slot_count])
    dlogits = (
        (jnp.exp(logits - log_all[:, None]) - hits.astype(WIDE)) * row_weight[:, None]
    ).astype(NARROW)
    row_grad = summed_block(
        row_blocks(contract_cols(dlogits, table_b), tensor_count), "tensor", NARROW
    )

    pooled = (pooled_sum / my_length.astype(WIDE))[None]
    embedding, embed_back = jax.vjp(
        lambda v: v * lax.rsqrt(jnp.sum(v * v, axis=-1, keepdims=True) + EPS), pooled
    )
    embedding_b = embedding.astype(NARROW)
    weight_c = LAMBDA / seq_total
    first_rank = jnp.where(tensor_rank == 0, 1.0, 0.0)
    keys_hat = normalize_keys(queue_all)
    masked, target, top_c, total_c, chosen_c = contrast_terms(
        embedding_b,
        keys_hat,
        data_rank,
        jnp.arange(keys_hat.shape[0]),
        doc_ids,
        queue_docs,
        false_pairs,
        positive_rows,
    )
    log_c = top_c + jnp.log(total_c)
    contrast_part = jnp.sum(log_c - chosen_c) * weight_c * first_rank
    dscores = ((jnp.exp(masked - log_c[:, None]) - target) * (weight_c / TAU)).astype(NARROW)
    embed_grad = jnp.dot(dscores, keys_hat, preferred_element_type=WIDE)
    pooled_grad = embed_back(embed_grad)[0] / my_length.astype(WIDE)

    final_grad = jnp.where(keep_own, pooled_grad, 0.0)
    final_grad = final_grad.at[own_slots].add(row_grad)
    pre_grad = norm_two(final_grad)[0]
    gain_two = jnp.sum(final_grad * layer_norm(pre_out, 1.0), axis=0)
    ffn_grad = jnp.concatenate(spread_blocks(pre_grad.astype(NARROW), "tensor"), axis=0)
    act_grad = jnp.dot(ffn_grad, down_b, preferred_element_type=WIDE)
    gate_grad, up_grad = (part.astype(NARROW) for part in act_back(act_grad))
    hidden_part = contract_cols(gate_grad, gate_b[:, :ff_own]) + contract_cols(
        up_grad, gate_b[:, ff_own:]
    )
    hidden_sum = summed_block(row_blocks(hidden_part, tensor_count), "tensor", NARROW)
    hidden_grad = hidden_sum + pre_grad
    down_grad = contract_rows(ffn_grad, activated_b)
    gate_w_grad = contract_rows(hidden_b, gate_grad)
    up_w_grad = contract_rows(hidden_b, up_grad)
    pre_one_grad = norm_one(hidden_grad)[0]
    gain_one = jnp.sum(hidden_grad * layer_norm(pre_one, 1.0), axis=0)
    branch_grad = pre_one_grad.astype(NARROW)
    attended_grad = contract_cols(branch_grad, attend_b[:, 3 * width :]).astype(NARROW)
    dq, dk, dv = attention_backward(
        queries, keys, values, bias, attended_grad, attended_t, log_total, tables, own_tables
    )
    x_part = contract_cols(dk, attend_b[:, width : 2 * width]) + contract_cols(
        dv, attend_b[:, 2 * width : 3 * width]
    )
    x_sum = summed_block(row_blocks(x_part, tensor_count), "tensor", NARROW)
    x_zero_grad = pre_one_grad + contract_cols(dq, attend_b[:, :width]) + x_sum
    embedded_grad = norm_zero(x_zero_grad)[0]
    gain_zero = jnp.sum(x_zero_grad * layer_norm(embedded, 1.0), axis=0)
    emb_all = jnp.concatenate(
        spread_blocks(embedded_grad.astype(NARROW), "tensor"), axis=0
    )
    attend_part = jnp.concatenate(
        [
            contract_rows(x_zero_b, dq),
            contract_rows(x_all_b, dk),
            contract_rows(x_all_b, dv),
            jnp.dot(attended_b, branch_grad, preferred_element_type=WIDE),
        ],
        axis=1,
    )
    attend_blocks = jnp.moveaxis(attend_part.reshape(width, tensor_count, attend_cols), 1, 0)
    attend_blocks = picked_blocks(attend_blocks, near)
    attend_grad = summed_block([attend_blocks[k] for k in range(tensor_count)], "tensor", WIDE)

    factor_t = jnp.swapaxes(factors, 1, 2)
    table_high, table_low, table_p = table_matrix(
        emb_all, shifted[None, :], rows_all, dlogits, embed_error[0].T, factor_t[4]
    )
    small_m, small_p = small_matrices(
        [attend_grad, gate_w_grad, up_w_grad, down_grad],
        [attend_error[0], gate_up_error[0, :, 0], gate_up_error[0, :, 1], down_error[0]],
        factor_t[:4],
    )
    parts = [small_p[k] for k in range(4)] + [table_p]
    spans, start = [], 0
    for part in parts:
        spans.append((start, part.shape[1]))
        start += part.shape[1]
    sums = summed_all(jnp.concatenate(parts, axis=1), "dp")
    bases_t = bases_of(sums, spans)
    small_basis = jnp.stack([bases_t[:, at : at + size] for at, size in spans[:4]])
    table_basis = bases_t[:, spans[4][0] :]
    small_back = small_backs(small_m, small_basis)
    tab_back = table_back(table_high, table_low, table_basis)
    gain_terms = jnp.stack([gain_zero, gain_one, gain_two])
    loss_terms = jnp.stack([masked_part, contrast_part])
    loss_row = jnp.zeros((1, width), WIDE).at[0, :2].set(loss_terms)
    packed = jnp.concatenate(
        [small_back.reshape(-1, width), tab_back, gain_terms, loss_row], axis=0
    )
    packed = summed_all(packed, "dp")
    errors = small_errors(small_m, small_back, small_basis)
    new_table_error = table_error(table_high, table_low, tab_back, table_basis, vocab_own).T
    own_t = packed[: 5 * RANK].reshape(5, RANK, width)
    square = jnp.sum(own_t * own_t)
    tail = packed[5 * RANK :].at[3, 2].set(square)
    shared = jnp.concatenate(
        [own_t[0], tail, jnp.pad(small_basis[0], ((0, 0), (0, width - attend_cols)))], axis=0
    )
    shared = picked_blocks(spread_blocks(shared, "tensor"), near)
    tail_sum = jnp.sum(shared[:, RANK : RANK + 4], axis=0)
    gains_grad = tail_sum[:3]
    loss_sums = tail_sum[3, :2]
    clip_norm = jnp.sqrt(tail_sum[3, 2] + jnp.sum(gains_grad * gains_grad))
    shrink = CLIP / jnp.maximum(clip_norm, CLIP)
    row_start = data_rank * row_count

    def rows_of(factor):
        return lax.dynamic_slice_in_dim(factor, row_start, row_count, factor.ndim - 1)

    reduced_attend = jnp.einsum(
        "tkd,tkn->dtn",
        rows_of(shared[:, :RANK]),
        shared[:, RANK + 4 :, :attend_cols],
        precision=HIGH,
    ).reshape(row_count, -1)
    own_rows_t = rows_of(own_t)

    def reduced(index, basis):
        return dot_in(own_rows_t[index], basis, ((0,), (0,)), precision=HIGH)

    reduced_gate_up = jnp.stack(
        [reduced(1, small_basis[1]), reduced(2, small_basis[2])], axis=1
    )
    reduced_down = reduced(3, small_basis[3])
    reduced_table = reduced(4, table_basis[:, :vocab_own])

    def advance(weight, moment, grad):
        fresh = MOMENTUM * moment + shrink * grad
        return (weight - LRATE * fresh, fresh)

    new_attend, new_attend_moment = advance(attend_weight, attend_moment, reduced_attend)
    new_gate_up, new_gate_up_moment = advance(gate_up, gate_up_moment, reduced_gate_up)
    new_down, new_down_moment = advance(down_weight, down_moment, reduced_down)
    new_table, new_table_moment = advance(embed_table, embed_moment, reduced_table)
    new_gains, new_gains_moment = advance(gains, gains_moment, gains_grad)
    return (
        new_attend,
        new_attend_moment,
        new_gate_up,
        new_gate_up_moment,
        new_down,
        new_down_moment,
        new_table,
        new_table_moment,
        new_gains,
        new_gains_moment,
        errors[0][None],
        jnp.stack([errors[1], errors[2]], axis=1)[None],
        errors[3][None],
        new_table_error[None],
        jnp.swapaxes(own_t, 1, 2),
        clip_norm,
        loss_sums[0],
        count,
        loss_sums[1],
    )


def solution(mesh):
    in_specs = (
        P("dp", None),
        P(),
        P(),
        P("dp", None, None),
        P(),
        P(),
        P(),
        P(),
        P("dp", None),
        P("dp", None),
        P("dp", None),
        P("dp", None, "tensor"),
        P("dp", None, "tensor"),
        P("dp", "tensor"),
        P("dp", "tensor"),
        P("dp", "tensor"),
        P("dp", "tensor"),
        P(),
        P(),
        P("dp", None, "tensor"),
        P("dp", None, None, "tensor"),
        P("dp", None, "tensor"),
        P("dp", None, "tensor"),
        P(None, None, "tensor"),
    )
    out_specs = (
        P("dp", None),
        P("dp", None),
        P("dp", None, "tensor"),
        P("dp", None, "tensor"),
        P("dp", "tensor"),
        P("dp", "tensor"),
        P("dp", "tensor"),
        P("dp", "tensor"),
        P(),
        P(),
        P("dp", None, "tensor"),
        P("dp", None, None, "tensor"),
        P("dp", None, "tensor"),
        P("dp", None, "tensor"),
        P(None, None, "tensor"),
        P(),
        P(),
        P(),
        P(),
    )
    return jax.shard_map(
        per_device, mesh=mesh, in_specs=in_specs, out_specs=out_specs, check_vma=False
    )
```

time: 2430 us -> 954 us (0.39)
  matrix products: 866 us -> 117 us
  other arithmetic: 532 us -> 86.1 us
  waiting for transfers between devices: 667 us -> 360 us
  Pallas kernels: 0 us -> 209 us
  local copies, waits for them, and re-layouts: 257 us -> 111 us
  blocking collectives: 61.3 us -> 0 us
  starting transfers between devices: 1.18 us -> 30.2 us
    dot_general x62 -> x25, matrix products: 847 us -> 96.9 us  [the longest x20 74.7 us: dot_in(): lax.dot_general(left, right, (axes, ((), ())), precision=precision, prefe...]
    psum x4 -> x0, waiting for transfers between devices: 341 us -> none  [the longest x1 111 us: per_device(): lax.psum((slotted(jnp.stack(backs)), gain_terms, loss_terms), ('dp', 'ten...]
    pallas_call x0 -> x11, Pallas kernels: none -> 209 us  [the longest x1 50.2 us: table_matrix(): pl.pallas_call(functools.partial(table_kernel, columns), grid=(tiles,), i...]
    convert_element_type x8 -> x12, other arithmetic: 194 us -> 13.2 us  [the longest x5 7.36 us: summed_block(): got = swap(held.pop(key ^ bit).astype(kind), axis, bit)]
    ppermute x0 -> x47, waiting for transfers between devices: none -> 174 us  [swap(): lax.ppermute(value, axis, [(index, index ^ bit) for index in range(size)])]
    reduce_sum x56 -> x8, other arithmetic: 147 us -> 6.2 us  [the longest x1 1.39 us: per_device(): total = jnp.sum(jnp.exp(logits - top[:, None]), axis=-1)]
    all_gather x3 -> x2, waiting for transfers between devices: 107 us -> 4.97 us  [the longest x1 4.95 us: per_device(): quarter_b = lax.all_gather(quarter.astype(NARROW), 'dp', axis=0, tiled=True)]
    reshape x10 -> x5, local copies, waits for them, and re-layouts: 56.7 us -> 0.36 us  [the longest x2 0.18 us: per_device(): theirs = other[:3 * picks].reshape(3, tensor_count, slot_count)]
  transfers between devices with their start and end apart: 12 -> 52, of which waited for: 9 -> 25; matrix products, arithmetic and copies ran while one was open for 21% -> 20% of each run, Pallas kernels for 0% -> 13%
where the time goes in v1:
time: 954 us; the launch traced here: 944 us
  waiting for transfers between devices  360 us (38%)
  Pallas kernels  209 us (22%)
  matrix products  117 us (12%)
  local copies, waits for them, and re-layouts  111 us (12%)
  other arithmetic  86.1 us (9%)
  between operations  30.6 us (3%)
  starting transfers between devices  30.2 us (3%)
    ppermute x47, waiting for transfers between devices, swap(): lax.ppermute(value, axis, [(index, index ^ bit) for index in range(size)])  174 us
    all_gather x1, waiting for transfers between devices, per_device(): lax.all_gather(embed_table.astype(NARROW), 'dp', axis=0, tiled=True)  158 us
    dot_general x20, matrix products, dot_in(): lax.dot_general(left, right, (axes, ((), ())), precision=precision, prefe...  74.7 us
    pallas_call x1, Pallas kernels, table_matrix(): pl.pallas_call(functools.partial(table_kernel, columns), grid=(tiles,), i...  50.2 us
    pallas_call x1, Pallas kernels, attention_backward(): pl.pallas_call(attend_back_kernel, grid=(pairs, 2), in_specs=[own_block,...  47.2 us
    unnamed x175, local copies, waits for them, and re-layouts  38.4 us
    ppermute x47, starting transfers between devices, swap(): lax.ppermute(value, axis, [(index, index ^ bit) for index in range(size)])  29.6 us
    pallas_call x1, Pallas kernels, attention_forward(): pl.pallas_call(attend_kernel, grid=(pairs, 2), in_specs=[pl.BlockSpec((ro...  24.1 us
  transfers between devices with their start and end apart: 52, of which 25 were waited for; matrix products, arithmetic and copies ran while one was open for 20% of the time, Pallas kernels for 13%

profile of v1, /device:TPU:0, one launch (start us, length us, event | category | flops | bytes accessed | tf_op | source)
XLA Modules:
  0.0 943.8 jit_solution(13889888257609982984)
XLA Ops:
  22.0 158.4 %all-gather.6.cloned.1.call-done = bf16[768,7632]{1,0:T(8,128)(2,1)} async-done(((bf16[96,7632]{1,0:T(8,128)(2,1)}), bf16[768,7632]{1,0:T(8,128)(2,1)}) %all-gather.6.cloned.1.call-update) | async-done | bytes 11722768 | tf_op jit(solution)/shard_map/all_gather | solution.py:627
  180.4 16.2 %copy.96 = bf16[768,7632]{0,1:T(8,128)(2,1)} copy(bf16[768,7632]{1,0:T(8,128)(2,1)} %all-gather.6.cloned.1.call-done) | data formatting | bytes 23445504 | tf_op jit(solution)/shard_map/all_gather | solution.py:627
  196.6 15.9 %gather_fusion = bf16[2048,768]{1,0:T(8,128)(2,1)} fusion(bf16[768,7632]{0,1:T(8,128)(2,1)} %copy.96, s32[2048]{0:T(1024)S(1)} %broadcast_clamp_fusion), kind=kCustom, calls=%fused_computation | custom fusion | bytes 6299648 | tf_op jit(solution)/shard_map/jit(_take)/gather | solution.py:667
  217.5 5.0 all-gather.8.cloned.1.call-done
  228.0 23.6 %collective-permute-done.4 = bf16[768,768]{1,0:T(8,128)(2,1)} collective-permute-done((bf16[768,768]{1,0:T(8,128)(2,1)}, bf16[768,768]{1,0:T(8,128)(2,1)}, u32[]{:S(2)}, u32[]{:S(2)}) %collective-permute-start.4) | collective-permute-done | bytes 1179680 | tf_op jit(solution)/shard_map/ppermute | solution.py:41
  251.6 14.3 %collective-permute-done.2 = bf16[512,768]{1,0:T(8,128)(2,1)S(1)} collective-permute-done((bf16[512,768]{1,0:T(8,128)(2,1)}, bf16[512,768]{1,0:T(8,128)(2,1)S(1)}, u32[]{:S(2)}, u32[]{:S(2)}) %collective-permute-start.2) | collective-permute-done | bytes 786464 | tf_op jit(solution)/shard_map/ppermute | solution.py:41
  276.5 9.0 collective-permute-done.7
  292.0 4.5 shard_map.375.q_ref
  296.5 7.5 pad_maximum_fusion.2.x_ref
  304.0 13.0 %shard_map.376.k_ref = bf16[2048,768]{1,0:T(8,128)(2,1)} custom-call(bf16[2048,768]{1,0:T(8,128)(2,1)} %pad_maximum_fusion.2.x_ref, bf16[768,768]{1,0:T(8,128)(2,1)} %get-tuple-element.193.w_ref, f32[2048,128]{1,0:T(8,128)} %copy-done.27, f32[2048,128]{1,0:T(8,128)} %copy-done.26), custom_call_target="tpu_custom_call" | custom-call | flops 2415919104 | bytes 7471104 | tf_op jit(solution)/shard_map/pallas_call | solution.py:143
  317.0 6.2 convolution_convert_fusion.v_ref
  324.3 24.1 %shard_map.377 = (f32[768,512]{1,0:T(8,128)}, f32[6,2,512]{2,1,0:T(2,128)}) custom-call(bf16[512,768]{1,0:T(8,128)(2,1)} %shard_map.375.q_ref, bf16[2048,768]{1,0:T(8,128)(2,1)} %shard_map.376.k_ref, bf16[2048,768]{1,0:T(8,128)(2,1)} %convolution_convert_fusion.v_ref, bf16[2048,128]{1,0:T(8,128)(2,1)} %broadcast_in_dim.167.bias_ref), custom_call_target="tpu_custom_call" | custom-call | flops 3221225472 | bytes 9437184 | tf_op jit(solution)/shard_map/pallas_call | solution.py:212
  354.0 18.6 %collective-permute-done.10 = bf16[512,768]{1,0:T(8,128)(2,1)} collective-permute-done((bf16[512,768]{1,0:T(8,128)(2,1)}, bf16[512,768]{1,0:T(8,128)(2,1)}, u32[]{:S(2)}, u32[]{:S(2)}) %collective-permute-start.10) | collective-permute-done | bytes 786464 | tf_op jit(solution)/shard_map/ppermute | solution.py:41
  375.2 4.9 fusion.29
  382.8 8.9 multiply_convert_fusion.1
  391.6 22.3 %all-gather.12.cloned.1.call-done = bf16[768,768]{1,0:T(8,128)(2,1)} async-done(((bf16[96,768]{1,0:T(8,128)(2,1)}), bf16[768,768]{1,0:T(8,128)(2,1)}) %all-gather.12.cloned.1.call-update) | async-done | bytes 1179664 | tf_op jit(solution)/shard_map/all_gather | solution.py:635
  413.9 7.5 fusion.141
  433.0 14.8 %collective-permute-done.14 = bf16[512,768]{1,0:T(8,128)(2,1)} collective-permute-done((bf16[512,768]{1,0:T(8,128)(2,1)}, bf16[512,768]{1,0:T(8,128)(2,1)}, u32[]{:S(2)}, u32[]{:S(2)}) %collective-permute-start.14) | collective-permute-done | bytes 786464 | tf_op jit(solution)/shard_map/ppermute | solution.py:41
  460.3 6.8 fusion.142
  487.8 3.9 multiply_convert_fusion.2.dlogits_ref
  491.7 9.4 fusion.143
  517.5 17.0 %collective-permute-done.24 = bf16[512,768]{1,0:T(8,128)(2,1)S(1)} collective-permute-done((bf16[512,768]{1,0:T(8,128)(2,1)S(1)}, bf16[512,768]{1,0:T(8,128)(2,1)S(1)}, u32[]{:S(2)}, u32[]{:S(2)}) %collective-permute-start.24) | collective-permute-done | bytes 786464 | tf_op jit(solution)/shard_map/ppermute | solution.py:41
  536.8 11.9 %multiply_convert_fusion = (bf16[2048,768]{1,0:T(8,128)(2,1)S(1)}, bf16[2048,768]{1,0:T(8,128)(2,1)S(1)}) fusion(f32[2048,768]{1,0:T(8,128)} %copy-done.75, f32[2048,768]{1,0:T(8,128)} %get-tuple-element.259, bf16[768,768]{1,0:T(8,128)(2,1)S(1)} %copy-done.62, bf16[512,768]{1,0:T(8,128)(2,1)S(1)} %collective-permute-done.25, ...), kind=kOutput, calls=%fused_computation.10 | convolution fusion | flops 2450522112 | bytes 23199744 | tf_op jit(solution)/shard_map/dot_general | solution.py:762
  555.6 10.0 %fusion.130 = (f32[1,768,1,768]{3,2,1,0:T(1,128)}, f32[1,768,1,768]{3,2,1,0:T(1,128)}) fusion(f32[1,768,2,768]{3,2,1,0:T(2,128)} %param.48), kind=kLoop, calls=%fused_computation.317 | loop fusion | bytes 9437184 | tf_op jit(solution)/shard_map/slice | solution.py:808
  569.6 4.2 copy_bitcast_fusion
  574.6 12.5 %collective-permute-done.28 = bf16[512,768]{1,0:T(8,128)(2,1)S(1)} collective-permute-done((bf16[512,768]{1,0:T(8,128)(2,1)S(1)}, bf16[512,768]{1,0:T(8,128)(2,1)S(1)}, u32[]{:S(2)}, u32[]{:S(2)}) %collective-permute-start.28) | collective-permute-done | bytes 786464 | tf_op jit(solution)/shard_map/ppermute | solution.py:41
  593.6 47.2 %shard_map.378 = (bf16[512,768]{1,0:T(8,128)(2,1)}, bf16[2048,768]{1,0:T(8,128)(2,1)}, bf16[2048,768]{1,0:T(8,128)(2,1)}) custom-call(bf16[512,768]{1,0:T(8,128)(2,1)} %shard_map.375.q_ref, bf16[2048,768]{1,0:T(8,128)(2,1)} %shard_map.376.k_ref, bf16[2048,768]{1,0:T(8,128)(2,1)} %convolution_convert_fusion.v_ref, ...), custom_call_target="tpu_custom_call" | custom-call | flops 8053063680 | bytes 15728640 | tf_op jit(solution)/shard_map/pallas_call | solution.py:298
  640.8 6.2 fusion.148
  647.0 4.1 fusion.20
  671.0 10.4 %collective-permute-done.34 = bf16[512,768]{1,0:T(8,128)(2,1)} collective-permute-done((bf16[512,768]{1,0:T(8,128)(2,1)}, bf16[512,768]{1,0:T(8,128)(2,1)}, u32[]{:S(2)}, u32[]{:S(2)}) %collective-permute-start.34) | collective-permute-done | bytes 786464 | tf_op jit(solution)/shard_map/ppermute | solution.py:41
  687.7 5.9 fusion.118.refs_1_
  693.6 6.1 fusion.117.refs_2_
  699.8 5.6 collective-permute-done.36
  705.4 4.2 fusion.39.refs_3_
  725.4 50.2 %shard_map.380 = (bf16[7680,768]{1,0:T(8,128)(2,1)}, bf16[7680,768]{1,0:T(8,128)(2,1)}, f32[8,7680]{1,0:T(8,128)}) custom-call(bf16[2048,768]{1,0:T(8,128)(2,1)} %pad_maximum_fusion.5.left_ref, s32[1,2048]{1,0:T(1,128)} %bitcast.222, bf16[160,768]{1,0:T(8,128)(2,1)} %pad_maximum_fusion.9.rows_ref, bf16[160,7632]{1,0:T(8,128)(2,1)} %copy-done.19, ...), custom_call_target="tpu_custom_call" | custom-call | flops 26165182464 | bytes 46891008 | tf_op jit(solution)/shard_map/pallas_call | solution.py:384
  775.6 4.4 fusion.7.refs_0_
  780.0 12.0 %shard_map.379 = (f32[4,768,768]{2,1,0:T(8,128)}, f32[4,8,768]{2,1,0:T(8,128)}) custom-call(f32[768,768]{1,0:T(8,128)} %fusion.7.refs_0_, f32[768,768]{1,0:T(8,128)} %fusion.118.refs_1_, f32[768,768]{1,0:T(8,128)} %fusion.117.refs_2_, f32[768,768]{1,0:T(8,128)} %fusion.39.refs_3_, f32[768,768]{1,0:T(8,128)} %bitcast.198, ...), custom_call_target="tpu_custom_call" | custom-call | flops 113246208 | bytes 28311552 | tf_op jit(solution)/shard_map/pallas_call | solution.py:425
  795.8 9.0 collective-permute-done.38
  805.9 7.8 collective-permute-done.39
  818.4 11.6 %collective-permute-done.40 = f32[8,10752]{1,0:T(8,128)S(1)} collective-permute-done((f32[8,10752]{1,0:T(8,128)S(1)}, f32[8,10752]{1,0:T(8,128)S(1)}, u32[]{:S(2)}, u32[]{:S(2)}) %collective-permute-start.40) | collective-permute-done | bytes 344096 | tf_op jit(solution)/shard_map/ppermute | solution.py:41
  830.7 4.2 shard_map.381
  838.0 6.9 shard_map.382.back_ref
  844.9 14.9 %shard_map.383.back_ref = f32[8,768]{1,0:T(8,128)} custom-call(bf16[7680,768]{1,0:T(8,128)(2,1)} %get-tuple-element.65.high_ref, bf16[7680,768]{1,0:T(8,128)(2,1)} %get-tuple-element.66.low_ref, f32[8,7680]{1,0:T(8,128)} %slice.450.basis_ref), custom_call_target="tpu_custom_call" | custom-call | flops 283115520 | bytes 23592960 | tf_op jit(solution)/shard_map/pallas_call | solution.py:501
  861.4 4.5 collective-permute-done.41
  866.0 8.0 shard_map.384
  880.1 5.8 copy.113
  885.9 23.8 %shard_map.385 = f32[7632,768]{1,0:T(8,128)} custom-call(bf16[7680,768]{1,0:T(8,128)(2,1)} %get-tuple-element.65.high_ref, bf16[7680,768]{1,0:T(8,128)(2,1)} %get-tuple-element.66.low_ref, f32[8,768]{1,0:T(8,128)} %shard_map.383.back_ref, f32[8,7680]{1,0:T(8,128)} %slice.450.basis_ref), custom_call_target="tpu_custom_call" | custom-call | flops 281346048 | bytes 46891008 | tf_op jit(solution)/shard_map/pallas_call | solution.py:541
  930.2 5.7 multiply_subtract_fusion
  (441 shorter events, 204.5 us)
Async XLA Ops:
  7.2 173.2 %all-gather.6.cloned.1.call-start = ((), (), s32[]{:S(2)}) async-start(), calls=%async_computation | async-start | bytes 13271040 | tf_op jit(solution)/shard_map/all_gather | solution.py:627
  10.4 212.0 %all-gather.8.cloned.1.call-start = ((), (), s32[]{:S(2)}) async-start(), calls=%async_computation.1 | async-start | bytes 1327104 | tf_op jit(solution)/shard_map/all_gather | solution.py:628
  12.1 361.7 %all-gather.10.cloned.1.call-start = ((), (), s32[]{:S(2)}) async-start(), calls=%async_computation.2 | async-start | bytes 2654208 | tf_op jit(solution)/shard_map/all_gather | solution.py:632
  217.5 6.4 collective-permute-start.1
  222.4 29.2 %collective-permute-start.4 = (bf16[768,768]{1,0:T(8,128)(2,1)}, bf16[768,768]{1,0:T(8,128)(2,1)}, u32[]{:S(2)}, u32[]{:S(2)}) collective-permute-start(bf16[768,768]{1,0:T(8,128)(2,1)} %all-gather.8.cloned.1.call-done), channel_id=1, source_target_pairs={{0,2},{1,3},{2,0},{3,1},{4,6},{5,7},{6,4},{7,5},{8,10},{9,11},{10,... | collective-permute-start | bytes 3538952 | tf_op jit(solution)/shard_map/ppermute | solution.py:41
  223.9 27.8 %collective-permute-start = (bf16[512,768]{1,0:T(8,128)(2,1)}, bf16[512,768]{1,0:T(8,128)(2,1)S(1)}, u32[]{:S(2)}, u32[]{:S(2)}) collective-permute-start(bf16[512,768]{1,0:T(8,128)(2,1)} %get-tuple-element.201), channel_id=1, source_target_pairs={{0,1},{1,0},{2,3},{3,2},{4,5},{5,4},{6,7},{7,6},{8,9},{9,8},{10,11... | collective-permute-start | bytes 2359304 | tf_op jit(solution)/shard_map/ppermute | solution.py:41
  226.1 39.8 %collective-permute-start.2 = (bf16[512,768]{1,0:T(8,128)(2,1)}, bf16[512,768]{1,0:T(8,128)(2,1)S(1)}, u32[]{:S(2)}, u32[]{:S(2)}) collective-permute-start(bf16[512,768]{1,0:T(8,128)(2,1)} %add_convert_fusion.1), channel_id=1, source_target_pairs={{0,2},{1,3},{2,0},{3,1},{4,6},{5,7},{6,4},{7,5},{8,10},{9,11},{10,... | collective-permute-start | bytes 2359304 | tf_op jit(solution)/shard_map/ppermute | solution.py:41
  227.6 186.3 %all-gather.12.cloned.1.call-start = ((), (), s32[]{:S(2)}) async-start(), calls=%async_computation.3 | async-start | bytes 1327104 | tf_op jit(solution)/shard_map/all_gather | solution.py:635
  227.7 58.5 %collective-permute-start.3 = (bf16[768,768]{1,0:T(8,128)(2,1)}, bf16[768,768]{1,0:T(8,128)(2,1)}, u32[]{:S(2)}, u32[]{:S(2)}) collective-permute-start(bf16[768,768]{1,0:T(8,128)(2,1)} %all-gather.8.cloned.1.call-done), channel_id=1, source_target_pairs={{0,1},{1,0},{2,3},{3,2},{4,5},{5,4},{6,7},{7,6},{8,9},{9,8},{10,11... | collective-permute-start | bytes 3538952 | tf_op jit(solution)/shard_map/ppermute | solution.py:41
  251.6 34.6 %collective-permute-start.5 = (bf16[768,768]{1,0:T(8,128)(2,1)}, bf16[768,768]{1,0:T(8,128)(2,1)}, u32[]{:S(2)}, u32[]{:S(2)}) collective-permute-start(bf16[768,768]{1,0:T(8,128)(2,1)} %collective-permute-done.4), channel_id=1, source_target_pairs={{0,1},{1,0},{2,3},{3,2},{4,5},{5,4},{6,7},{7,6},{8,9},{9,8},{10,11... | collective-permute-start | bytes 3538952 | tf_op jit(solution)/shard_map/ppermute | solution.py:41
  268.1 17.4 %collective-permute-start.7 = (bf16[512,768]{1,0:T(8,128)(2,1)S(1)}, bf16[512,768]{1,0:T(8,128)(2,1)}, u32[]{:S(2)}, u32[]{:S(2)}) collective-permute-start(bf16[512,768]{1,0:T(8,128)(2,1)S(1)} %multiply_convert_fusion.4.x_ref), channel_id=1, source_target_pairs={{0,2},{1,3},{2,0},{3,1},{4,6},{5,7},{6,4},{7,5},{8,10},{9,11},{10,... | collective-permute-start | bytes 2359304 | tf_op jit(solution)/shard_map/ppermute | solution.py:41
  276.4 20.0 %collective-permute-start.6 = (bf16[512,768]{1,0:T(8,128)(2,1)S(1)}, bf16[512,768]{1,0:T(8,128)(2,1)S(1)}, u32[]{:S(2)}, u32[]{:S(2)}) collective-permute-start(bf16[512,768]{1,0:T(8,128)(2,1)S(1)} %multiply_convert_fusion.4.x_ref), channel_id=1, source_target_pairs={{0,1},{1,0},{2,3},{3,2},{4,5},{5,4},{6,7},{7,6},{8,9},{9,8},{10,11... | collective-permute-start | bytes 2359304 | tf_op jit(solution)/shard_map/ppermute | solution.py:41
  285.5 11.0 %collective-permute-start.8 = (bf16[512,768]{1,0:T(8,128)(2,1)}, bf16[512,768]{1,0:T(8,128)(2,1)S(1)}, u32[]{:S(2)}, u32[]{:S(2)}) collective-permute-start(bf16[512,768]{1,0:T(8,128)(2,1)} %collective-permute-done.7), channel_id=1, source_target_pairs={{0,1},{1,0},{2,3},{3,2},{4,5},{5,4},{6,7},{7,6},{8,9},{9,8},{10,11... | collective-permute-start | bytes 2359304 | tf_op jit(solution)/shard_map/ppermute | solution.py:41
  352.3 20.3 %collective-permute-start.10 = (bf16[512,768]{1,0:T(8,128)(2,1)}, bf16[512,768]{1,0:T(8,128)(2,1)}, u32[]{:S(2)}, u32[]{:S(2)}) collective-permute-start(bf16[512,768]{1,0:T(8,128)(2,1)} %multiply_convert_fusion.3), channel_id=1, source_target_pairs={{0,2},{1,3},{2,0},{3,1},{4,6},{5,7},{6,4},{7,5},{8,10},{9,11},{10,... | collective-permute-start | bytes 2359304 | tf_op jit(solution)/shard_map/ppermute | solution.py:41
  353.8 20.0 %collective-permute-start.9 = (bf16[512,768]{1,0:T(8,128)(2,1)}, bf16[512,768]{1,0:T(8,128)(2,1)}, u32[]{:S(2)}, u32[]{:S(2)}) collective-permute-start(bf16[512,768]{1,0:T(8,128)(2,1)} %multiply_convert_fusion.3), channel_id=1, source_target_pairs={{0,1},{1,0},{2,3},{3,2},{4,5},{5,4},{6,7},{7,6},{8,9},{9,8},{10,11... | collective-permute-start | bytes 2359304 | tf_op jit(solution)/shard_map/ppermute | solution.py:41
  372.6 2.6 collective-permute-start.11
  373.3 96.3 %all-gather.14.cloned.1.call-start = ((), (), s32[]{:S(2)}) async-start(), calls=%async_computation.4 | async-start | bytes 1769472 | tf_op jit(solution)/shard_map/all_gather | solution.py:636
  422.6 2.6 collective-permute-start.13
  422.7 10.2 %collective-permute-start.12 = (bf16[512,768]{1,0:T(8,128)(2,1)}, bf16[512,768]{1,0:T(8,128)(2,1)}, u32[]{:S(2)}, u32[]{:S(2)}) collective-permute-start(bf16[512,768]{1,0:T(8,128)(2,1)} %get-tuple-element.199), channel_id=1, source_target_pairs={{0,1},{1,0},{2,3},{3,2},{4,5},{5,4},{6,7},{7,6},{8,9},{9,8},{10,11... | collective-permute-start | bytes 2359304 | tf_op jit(solution)/shard_map/ppermute | solution.py:41
  427.9 19.9 %collective-permute-start.14 = (bf16[512,768]{1,0:T(8,128)(2,1)}, bf16[512,768]{1,0:T(8,128)(2,1)}, u32[]{:S(2)}, u32[]{:S(2)}) collective-permute-start(bf16[512,768]{1,0:T(8,128)(2,1)} %fusion.14), channel_id=1, source_target_pairs={{0,2},{1,3},{2,0},{3,1},{4,6},{5,7},{6,4},{7,5},{8,10},{9,11},{10,... | collective-permute-start | bytes 2359304 | tf_op jit(solution)/shard_map/ppermute | solution.py:41
  454.8 4.3 collective-permute-start.16
  469.5 2.2 collective-permute-start.18
  472.1 3.7 collective-permute-start.19
  502.0 3.4 collective-permute-start.20
  502.5 4.4 collective-permute-start.22
  515.9 18.5 %collective-permute-start.24 = (bf16[512,768]{1,0:T(8,128)(2,1)S(1)}, bf16[512,768]{1,0:T(8,128)(2,1)S(1)}, u32[]{:S(2)}, u32[]{:S(2)}) collective-permute-start(bf16[512,768]{1,0:T(8,128)(2,1)S(1)} %add_convert_fusion.3), channel_id=1, source_target_pairs={{0,2},{1,3},{2,0},{3,1},{4,6},{5,7},{6,4},{7,5},{8,10},{9,11},{10,... | collective-permute-start | bytes 2359304 | tf_op jit(solution)/shard_map/ppermute | solution.py:41
  517.5 18.3 %collective-permute-start.23 = (bf16[512,768]{1,0:T(8,128)(2,1)S(1)}, bf16[512,768]{1,0:T(8,128)(2,1)S(1)}, u32[]{:S(2)}, u32[]{:S(2)}) collective-permute-start(bf16[512,768]{1,0:T(8,128)(2,1)S(1)} %add_convert_fusion.3), channel_id=1, source_target_pairs={{0,1},{1,0},{2,3},{3,2},{4,5},{5,4},{6,7},{7,6},{8,9},{9,8},{10,11... | collective-permute-start | bytes 2359304 | tf_op jit(solution)/shard_map/ppermute | solution.py:41
  534.5 2.3 collective-permute-start.25
  555.4 10.5 %collective-permute-start.27 = (bf16[512,768]{1,0:T(8,128)(2,1)}, bf16[512,768]{1,0:T(8,128)(2,1)}, u32[]{:S(2)}, u32[]{:S(2)}) collective-permute-start(bf16[512,768]{1,0:T(8,128)(2,1)} %get-tuple-element.198), channel_id=1, source_target_pairs={{0,1},{1,0},{2,3},{3,2},{4,5},{5,4},{6,7},{7,6},{8,9},{9,8},{10,11... | collective-permute-start | bytes 2359304 | tf_op jit(solution)/shard_map/ppermute | solution.py:41
  565.6 9.0 collective-permute-start.26
  567.5 19.6 %collective-permute-start.28 = (bf16[512,768]{1,0:T(8,128)(2,1)S(1)}, bf16[512,768]{1,0:T(8,128)(2,1)S(1)}, u32[]{:S(2)}, u32[]{:S(2)}) collective-permute-start(bf16[512,768]{1,0:T(8,128)(2,1)S(1)} %fusion.11), channel_id=1, source_target_pairs={{0,2},{1,3},{2,0},{3,1},{4,6},{5,7},{6,4},{7,5},{8,10},{9,11},{10,... | collective-permute-start | bytes 2359304 | tf_op jit(solution)/shard_map/ppermute | solution.py:41
  654.8 5.3 collective-permute-start.33
  657.1 13.8 %collective-permute-start.32 = (bf16[512,768]{1,0:T(8,128)(2,1)}, bf16[512,768]{1,0:T(8,128)(2,1)}, u32[]{:S(2)}, u32[]{:S(2)}) collective-permute-start(bf16[512,768]{1,0:T(8,128)(2,1)} %get-tuple-element.195), channel_id=1, source_target_pairs={{0,1},{1,0},{2,3},{3,2},{4,5},{5,4},{6,7},{7,6},{8,9},{9,8},{10,11... | collective-permute-start | bytes 2359304 | tf_op jit(solution)/shard_map/ppermute | solution.py:41
  661.1 20.3 %collective-permute-start.34 = (bf16[512,768]{1,0:T(8,128)(2,1)}, bf16[512,768]{1,0:T(8,128)(2,1)}, u32[]{:S(2)}, u32[]{:S(2)}) collective-permute-start(bf16[512,768]{1,0:T(8,128)(2,1)} %fusion.8), channel_id=1, source_target_pairs={{0,2},{1,3},{2,0},{3,1},{4,6},{5,7},{6,4},{7,5},{8,10},{9,11},{10,... | collective-permute-start | bytes 2359304 | tf_op jit(solution)/shard_map/ppermute | solution.py:41
  670.8 48.6 %collective-permute-start.30 = (f32[768,768]{1,0:T(8,128)}, f32[768,768]{1,0:T(8,128)}, u32[]{:S(2)}, u32[]{:S(2)}) collective-permute-start(f32[768,768]{1,0:T(8,128)} %bitcast.200), channel_id=1, source_target_pairs={{0,1},{1,0},{2,3},{3,2},{4,5},{5,4},{6,7},{7,6},{8,9},{9,8},{10,11... | collective-permute-start | bytes 7077896 | tf_op jit(solution)/shard_map/ppermute | solution.py:41
  686.1 19.2 %collective-permute-start.36 = (bf16[512,768]{1,0:T(8,128)(2,1)S(1)}, bf16[512,768]{1,0:T(8,128)(2,1)S(1)}, u32[]{:S(2)}, u32[]{:S(2)}) collective-permute-start(bf16[512,768]{1,0:T(8,128)(2,1)S(1)} %add_convert_fusion), channel_id=1, source_target_pairs={{0,2},{1,3},{2,0},{3,1},{4,6},{5,7},{6,4},{7,5},{8,10},{9,11},{10,... | collective-permute-start | bytes 2359304 | tf_op jit(solution)/shard_map/ppermute | solution.py:41
  699.8 23.8 %collective-permute-start.35 = (bf16[512,768]{1,0:T(8,128)(2,1)S(1)}, bf16[512,768]{1,0:T(8,128)(2,1)S(1)}, u32[]{:S(2)}, u32[]{:S(2)}) collective-permute-start(bf16[512,768]{1,0:T(8,128)(2,1)S(1)} %add_convert_fusion), channel_id=1, source_target_pairs={{0,1},{1,0},{2,3},{3,2},{4,5},{5,4},{6,7},{7,6},{8,9},{9,8},{10,11... | collective-permute-start | bytes 2359304 | tf_op jit(solution)/shard_map/ppermute | solution.py:41
  705.4 18.3 %collective-permute-start.37 = (bf16[512,768]{1,0:T(8,128)(2,1)S(1)}, bf16[512,768]{1,0:T(8,128)(2,1)S(1)}, u32[]{:S(2)}, u32[]{:S(2)}) collective-permute-start(bf16[512,768]{1,0:T(8,128)(2,1)S(1)} %collective-permute-done.36), channel_id=1, source_target_pairs={{0,1},{1,0},{2,3},{3,2},{4,5},{5,4},{6,7},{7,6},{8,9},{9,8},{10,11... | collective-permute-start | bytes 2359304 | tf_op jit(solution)/shard_map/ppermute | solution.py:41
  715.7 59.9 %collective-permute-start.29 = (f32[768,768]{1,0:T(8,128)}, f32[768,768]{1,0:T(8,128)}, u32[]{:S(2)}, u32[]{:S(2)}) collective-permute-start(f32[768,768]{1,0:T(8,128)} %bitcast.201), channel_id=1, source_target_pairs={{0,1},{1,0},{2,3},{3,2},{4,5},{5,4},{6,7},{7,6},{8,9},{9,8},{10,11... | collective-permute-start | bytes 7077896 | tf_op jit(solution)/shard_map/ppermute | solution.py:41
  722.1 53.5 %collective-permute-start.31 = (f32[768,768]{1,0:T(8,128)S(1)}, f32[768,768]{1,0:T(8,128)}, u32[]{:S(2)}, u32[]{:S(2)}) collective-permute-start(f32[768,768]{1,0:T(8,128)S(1)} %bitcast_add_fusion), channel_id=1, source_target_pairs={{0,2},{1,3},{2,0},{3,1},{4,6},{5,7},{6,4},{7,5},{8,10},{9,11},{10,... | collective-permute-start | bytes 7077896 | tf_op jit(solution)/shard_map/ppermute | solution.py:41
  795.0 9.8 %collective-permute-start.38 = (f32[8,10752]{1,0:T(8,128)S(1)}, f32[8,10752]{1,0:T(8,128)S(1)}, u32[]{:S(2)}, u32[]{:S(2)}) collective-permute-start(f32[8,10752]{1,0:T(8,128)S(1)} %constant_dynamic-update-slice_fusion), channel_id=1, source_target_pairs={{0,4},{4,0},{8,12},{12,8},{16,20},{20,16},{24,28},{28,24},{1,5},{5... | collective-permute-start | bytes 1032200 | tf_op jit(solution)/shard_map/ppermute | solution.py:41
  804.8 8.9 collective-permute-start.39
  813.7 16.2 %collective-permute-start.40 = (f32[8,10752]{1,0:T(8,128)S(1)}, f32[8,10752]{1,0:T(8,128)S(1)}, u32[]{:S(2)}, u32[]{:S(2)}) collective-permute-start(f32[8,10752]{1,0:T(8,128)S(1)} %add.426), channel_id=1, source_target_pairs={{0,16},{4,20},{8,24},{12,28},{16,0},{20,4},{24,8},{28,12},{1,17},{... | collective-permute-start | bytes 1032200 | tf_op jit(solution)/shard_map/ppermute | solution.py:41
  860.6 5.3 collective-permute-start.41
  865.9 8.1 collective-permute-start.42
  874.0 35.7 %collective-permute-start.43 = (f32[44,768]{1,0:T(8,128)S(1)}, f32[44,768]{1,0:T(8,128)S(1)}, u32[]{:S(2)}, u32[]{:S(2)}) collective-permute-start(f32[44,768]{1,0:T(8,128)S(1)} %add.430), channel_id=1, source_target_pairs={{0,16},{4,20},{8,24},{12,28},{16,0},{20,4},{24,8},{28,12},{1,17},{... | collective-permute-start | bytes 405512 | tf_op jit(solution)/shard_map/ppermute | solution.py:41
  912.0 4.4 collective-permute-start.45
  912.1 4.9 collective-permute-start.44
  (82 other events, 1209.3 us)
Sparse Core Ops, SparseCore 0:
  10.8 169.5 all-gather.5
  183.1 39.2 all-gather.7
  227.7 50.8 all-gather.9
  373.4 40.4 all-gather.11
  422.8 42.7 all-gather.13

commit v2 on v1

v2 whole, which is shorter than its diff:
```python
import functools

import jax
import jax.numpy as jnp
from jax import lax
from jax.experimental import pallas as pl
from jax.experimental.pallas import tpu as pltpu
from jax.sharding import PartitionSpec as P

HEADS = 12
HEAD_DIM = 64
RANK = 8
PAIR = 2 * HEAD_DIM
TILE = 1280
PARTS = 3
CHUNK = 256

EPS = 1e-05
ROPE_BASE = 1000.0
TAU = 0.02
LAMBDA = 1.0
CLIP = 0.02
LRATE = 5000.0
MOMENTUM = 0.9
WIDE = jnp.float32
NARROW = jnp.bfloat16
HIGH = lax.Precision.HIGHEST
NEGATIVE = -1e30
VMEM_BYTES = 56 * 1024 * 1024


def params():
    return pltpu.CompilerParams(vmem_limit_bytes=VMEM_BYTES)


def axis_bits(axis):
    size = lax.axis_size(axis)
    return [1 << place for place in range(size.bit_length() - 1)]


def swap(value, axis, bit):
    size = lax.axis_size(axis)
    return lax.ppermute(value, axis, [(index, index ^ bit) for index in range(size)])


def spread_blocks(value, axis):
    held = {0: value}
    for bit in reversed(axis_bits(axis)):
        for key in sorted(held):
            held[key ^ bit] = swap(held[key], axis, bit)
    return [held[key] for key in range(len(held))]


def summed_block(blocks, axis, kind):
    held = dict(enumerate(blocks))
    for bit in axis_bits(axis):
        for key in sorted((k for k in held if not k & bit), reverse=True):
            if key in held:
                got = swap(held.pop(key ^ bit).astype(kind), axis, bit)
                held[key] = held[key].astype(WIDE) + got.astype(WIDE)
    return held[0]


def summed_pair(blocks, axis):
    held = dict(enumerate(blocks))
    bits = axis_bits(axis)
    for bit in bits[:-1]:
        for key in sorted((k for k in held if not k & bit), reverse=True):
            if key in held:
                got = swap(held.pop(key ^ bit), axis, bit)
                held[key] = (held[key].astype(WIDE) + got.astype(WIDE)).astype(NARROW)
    if not bits:
        return held[0], jnp.zeros_like(held[0])
    return held[0], swap(held[bits[-1]], axis, bits[-1])


def summed_all(value, axis):
    for bit in axis_bits(axis):
        value = value + swap(value, axis, bit)
    return value


def picked_blocks(blocks, order):
    stacked = blocks if isinstance(blocks, jax.Array) else jnp.stack(blocks)
    return jnp.stack(
        [
            lax.dynamic_index_in_dim(stacked, order[k], 0, keepdims=False)
            for k in range(stacked.shape[0])
        ]
    )


def gathered_rows(value, axis):
    size = lax.axis_size(axis)
    if size > 8:
        return lax.all_gather(value, axis, axis=0, tiled=True)
    rank, rows = lax.axis_index(axis), value.shape[0]
    whole = jnp.zeros((size * rows,) + value.shape[1:], value.dtype)
    for key in range(size):
        part = value
        if key:
            part = lax.ppermute(value, axis, [(index, index ^ key) for index in range(size)])
        whole = lax.dynamic_update_slice_in_dim(whole, part, (rank ^ key) * rows, 0)
    return whole


def row_blocks(value, count):
    rows = value.shape[0] // count
    return [value[k * rows : (k + 1) * rows] for k in range(count)]


def layer_norm(values, gain):
    mean = jnp.mean(values, axis=-1, keepdims=True)
    centred = values - mean
    spread = jnp.mean(centred * centred, axis=-1, keepdims=True)
    return centred * lax.rsqrt(spread + EPS) * gain


def swiglu(gate, up):
    return jax.nn.silu(gate) * up


def dot_in(left, right, axes, precision=None):
    return lax.dot_general(
        left, right, (axes, ((), ())), precision=precision, preferred_element_type=WIDE
    )


def contract_rows(left, right):
    return dot_in(left, right, ((0,), (0,)))


def contract_cols(left, right):
    return dot_in(left, right, ((1,), (1,)))


def halves(value):
    high = value.astype(NARROW)
    return high, (value - high.astype(WIDE)).astype(NARROW)


def turn(piece, cosine, sine):
    lane = lax.broadcasted_iota(jnp.int32, piece.shape, 1) % HEAD_DIM
    half = HEAD_DIM // 2
    ahead = pltpu.roll(piece, PAIR - half, 1)
    behind = pltpu.roll(piece, half, 1)
    return piece * cosine + jnp.where(lane < half, -ahead, behind) * sine


def rotary_tables(places):
    half = HEAD_DIM // 2
    column = (jnp.arange(PAIR) % half).astype(WIDE)
    freq = ROPE_BASE ** (-2.0 * column / HEAD_DIM)
    angle = places.astype(WIDE)[:, None] * freq[None, :]
    return (jnp.cos(angle), jnp.sin(angle))


def project_kernel(count, x_ref, *refs):
    weights, (cos_ref, sin_ref), outs = refs[:count], refs[count : count + 2], refs[count + 2 :]
    x, cosine, sine = x_ref[...], cos_ref[...], sin_ref[...]
    for kind, (w_ref, out_ref) in enumerate(zip(weights, outs), 3 - count):
        for at in range(0, out_ref.shape[1], 2 * PAIR):
            flat = jnp.dot(x, w_ref[:, at : at + 2 * PAIR], preferred_element_type=WIDE)
            for start in range(0, 2 * PAIR, PAIR):
                piece = flat[:, start : start + PAIR]
                if kind < 2:
                    piece = turn(piece, cosine, sine)
                piece = piece.astype(NARROW)
                if kind == 0:
                    piece = (piece.astype(WIDE) * HEAD_DIM ** (-0.5)).astype(NARROW)
                out_ref[:, at + start : at + start + PAIR] = piece


def project(count, x, weight, cosine, sine):
    rows, width = x.shape
    still = lambda i: (0, 0)
    block = pl.BlockSpec((rows, width), still)
    lanes = pl.BlockSpec((rows, PAIR), still)
    return pl.pallas_call(
        functools.partial(project_kernel, count),
        grid=(1,),
        in_specs=[block]
        + [weight_block(width, width, kind) for kind in range(3 - count, 3)]
        + [lanes, lanes],
        out_specs=[block] * count,
        out_shape=[jax.ShapeDtypeStruct((rows, width), NARROW)] * count,
        compiler_params=params(),
        cost_estimate=pl.CostEstimate(
            flops=2 * count * rows * width * width,
            bytes_accessed=2 * count * width * (rows + width),
            transcendentals=0,
        ),
    )(x, *[weight] * count, cosine, sine)


def lookup_kernel(row_count, start_ref, ids_ref, table_ref, out_ref, held):
    groups, block = out_ref.shape[1] // row_count, out_ref.shape[0]
    start = start_ref[0]
    for group in range(groups):

        def move(at, carry):
            for place in range(8):
                index = ids_ref[group, start + at * 8 + place]
                held[at, place : place + 1, :] = table_ref[index]
            return carry

        lax.fori_loop(0, block // 8, move, 0, unroll=4)
        rows = held[...].reshape(block, held.shape[2])[:, :row_count]
        out_ref[:, group * row_count : (group + 1) * row_count] = rows.astype(NARROW)


def lookup(ids, table, start, block, row_count):
    groups = ids.shape[0]
    return pl.pallas_call(
        functools.partial(lookup_kernel, row_count),
        in_specs=[
            pl.BlockSpec(memory_space=pltpu.SMEM),
            pl.BlockSpec(memory_space=pltpu.SMEM),
            pl.BlockSpec(memory_space=pltpu.VMEM),
        ],
        out_specs=pl.BlockSpec(memory_space=pltpu.VMEM),
        out_shape=jax.ShapeDtypeStruct((block, groups * row_count), NARROW),
        scratch_shapes=[pltpu.VMEM((block // 8, 8, table.shape[2]), WIDE)],
        compiler_params=params(),
        cost_estimate=pl.CostEstimate(
            flops=groups * block * 4096, bytes_accessed=4 * table.size, transcendentals=0
        ),
    )(start, ids, table)


def norm_parts(values):
    mean = jnp.mean(values, axis=-1, keepdims=True)
    centred = values - mean
    scale = lax.rsqrt(jnp.mean(centred * centred, axis=-1, keepdims=True) + EPS)
    return centred * scale, scale


def norm_back(grad, values, gain):
    unit, scale = norm_parts(values)
    inner = grad * gain
    first = jnp.mean(inner, axis=-1, keepdims=True)
    second = jnp.mean(inner * unit, axis=-1, keepdims=True)
    return (inner - first - unit * second) * scale, jnp.sum(grad * unit, axis=0, keepdims=True)


def whole_call(kernel, outs, flops, *operands):
    return pl.pallas_call(
        kernel,
        out_shape=[jax.ShapeDtypeStruct(shape, kind) for shape, kind in outs],
        compiler_params=params(),
        cost_estimate=pl.CostEstimate(
            flops=flops,
            bytes_accessed=sum(4 * operand.size for operand in operands),
            transcendentals=0,
        ),
    )(*operands)


def norm_kernel(gain_ref, *refs):
    inputs, (out_ref, narrow_ref) = refs[:-2], refs[-2:]
    total = inputs[0][...].astype(WIDE)
    for ref in inputs[1:]:
        total = total + ref[...].astype(WIDE)
    out = norm_parts(total)[0] * gain_ref[...]
    out_ref[...] = out
    narrow_ref[...] = out.astype(NARROW)


def norm_forward(gain, *parts):
    shape = parts[0].shape
    return whole_call(norm_kernel, [(shape, WIDE), (shape, NARROW)], 20 * parts[0].size, gain, *parts)


def merge_kernel(attended_ref, weight_ref, x_ref, gain_ref, narrow_out, pre_ref, out_ref, out_b_ref):
    narrow = attended_ref[...].astype(NARROW)
    narrow_out[...] = narrow
    pre = x_ref[...] + contract_rows(narrow, weight_ref[...])
    pre_ref[...] = pre
    out = norm_parts(pre)[0] * gain_ref[...]
    out_ref[...] = out
    out_b_ref[...] = out.astype(NARROW)


def merge_branch(attended_t, weight, x_zero, gain):
    rows, width = x_zero.shape
    shape = (rows, width)
    return whole_call(
        merge_kernel,
        [((width, rows), NARROW), (shape, WIDE), (shape, WIDE), (shape, NARROW)],
        2 * rows * width * width,
        attended_t,
        weight,
        x_zero,
        gain,
    )


def last_kernel(length_ref, slots_ref, rows_ref, pooled_ref, hidden_ref, local_ref, got_ref, gain_ref, out_ref, narrow_ref, sum_ref):
    total = hidden_ref[...] + local_ref[...].astype(WIDE) + got_ref[...].astype(WIDE)
    spread = rows_ref[...]
    place = lax.broadcasted_iota(jnp.int32, (total.shape[0], slots_ref.shape[1]), 0)
    hot = (place == slots_ref[...]).astype(WIDE).astype(NARROW)
    high, low = halves(spread)
    grad = jnp.dot(hot, high, preferred_element_type=WIDE)
    grad = grad + jnp.dot(hot, low, preferred_element_type=WIDE)
    index = lax.broadcasted_iota(jnp.int32, (total.shape[0], 1), 0)
    grad = grad + jnp.where(index < length_ref[0], pooled_ref[...], 0.0)
    out, gain_grad = norm_back(grad, total, gain_ref[...])
    out_ref[...] = out
    narrow_ref[...] = out.astype(NARROW)
    sum_ref[...] = gain_grad


def last_back(length, slots, row_grad, pooled_grad, hidden_in, local, got, gain):
    shape = hidden_in.shape
    return pl.pallas_call(
        last_kernel,
        in_specs=[pl.BlockSpec(memory_space=pltpu.SMEM)]
        + [pl.BlockSpec(memory_space=pltpu.VMEM)] * 7,
        out_shape=[
            jax.ShapeDtypeStruct(shape, WIDE),
            jax.ShapeDtypeStruct(shape, NARROW),
            jax.ShapeDtypeStruct((1, shape[1]), WIDE),
        ],
        compiler_params=params(),
        cost_estimate=pl.CostEstimate(
            flops=200 * hidden_in.size, bytes_accessed=20 * hidden_in.size, transcendentals=0
        ),
    )(length, slots, row_grad, pooled_grad, hidden_in, local, got, gain)


def branch_back_kernel(grad_ref, local_ref, got_ref, pre_ref, gain_ref, weight_ref, out_ref, narrow_ref, attended_ref, sum_ref):
    grad = grad_ref[...] + local_ref[...].astype(WIDE) + got_ref[...].astype(WIDE)
    out, gain_grad = norm_back(grad, pre_ref[...], gain_ref[...])
    narrow = out.astype(NARROW)
    out_ref[...] = out
    narrow_ref[...] = narrow
    sum_ref[...] = gain_grad
    attended_ref[...] = contract_cols(narrow, weight_ref[...]).astype(NARROW)


def branch_back(pre_grad, local, got, pre_one, gain, weight):
    rows, width = pre_grad.shape
    shape = (rows, width)
    return whole_call(
        branch_back_kernel,
        [(shape, WIDE), (shape, NARROW), (shape, NARROW), ((1, width), WIDE)],
        2 * rows * width * width,
        pre_grad,
        local,
        got,
        pre_one,
        gain,
        weight,
    )


def first_back_kernel(grad_ref, dq_ref, weight_ref, local_ref, got_ref, value_ref, gain_ref, out_ref, sum_ref):
    grad = grad_ref[...] + local_ref[...].astype(WIDE) + got_ref[...].astype(WIDE)
    grad = grad + contract_cols(dq_ref[...], weight_ref[...])
    out, gain_grad = norm_back(grad, value_ref[...].astype(WIDE), gain_ref[...])
    out_ref[...] = out.astype(NARROW)
    sum_ref[...] = gain_grad


def first_back(pre_one_grad, dq, weight, local, got, embedded, gain):
    rows, width = pre_one_grad.shape
    return whole_call(
        first_back_kernel,
        [((rows, width), NARROW), ((1, width), WIDE)],
        2 * rows * width * width,
        pre_one_grad,
        dq,
        weight,
        local,
        got,
        embedded,
        gain,
    )


def ffn_kernel(x_ref, gate_ref, up_ref, down_ref, gate_out, up_out, act_ref, out_ref):
    x = x_ref[...]
    gate = jnp.dot(x, gate_ref[...], preferred_element_type=WIDE)
    up = jnp.dot(x, up_ref[...], preferred_element_type=WIDE)
    gate_out[...] = gate
    up_out[...] = up
    act = (gate / (1.0 + jnp.exp(-gate)) * up).astype(NARROW)
    act_ref[...] = act
    out_ref[...] = contract_cols(act, down_ref[...]).astype(NARROW)


def weight_block(width, hidden, index):
    return pl.BlockSpec((width, hidden), lambda i: (0, index))


def ffn_forward(x, weights):
    rows, width = x.shape
    hidden = weights.shape[1] // 4
    block = min(512, rows)
    tall = lambda i: (i, 0)
    return pl.pallas_call(
        ffn_kernel,
        grid=(rows // block,),
        in_specs=[pl.BlockSpec((block, width), tall)]
        + [weight_block(width, hidden, k) for k in range(1, 4)],
        out_specs=[
            pl.BlockSpec((block, hidden), tall),
            pl.BlockSpec((block, hidden), tall),
            pl.BlockSpec((block, hidden), tall),
            pl.BlockSpec((block, width), tall),
        ],
        out_shape=[
            jax.ShapeDtypeStruct((rows, hidden), WIDE),
            jax.ShapeDtypeStruct((rows, hidden), WIDE),
            jax.ShapeDtypeStruct((rows, hidden), NARROW),
            jax.ShapeDtypeStruct((rows, width), NARROW),
        ],
        compiler_params=params(),
        cost_estimate=pl.CostEstimate(
            flops=6 * rows * width * hidden,
            bytes_accessed=14 * rows * width + 6 * width * hidden,
            transcendentals=rows * hidden,
        ),
    )(x, weights, weights, weights)


def ffn_back_kernel(grad_ref, gate_in, up_in, gate_ref, up_ref, down_ref, dgate_ref, dup_ref, out_ref):
    act_grad = jnp.dot(grad_ref[...], down_ref[...], preferred_element_type=WIDE)
    gate, up = gate_in[...], up_in[...]
    share = 1.0 / (1.0 + jnp.exp(-gate))
    dgate = (act_grad * up * (share * (1.0 + gate * (1.0 - share)))).astype(NARROW)
    dup = (act_grad * (gate * share)).astype(NARROW)
    dgate_ref[...] = dgate
    dup_ref[...] = dup
    out_ref[...] = (
        contract_cols(dgate, gate_ref[...]) + contract_cols(dup, up_ref[...])
    ).astype(NARROW)


def ffn_backward(grad, gate, up, weights):
    rows, width = grad.shape
    hidden = weights.shape[1] // 4
    block = min(512, rows)
    tall = lambda i: (i, 0)
    return pl.pallas_call(
        ffn_back_kernel,
        grid=(rows // block,),
        in_specs=[
            pl.BlockSpec((block, width), tall),
            pl.BlockSpec((block, hidden), tall),
            pl.BlockSpec((block, hidden), tall),
        ]
        + [weight_block(width, hidden, k) for k in range(1, 4)],
        out_specs=[
            pl.BlockSpec((block, hidden), tall),
            pl.BlockSpec((block, hidden), tall),
            pl.BlockSpec((block, width), tall),
        ],
        out_shape=[
            jax.ShapeDtypeStruct((rows, hidden), NARROW),
            jax.ShapeDtypeStruct((rows, hidden), NARROW),
            jax.ShapeDtypeStruct((rows, width), NARROW),
        ],
        compiler_params=params(),
        cost_estimate=pl.CostEstimate(
            flops=6 * rows * width * hidden,
            bytes_accessed=16 * rows * width + 6 * width * hidden,
            transcendentals=rows * hidden,
        ),
    )(grad, gate, up, weights, weights, weights)


def logits_kernel(columns, tile, rows_ref, table_ref, targets_ref, out_ref, stats_ref, top_ref, sum_ref, hit_ref):
    step = pl.program_id(0)

    @pl.when(step == 0)
    def _():
        top_ref[...] = jnp.full(top_ref.shape, NEGATIVE, WIDE)
        sum_ref[...] = jnp.zeros(sum_ref.shape, WIDE)
        hit_ref[...] = jnp.zeros(hit_ref.shape, WIDE)

    logits = jnp.dot(rows_ref[...], table_ref[...], preferred_element_type=WIDE)
    out_ref[...] = logits
    place = step * tile + lax.broadcasted_iota(jnp.int32, (1, tile), 1)
    seen = jnp.where(place < columns, logits, NEGATIVE)
    hits = jnp.where((place == targets_ref[...]) & (place < columns), seen, 0.0)
    pieces = [slice(at, at + 128) for at in range(0, tile, 128)]
    before = top_ref[...]
    top = before
    for piece in pieces:
        top = jnp.maximum(top, seen[:, piece])
    total = sum_ref[...] * jnp.exp(before - top)
    hit = hit_ref[...]
    for piece in pieces:
        total = total + jnp.exp(seen[:, piece] - top)
        hit = hit + hits[:, piece]
    top_ref[...] = top
    sum_ref[...] = total
    hit_ref[...] = hit

    @pl.when(step == pl.num_programs(0) - 1)
    def _():
        peak = jnp.max(top, axis=1, keepdims=True)
        whole = jnp.sum(total * jnp.exp(top - peak), axis=1, keepdims=True)
        found = jnp.sum(hit, axis=1, keepdims=True)
        lane = lax.broadcasted_iota(jnp.int32, (1, 128), 1)
        stats_ref[...] = jnp.where(
            lane == 0, peak, jnp.where(lane == 1, whole, jnp.where(lane == 2, found, 0.0))
        )


def vocab_logits(rows_all, table, targets):
    picks, width = rows_all.shape
    columns = table.shape[1]
    tiles = -(-columns // TILE)
    tile = TILE
    still = lambda j: (0, 0)
    along = lambda j: (0, j)
    return pl.pallas_call(
        functools.partial(logits_kernel, columns, tile),
        grid=(tiles * TILE // tile,),
        in_specs=[
            pl.BlockSpec((picks, width), still),
            pl.BlockSpec((width, tile), along),
            pl.BlockSpec((picks, 1), still),
        ],
        out_specs=[pl.BlockSpec((picks, tile), along), pl.BlockSpec((picks, 128), still)],
        out_shape=[
            jax.ShapeDtypeStruct((picks, tiles * TILE), WIDE),
            jax.ShapeDtypeStruct((picks, 128), WIDE),
        ],
        scratch_shapes=[pltpu.VMEM((picks, 128), WIDE)] * 3,
        compiler_params=params(),
        cost_estimate=pl.CostEstimate(
            flops=2 * picks * width * columns,
            bytes_accessed=2 * width * columns,
            transcendentals=picks * columns,
        ),
    )(rows_all, table, targets)


def combine_kernel(count, slots, bit, mine_ref, other_ref, out_ref):
    lane = lax.broadcasted_iota(jnp.int32, (1, 128), 1)
    for block in range(count):
        mine = mine_ref[block * slots : (block + 1) * slots, :]
        other = other_ref[(block ^ bit) * slots : ((block ^ bit) + 1) * slots, :]
        peak = jnp.maximum(mine[:, :1], other[:, :1])
        total = mine[:, 1:2] * jnp.exp(mine[:, :1] - peak)
        total = total + other[:, 1:2] * jnp.exp(other[:, :1] - peak)
        out_ref[block * slots : (block + 1) * slots, :] = jnp.where(
            lane == 0, peak, jnp.where(lane == 1, total, mine + other)
        )
    rest = count * slots
    out_ref[rest:, :] = mine_ref[rest:, :] + other_ref[rest:, :]


def dlogits_kernel(columns, tile, logits_ref, table_ref, targets_ref, stats_ref, weight_ref, out_ref, grad_ref):
    step = pl.program_id(0)
    log_all = stats_ref[:, :1] + jnp.log(stats_ref[:, 1:2])
    place = step * tile + lax.broadcasted_iota(jnp.int32, (1, tile), 1)
    share = jnp.exp(logits_ref[...] - log_all) - jnp.where(place == targets_ref[...], 1.0, 0.0)
    grad = jnp.where(place < columns, share * weight_ref[...], 0.0).astype(NARROW)
    out_ref[...] = grad
    column = step * tile + lax.broadcasted_iota(jnp.int32, (1, tile), 1)
    table = jnp.where(column < columns, table_ref[...].astype(WIDE), 0.0).astype(NARROW)
    part = contract_cols(grad, table)

    @pl.when(step == 0)
    def _():
        grad_ref[...] = part

    @pl.when(step > 0)
    def _():
        grad_ref[...] += part


def vocab_back(logits, table, targets, stats, weight):
    picks = targets.shape[0]
    width, columns = table.shape
    tile = TILE
    still = lambda j: (0, 0)
    along = lambda j: (0, j)
    return pl.pallas_call(
        functools.partial(dlogits_kernel, columns, tile),
        grid=(logits.shape[1] // tile,),
        in_specs=[
            pl.BlockSpec((picks, tile), along),
            pl.BlockSpec((width, tile), along),
            pl.BlockSpec((picks, 1), still),
            pl.BlockSpec((picks, 128), still),
            pl.BlockSpec((picks, 1), still),
        ],
        out_specs=[pl.BlockSpec((picks, tile), along), pl.BlockSpec((picks, width), still)],
        out_shape=[
            jax.ShapeDtypeStruct(logits.shape, NARROW),
            jax.ShapeDtypeStruct((picks, width), WIDE),
        ],
        compiler_params=params(),
        cost_estimate=pl.CostEstimate(
            flops=2 * picks * width * columns,
            bytes_accessed=2 * width * columns,
            transcendentals=picks * columns,
        ),
    )(logits, table, targets, stats, weight)


def contrast_kernel(weight, length_ref, pooled_ref, keys_ref, blocked_ref, target_ref, grad_ref, part_ref):
    length = length_ref[0].astype(WIDE)
    pooled = pooled_ref[...] / length
    scale = lax.rsqrt(jnp.sum(pooled * pooled, axis=-1, keepdims=True) + EPS)
    narrow = jnp.broadcast_to(pooled * scale, (8, pooled.shape[1])).astype(NARROW)
    keys = keys_ref[...]
    scores = contract_cols(narrow, keys)[:1] / TAU
    target = target_ref[...]
    masked = jnp.where(blocked_ref[...] > 0.0, NEGATIVE, scores)
    top = jnp.max(masked, axis=-1, keepdims=True)
    log_c = top + jnp.log(jnp.sum(jnp.exp(masked - top), axis=-1, keepdims=True))
    chosen = jnp.sum(jnp.where(target > 0.0, scores, 0.0), axis=-1, keepdims=True)
    part_ref[...] = jnp.broadcast_to((log_c - chosen) * weight, part_ref.shape)
    dscores = ((jnp.exp(masked - log_c) - target) * (weight / TAU)).astype(NARROW)
    dscores = jnp.broadcast_to(dscores.astype(WIDE), (8, dscores.shape[1])).astype(NARROW)
    grad = jnp.dot(dscores, keys, preferred_element_type=WIDE)[:1]
    inner = jnp.sum(pooled * grad, axis=-1, keepdims=True)
    grad_ref[...] = (grad - pooled * (inner * scale * scale)) * scale / length


def contrast(weight, length, pooled_sum, keys_hat, blocked, target):
    width = pooled_sum.shape[1]
    return pl.pallas_call(
        functools.partial(contrast_kernel, weight),
        in_specs=[pl.BlockSpec(memory_space=pltpu.SMEM)]
        + [pl.BlockSpec(memory_space=pltpu.VMEM)] * 4,
        out_shape=[
            jax.ShapeDtypeStruct((1, width), WIDE),
            jax.ShapeDtypeStruct((1, 128), WIDE),
        ],
        compiler_params=params(),
        cost_estimate=pl.CostEstimate(
            flops=4 * keys_hat.size, bytes_accessed=2 * keys_hat.size, transcendentals=0
        ),
    )(length, pooled_sum, keys_hat, blocked, target)


def head_lanes(head):
    lane = lax.broadcasted_iota(jnp.int32, (1, PAIR), 1)
    return (lane // HEAD_DIM) == head, lane == HEAD_DIM * (1 - head)


def attend_kernel(count, q_ref, *refs):
    k_refs, v_refs, bias_refs = refs[:count], refs[count : 2 * count], refs[2 * count : 3 * count]
    out_ref, log_ref, s_ref = refs[3 * count :]
    head = pl.program_id(1)
    mine, spare = head_lanes(head)
    step = k_refs[0].shape[0]
    blocks = [pl.ds(k * step, step) for k in range(count)]
    query = jnp.where(spare, 1.0, jnp.where(mine, q_ref[...].astype(WIDE), 0.0)).astype(NARROW)
    top = None
    for rows, k_ref, bias_ref in zip(blocks, k_refs, bias_refs):
        key = jnp.where(spare, bias_ref[...].astype(WIDE), k_ref[...].astype(WIDE))
        scores = contract_cols(key.astype(NARROW), query)
        s_ref[rows, :] = scores
        peak = jnp.max(scores, axis=0, keepdims=True)
        top = peak if top is None else jnp.maximum(top, peak)
    total = None
    for rows in blocks:
        powers = jnp.exp(s_ref[rows, :] - top)
        s_ref[rows, :] = powers
        part = jnp.sum(powers, axis=0, keepdims=True)
        total = part if total is None else total + part
    share = 1.0 / total
    result = None
    for rows, v_ref in zip(blocks, v_refs):
        probs = (s_ref[rows, :] * share).astype(NARROW)
        part = contract_rows(v_ref[...], probs)
        result = part if result is None else result + part
    log_ref[0, pl.ds(head, 1), :] = top + jnp.log(total)

    @pl.when(head == 0)
    def _():
        out_ref[...] = result

    @pl.when(head == 1)
    def _():
        out_ref[HEAD_DIM:, :] = result[HEAD_DIM:, :]


def attention_forward(queries, keys, values, biases):
    rows, width = queries.shape
    count = len(keys)
    length = rows * count
    pairs = width // PAIR
    lanes = pl.BlockSpec((rows, PAIR), lambda i, h: (0, i))
    still = pl.BlockSpec((rows, PAIR), lambda i, h: (0, 0))
    return pl.pallas_call(
        functools.partial(attend_kernel, count),
        grid=(pairs, 2),
        in_specs=[lanes] * (1 + 2 * count) + [still] * count,
        out_specs=[
            pl.BlockSpec((PAIR, rows), lambda i, h: (i, 0)),
            pl.BlockSpec((1, 2, rows), lambda i, h: (i, 0, 0)),
        ],
        out_shape=[
            jax.ShapeDtypeStruct((width, rows), WIDE),
            jax.ShapeDtypeStruct((pairs, 2, rows), WIDE),
        ],
        scratch_shapes=[pltpu.VMEM((length, rows), WIDE)],
        compiler_params=params(),
        cost_estimate=pl.CostEstimate(
            flops=4 * rows * length * width,
            bytes_accessed=4 * length * width + 8 * rows * width,
            transcendentals=rows * length * HEADS,
        ),
    )(queries, *keys, *values, *biases)


def attend_back_kernel(count, q_ref, grad_ref, out_ref, log_ref, *refs):
    groups = [refs[k * count : (k + 1) * count] for k in range(5)]
    k_refs, v_refs, bias_refs, cos_refs, sin_refs = groups
    rest = refs[5 * count :]
    dq_ref, dk_refs, dv_refs = rest[0], rest[1 : 1 + count], rest[1 + count : 1 + 2 * count]
    dk_sum, dv_sum, dq_sum = rest[1 + 2 * count :]
    head = pl.program_id(1)
    mine, spare = head_lanes(head)
    step, scale = k_refs[0].shape[0], HEAD_DIM ** (-0.5)
    own = jnp.where(mine, q_ref[...].astype(WIDE), 0.0)
    query = own.astype(NARROW)
    asked = jnp.where(spare, 1.0, own).astype(NARROW)
    grad_wide = jnp.where(mine, grad_ref[...].astype(WIDE), 0.0)
    grad = grad_wide.astype(NARROW)
    delta = jnp.sum(grad_wide.T * out_ref[...], axis=0, keepdims=True)
    log_total = log_ref[0, pl.ds(head, 1), :]
    dq = None
    for k in range(count):
        rows = pl.ds(k * step, step)
        key_block = k_refs[k][...]
        key = jnp.where(spare, bias_refs[k][...].astype(WIDE), key_block.astype(WIDE))
        scores = contract_cols(key.astype(NARROW), asked)
        probs = jnp.exp(scores - log_total)
        dprobs = contract_cols(v_refs[k][...], grad)
        dv = jnp.dot(probs.astype(NARROW), grad, preferred_element_type=WIDE)
        dscores = (probs * (dprobs - delta)).astype(NARROW)
        dk = jnp.dot(dscores, query, preferred_element_type=WIDE)
        part = contract_rows(key_block, dscores)
        dq = part if dq is None else dq + part

        @pl.when(head == 0)
        def _():
            dk_sum[rows, :] = dk
            dv_sum[rows, :] = dv

        @pl.when(head == 1)
        def _():
            total = dk_sum[rows, :] + dk
            dk_refs[k][...] = turn(total, cos_refs[k][...], -sin_refs[k][...]).astype(NARROW)
            dv_refs[k][...] = (dv_sum[rows, :] + dv).astype(NARROW)

    @pl.when(head == 0)
    def _():
        dq_sum[...] = dq

    @pl.when(head == 1)
    def _():
        dq_sum[HEAD_DIM:, :] = dq[HEAD_DIM:, :]
        total = dq_sum[...].T * scale
        dq_ref[...] = turn(total, cos_refs[0][...], -sin_refs[0][...]).astype(NARROW)


def attention_backward(queries, keys, values, biases, grad, out_t, log_total, cosines, sines):
    rows, width = queries.shape
    count = len(keys)
    length = rows * count
    pairs = width // PAIR
    lanes = pl.BlockSpec((rows, PAIR), lambda i, h: (0, i))
    still = pl.BlockSpec((rows, PAIR), lambda i, h: (0, 0))
    found = pl.pallas_call(
        functools.partial(attend_back_kernel, count),
        grid=(pairs, 2),
        in_specs=[
            lanes,
            lanes,
            pl.BlockSpec((PAIR, rows), lambda i, h: (i, 0)),
            pl.BlockSpec((1, 2, rows), lambda i, h: (i, 0, 0)),
        ]
        + [lanes] * (2 * count)
        + [still] * (3 * count),
        out_specs=[lanes] * (1 + 2 * count),
        out_shape=[jax.ShapeDtypeStruct((rows, width), NARROW)] * (1 + 2 * count),
        scratch_shapes=[
            pltpu.VMEM((length, PAIR), WIDE),
            pltpu.VMEM((length, PAIR), WIDE),
            pltpu.VMEM((PAIR, rows), WIDE),
        ],
        compiler_params=params(),
        cost_estimate=pl.CostEstimate(
            flops=10 * rows * length * width,
            bytes_accessed=8 * length * width + 8 * rows * width,
            transcendentals=rows * length * HEADS,
        ),
    )(queries, grad, out_t, log_total, *keys, *values, *biases, *cosines, *sines)
    return found[0], found[1 : 1 + count], found[1 + count :]


def project_down(matrix, factor_t):
    high, low = halves(matrix)
    factor_high, factor_low = halves(factor_t)
    both = jnp.concatenate([factor_high, factor_low], axis=0)
    first = jnp.dot(both, high, preferred_element_type=WIDE)
    second = jnp.dot(factor_high, low, preferred_element_type=WIDE)
    return first[:RANK] + first[RANK:] + second


def project_back(matrix, basis_t):
    high, low = halves(matrix)
    basis_high, basis_low = halves(basis_t)
    both = jnp.concatenate([basis_high, basis_low], axis=0)
    first = contract_cols(both, high)
    second = contract_cols(basis_high, low)
    return first[:RANK] + first[RANK:] + second


def expand(back_t, basis_t):
    back_high, back_low = halves(back_t)
    basis_high, basis_low = halves(basis_t)
    left = jnp.concatenate([back_high, back_low, back_high], axis=0)
    right = jnp.concatenate([basis_high, basis_high, basis_low], axis=0)
    return contract_rows(left, right)


def table_kernel(columns, first, starts_ref, left_ref, tokens_ref, rows_ref, dlogits_ref, error_ref, factor_ref, high_ref, low_ref, p_ref, sum_ref):
    tile = first + pl.program_id(0)
    place = tile * TILE + lax.broadcasted_iota(jnp.int32, (TILE, 1), 0)
    sum_ref[...] = error_ref[...] + contract_rows(dlogits_ref[...], rows_ref[...])

    def visit(chunk, carry):
        at = pl.ds(pl.multiple_of(chunk * CHUNK, CHUNK), CHUNK)
        hot = jnp.where(tokens_ref[:, at] == place, 1.0, 0.0).astype(NARROW)
        sum_ref[...] += jnp.dot(hot, left_ref[at, :], preferred_element_type=WIDE)
        return carry

    lax.fori_loop(
        starts_ref[tile] // CHUNK, (starts_ref[tile + 1] + CHUNK - 1) // CHUNK, visit, 0
    )
    total = jnp.where(place < columns, sum_ref[...], 0.0)
    high, low = halves(total)
    high_ref[...] = high
    low_ref[...] = low
    factor_high, factor_low = halves(factor_ref[...])
    both = jnp.concatenate([factor_high, factor_low], axis=0)
    found = contract_cols(high, both).T
    rest = contract_cols(low, both).T
    p_ref[...] = found[:RANK] + found[RANK:] + rest[:RANK]


def table_matrix(bounds, starts, left, tokens, rows, dlogits, error, factor_t):
    columns, width = error.shape
    slots = left.shape[0]
    picks = rows.shape[0]
    first, tiles = bounds[0], bounds[1] - bounds[0]
    still = lambda j: (0, 0)
    down = lambda j: (j, 0)
    return pl.pallas_call(
        functools.partial(table_kernel, columns, first),
        grid=(tiles,),
        in_specs=[
            pl.BlockSpec(memory_space=pltpu.SMEM),
            pl.BlockSpec((slots, width), still),
            pl.BlockSpec((1, slots), still),
            pl.BlockSpec((picks, width), still),
            pl.BlockSpec((picks, TILE), lambda j: (0, first + j)),
            pl.BlockSpec((TILE, width), lambda j: (first + j, 0)),
            pl.BlockSpec((RANK, width), still),
        ],
        out_specs=[
            pl.BlockSpec((TILE, width), down),
            pl.BlockSpec((TILE, width), down),
            pl.BlockSpec((RANK, TILE), lambda j: (0, j)),
        ],
        out_shape=[
            jax.ShapeDtypeStruct((tiles * TILE, width), NARROW),
            jax.ShapeDtypeStruct((tiles * TILE, width), NARROW),
            jax.ShapeDtypeStruct((RANK, tiles * TILE), WIDE),
        ],
        scratch_shapes=[pltpu.VMEM((TILE, width), WIDE)],
        compiler_params=params(),
        cost_estimate=pl.CostEstimate(
            flops=2 * width * tiles * TILE * (slots // 4 + picks + 24),
            bytes_accessed=8 * width * tiles * TILE,
            transcendentals=0,
        ),
    )(starts, left, tokens, rows, dlogits, error, factor_t)


def partial_kernel(*refs):
    count = (len(refs) - 1) // 2
    for index in range(count):
        refs[-1][index] = project_down(refs[index][...], refs[count + index][...])


def partial_projections(matrices, factors_t):
    count, (width, columns) = len(matrices), matrices[0].shape
    return whole_call(
        partial_kernel,
        [((count, RANK, columns), WIDE)],
        48 * count * width * columns,
        *matrices,
        *factors_t,
    )[0]


def small_kernel(count, *refs):
    grads, errors, factor_ref = refs[:count], refs[count : 2 * count], refs[2 * count]
    m_ref, p_ref = refs[2 * count + 1 :]
    for index in range(count):
        total = grads[index][...] + errors[index][...]
        m_ref[index] = total
        p_ref[index] = project_down(total, factor_ref[index])


def small_matrices(grads, errors, factor_t):
    count, (width, columns) = len(grads), grads[0].shape
    return pl.pallas_call(
        functools.partial(small_kernel, count),
        out_shape=[
            jax.ShapeDtypeStruct((count, width, columns), WIDE),
            jax.ShapeDtypeStruct((count, RANK, columns), WIDE),
        ],
        compiler_params=params(),
        cost_estimate=pl.CostEstimate(
            flops=48 * count * width * columns,
            bytes_accessed=12 * count * width * columns,
            transcendentals=0,
        ),
    )(*grads, *errors, factor_t)


def basis_kernel(spans, p_ref, out_ref):
    index = lax.broadcasted_iota(jnp.int32, (RANK, 1), 0)
    for start, size in spans:
        rows = p_ref[:, pl.ds(start, size)]
        for place in range(RANK):
            row = rows[place : place + 1, :]
            row = row * lax.rsqrt(jnp.sum(row * row, axis=1, keepdims=True))
            inner = jnp.sum(rows * row, axis=1, keepdims=True)
            rows = jnp.where(index == place, row, rows - jnp.where(index > place, inner, 0.0) * row)
        out_ref[:, pl.ds(start, size)] = rows


def bases_of(sums, spans):
    return pl.pallas_call(
        functools.partial(basis_kernel, spans),
        out_shape=jax.ShapeDtypeStruct(sums.shape, WIDE),
        compiler_params=params(),
        cost_estimate=pl.CostEstimate(
            flops=64 * sums.size, bytes_accessed=8 * sums.size, transcendentals=40
        ),
    )(sums)


def small_back_kernel(m_ref, basis_ref, back_ref):
    for index in range(m_ref.shape[0]):
        back_ref[index] = project_back(m_ref[index], basis_ref[index])


def small_backs(matrices, basis):
    count, width, columns = matrices.shape
    return pl.pallas_call(
        small_back_kernel,
        out_shape=jax.ShapeDtypeStruct((count, RANK, width), WIDE),
        compiler_params=params(),
        cost_estimate=pl.CostEstimate(
            flops=48 * count * width * columns,
            bytes_accessed=4 * count * width * columns,
            transcendentals=0,
        ),
    )(matrices, basis)


def table_specs(parts, width):
    bounds, first = [], 0
    for part in parts:
        bounds.append((first, first + part.shape[0] // TILE))
        first = bounds[-1][1]
    specs = [
        pl.BlockSpec(
            (TILE, width), lambda j, low=low, high=high: (jnp.clip(j, low, high - 1) - low, 0)
        )
        for low, high in bounds
    ]
    return bounds, specs


def table_back_kernel(bounds, *refs):
    highs, lows = refs[: len(bounds)], refs[len(bounds) : 2 * len(bounds)]
    basis_ref, back_ref = refs[2 * len(bounds) :]
    step = pl.program_id(0)
    basis_high, basis_low = halves(basis_ref[...])
    both = jnp.concatenate([basis_high, basis_low], axis=0)

    @pl.when(step == 0)
    def _():
        back_ref[...] = jnp.zeros(back_ref.shape, WIDE)

    for (low, high), high_ref, low_ref in zip(bounds, highs, lows):

        @pl.when((step >= low) & (step < high))
        def _():
            first = jnp.dot(both, high_ref[...], preferred_element_type=WIDE)
            second = jnp.dot(basis_high, low_ref[...], preferred_element_type=WIDE)
            back_ref[...] += first[:RANK] + first[RANK:] + second


def table_back(highs, lows, basis):
    width = highs[0].shape[1]
    columns = basis.shape[1]
    bounds, specs = table_specs(highs, width)
    return pl.pallas_call(
        functools.partial(table_back_kernel, bounds),
        grid=(columns // TILE,),
        in_specs=specs + specs + [pl.BlockSpec((RANK, TILE), lambda j: (0, j))],
        out_specs=pl.BlockSpec((RANK, width), lambda j: (0, 0)),
        out_shape=jax.ShapeDtypeStruct((RANK, width), WIDE),
        compiler_params=params(),
        cost_estimate=pl.CostEstimate(
            flops=48 * width * columns, bytes_accessed=4 * width * columns, transcendentals=0
        ),
    )(*highs, *lows, basis)


def small_error_kernel(m_ref, back_ref, basis_ref, *out_refs):
    for index, out_ref in enumerate(out_refs):
        out_ref[...] = m_ref[index] - expand(back_ref[index], basis_ref[index])


def small_errors(matrices, backs, basis):
    count, width, columns = matrices.shape
    return pl.pallas_call(
        small_error_kernel,
        out_shape=[jax.ShapeDtypeStruct((width, columns), WIDE)] * count,
        compiler_params=params(),
        cost_estimate=pl.CostEstimate(
            flops=48 * count * width * columns,
            bytes_accessed=8 * count * width * columns,
            transcendentals=0,
        ),
    )(matrices, backs, basis)


def table_error_kernel(bounds, *refs):
    highs, lows = refs[: len(bounds)], refs[len(bounds) : 2 * len(bounds)]
    back_ref, basis_ref, out_ref = refs[2 * len(bounds) :]
    step = pl.program_id(0)
    for (low, high), high_ref, low_ref in zip(bounds, highs, lows):

        @pl.when((step >= low) & (step < high))
        def _():
            whole = high_ref[...].astype(WIDE) + low_ref[...].astype(WIDE)
            out_ref[...] = whole - expand(basis_ref[...], back_ref[...])


def table_error(highs, lows, back, basis, columns):
    width = highs[0].shape[1]
    bounds, specs = table_specs(highs, width)
    return pl.pallas_call(
        functools.partial(table_error_kernel, bounds),
        grid=(basis.shape[1] // TILE,),
        in_specs=specs
        + specs
        + [
            pl.BlockSpec((RANK, width), lambda j: (0, 0)),
            pl.BlockSpec((RANK, TILE), lambda j: (0, j)),
        ],
        out_specs=pl.BlockSpec((TILE, width), lambda j: (j, 0)),
        out_shape=jax.ShapeDtypeStruct((columns, width), WIDE),
        compiler_params=params(),
        cost_estimate=pl.CostEstimate(
            flops=48 * width * columns, bytes_accessed=8 * width * columns, transcendentals=0
        ),
    )(*highs, *lows, back, basis)


def normalize_keys(raw_keys):
    wide_keys = raw_keys.astype(WIDE)
    return (
        wide_keys * lax.rsqrt(jnp.sum(wide_keys * wide_keys, axis=-1, keepdims=True) + EPS)
    ).astype(NARROW)


def per_device(
    token_ids,
    seq_lengths,
    mask_slots,
    mask_targets,
    positive_rows,
    doc_ids,
    false_pairs,
    queue_docs,
    queue_embed,
    attend_weight,
    attend_moment,
    gate_up,
    gate_up_moment,
    down_weight,
    down_moment,
    embed_table,
    embed_moment,
    gains,
    gains_moment,
    attend_error,
    gate_up_error,
    down_error,
    embed_error,
    factors,
):
    tensor_count = lax.axis_size("tensor")
    tensor_rank = lax.axis_index("tensor")
    data_count = lax.axis_size("dp")
    data_rank = lax.axis_index("dp")
    groups, seq_len = token_ids.shape
    width = gains.shape[1]
    total_rows = groups * seq_len
    own_rows = total_rows // tensor_count
    slot_count = mask_slots.shape[2]
    seq_total = groups * data_count
    near = jnp.arange(tensor_count) ^ tensor_rank
    row_count = attend_weight.shape[0]

    tokens_all = lax.all_to_all(
        jnp.broadcast_to(token_ids, (data_count, seq_len)), "dp", 0, 0, tiled=True
    )
    vocab_own = embed_table.shape[1]
    vocab_start = tensor_rank * vocab_own
    ids = tokens_all - vocab_start
    ids = jnp.where((ids >= 0) & (ids < vocab_own), ids, vocab_own)
    fill = -(-row_count // 128) * 128 - row_count
    table_local = embed_table.astype(NARROW)
    table_rows = jnp.pad(table_local.astype(WIDE).T, ((0, 1), (0, fill)))[:, None]
    looked = {}
    for key in reversed(range(tensor_count)):
        start = ((tensor_rank ^ key) * own_rows).reshape(1)
        looked[key] = lookup(ids, table_rows, start, own_rows, row_count)
    mine = summed_block([looked[key] for key in range(tensor_count)], "tensor", NARROW)
    side = (seq_lengths, mask_slots, mask_targets, positive_rows, doc_ids, false_pairs)
    side = side + (queue_docs, factors, gate_up_error, down_error, attend_error, data_rank)
    side, near_ids, near, _ = lax.optimization_barrier((side, token_ids, near, looked[0]))
    seq_lengths, mask_slots, mask_targets, positive_rows, doc_ids, false_pairs = side[:6]
    queue_docs, factors, gate_up_error, down_error, attend_error, data_rank = side[6:]
    pieces = mine.astype(NARROW).T.reshape(data_count, row_count, own_rows)
    embedded = lax.all_to_all(pieces, "dp", 0, 0).reshape(width, own_rows).T

    attend_cols = attend_error.shape[2]
    quarter = lax.dynamic_slice_in_dim(attend_weight, tensor_rank * attend_cols, attend_cols, 1)
    joined = jnp.concatenate(
        [quarter, gate_up[:, 0], gate_up[:, 1], down_weight], axis=1
    ).astype(NARROW)
    joined_b = lax.all_gather(joined, "dp", axis=0, tiled=True)
    quarter_b, ffn_b = joined_b[:, :attend_cols], joined_b
    attend_near = picked_blocks(spread_blocks(quarter_b, "tensor"), near)
    attend_b = jnp.concatenate([attend_near[k] for k in range(tensor_count)], axis=1)
    table_local, _ = lax.optimization_barrier((table_local, looked[tensor_count - 1]))
    table_b = lax.all_gather(table_local, "dp", axis=0, tiled=True)

    every_rows = mask_slots + own_rows * jnp.arange(tensor_count)[None, :, None]
    every_len = seq_lengths[:, None, None]
    count = jnp.sum((every_rows < every_len).astype(WIDE))
    my_length = lax.dynamic_index_in_dim(seq_lengths, data_rank, 0, keepdims=False)
    group_valid = lax.dynamic_index_in_dim(every_rows < every_len, data_rank, 0, keepdims=False)
    own_slots = lax.dynamic_slice(
        mask_slots, (data_rank, tensor_rank, 0), (1, 1, slot_count)
    ).reshape(1, slot_count)
    own_length = (my_length - tensor_rank * own_rows).reshape(1)
    valid_rows = picked_blocks(group_valid, near).reshape(-1, 1).astype(WIDE)
    row_weight = valid_rows / count
    targets = picked_blocks(mask_targets[0], near).reshape(-1, 1) - vocab_start
    near_tokens = picked_blocks(near_ids.reshape(tensor_count, own_rows), near).reshape(1, -1)
    shifted = near_tokens - vocab_start
    tiles = -(-vocab_own // TILE)
    index = jnp.arange(total_rows)
    before = (shifted < shifted.T) | ((shifted == shifted.T) & (index[None, :] < index[:, None]))
    ranks = jnp.sum(before.astype(jnp.int32), axis=1)
    ordered = ranks[None, :] == index[:, None]
    sorted_ids = jnp.sum(jnp.where(ordered, shifted, 0), axis=1)[None, :]
    starts = jnp.sum(
        (shifted < jnp.minimum(jnp.arange(tiles + 1) * TILE, vocab_own)[:, None]).astype(jnp.int32),
        axis=1,
    )
    places = near[:, None] * own_rows + jnp.arange(own_rows)[None, :]
    cosine, sine = rotary_tables(places.reshape(-1))
    cosines, sines = row_blocks(cosine, tensor_count), row_blocks(sine, tensor_count)
    bias = jnp.where(places < my_length, 0.0, NEGATIVE).astype(NARROW)
    biases = [jnp.broadcast_to(bias[k][:, None], (own_rows, PAIR)) for k in range(tensor_count)]
    columns = jnp.arange(queue_docs.shape[0])
    pick = lambda array: lax.dynamic_slice_in_dim(array, data_rank, 1, 0)
    target_c = columns[None, :] == pick(positive_rows)[:, None]
    blocked = (queue_docs[None, :] == pick(doc_ids)[:, None]) | jnp.any(
        pick(false_pairs)[:, :, None] == columns[None, None, :], axis=1
    )
    blocked = (blocked & jnp.logical_not(target_c)).astype(WIDE)
    target_c = target_c.astype(WIDE)

    x_zero, x_zero_b = norm_forward(gains[:1], embedded)
    x_blocks = spread_blocks(x_zero_b, "tensor")
    queries, first_key, first_value = project(3, x_zero_b, attend_b, cosines[0], sines[0])
    keys, values = [first_key], [first_value]
    for k in range(1, tensor_count):
        key, value = project(2, x_blocks[k], attend_b, cosines[k], sines[k])
        keys.append(key)
        values.append(value)
    attended_t, log_total = attention_forward(queries, keys, values, biases)
    queue_local, _ = lax.optimization_barrier((queue_embed, log_total))
    queue_all = lax.all_gather(queue_local, "dp", axis=0, tiled=True)
    keys_hat = normalize_keys(queue_all)
    weight_out = attend_b[:, 3 * width :]
    attended_b, pre_one, hidden_in, hidden_in_b = merge_branch(
        attended_t, weight_out, x_zero, gains[1:2]
    )
    hidden_blocks = spread_blocks(hidden_in_b, "tensor")
    half = max(1, tensor_count // 2)
    hidden_parts = [
        jnp.concatenate(hidden_blocks[at : at + half], axis=0)
        for at in range(0, tensor_count, half)
    ]
    states = []
    for part in hidden_parts:
        if states:
            part, _ = lax.optimization_barrier((part, states[-1][3]))
        states.append(ffn_forward(part, ffn_b))
    ffn_blocks = [block for state in states for block in row_blocks(state[3], half)]
    ffn_mine, ffn_got = summed_pair(ffn_blocks, "tensor")
    final, _ = norm_forward(gains[2:], hidden_in, ffn_mine, ffn_got)

    factor_t = jnp.swapaxes(factors, 1, 2)
    factor_near = spread_blocks(factor_t[0], "tensor")
    error_p = partial_projections([attend_error[0]], [factor_t[0]])[0]
    ff_own = down_weight.shape[1]

    keep_own = (places[0] < my_length)[:, None]
    pool_part = jnp.sum(jnp.where(keep_own, final, 0.0), axis=0)
    picked = jnp.take(final, own_slots[0], axis=0).astype(NARROW)
    rows_all = jnp.concatenate(spread_blocks(picked, "tensor"), axis=0)
    logits, stats = vocab_logits(rows_all, table_b, targets)
    picks = rows_all.shape[0]
    pool_rows = jnp.pad(pool_part.reshape(-1, 128), ((0, 8 - width // 128), (0, 0)))
    stats = jnp.concatenate([stats, pool_rows], axis=0)
    for bit in axis_bits("tensor"):
        other = swap(stats, "tensor", bit)
        stats = whole_call(
            functools.partial(combine_kernel, tensor_count, slot_count, bit),
            [(stats.shape, WIDE)],
            20 * stats.size,
            stats,
            other,
        )[0]
    pooled_sum = stats[picks : picks + width // 128].reshape(1, width)
    own_stats = stats[:slot_count]
    cross = own_stats[:, 0] + jnp.log(own_stats[:, 1]) - own_stats[:, 2]
    masked_part = jnp.sum(valid_rows[:slot_count, 0] * cross)
    dlogits, row_part = vocab_back(logits, table_b, targets, stats[:picks], row_weight)
    row_grad = summed_block(row_blocks(row_part, tensor_count), "tensor", NARROW)

    weight_c = LAMBDA / seq_total
    first_rank = jnp.where(tensor_rank == 0, 1.0, 0.0)
    pooled_grad, contrast_row = contrast(
        weight_c, my_length.reshape(1), pooled_sum, keys_hat, blocked, target_c
    )
    contrast_part = contrast_row[0, 0] * first_rank

    pre_grad, pre_grad_b, gain_two = last_back(
        own_length, own_slots, row_grad, pooled_grad, hidden_in, ffn_mine, ffn_got, gains[2:]
    )
    grad_blocks = spread_blocks(pre_grad_b, "tensor")
    grad_parts = [
        jnp.concatenate(grad_blocks[at : at + half], axis=0) for at in range(0, tensor_count, half)
    ]
    backs = [
        ffn_backward(part, state[0], state[1], ffn_b) for part, state in zip(grad_parts, states)
    ]
    hidden_sums = [block for back in backs for block in row_blocks(back[2], half)]
    hidden_mine, hidden_got = summed_pair(hidden_sums, "tensor")
    down_grad = sum(contract_rows(part, state[2]) for part, state in zip(grad_parts, states))
    gate_w_grad = sum(contract_rows(part, back[0]) for part, back in zip(hidden_parts, backs))
    up_w_grad = sum(contract_rows(part, back[1]) for part, back in zip(hidden_parts, backs))
    pre_one_grad, branch_grad, attended_grad, gain_one = branch_back(
        pre_grad, hidden_mine, hidden_got, pre_one, gains[1:2], weight_out
    )
    dq, dk, dv = attention_backward(
        queries, keys, values, biases, attended_grad, attended_t, log_total, cosines, sines
    )
    weight_k, weight_v = attend_b[:, width : 2 * width], attend_b[:, 2 * width : 3 * width]
    x_parts = [
        (contract_cols(dk[k], weight_k) + contract_cols(dv[k], weight_v)).astype(NARROW)
        for k in range(tensor_count)
    ]
    x_mine, x_got = summed_pair(x_parts, "tensor")
    embedded_grad, gain_zero = first_back(
        pre_one_grad, dq, attend_b[:, :width], x_mine, x_got, embedded, gains[:1]
    )
    emb_all = jnp.concatenate(spread_blocks(embedded_grad, "tensor"), axis=0)
    emb_all = jnp.dot(ordered.astype(NARROW), emb_all)
    attend_part = jnp.concatenate(
        [
            contract_rows(x_zero_b, dq),
            sum(contract_rows(x_blocks[k], dk[k]) for k in range(tensor_count)),
            sum(contract_rows(x_blocks[k], dv[k]) for k in range(tensor_count)),
            jnp.dot(attended_b, branch_grad, preferred_element_type=WIDE),
        ],
        axis=1,
    )
    attend_blocks = jnp.moveaxis(attend_part.reshape(width, tensor_count, attend_cols), 1, 0)
    attend_blocks = picked_blocks(attend_blocks, near)
    attend_p = partial_projections(
        [attend_blocks[k] for k in range(tensor_count)], factor_near
    )
    attend_p = summed_block([attend_p[k] for k in range(tensor_count)], "tensor", WIDE)
    attend_p = attend_p + error_p
    attend_held = dict(enumerate(attend_blocks[k] for k in range(tensor_count)))
    bits = axis_bits("tensor")
    for bit in bits[:-1]:
        for key in sorted((k for k in attend_held if not k & bit), reverse=True):
            attend_held[key] = attend_held[key] + swap(attend_held.pop(key ^ bit), "tensor", bit)
    emb_all, attend_held[bits[-1]] = lax.optimization_barrier((emb_all, attend_held[bits[-1]]))
    attend_grad = attend_held[0] + swap(attend_held[bits[-1]], "tensor", bits[-1])

    other_m, other_p = small_matrices(
        [gate_w_grad, up_w_grad, down_grad],
        [gate_up_error[0, :, 0], gate_up_error[0, :, 1], down_error[0]],
        factor_t[1:4],
    )
    other_sum = summed_all(jnp.concatenate([other_p[k] for k in range(3)], axis=1), "dp")
    cuts = [tiles * part // PARTS for part in range(PARTS + 1)]
    table_parts, table_sums = [], []
    for bounds in zip(cuts, cuts[1:]):
        found = table_matrix(
            bounds, starts, emb_all, sorted_ids, rows_all, dlogits, embed_error[0].T, factor_t[4]
        )
        table_parts.append(found)
        piece = found[2]
        if bounds[1] == tiles:
            piece = jnp.concatenate([piece, attend_p], axis=1)
        table_sums.append(summed_all(piece, "dp"))
    highs, lows = [part[0] for part in table_parts], [part[1] for part in table_parts]
    parts = [table_sums[-1][:, -attend_cols:], other_sum] + table_sums[:-1]
    parts.append(table_sums[-1][:, :-attend_cols])
    sums = jnp.concatenate(parts, axis=1)
    first_m = (attend_grad + attend_error[0])[None]
    spans, start = [], 0
    for size in (attend_cols, ff_own, ff_own, ff_own, tiles * TILE):
        spans.append((start, size))
        start += size
    bases_t = bases_of(sums, spans)
    small_basis = jnp.stack([bases_t[:, at : at + size] for at, size in spans[:4]])
    table_basis = bases_t[:, spans[4][0] :]
    other_back = small_backs(other_m, small_basis[1:])
    tab_back = table_back(highs, lows, table_basis)
    gain_terms = jnp.concatenate([gain_zero, gain_one, gain_two], axis=0)
    loss_terms = jnp.stack([masked_part, contrast_part])
    loss_row = jnp.zeros((1, width), WIDE).at[0, :2].set(loss_terms)
    packed = jnp.concatenate(
        [other_back.reshape(-1, width), tab_back, gain_terms, loss_row], axis=0
    )
    packed = summed_all(packed, "dp")
    first_back_t = small_backs(first_m, small_basis[:1])
    first_sum = summed_all(first_back_t[0], "dp")
    errors = small_errors(first_m, first_back_t, small_basis[:1]) + small_errors(
        other_m, other_back, small_basis[1:]
    )
    new_table_error = table_error(highs, lows, tab_back, table_basis, vocab_own).T
    own_t = jnp.concatenate([first_sum, packed[: 4 * RANK]], axis=0).reshape(5, RANK, width)
    square = jnp.sum(own_t * own_t)
    tail = packed[4 * RANK :].at[3, 2].set(square)
    shared = jnp.concatenate(
        [own_t[0], tail, jnp.pad(small_basis[0], ((0, 0), (0, width - attend_cols)))], axis=0
    )
    shared = picked_blocks(spread_blocks(shared, "tensor"), near)
    tail_sum = jnp.sum(shared[:, RANK : RANK + 4], axis=0)
    gains_grad = tail_sum[:3]
    loss_sums = tail_sum[3, :2]
    clip_norm = jnp.sqrt(tail_sum[3, 2] + jnp.sum(gains_grad * gains_grad))
    shrink = CLIP / jnp.maximum(clip_norm, CLIP)
    row_start = data_rank * row_count

    def rows_of(factor):
        return lax.dynamic_slice_in_dim(factor, row_start, row_count, factor.ndim - 1)

    reduced_attend = jnp.einsum(
        "tkd,tkn->dtn",
        rows_of(shared[:, :RANK]),
        shared[:, RANK + 4 :, :attend_cols],
        precision=HIGH,
    ).reshape(row_count, -1)
    own_rows_t = rows_of(own_t)

    def reduced(index, basis):
        return dot_in(own_rows_t[index], basis, ((0,), (0,)), precision=HIGH)

    reduced_gate_up = jnp.stack(
        [reduced(1, small_basis[1]), reduced(2, small_basis[2])], axis=1
    )
    reduced_down = reduced(3, small_basis[3])
    reduced_table = reduced(4, table_basis[:, :vocab_own])

    def advance(weight, moment, grad):
        fresh = MOMENTUM * moment + shrink * grad
        return (weight - LRATE * fresh, fresh)

    new_attend, new_attend_moment = advance(attend_weight, attend_moment, reduced_attend)
    new_gate_up, new_gate_up_moment = advance(gate_up, gate_up_moment, reduced_gate_up)
    new_down, new_down_moment = advance(down_weight, down_moment, reduced_down)
    new_table, new_table_moment = advance(embed_table, embed_moment, reduced_table)
    new_gains, new_gains_moment = advance(gains, gains_moment, gains_grad)
    return (
        new_attend,
        new_attend_moment,
        new_gate_up,
        new_gate_up_moment,
        new_down,
        new_down_moment,
        new_table,
        new_table_moment,
        new_gains,
        new_gains_moment,
        errors[0][None],
        jnp.stack([errors[1], errors[2]], axis=1)[None],
        errors[3][None],
        new_table_error[None],
        jnp.swapaxes(own_t, 1, 2),
        clip_norm,
        loss_sums[0],
        count,
        loss_sums[1],
    )


def solution(mesh):
    in_specs = (
        P("dp", None),
        P(),
        P(),
        P("dp", None, None),
        P(),
        P(),
        P(),
        P(),
        P("dp", None),
        P("dp", None),
        P("dp", None),
        P("dp", None, "tensor"),
        P("dp", None, "tensor"),
        P("dp", "tensor"),
        P("dp", "tensor"),
        P("dp", "tensor"),
        P("dp", "tensor"),
        P(),
        P(),
        P("dp", None, "tensor"),
        P("dp", None, None, "tensor"),
        P("dp", None, "tensor"),
        P("dp", None, "tensor"),
        P(None, None, "tensor"),
    )
    out_specs = (
        P("dp", None),
        P("dp", None),
        P("dp", None, "tensor"),
        P("dp", None, "tensor"),
        P("dp", "tensor"),
        P("dp", "tensor"),
        P("dp", "tensor"),
        P("dp", "tensor"),
        P(),
        P(),
        P("dp", None, "tensor"),
        P("dp", None, None, "tensor"),
        P("dp", None, "tensor"),
        P("dp", None, "tensor"),
        P(None, None, "tensor"),
        P(),
        P(),
        P(),
        P(),
    )
    return jax.shard_map(
        per_device, mesh=mesh, in_specs=in_specs, out_specs=out_specs, check_vma=False
    )
```

time: 954 us -> 786 us (0.82)
  waiting for transfers between devices: 360 us -> 123 us
  Pallas kernels: 209 us -> 343 us
  matrix products: 117 us -> 57.8 us
  starting transfers between devices: 30.2 us -> 60.3 us
  other arithmetic: 86.1 us -> 69.5 us
  local copies, waits for them, and re-layouts: 111 us -> 96.6 us
    all_gather x5 -> x3, waiting for transfers between devices: 186 us -> 5.68 us  [the longest x1 4.42 us: per_device(): joined_b = lax.all_gather(joined, 'dp', axis=0, tiled=True)]
    pallas_call x7 -> x32, Pallas kernels: 178 us -> 311 us  [the longest x4 52.4 us: lookup(): pl.pallas_call(functools.partial(lookup_kernel, row_count), in_specs=[pl....]
    ppermute x47 -> x65, waiting for transfers between devices: 174 us -> 102 us  [swap(): lax.ppermute(value, axis, [(index, index ^ bit) for index in range(size)])]
    dot_general x6 -> x1, matrix products: 40.6 us -> 9.05 us  [per_device(): emb_all = jnp.dot(ordered.astype(NARROW), emb_all)]
    dot_general x20 -> x27, matrix products: 74.7 us -> 46.6 us  [dot_in(): lax.dot_general(left, right, (axes, ((), ())), precision=precision, prefe...]
    ppermute x47 -> x65, starting transfers between devices: 29.6 us -> 49.1 us  [swap(): lax.ppermute(value, axis, [(index, index ^ bit) for index in range(size)])]
    all_gather x1 -> x0, local copies, waits for them, and re-layouts: 16.2 us -> none  [per_device(): lax.all_gather(embed_table.astype(NARROW), 'dp', axis=0, tiled=True)]
    gather x2 -> x1, local copies, waits for them, and re-layouts: 17.8 us -> 2.09 us  [per_device(): picked = jnp.take(final, own_slots[0], axis=0).astype(NARROW)]
  transfers between devices with their start and end apart: 52 -> 70, of which waited for: 25 -> 22; matrix products, arithmetic and copies ran while one was open for 20% -> 24% of each run, Pallas kernels for 13% -> 44%
where the time goes in v2:
time: 786 us; the launch traced here: 777 us
  Pallas kernels  343 us (44%)
  waiting for transfers between devices  123 us (16%)
  local copies, waits for them, and re-layouts  96.6 us (12%)
  other arithmetic  69.5 us (9%)
  starting transfers between devices  60.3 us (8%)
  matrix products  57.8 us (7%)
  between operations  27.1 us (3%)
    ppermute x65, waiting for transfers between devices, swap(): lax.ppermute(value, axis, [(index, index ^ bit) for index in range(size)])  102 us
    pallas_call x4, Pallas kernels, lookup(): pl.pallas_call(functools.partial(lookup_kernel, row_count), in_specs=[pl....  52.4 us
    ppermute x65, starting transfers between devices, swap(): lax.ppermute(value, axis, [(index, index ^ bit) for index in range(size)])  49.1 us
    pallas_call x1, Pallas kernels, attention_backward(): pl.pallas_call(functools.partial(attend_back_kernel, count), grid=(pairs,...  47.7 us
    dot_general x27, matrix products, dot_in(): lax.dot_general(left, right, (axes, ((), ())), precision=precision, prefe...  46.6 us
    unnamed x203, local copies, waits for them, and re-layouts  40.7 us
    pallas_call x9, Pallas kernels, whole_call(): pl.pallas_call(kernel, out_shape=[jax.ShapeDtypeStruct(shape, kind) for s...  35.2 us
    pallas_call x3, Pallas kernels, table_matrix(): pl.pallas_call(functools.partial(table_kernel, columns, first), grid=(til...  32.2 us
  transfers between devices with their start and end apart: 70, of which 22 were waited for; matrix products, arithmetic and copies ran while one was open for 24% of the time, Pallas kernels for 44%

profile of v2, /device:TPU:0, one launch (start us, length us, event | category | flops | bytes accessed | tf_op | source)
XLA Modules:
  0.0 777.2 jit_solution(18315269077457958287)
XLA Ops:
  12.1 7.3 all-to-all-start
  23.1 9.0 %copy.105.table_ref = f32[7633,1,128]{2,1,0:T(1,128)} copy(f32[7633,1,128]{0,2,1:T(8,128)} %bitcast_convert_fusion) | data formatting | bytes 7816192 | tf_op jit(solution)/shard_map/broadcast_in_dim | solution.py:1137
  32.8 13.1 %shard_map.381 = bf16[512,768]{1,0:T(8,128)(2,1)} custom-call(s32[1]{0:T(128)} %bitcast.8.start_ref, s32[8,2048]{1,0:T(8,128)} %bitcast_select_fusion.ids_ref, f32[7633,1,128]{2,1,0:T(1,128)} %copy.105.table_ref), custom_call_target="tpu_custom_call" | custom-call | flops 16777216 | bytes 3908096 | tf_op jit(solution)/shard_map/pallas_call | solution.py:214
  46.0 13.1 %shard_map.379 = bf16[512,768]{1,0:T(8,128)(2,1)} custom-call(s32[1]{0:T(128)} %bitcast.5.start_ref, s32[8,2048]{1,0:T(8,128)} %bitcast_select_fusion.ids_ref, f32[7633,1,128]{2,1,0:T(1,128)} %copy.105.table_ref), custom_call_target="tpu_custom_call" | custom-call | flops 16777216 | bytes 3908096 | tf_op jit(solution)/shard_map/pallas_call | solution.py:214
  59.6 13.1 %shard_map.380 = bf16[512,768]{1,0:T(8,128)(2,1)} custom-call(s32[1]{0:T(128)} %bitcast.7.start_ref, s32[8,2048]{1,0:T(8,128)} %bitcast_select_fusion.ids_ref, f32[7633,1,128]{2,1,0:T(1,128)} %copy.105.table_ref), custom_call_target="tpu_custom_call" | custom-call | flops 16777216 | bytes 3908096 | tf_op jit(solution)/shard_map/pallas_call | solution.py:214
  76.7 13.1 %shard_map.378 = bf16[512,768]{1,0:T(8,128)(2,1)} custom-call(s32[1]{0:T(128)} %bitcast.start_ref, s32[8,2048]{1,0:T(8,128)} %bitcast_select_fusion.ids_ref, f32[7633,1,128]{2,1,0:T(1,128)} %copy.105.table_ref), custom_call_target="tpu_custom_call" | custom-call | flops 16777216 | bytes 3908096 | tf_op jit(solution)/shard_map/pallas_call | solution.py:214
  114.4 9.5 %collective-permute-done.4 = bf16[768,768]{1,0:T(8,128)(2,1)} collective-permute-done((bf16[768,768]{1,0:T(8,128)(2,1)}, bf16[768,768]{1,0:T(8,128)(2,1)}, u32[]{:S(2)}, u32[]{:S(2)}) %collective-permute-start.4) | collective-permute-done | bytes 1179680 | tf_op jit(solution)/shard_map/ppermute | solution.py:43
  129.0 15.0 %all-to-all-done.1 = bf16[8,96,512]{2,1,0:T(8,128)(2,1)S(1)} async-done(((bf16[8,96,512]{2,1,0:T(8,128)(2,1)}), bf16[8,96,512]{2,1,0:T(8,128)(2,1)S(1)}, u32[]{:S(2)}, u32[]{:S(2)}) %all-to-all-start.1) | async-done | bytes 786464 | tf_op jit(solution)/shard_map/all_to_all | solution.py:1149
  153.8 6.6 collective-permute-done.7.x_ref
  166.2 4.4 shard_map.385
  171.6 4.5 shard_map.384
  177.0 4.8 shard_map.386
  181.8 5.7 shard_map.383
  190.6 24.6 %shard_map.387 = (f32[768,512]{1,0:T(8,128)}, f32[6,2,512]{2,1,0:T(2,128)}) custom-call(bf16[512,768]{1,0:T(8,128)(2,1)} %get-tuple-element.134.q_ref, bf16[512,768]{1,0:T(8,128)(2,1)} %get-tuple-element.138.refs_0_, bf16[512,768]{1,0:T(8,128)(2,1)} %get-tuple-element.139.refs_1_, bf16[512,768]{1,0:T(8,128)(2,1)} %get-tuple-element.140.refs_2_, ...), custom_call_target="tpu_custom_call" | custom-call | flops 3221225472 | bytes 9437184 | tf_op jit(solution)/shard_map/pallas_call | solution.py:695
  215.2 5.1 shard_map.388
  223.9 16.3 %collective-permute-done.11 = bf16[512,768]{1,0:T(8,128)(2,1)S(1)} collective-permute-done((bf16[512,768]{1,0:T(8,128)(2,1)}, bf16[512,768]{1,0:T(8,128)(2,1)S(1)}, u32[]{:S(2)}, u32[]{:S(2)}) %collective-permute-start.11) | collective-permute-done | bytes 786464 | tf_op jit(solution)/shard_map/ppermute | solution.py:43
  247.2 8.2 %shard_map.389 = (f32[1024,768]{1,0:T(8,128)}, f32[1024,768]{1,0:T(8,128)}, bf16[1024,768]{1,0:T(8,128)(2,1)}, bf16[1024,768]{1,0:T(8,128)(2,1)}) custom-call(bf16[1024,768]{1,0:T(8,128)(2,1)} %copy-done.20, bf16[768,3072]{1,0:T(8,128)(2,1)} %all-gather.4.cloned.1.call-done.gate_ref.up_ref.down_ref, ...), custom_call_target="tpu_custom_call" | custom-call | flops 3623878656 | bytes 14548992 | tf_op jit(solution)/shard_map/pallas_call | solution.py:402
  257.8 8.7 %shard_map.390 = (f32[1024,768]{1,0:T(8,128)}, f32[1024,768]{1,0:T(8,128)}, bf16[1024,768]{1,0:T(8,128)(2,1)}, bf16[1024,768]{1,0:T(8,128)(2,1)}) custom-call(bf16[1024,768]{1,0:T(8,128)(2,1)} %copy-done.18, bf16[768,3072]{1,0:T(8,128)(2,1)} %all-gather.4.cloned.1.call-done.gate_ref.up_ref.down_ref, ...), custom_call_target="tpu_custom_call" | custom-call | flops 3623878656 | bytes 14548992 | tf_op jit(solution)/shard_map/pallas_call | solution.py:402
  275.2 5.2 convert_reduce_fusion
  281.6 12.7 %collective-permute-done.14.refs_2_.got_ref = bf16[512,768]{1,0:T(8,128)(2,1)S(1)} collective-permute-done((bf16[512,768]{1,0:T(8,128)(2,1)S(1)}, bf16[512,768]{1,0:T(8,128)(2,1)S(1)}, u32[]{:S(2)}, u32[]{:S(2)}) %collective-permute-start.14) | collective-permute-done | bytes 786464 | tf_op jit(solution)/shard_map/ppermute | solution.py:43
  307.9 9.6 %shard_map.392 = (f32[160,7680]{1,0:T(8,128)}, f32[160,128]{1,0:T(8,128)}) custom-call(bf16[160,768]{1,0:T(8,128)(2,1)} %pad_maximum_fusion.5.rows_ref, bf16[768,7632]{1,0:T(8,128)(2,1)} %all-gather.6.cloned.1.call-done.table_ref, s32[160,1]{1,0:T(8,128)} %sub.76.targets_ref), custom_call_target="tpu_custom_call" | custom-call | flops 1875640320 | bytes 11722752 | tf_op jit(solution)/shard_map/pallas_call | solution.py:520
  333.0 11.3 %shard_map.395 = (bf16[160,7680]{1,0:T(8,128)(2,1)}, f32[160,768]{1,0:T(8,128)}) custom-call(f32[160,7680]{1,0:T(8,128)} %get-tuple-element.156.logits_ref, bf16[768,7632]{1,0:T(8,128)(2,1)} %all-gather.6.cloned.1.call-done.table_ref, s32[160,1]{1,0:T(8,128)} %sub.76.targets_ref, f32[160,128]{1,0:T(8,128)} %slice.397.stats_ref, f32[160,1]{1,0:T(8,128)} %div.23.weight_ref), custom_call_target="tpu_custom_call" | custom-call | flops 1875640320 | bytes 11722752 | tf_op jit(solution)/shard_map/pallas_call | solution.py:584
  354.1 4.7 shard_map.397
  371.8 6.5 collective-permute-done.25
  382.5 9.8 %shard_map.398 = (bf16[1024,768]{1,0:T(8,128)(2,1)}, bf16[1024,768]{1,0:T(8,128)(2,1)}, bf16[1024,768]{1,0:T(8,128)(2,1)}) custom-call(bf16[1024,768]{1,0:T(8,128)(2,1)} %copy-done.22, f32[1024,768]{1,0:T(8,128)} %get-tuple-element.168.gate_in, f32[1024,768]{1,0:T(8,128)} %get-tuple-element.169.up_in, ...), custom_call_target="tpu_custom_call" | custom-call | flops 3623878656 | bytes 16121856 | tf_op jit(solution)/shard_map/pallas_call | solution.py:446
  396.5 10.1 %shard_map.399 = (bf16[1024,768]{1,0:T(8,128)(2,1)}, bf16[1024,768]{1,0:T(8,128)(2,1)}, bf16[1024,768]{1,0:T(8,128)(2,1)}) custom-call(bf16[1024,768]{1,0:T(8,128)(2,1)} %copy-done.24, f32[1024,768]{1,0:T(8,128)} %get-tuple-element.171.gate_in, f32[1024,768]{1,0:T(8,128)} %get-tuple-element.172.up_in, ...), custom_call_target="tpu_custom_call" | custom-call | flops 3623878656 | bytes 16121856 | tf_op jit(solution)/shard_map/pallas_call | solution.py:446
  424.8 11.1 %collective-permute-done.28.got_ref = bf16[512,768]{1,0:T(8,128)(2,1)S(1)} collective-permute-done((bf16[512,768]{1,0:T(8,128)(2,1)S(1)}, bf16[512,768]{1,0:T(8,128)(2,1)S(1)}, u32[]{:S(2)}, u32[]{:S(2)}) %collective-permute-start.28) | collective-permute-done | bytes 786464 | tf_op jit(solution)/shard_map/ppermute | solution.py:43
  436.8 5.7 shard_map.400
  442.5 47.7 %shard_map.401 = (bf16[512,768]{1,0:T(8,128)(2,1)}, bf16[512,768]{1,0:T(8,128)(2,1)}, bf16[512,768]{1,0:T(8,128)(2,1)}, bf16[512,768]{1,0:T(8,128)(2,1)}, bf16[5...) custom-call(bf16[512,768]{1,0:T(8,128)(2,1)} %get-tuple-element.134., ...), custom_call_target="tpu_custom_call" | custom-call | flops 8053063680 | bytes 15728640 | tf_op jit(solution)/shard_map/pallas_call | solution.py:776
  523.2 8.1 %collective-permute-done.32.got_ref = bf16[512,768]{1,0:T(8,128)(2,1)} collective-permute-done((bf16[512,768]{1,0:T(8,128)(2,1)}, bf16[512,768]{1,0:T(8,128)(2,1)}, u32[]{:S(2)}, u32[]{:S(2)}) %collective-permute-start.32) | collective-permute-done | bytes 786464 | tf_op jit(solution)/shard_map/ppermute | solution.py:43
  531.3 5.2 shard_map.402
  537.1 4.5 convolution_add_fusion.refs_2_
  541.6 9.4 %shard_map.406 = (f32[3,768,768]{2,1,0:T(8,128)}, f32[3,8,768]{2,1,0:T(8,128)}) custom-call(f32[768,768]{1,0:T(8,128)} %convolution_add_fusion.2.refs_0_, f32[768,768]{1,0:T(8,128)} %convolution_add_fusion.1.refs_1_, f32[768,768]{1,0:T(8,128)} %convolution_add_fusion.refs_2_, f32[768,768]{1,0:T(8,128)} %get-tuple-element.316.refs_3_, ...), custom_call_target="tpu_custom_call" | custom-call | flops 84934656 | bytes 21233664 | tf_op jit(solution)/shard_map/pallas_call | solution.py:922
  559.1 6.1 shard_map.404
  575.9 9.0 %fusion.left_ref = bf16[2048,768]{1,0:T(8,128)(2,1)} fusion(s32[2048]{0:T(1024)S(1)} %convert_reduce_fusion, bf16[512,768]{1,0:T(8,128)(2,1)S(1)} %collective-permute-done.35, bf16[512,768]{1,0:T(8,128)(2,1)S(1)} %collective-permute-done.34, bf16[512,768]{1,0:T(8,128)(2,1)S(1)} %collective-permute-done.33, bf16[512,768]{1,0:T(8,128)(2,1)S(1)} %copy-done.89), kind=kOutput, calls=%fused_computation.3 | convolution fusion | flops 6459228160 | bytes 6299648 | tf_op jit(solution)/shard_map/dot_general | solution.py:1299
  585.0 10.4 %shard_map.403 = (bf16[2560,768]{1,0:T(8,128)(2,1)}, bf16[2560,768]{1,0:T(8,128)(2,1)}, f32[8,2560]{1,0:T(8,128)}) custom-call(s32[7]{0:T(128)} %convert_reduce_fusion.1.starts_ref, bf16[2048,768]{1,0:T(8,128)(2,1)} %fusion.left_ref, s32[1,2048]{1,0:T(1,128)} %bitcast.273, bf16[160,768]{1,0:T(8,128)(2,1)} %pad_maximum_fusion.5.rows_ref, ...), custom_call_target="tpu_custom_call" | custom-call | flops 2736783360 | bytes 15728640 | tf_op jit(solution)/shard_map/pallas_call | solution.py:862
  595.4 10.5 %shard_map.407 = (bf16[2560,768]{1,0:T(8,128)(2,1)}, bf16[2560,768]{1,0:T(8,128)(2,1)}, f32[8,2560]{1,0:T(8,128)}) custom-call(s32[7]{0:T(128)} %convert_reduce_fusion.1.starts_ref, bf16[2048,768]{1,0:T(8,128)(2,1)} %fusion.left_ref, s32[1,2048]{1,0:T(1,128)} %bitcast.274, bf16[160,768]{1,0:T(8,128)(2,1)} %pad_maximum_fusion.5.rows_ref, ...), custom_call_target="tpu_custom_call" | custom-call | flops 2736783360 | bytes 15728640 | tf_op jit(solution)/shard_map/pallas_call | solution.py:862
  609.1 11.3 %shard_map.408 = (bf16[2560,768]{1,0:T(8,128)(2,1)}, bf16[2560,768]{1,0:T(8,128)(2,1)}, f32[8,2560]{1,0:T(8,128)}) custom-call(s32[7]{0:T(128)} %convert_reduce_fusion.1.starts_ref, bf16[2048,768]{1,0:T(8,128)(2,1)} %fusion.left_ref, s32[1,2048]{1,0:T(1,128)} %bitcast.275, bf16[160,768]{1,0:T(8,128)(2,1)} %pad_maximum_fusion.5.rows_ref, ...), custom_call_target="tpu_custom_call" | custom-call | flops 2736783360 | bytes 15728640 | tf_op jit(solution)/shard_map/pallas_call | solution.py:862
  630.4 4.6 collective-permute-start.46
  641.0 5.8 collective-permute-done.49
  658.5 5.6 shard_map.411.back_ref
  664.2 12.6 %shard_map.412.refs_6_ = f32[8,768]{1,0:T(8,128)} custom-call(bf16[2560,768]{1,0:T(8,128)(2,1)} %get-tuple-element.208.refs_0_, bf16[2560,768]{1,0:T(8,128)(2,1)} %get-tuple-element.209.refs_1_, bf16[2560,768]{1,0:T(8,128)(2,1)} %get-tuple-element.210.refs_2_, bf16[2560,768]{1,0:T(8,128)(2,1)} %get-tuple-element.211.refs_3_, ...), custom_call_target="tpu_custom_call" | custom-call | flops 283115520 | bytes 23592960 | tf_op jit(solution)/shard_map/pallas_call | solution.py:1017
  682.6 7.9 %collective-permute-done.37 = f32[768,768]{1,0:T(8,128)} collective-permute-done((f32[768,768]{1,0:T(8,128)}, f32[768,768]{1,0:T(8,128)}, u32[]{:S(2)}, u32[]{:S(2)}) %collective-permute-start.37) | collective-permute-done | bytes 2359328 | tf_op jit(solution)/shard_map/ppermute | solution.py:43
  690.5 5.2 add_bitcast_fusion.m_ref
  699.9 6.5 shard_map.414
  713.1 5.8 copy.126
  719.1 20.6 %shard_map.415 = f32[7632,768]{1,0:T(8,128)} custom-call(bf16[2560,768]{1,0:T(8,128)(2,1)} %get-tuple-element.208.refs_0_, bf16[2560,768]{1,0:T(8,128)(2,1)} %get-tuple-element.209.refs_1_, bf16[2560,768]{1,0:T(8,128)(2,1)} %get-tuple-element.210.refs_2_, bf16[2560,768]{1,0:T(8,128)(2,1)} %get-tuple-element.211.refs_3_, ...), custom_call_target="tpu_custom_call" | custom-call | flops 281346048 | bytes 46891008 | tf_op jit(solution)/shard_map/pallas_call | solution.py:1064
  763.7 5.7 multiply_subtract_fusion
  (508 shorter events, 279.0 us)
Async XLA Ops:
  7.2 87.0 %all-gather.4.cloned.1.call-start = ((), (), s32[]{:S(2)}) async-start(), calls=%async_computation.2 | async-start | bytes 5308416 | tf_op jit(solution)/shard_map/all_gather | solution.py:1156
  12.1 20.0 %all-to-all-start = ((s32[8,1,2048]{2,1,0:T(1,128)}), s32[8,1,2048]{2,1,0:T(1,128)S(1)}, u32[]{:S(2)}, u32[]{:S(2)}) async-start(s32[8,1,2048]{2,1,0:T(1,128)} %broadcast_in_dim.118), calls=%async_computation | async-start | bytes 131072 | tf_op jit(solution)/shard_map/all_to_all | solution.py:1128
  19.4 288.5 %all-gather.6.cloned.1.call-start = ((), (), s32[]{:S(2)}) async-start(), calls=%async_computation.3 | async-start | bytes 13271040 | tf_op jit(solution)/shard_map/all_gather | solution.py:1161
  45.9 26.8 %collective-permute-start.1 = (bf16[512,768]{1,0:T(8,128)(2,1)}, bf16[512,768]{1,0:T(8,128)(2,1)S(1)}, u32[]{:S(2)}, u32[]{:S(2)}) collective-permute-start(bf16[512,768]{1,0:T(8,128)(2,1)} %shard_map.381), channel_id=1, source_target_pairs={{0,1},{1,0},{2,3},{3,2},{4,5},{5,4},{6,7},{7,6},{8,9},{9,8},{10,11... | collective-permute-start | bytes 2359304 | tf_op jit(solution)/shard_map/ppermute | solution.py:43
  59.1 39.0 %collective-permute-start = (bf16[512,768]{1,0:T(8,128)(2,1)}, bf16[512,768]{1,0:T(8,128)(2,1)S(1)}, u32[]{:S(2)}, u32[]{:S(2)}) collective-permute-start(bf16[512,768]{1,0:T(8,128)(2,1)} %shard_map.379), channel_id=1, source_target_pairs={{0,1},{1,0},{2,3},{3,2},{4,5},{5,4},{6,7},{7,6},{8,9},{9,8},{10,11... | collective-permute-start | bytes 2359304 | tf_op jit(solution)/shard_map/ppermute | solution.py:43
  74.0 24.1 %collective-permute-start.2 = (bf16[512,768]{1,0:T(8,128)(2,1)S(1)}, bf16[512,768]{1,0:T(8,128)(2,1)}, u32[]{:S(2)}, u32[]{:S(2)}) collective-permute-start(bf16[512,768]{1,0:T(8,128)(2,1)S(1)} %add_convert_fusion.11), channel_id=1, source_target_pairs={{0,2},{1,3},{2,0},{3,1},{4,6},{5,7},{6,4},{7,5},{8,10},{9,11},{10,... | collective-permute-start | bytes 2359304 | tf_op jit(solution)/shard_map/ppermute | solution.py:43
  96.6 27.3 %collective-permute-start.4 = (bf16[768,768]{1,0:T(8,128)(2,1)}, bf16[768,768]{1,0:T(8,128)(2,1)}, u32[]{:S(2)}, u32[]{:S(2)}) collective-permute-start(bf16[768,768]{1,0:T(8,128)(2,1)} %get-tuple-element.322), channel_id=1, source_target_pairs={{0,2},{1,3},{2,0},{3,1},{4,6},{5,7},{6,4},{7,5},{8,10},{9,11},{10,... | collective-permute-start | bytes 3538952 | tf_op jit(solution)/shard_map/ppermute | solution.py:43
  100.7 43.3 %all-to-all-start.1 = ((bf16[8,96,512]{2,1,0:T(8,128)(2,1)}), bf16[8,96,512]{2,1,0:T(8,128)(2,1)S(1)}, u32[]{:S(2)}, u32[]{:S(2)}) async-start(bf16[8,96,512]{2,1,0:T(8,128)(2,1)} %bitcast.10), calls=%async_computation.1 | async-start | bytes 1572864 | tf_op jit(solution)/shard_map/all_to_all | solution.py:1149
  104.3 215.9 %all-gather.8.cloned.1.call-start = ((), (), s32[]{:S(2)}) async-start(), calls=%async_computation.4 | async-start | bytes 1769472 | tf_op jit(solution)/shard_map/all_gather | solution.py:1211
  113.6 445.4 %collective-permute-start.38 = (f32[8,768]{1,0:T(8,128)}, f32[8,768]{1,0:T(8,128)}, u32[]{:S(2)}, u32[]{:S(2)}) collective-permute-start(f32[8,768]{1,0:T(8,128)} %get-tuple-element.348.refs_4_.refs_1_), channel_id=1, source_target_pairs={{0,1},{1,0},{2,3},{3,2},{4,5},{5,4},{6,7},{7,6},{8,9},{9,8},{10,11... | collective-permute-start | bytes 73736 | tf_op jit(solution)/shard_map/ppermute | solution.py:43
  113.6 257.5 %collective-permute-start.39 = (f32[8,768]{1,0:T(8,128)}, f32[8,768]{1,0:T(8,128)}, u32[]{:S(2)}, u32[]{:S(2)}) collective-permute-start(f32[8,768]{1,0:T(8,128)} %get-tuple-element.348.refs_4_.refs_1_), channel_id=1, source_target_pairs={{0,2},{1,3},{2,0},{3,1},{4,6},{5,7},{6,4},{7,5},{8,10},{9,11},{10,... | collective-permute-start | bytes 73736 | tf_op jit(solution)/shard_map/ppermute | solution.py:43
  114.1 46.3 %collective-permute-start.3 = (bf16[768,768]{1,0:T(8,128)(2,1)}, bf16[768,768]{1,0:T(8,128)(2,1)S(1)}, u32[]{:S(2)}, u32[]{:S(2)}) collective-permute-start(bf16[768,768]{1,0:T(8,128)(2,1)} %get-tuple-element.322), channel_id=1, source_target_pairs={{0,1},{1,0},{2,3},{3,2},{4,5},{5,4},{6,7},{7,6},{8,9},{9,8},{10,11... | collective-permute-start | bytes 3538952 | tf_op jit(solution)/shard_map/ppermute | solution.py:43
  123.9 37.0 %collective-permute-start.5 = (bf16[768,768]{1,0:T(8,128)(2,1)}, bf16[768,768]{1,0:T(8,128)(2,1)}, u32[]{:S(2)}, u32[]{:S(2)}) collective-permute-start(bf16[768,768]{1,0:T(8,128)(2,1)} %collective-permute-done.4), channel_id=1, source_target_pairs={{0,1},{1,0},{2,3},{3,2},{4,5},{5,4},{6,7},{7,6},{8,9},{9,8},{10,11... | collective-permute-start | bytes 3538952 | tf_op jit(solution)/shard_map/ppermute | solution.py:43
  148.2 12.2 %collective-permute-start.7 = (bf16[512,768]{1,0:T(8,128)(2,1)}, bf16[512,768]{1,0:T(8,128)(2,1)S(1)}, u32[]{:S(2)}, u32[]{:S(2)}) collective-permute-start(bf16[512,768]{1,0:T(8,128)(2,1)} %get-tuple-element.132.x_ref), channel_id=1, source_target_pairs={{0,2},{1,3},{2,0},{3,1},{4,6},{5,7},{6,4},{7,5},{8,10},{9,11},{10,... | collective-permute-start | bytes 2359304 | tf_op jit(solution)/shard_map/ppermute | solution.py:43
  160.4 10.3 %collective-permute-start.6 = (bf16[512,768]{1,0:T(8,128)(2,1)S(1)}, bf16[512,768]{1,0:T(8,128)(2,1)S(1)}, u32[]{:S(2)}, u32[]{:S(2)}) collective-permute-start(bf16[512,768]{1,0:T(8,128)(2,1)S(1)} %copy-done.2), channel_id=1, source_target_pairs={{0,1},{1,0},{2,3},{3,2},{4,5},{5,4},{6,7},{7,6},{8,9},{9,8},{10,11... | collective-permute-start | bytes 2359304 | tf_op jit(solution)/shard_map/ppermute | solution.py:43
  160.4 15.7 %collective-permute-start.8 = (bf16[512,768]{1,0:T(8,128)(2,1)S(1)}, bf16[512,768]{1,0:T(8,128)(2,1)S(1)}, u32[]{:S(2)}, u32[]{:S(2)}) collective-permute-start(bf16[512,768]{1,0:T(8,128)(2,1)S(1)} %collective-permute-done.7.x_ref), channel_id=1, source_target_pairs={{0,1},{1,0},{2,3},{3,2},{4,5},{5,4},{6,7},{7,6},{8,9},{9,8},{10,11... | collective-permute-start | bytes 2359304 | tf_op jit(solution)/shard_map/ppermute | solution.py:43
  220.3 19.8 %collective-permute-start.11 = (bf16[512,768]{1,0:T(8,128)(2,1)}, bf16[512,768]{1,0:T(8,128)(2,1)S(1)}, u32[]{:S(2)}, u32[]{:S(2)}) collective-permute-start(bf16[512,768]{1,0:T(8,128)(2,1)} %get-tuple-element.149), channel_id=1, source_target_pairs={{0,2},{1,3},{2,0},{3,1},{4,6},{5,7},{6,4},{7,5},{8,10},{9,11},{10,... | collective-permute-start | bytes 2359304 | tf_op jit(solution)/shard_map/ppermute | solution.py:43
  223.7 21.2 %collective-permute-start.9 = (bf16[512,768]{1,0:T(8,128)(2,1)}, bf16[512,768]{1,0:T(8,128)(2,1)}, u32[]{:S(2)}, u32[]{:S(2)}) collective-permute-start(bf16[512,768]{1,0:T(8,128)(2,1)} %get-tuple-element.149), channel_id=1, source_target_pairs={{0,1},{1,0},{2,3},{3,2},{4,5},{5,4},{6,7},{7,6},{8,9},{9,8},{10,11... | collective-permute-start | bytes 2359304 | tf_op jit(solution)/shard_map/ppermute | solution.py:43
  240.1 15.3 %collective-permute-start.12 = (bf16[512,768]{1,0:T(8,128)(2,1)S(1)}, bf16[512,768]{1,0:T(8,128)(2,1)}, u32[]{:S(2)}, u32[]{:S(2)}) collective-permute-start(bf16[512,768]{1,0:T(8,128)(2,1)S(1)} %collective-permute-done.11), channel_id=1, source_target_pairs={{0,1},{1,0},{2,3},{3,2},{4,5},{5,4},{6,7},{7,6},{8,9},{9,8},{10,11... | collective-permute-start | bytes 2359304 | tf_op jit(solution)/shard_map/ppermute | solution.py:43
  274.4 19.9 %collective-permute-start.14 = (bf16[512,768]{1,0:T(8,128)(2,1)S(1)}, bf16[512,768]{1,0:T(8,128)(2,1)S(1)}, u32[]{:S(2)}, u32[]{:S(2)}) collective-permute-start(bf16[512,768]{1,0:T(8,128)(2,1)S(1)} %add_convert_fusion.8), channel_id=1, source_target_pairs={{0,2},{1,3},{2,0},{3,1},{4,6},{5,7},{6,4},{7,5},{8,10},{9,11},{10,... | collective-permute-start | bytes 2359304 | tf_op jit(solution)/shard_map/ppermute | solution.py:43
  358.9 19.4 %collective-permute-start.25 = (bf16[512,768]{1,0:T(8,128)(2,1)}, bf16[512,768]{1,0:T(8,128)(2,1)S(1)}, u32[]{:S(2)}, u32[]{:S(2)}) collective-permute-start(bf16[512,768]{1,0:T(8,128)(2,1)} %get-tuple-element.167), channel_id=1, source_target_pairs={{0,2},{1,3},{2,0},{3,1},{4,6},{5,7},{6,4},{7,5},{8,10},{9,11},{10,... | collective-permute-start | bytes 2359304 | tf_op jit(solution)/shard_map/ppermute | solution.py:43
  364.5 15.6 %collective-permute-start.23 = (bf16[512,768]{1,0:T(8,128)(2,1)}, bf16[512,768]{1,0:T(8,128)(2,1)}, u32[]{:S(2)}, u32[]{:S(2)}) collective-permute-start(bf16[512,768]{1,0:T(8,128)(2,1)} %get-tuple-element.167), channel_id=1, source_target_pairs={{0,1},{1,0},{2,3},{3,2},{4,5},{5,4},{6,7},{7,6},{8,9},{9,8},{10,11... | collective-permute-start | bytes 2359304 | tf_op jit(solution)/shard_map/ppermute | solution.py:43
  371.1 187.9 %collective-permute-start.40 = (f32[8,768]{1,0:T(8,128)}, f32[8,768]{1,0:T(8,128)}, u32[]{:S(2)}, u32[]{:S(2)}) collective-permute-start(f32[8,768]{1,0:T(8,128)} %collective-permute-done.39.refs_6_), channel_id=1, source_target_pairs={{0,1},{1,0},{2,3},{3,2},{4,5},{5,4},{6,7},{7,6},{8,9},{9,8},{10,11... | collective-permute-start | bytes 73736 | tf_op jit(solution)/shard_map/ppermute | solution.py:43
  378.3 15.8 %collective-permute-start.26 = (bf16[512,768]{1,0:T(8,128)(2,1)S(1)}, bf16[512,768]{1,0:T(8,128)(2,1)}, u32[]{:S(2)}, u32[]{:S(2)}) collective-permute-start(bf16[512,768]{1,0:T(8,128)(2,1)S(1)} %collective-permute-done.25), channel_id=1, source_target_pairs={{0,1},{1,0},{2,3},{3,2},{4,5},{5,4},{6,7},{7,6},{8,9},{9,8},{10,11... | collective-permute-start | bytes 2359304 | tf_op jit(solution)/shard_map/ppermute | solution.py:43
  393.5 26.8 %collective-permute-start.24 = (bf16[512,768]{1,0:T(8,128)(2,1)S(1)}, bf16[512,768]{1,0:T(8,128)(2,1)S(1)}, u32[]{:S(2)}, u32[]{:S(2)}) collective-permute-start(bf16[512,768]{1,0:T(8,128)(2,1)S(1)} %slice.339), channel_id=1, source_target_pairs={{0,1},{1,0},{2,3},{3,2},{4,5},{5,4},{6,7},{7,6},{8,9},{9,8},{10,11... | collective-permute-start | bytes 2359304 | tf_op jit(solution)/shard_map/ppermute | solution.py:43
  416.2 19.8 %collective-permute-start.28 = (bf16[512,768]{1,0:T(8,128)(2,1)S(1)}, bf16[512,768]{1,0:T(8,128)(2,1)S(1)}, u32[]{:S(2)}, u32[]{:S(2)}) collective-permute-start(bf16[512,768]{1,0:T(8,128)(2,1)S(1)} %add_convert_fusion.6), channel_id=1, source_target_pairs={{0,2},{1,3},{2,0},{3,1},{4,6},{5,7},{6,4},{7,5},{8,10},{9,11},{10,... | collective-permute-start | bytes 2359304 | tf_op jit(solution)/shard_map/ppermute | solution.py:43
  497.4 23.0 %collective-permute-start.30 = (bf16[512,768]{1,0:T(8,128)(2,1)}, bf16[512,768]{1,0:T(8,128)(2,1)}, u32[]{:S(2)}, u32[]{:S(2)}) collective-permute-start(bf16[512,768]{1,0:T(8,128)(2,1)} %add_convert_fusion.4), channel_id=1, source_target_pairs={{0,1},{1,0},{2,3},{3,2},{4,5},{5,4},{6,7},{7,6},{8,9},{9,8},{10,11... | collective-permute-start | bytes 2359304 | tf_op jit(solution)/shard_map/ppermute | solution.py:43
  499.3 10.0 %collective-permute-start.31 = (bf16[512,768]{1,0:T(8,128)(2,1)S(1)}, bf16[512,768]{1,0:T(8,128)(2,1)S(1)}, u32[]{:S(2)}, u32[]{:S(2)}) collective-permute-start(bf16[512,768]{1,0:T(8,128)(2,1)S(1)} %add_convert_fusion.1), channel_id=1, source_target_pairs={{0,1},{1,0},{2,3},{3,2},{4,5},{5,4},{6,7},{7,6},{8,9},{9,8},{10,11... | collective-permute-start | bytes 2359304 | tf_op jit(solution)/shard_map/ppermute | solution.py:43
  511.1 20.2 %collective-permute-start.32 = (bf16[512,768]{1,0:T(8,128)(2,1)}, bf16[512,768]{1,0:T(8,128)(2,1)}, u32[]{:S(2)}, u32[]{:S(2)}) collective-permute-start(bf16[512,768]{1,0:T(8,128)(2,1)} %add_convert_fusion), channel_id=1, source_target_pairs={{0,2},{1,3},{2,0},{3,1},{4,6},{5,7},{6,4},{7,5},{8,10},{9,11},{10,... | collective-permute-start | bytes 2359304 | tf_op jit(solution)/shard_map/ppermute | solution.py:43
  517.8 54.6 %collective-permute-start.36 = (f32[768,768]{1,0:T(8,128)}, f32[768,768]{1,0:T(8,128)}, u32[]{:S(2)}, u32[]{:S(2)}) collective-permute-start(f32[768,768]{1,0:T(8,128)} %bitcast.258), channel_id=1, source_target_pairs={{0,1},{1,0},{2,3},{3,2},{4,5},{5,4},{6,7},{7,6},{8,9},{9,8},{10,11... | collective-permute-start | bytes 7077896 | tf_op jit(solution)/shard_map/ppermute | solution.py:43
  536.5 32.8 %collective-permute-start.34 = (bf16[512,768]{1,0:T(8,128)(2,1)}, bf16[512,768]{1,0:T(8,128)(2,1)S(1)}, u32[]{:S(2)}, u32[]{:S(2)}) collective-permute-start(bf16[512,768]{1,0:T(8,128)(2,1)} %get-tuple-element.189), channel_id=1, source_target_pairs={{0,2},{1,3},{2,0},{3,1},{4,6},{5,7},{6,4},{7,5},{8,10},{9,11},{10,... | collective-permute-start | bytes 2359304 | tf_op jit(solution)/shard_map/ppermute | solution.py:43
  569.8 56.4 %collective-permute-start.47 = (f32[8,2304]{1,0:T(8,128)S(1)}, f32[8,2304]{1,0:T(8,128)S(1)}, u32[]{:S(2)}, u32[]{:S(2)}) collective-permute-start(f32[8,2304]{1,0:T(8,128)S(1)} %pad_maximum_fusion.8), channel_id=1, source_target_pairs={{0,4},{4,0},{8,12},{12,8},{16,20},{20,16},{24,28},{28,24},{1,5},{5... | collective-permute-start | bytes 221192 | tf_op jit(solution)/shard_map/ppermute | solution.py:43
  605.9 16.6 %collective-permute-start.44 = (f32[8,3328]{1,0:T(8,128)S(1)}, f32[8,3328]{1,0:T(8,128)S(1)}, u32[]{:S(2)}, u32[]{:S(2)}) collective-permute-start(f32[8,3328]{1,0:T(8,128)S(1)} %pad_maximum_fusion.7), channel_id=1, source_target_pairs={{0,4},{4,0},{8,12},{12,8},{16,20},{20,16},{24,28},{28,24},{1,5},{5... | collective-permute-start | bytes 319496 | tf_op jit(solution)/shard_map/ppermute | solution.py:43
  620.5 8.2 %collective-permute-start.53 = (f32[8,2560]{1,0:T(8,128)}, f32[8,2560]{1,0:T(8,128)S(1)}, u32[]{:S(2)}, u32[]{:S(2)}) collective-permute-start(f32[8,2560]{1,0:T(8,128)} %get-tuple-element.206), channel_id=1, source_target_pairs={{0,4},{4,0},{8,12},{12,8},{16,20},{20,16},{24,28},{28,24},{1,5},{5... | collective-permute-start | bytes 245768 | tf_op jit(solution)/shard_map/ppermute | solution.py:43
  626.3 10.0 %collective-permute-start.48 = (f32[8,2304]{1,0:T(8,128)S(1)}, f32[8,2304]{1,0:T(8,128)S(1)}, u32[]{:S(2)}, u32[]{:S(2)}) collective-permute-start(f32[8,2304]{1,0:T(8,128)S(1)} %fusion.74), channel_id=1, source_target_pairs={{0,8},{4,12},{8,0},{12,4},{16,24},{20,28},{24,16},{28,20},{1,9},{5... | collective-permute-start | bytes 221192 | tf_op jit(solution)/shard_map/ppermute | solution.py:43
  626.4 10.1 %collective-permute-start.51 = (f32[8,2560]{1,0:T(8,128)S(1)}, f32[8,2560]{1,0:T(8,128)S(1)}, u32[]{:S(2)}, u32[]{:S(2)}) collective-permute-start(f32[8,2560]{1,0:T(8,128)S(1)} %add.382), channel_id=1, source_target_pairs={{0,8},{4,12},{8,0},{12,4},{16,24},{20,28},{24,16},{28,20},{1,9},{5... | collective-permute-start | bytes 245768 | tf_op jit(solution)/shard_map/ppermute | solution.py:43
  629.6 8.3 %collective-permute-start.54 = (f32[8,2560]{1,0:T(8,128)S(1)}, f32[8,2560]{1,0:T(8,128)S(1)}, u32[]{:S(2)}, u32[]{:S(2)}) collective-permute-start(f32[8,2560]{1,0:T(8,128)S(1)} %add.385), channel_id=1, source_target_pairs={{0,8},{4,12},{8,0},{12,4},{16,24},{20,28},{24,16},{28,20},{1,9},{5... | collective-permute-start | bytes 245768 | tf_op jit(solution)/shard_map/ppermute | solution.py:43
  630.4 10.6 %collective-permute-start.46 = (f32[8,3328]{1,0:T(8,128)S(1)}, f32[8,3328]{1,0:T(8,128)S(1)}, u32[]{:S(2)}, u32[]{:S(2)}) collective-permute-start(f32[8,3328]{1,0:T(8,128)S(1)} %add.374), channel_id=1, source_target_pairs={{0,16},{4,20},{8,24},{12,28},{16,0},{20,4},{24,8},{28,12},{1,17},{... | collective-permute-start | bytes 319496 | tf_op jit(solution)/shard_map/ppermute | solution.py:43
  636.3 10.6 %collective-permute-start.49 = (f32[8,2304]{1,0:T(8,128)S(1)}, f32[8,2304]{1,0:T(8,128)S(1)}, u32[]{:S(2)}, u32[]{:S(2)}) collective-permute-start(f32[8,2304]{1,0:T(8,128)S(1)} %add.380), channel_id=1, source_target_pairs={{0,16},{4,20},{8,24},{12,28},{16,0},{20,4},{24,8},{28,12},{1,17},{... | collective-permute-start | bytes 221192 | tf_op jit(solution)/shard_map/ppermute | solution.py:43
  636.4 46.2 %collective-permute-start.29 = (f32[768,768]{1,0:T(8,128)}, f32[768,768]{1,0:T(8,128)}, u32[]{:S(2)}, u32[]{:S(2)}) collective-permute-start(f32[768,768]{1,0:T(8,128)} %bitcast.47.refs_1_), channel_id=1, source_target_pairs={{0,1},{1,0},{2,3},{3,2},{4,5},{5,4},{6,7},{7,6},{8,9},{9,8},{10,11... | collective-permute-start | bytes 7077896 | tf_op jit(solution)/shard_map/ppermute | solution.py:43
  636.5 54.0 %collective-permute-start.37 = (f32[768,768]{1,0:T(8,128)}, f32[768,768]{1,0:T(8,128)}, u32[]{:S(2)}, u32[]{:S(2)}) collective-permute-start(f32[768,768]{1,0:T(8,128)} %bitcast_add_fusion.1), channel_id=1, source_target_pairs={{0,2},{1,3},{2,0},{3,1},{4,6},{5,7},{6,4},{7,5},{8,10},{9,11},{10,... | collective-permute-start | bytes 7077896 | tf_op jit(solution)/shard_map/ppermute | solution.py:43
  637.9 10.8 %collective-permute-start.52 = (f32[8,2560]{1,0:T(8,128)S(1)}, f32[8,2560]{1,0:T(8,128)S(1)}, u32[]{:S(2)}, u32[]{:S(2)}) collective-permute-start(f32[8,2560]{1,0:T(8,128)S(1)} %add.383), channel_id=1, source_target_pairs={{0,16},{4,20},{8,24},{12,28},{16,0},{20,4},{24,8},{28,12},{1,17},{... | collective-permute-start | bytes 245768 | tf_op jit(solution)/shard_map/ppermute | solution.py:43
  641.0 8.9 %collective-permute-start.55 = (f32[8,2560]{1,0:T(8,128)S(1)}, f32[8,2560]{1,0:T(8,128)S(1)}, u32[]{:S(2)}, u32[]{:S(2)}) collective-permute-start(f32[8,2560]{1,0:T(8,128)S(1)} %add.386), channel_id=1, source_target_pairs={{0,16},{4,20},{8,24},{12,28},{16,0},{20,4},{24,8},{28,12},{1,17},{... | collective-permute-start | bytes 245768 | tf_op jit(solution)/shard_map/ppermute | solution.py:43
  682.5 23.9 %collective-permute-start.60 = (f32[36,768]{1,0:T(8,128)S(1)}, f32[36,768]{1,0:T(8,128)S(1)}, u32[]{:S(2)}, u32[]{:S(2)}) collective-permute-start(f32[36,768]{1,0:T(8,128)S(1)} %add.392), channel_id=1, source_target_pairs={{0,8},{4,12},{8,0},{12,4},{16,24},{20,28},{24,16},{28,20},{1,9},{5... | collective-permute-start | bytes 331784 | tf_op jit(solution)/shard_map/ppermute | solution.py:43
  698.7 10.6 %collective-permute-start.56 = (f32[8,768]{1,0:T(8,128)}, f32[8,768]{1,0:T(8,128)S(1)}, u32[]{:S(2)}, u32[]{:S(2)}) collective-permute-start(f32[8,768]{1,0:T(8,128)} %bitcast.270), channel_id=1, source_target_pairs={{0,4},{4,0},{8,12},{12,8},{16,20},{20,16},{24,28},{28,24},{1,5},{5... | collective-permute-start | bytes 73736 | tf_op jit(solution)/shard_map/ppermute | solution.py:43
  706.4 33.3 %collective-permute-start.61 = (f32[36,768]{1,0:T(8,128)S(1)}, f32[36,768]{1,0:T(8,128)S(1)}, u32[]{:S(2)}, u32[]{:S(2)}) collective-permute-start(f32[36,768]{1,0:T(8,128)S(1)} %add.393), channel_id=1, source_target_pairs={{0,16},{4,20},{8,24},{12,28},{16,0},{20,4},{24,8},{28,12},{1,17},{... | collective-permute-start | bytes 331784 | tf_op jit(solution)/shard_map/ppermute | solution.py:43
  709.3 9.6 %collective-permute-start.57 = (f32[8,768]{1,0:T(8,128)S(1)}, f32[8,768]{1,0:T(8,128)S(1)}, u32[]{:S(2)}, u32[]{:S(2)}) collective-permute-start(f32[8,768]{1,0:T(8,128)S(1)} %bitcast_add_fusion), channel_id=1, source_target_pairs={{0,8},{4,12},{8,0},{12,4},{16,24},{20,28},{24,16},{28,20},{1,9},{5... | collective-permute-start | bytes 73736 | tf_op jit(solution)/shard_map/ppermute | solution.py:43
  718.9 24.4 %collective-permute-start.58 = (f32[8,768]{1,0:T(8,128)S(1)}, f32[8,768]{1,0:T(8,128)S(1)}, u32[]{:S(2)}, u32[]{:S(2)}) collective-permute-start(f32[8,768]{1,0:T(8,128)S(1)} %add.389), channel_id=1, source_target_pairs={{0,16},{4,20},{8,24},{12,28},{16,0},{20,4},{24,8},{28,12},{1,17},{... | collective-permute-start | bytes 73736 | tf_op jit(solution)/shard_map/ppermute | solution.py:43
  (115 other events, 1289.7 us)
Sparse Core Ops, SparseCore 0:
  11.6 82.5 all-gather.3
  96.4 179.5 all-gather.5
  278.1 42.0 all-gather.7

commit v3 on v2

--- a/solution.py
+++ b/solution.py
@@ -1,4 +1,5 @@
 import functools
+import math
 
 import jax
 import jax.numpy as jnp
@@ -11,8 +12,8 @@
 HEAD_DIM = 64
 RANK = 8
 PAIR = 2 * HEAD_DIM
-TILE = 1280
-PARTS = 3
+TILE = 640
+WIDE_TILE = 1280
 CHUNK = 256
 
 EPS = 1e-05
@@ -26,11 +27,10 @@
 NARROW = jnp.bfloat16
 HIGH = lax.Precision.HIGHEST
 NEGATIVE = -1e30
-VMEM_BYTES = 56 * 1024 * 1024
-
-
-def params():
-    return pltpu.CompilerParams(vmem_limit_bytes=VMEM_BYTES)
+
+
+def params(mebibytes):
+    return pltpu.CompilerParams(vmem_limit_bytes=mebibytes * 1024 * 1024)
 
 
 def axis_bits(axis):
@@ -184,13 +184,33 @@
         + [lanes, lanes],
         out_specs=[block] * count,
         out_shape=[jax.ShapeDtypeStruct((rows, width), NARROW)] * count,
-        compiler_params=params(),
+        compiler_params=params(20),
         cost_estimate=pl.CostEstimate(
             flops=2 * count * rows * width * width,
             bytes_accessed=2 * count * width * (rows + width),
             transcendentals=0,
         ),
     )(x, *[weight] * count, cosine, sine)
+
+
+def turn_table_kernel(table_ref, out_ref):
+    rows, columns = table_ref.shape
+    empty = jnp.zeros((columns, out_ref.shape[1] - rows), WIDE)
+    for at in range(0, columns, 128):
+        size = min(128, columns - at)
+        piece = table_ref[:, at : at + size].astype(NARROW).astype(WIDE).T
+        if rows < out_ref.shape[1]:
+            piece = jnp.concatenate([piece, empty[:size]], axis=1)
+        out_ref[at : at + size, :] = piece
+    out_ref[columns:, :] = jnp.zeros((out_ref.shape[0] - columns, out_ref.shape[1]), WIDE)
+
+
+def turned_table(table):
+    rows, columns = table.shape
+    lanes = -(-rows // 128) * 128
+    return whole_call(
+        turn_table_kernel, [((columns // 8 * 8 + 8, lanes), WIDE)], 8 * table.size, table
+    )[0]
 
 
 def lookup_kernel(row_count, start_ref, ids_ref, table_ref, out_ref, held):
@@ -199,18 +219,18 @@
     for group in range(groups):
 
         def move(at, carry):
+            base = start + (group * block + at * 8)
             for place in range(8):
-                index = ids_ref[group, start + at * 8 + place]
-                held[at, place : place + 1, :] = table_ref[index]
+                index = ids_ref[base + place]
+                held[at, place : place + 1, :] = table_ref[pl.ds(index, 1), :]
             return carry
 
-        lax.fori_loop(0, block // 8, move, 0, unroll=4)
+        lax.fori_loop(0, block // 8, move, 0, unroll=8)
         rows = held[...].reshape(block, held.shape[2])[:, :row_count]
         out_ref[:, group * row_count : (group + 1) * row_count] = rows.astype(NARROW)
 
 
-def lookup(ids, table, start, block, row_count):
-    groups = ids.shape[0]
+def lookup(ids, table, start, groups, block, row_count):
     return pl.pallas_call(
         functools.partial(lookup_kernel, row_count),
         in_specs=[
@@ -220,8 +240,8 @@
         ],
         out_specs=pl.BlockSpec(memory_space=pltpu.VMEM),
         out_shape=jax.ShapeDtypeStruct((block, groups * row_count), NARROW),
-        scratch_shapes=[pltpu.VMEM((block // 8, 8, table.shape[2]), WIDE)],
-        compiler_params=params(),
+        scratch_shapes=[pltpu.VMEM((block // 8, 8, table.shape[1]), WIDE)],
+        compiler_params=params(10),
         cost_estimate=pl.CostEstimate(
             flops=groups * block * 4096, bytes_accessed=4 * table.size, transcendentals=0
         ),
@@ -244,10 +264,13 @@
 
 
 def whole_call(kernel, outs, flops, *operands):
+    moved = sum(operand.size * operand.dtype.itemsize for operand in operands)
+    moved += sum(math.prod(shape) * jnp.dtype(kind).itemsize for shape, kind in outs)
+    budget = 8 + moved * 2 // (1 << 20)
     return pl.pallas_call(
         kernel,
         out_shape=[jax.ShapeDtypeStruct(shape, kind) for shape, kind in outs],
-        compiler_params=params(),
+        compiler_params=params(budget),
         cost_estimate=pl.CostEstimate(
             flops=flops,
             bytes_accessed=sum(4 * operand.size for operand in operands),
@@ -322,7 +345,7 @@
             jax.ShapeDtypeStruct(shape, NARROW),
             jax.ShapeDtypeStruct((1, shape[1]), WIDE),
         ],
-        compiler_params=params(),
+        compiler_params=params(24),
         cost_estimate=pl.CostEstimate(
             flops=200 * hidden_in.size, bytes_accessed=20 * hidden_in.size, transcendentals=0
         ),
@@ -379,7 +402,8 @@
     )
 
 
-def ffn_kernel(x_ref, gate_ref, up_ref, down_ref, gate_out, up_out, act_ref, out_ref):
+def ffn_step(x_ref, weights, gate_out, up_out, act_ref, x_out, out_ref):
+    gate_ref, up_ref, down_ref = weights
     x = x_ref[...]
     gate = jnp.dot(x, gate_ref[...], preferred_element_type=WIDE)
     up = jnp.dot(x, up_ref[...], preferred_element_type=WIDE)
@@ -387,46 +411,55 @@
     up_out[...] = up
     act = (gate / (1.0 + jnp.exp(-gate)) * up).astype(NARROW)
     act_ref[...] = act
+    x_out[...] = x
     out_ref[...] = contract_cols(act, down_ref[...]).astype(NARROW)
+
+
+def ffn_kernel(first_ref, second_ref, *refs):
+    weights, kept, outs = refs[:3], refs[3:7], refs[7:]
+    for step, x_ref in enumerate((first_ref, second_ref)):
+
+        @pl.when(pl.program_id(0) == step)
+        def _():
+            ffn_step(x_ref, weights, *kept, outs[step])
 
 
 def weight_block(width, hidden, index):
     return pl.BlockSpec((width, hidden), lambda i: (0, index))
 
 
-def ffn_forward(x, weights):
-    rows, width = x.shape
-    hidden = weights.shape[1] // 4
-    block = min(512, rows)
+def ffn_forward(first, second, weights, hidden):
+    rows, width = first.shape
+    whole = pl.BlockSpec((rows, width), lambda i: (0, 0))
     tall = lambda i: (i, 0)
     return pl.pallas_call(
         ffn_kernel,
-        grid=(rows // block,),
-        in_specs=[pl.BlockSpec((block, width), tall)]
-        + [weight_block(width, hidden, k) for k in range(1, 4)],
-        out_specs=[
-            pl.BlockSpec((block, hidden), tall),
-            pl.BlockSpec((block, hidden), tall),
-            pl.BlockSpec((block, hidden), tall),
-            pl.BlockSpec((block, width), tall),
-        ],
+        grid=(2,),
+        in_specs=[whole, whole] + [weight_block(width, hidden, k) for k in range(1, 4)],
+        out_specs=[pl.BlockSpec((rows, hidden), tall)] * 3
+        + [pl.BlockSpec((rows, width), tall), whole, whole],
         out_shape=[
-            jax.ShapeDtypeStruct((rows, hidden), WIDE),
-            jax.ShapeDtypeStruct((rows, hidden), WIDE),
-            jax.ShapeDtypeStruct((rows, hidden), NARROW),
+            jax.ShapeDtypeStruct((2 * rows, hidden), WIDE),
+            jax.ShapeDtypeStruct((2 * rows, hidden), WIDE),
+            jax.ShapeDtypeStruct((2 * rows, hidden), NARROW),
+            jax.ShapeDtypeStruct((2 * rows, width), NARROW),
             jax.ShapeDtypeStruct((rows, width), NARROW),
-        ],
-        compiler_params=params(),
-        cost_estimate=pl.CostEstimate(
-            flops=6 * rows * width * hidden,
-            bytes_accessed=14 * rows * width + 6 * width * hidden,
-            transcendentals=rows * hidden,
-        ),
-    )(x, weights, weights, weights)
-
-
-def ffn_back_kernel(grad_ref, gate_in, up_in, gate_ref, up_ref, down_ref, dgate_ref, dup_ref, out_ref):
-    act_grad = jnp.dot(grad_ref[...], down_ref[...], preferred_element_type=WIDE)
+            jax.ShapeDtypeStruct((rows, width), NARROW),
+        ],
+        compiler_params=params(32),
+        cost_estimate=pl.CostEstimate(
+            flops=12 * rows * width * hidden,
+            bytes_accessed=28 * rows * width + 6 * width * hidden,
+            transcendentals=2 * rows * hidden,
+        ),
+    )(first, second, weights, weights, weights)
+
+
+def ffn_back_step(grad_ref, gate_in, up_in, weights, dgate_ref, dup_ref, grad_out, out_ref):
+    gate_ref, up_ref, down_ref = weights
+    grad = grad_ref[...]
+    grad_out[...] = grad
+    act_grad = jnp.dot(grad, down_ref[...], preferred_element_type=WIDE)
     gate, up = gate_in[...], up_in[...]
     share = 1.0 / (1.0 + jnp.exp(-gate))
     dgate = (act_grad * up * (share * (1.0 + gate * (1.0 - share)))).astype(NARROW)
@@ -438,37 +471,98 @@
     ).astype(NARROW)
 
 
-def ffn_backward(grad, gate, up, weights):
-    rows, width = grad.shape
-    hidden = weights.shape[1] // 4
-    block = min(512, rows)
+def ffn_back_kernel(first_ref, second_ref, gate_in, up_in, *refs):
+    weights, kept, outs = refs[:3], refs[3:6], refs[6:]
+    for step, grad_ref in enumerate((first_ref, second_ref)):
+
+        @pl.when(pl.program_id(0) == step)
+        def _():
+            ffn_back_step(grad_ref, gate_in, up_in, weights, *kept, outs[step])
+
+
+def ffn_backward(first, second, gate, up, weights):
+    rows, width = first.shape
+    hidden = gate.shape[1]
+    whole = pl.BlockSpec((rows, width), lambda i: (0, 0))
     tall = lambda i: (i, 0)
     return pl.pallas_call(
         ffn_back_kernel,
-        grid=(rows // block,),
-        in_specs=[
-            pl.BlockSpec((block, width), tall),
-            pl.BlockSpec((block, hidden), tall),
-            pl.BlockSpec((block, hidden), tall),
-        ]
+        grid=(2,),
+        in_specs=[whole, whole]
+        + [pl.BlockSpec((rows, hidden), tall)] * 2
         + [weight_block(width, hidden, k) for k in range(1, 4)],
-        out_specs=[
-            pl.BlockSpec((block, hidden), tall),
-            pl.BlockSpec((block, hidden), tall),
-            pl.BlockSpec((block, width), tall),
-        ],
+        out_specs=[pl.BlockSpec((rows, hidden), tall)] * 2
+        + [pl.BlockSpec((rows, width), tall), whole, whole],
         out_shape=[
-            jax.ShapeDtypeStruct((rows, hidden), NARROW),
-            jax.ShapeDtypeStruct((rows, hidden), NARROW),
+            jax.ShapeDtypeStruct((2 * rows, hidden), NARROW),
+            jax.ShapeDtypeStruct((2 * rows, hidden), NARROW),
+            jax.ShapeDtypeStruct((2 * rows, width), NARROW),
             jax.ShapeDtypeStruct((rows, width), NARROW),
-        ],
-        compiler_params=params(),
-        cost_estimate=pl.CostEstimate(
-            flops=6 * rows * width * hidden,
-            bytes_accessed=16 * rows * width + 6 * width * hidden,
-            transcendentals=rows * hidden,
-        ),
-    )(grad, gate, up, weights, weights, weights)
+            jax.ShapeDtypeStruct((rows, width), NARROW),
+        ],
+        compiler_params=params(34),
+        cost_estimate=pl.CostEstimate(
+            flops=12 * rows * width * hidden,
+            bytes_accessed=32 * rows * width + 6 * width * hidden,
+            transcendentals=2 * rows * hidden,
+        ),
+    )(first, second, gate, up, weights, weights, weights)
+
+
+def input_kernel(first_k, first_v, second_k, second_v, key_ref, value_ref, *outs):
+    for dk_ref, dv_ref, out_ref in zip((first_k, second_k), (first_v, second_v), outs):
+        total = contract_cols(dk_ref[...], key_ref[...])
+        total = total + contract_cols(dv_ref[...], value_ref[...])
+        out_ref[...] = total.astype(NARROW)
+
+
+def input_grads(first_k, first_v, second_k, second_v, weights):
+    rows, width = first_k.shape
+    whole = pl.BlockSpec((rows, width), lambda i: (0, 0))
+    return pl.pallas_call(
+        input_kernel,
+        grid=(1,),
+        in_specs=[whole] * 4 + [weight_block(width, width, k) for k in (1, 2)],
+        out_specs=[whole] * 2,
+        out_shape=[jax.ShapeDtypeStruct((rows, width), NARROW)] * 2,
+        compiler_params=params(24),
+        cost_estimate=pl.CostEstimate(
+            flops=8 * rows * width * width,
+            bytes_accessed=12 * rows * width + 4 * width * width,
+            transcendentals=0,
+        ),
+    )(first_k, first_v, second_k, second_v, weights, weights)
+
+
+def paired(value, work):
+    near_bit, *far_bits = axis_bits("tensor")
+    held = {0: value}
+    for bit in reversed(far_bits):
+        for key in sorted(held):
+            held[key ^ bit] = swap(held[key], "tensor", bit)
+    results, sums = [], {}
+    for key in sorted(held):
+        block = held[key]
+        if results:
+            block, _ = lax.optimization_barrier((block, results[-1][-1]))
+        results.append(work(len(results), block, swap(block, "tensor", near_bit)))
+        sums[key] = near_sum(*results[-1][-2:])
+    return results, sums
+
+
+def near_sum(own, other):
+    got = swap(other, "tensor", axis_bits("tensor")[0])
+    return (own.astype(WIDE) + got.astype(WIDE)).astype(NARROW)
+
+
+def far_sum(sums):
+    sums = dict(sums)
+    near_bit, *far_bits = axis_bits("tensor")
+    for bit in far_bits[:-1]:
+        for key in sorted(k for k in sums if not k & bit):
+            got = swap(sums.pop(key ^ bit), "tensor", bit)
+            sums[key] = (sums[key].astype(WIDE) + got.astype(WIDE)).astype(NARROW)
+    return sums[0], sums[far_bits[-1]], swap(sums[far_bits[-1]], "tensor", far_bits[-1])
 
 
 def logits_kernel(columns, tile, rows_ref, table_ref, targets_ref, out_ref, stats_ref, top_ref, sum_ref, hit_ref):
@@ -514,7 +608,7 @@
     picks, width = rows_all.shape
     columns = table.shape[1]
     tiles = -(-columns // TILE)
-    tile = TILE
+    tile = WIDE_TILE
     still = lambda j: (0, 0)
     along = lambda j: (0, j)
     return pl.pallas_call(
@@ -531,7 +625,7 @@
             jax.ShapeDtypeStruct((picks, 128), WIDE),
         ],
         scratch_shapes=[pltpu.VMEM((picks, 128), WIDE)] * 3,
-        compiler_params=params(),
+        compiler_params=params(14),
         cost_estimate=pl.CostEstimate(
             flops=2 * picks * width * columns,
             bytes_accessed=2 * width * columns,
@@ -578,7 +672,7 @@
 def vocab_back(logits, table, targets, stats, weight):
     picks = targets.shape[0]
     width, columns = table.shape
-    tile = TILE
+    tile = WIDE_TILE
     still = lambda j: (0, 0)
     along = lambda j: (0, j)
     return pl.pallas_call(
@@ -596,7 +690,7 @@
             jax.ShapeDtypeStruct(logits.shape, NARROW),
             jax.ShapeDtypeStruct((picks, width), WIDE),
         ],
-        compiler_params=params(),
+        compiler_params=params(14),
         cost_estimate=pl.CostEstimate(
             flops=2 * picks * width * columns,
             bytes_accessed=2 * width * columns,
@@ -635,7 +729,7 @@
             jax.ShapeDtypeStruct((1, width), WIDE),
             jax.ShapeDtypeStruct((1, 128), WIDE),
         ],
-        compiler_params=params(),
+        compiler_params=params(8),
         cost_estimate=pl.CostEstimate(
             flops=4 * keys_hat.size, bytes_accessed=2 * keys_hat.size, transcendentals=0
         ),
@@ -705,7 +799,7 @@
             jax.ShapeDtypeStruct((pairs, 2, rows), WIDE),
         ],
         scratch_shapes=[pltpu.VMEM((length, rows), WIDE)],
-        compiler_params=params(),
+        compiler_params=params(22),
         cost_estimate=pl.CostEstimate(
             flops=4 * rows * length * width,
             bytes_accessed=4 * length * width + 8 * rows * width,
@@ -791,7 +885,7 @@
             pltpu.VMEM((length, PAIR), WIDE),
             pltpu.VMEM((PAIR, rows), WIDE),
         ],
-        compiler_params=params(),
+        compiler_params=params(24),
         cost_estimate=pl.CostEstimate(
             flops=10 * rows * length * width,
             bytes_accessed=8 * length * width + 8 * rows * width,
@@ -882,7 +976,7 @@
             jax.ShapeDtypeStruct((RANK, tiles * TILE), WIDE),
         ],
         scratch_shapes=[pltpu.VMEM((TILE, width), WIDE)],
-        compiler_params=params(),
+        compiler_params=params(32),
         cost_estimate=pl.CostEstimate(
             flops=2 * width * tiles * TILE * (slots // 4 + picks + 24),
             bytes_accessed=8 * width * tiles * TILE,
@@ -925,7 +1019,7 @@
             jax.ShapeDtypeStruct((count, width, columns), WIDE),
             jax.ShapeDtypeStruct((count, RANK, columns), WIDE),
         ],
-        compiler_params=params(),
+        compiler_params=params(36),
         cost_estimate=pl.CostEstimate(
             flops=48 * count * width * columns,
             bytes_accessed=12 * count * width * columns,
@@ -950,7 +1044,7 @@
     return pl.pallas_call(
         functools.partial(basis_kernel, spans),
         out_shape=jax.ShapeDtypeStruct(sums.shape, WIDE),
-        compiler_params=params(),
+        compiler_params=params(8),
         cost_estimate=pl.CostEstimate(
             flops=64 * sums.size, bytes_accessed=8 * sums.size, transcendentals=40
         ),
@@ -967,7 +1061,7 @@
     return pl.pallas_call(
         small_back_kernel,
         out_shape=jax.ShapeDtypeStruct((count, RANK, width), WIDE),
-        compiler_params=params(),
+        compiler_params=params(24),
         cost_estimate=pl.CostEstimate(
             flops=48 * count * width * columns,
             bytes_accessed=4 * count * width * columns,
@@ -1020,7 +1114,7 @@
         in_specs=specs + specs + [pl.BlockSpec((RANK, TILE), lambda j: (0, j))],
         out_specs=pl.BlockSpec((RANK, width), lambda j: (0, 0)),
         out_shape=jax.ShapeDtypeStruct((RANK, width), WIDE),
-        compiler_params=params(),
+        compiler_params=params(18),
         cost_estimate=pl.CostEstimate(
             flops=48 * width * columns, bytes_accessed=4 * width * columns, transcendentals=0
         ),
@@ -1037,7 +1131,7 @@
     return pl.pallas_call(
         small_error_kernel,
         out_shape=[jax.ShapeDtypeStruct((width, columns), WIDE)] * count,
-        compiler_params=params(),
+        compiler_params=params(32),
         cost_estimate=pl.CostEstimate(
             flops=48 * count * width * columns,
             bytes_accessed=8 * count * width * columns,
@@ -1072,7 +1166,7 @@
         ],
         out_specs=pl.BlockSpec((TILE, width), lambda j: (j, 0)),
         out_shape=jax.ShapeDtypeStruct((columns, width), WIDE),
-        compiler_params=params(),
+        compiler_params=params(24),
         cost_estimate=pl.CostEstimate(
             flops=48 * width * columns, bytes_accessed=8 * width * columns, transcendentals=0
         ),
@@ -1132,33 +1226,52 @@
     vocab_start = tensor_rank * vocab_own
     ids = tokens_all - vocab_start
     ids = jnp.where((ids >= 0) & (ids < vocab_own), ids, vocab_own)
-    fill = -(-row_count // 128) * 128 - row_count
     table_local = embed_table.astype(NARROW)
-    table_rows = jnp.pad(table_local.astype(WIDE).T, ((0, 1), (0, fill)))[:, None]
-    looked = {}
+    table_rows = turned_table(embed_table)
+    ids = jnp.swapaxes(ids.reshape(data_count, tensor_count, own_rows), 0, 1).reshape(-1)
+    looked, looked_sums = {}, {}
     for key in reversed(range(tensor_count)):
-        start = ((tensor_rank ^ key) * own_rows).reshape(1)
-        looked[key] = lookup(ids, table_rows, start, own_rows, row_count)
-    mine = summed_block([looked[key] for key in range(tensor_count)], "tensor", NARROW)
-    side = (seq_lengths, mask_slots, mask_targets, positive_rows, doc_ids, false_pairs)
-    side = side + (queue_docs, factors, gate_up_error, down_error, attend_error, data_rank)
-    side, near_ids, near, _ = lax.optimization_barrier((side, token_ids, near, looked[0]))
-    seq_lengths, mask_slots, mask_targets, positive_rows, doc_ids, false_pairs = side[:6]
-    queue_docs, factors, gate_up_error, down_error, attend_error, data_rank = side[6:]
-    pieces = mine.astype(NARROW).T.reshape(data_count, row_count, own_rows)
+        start = ((tensor_rank ^ key) * (data_count * own_rows)).reshape(1)
+        looked[key] = lookup(ids, table_rows, start, data_count, own_rows, row_count)
+        if key == 1:
+            for base in range(2, tensor_count, 2):
+                looked_sums[base] = near_sum(looked[base], looked[base + 1])
+            ids, looked_sums, looked[1] = lax.optimization_barrier((ids, looked_sums, looked[1]))
+        elif key:
+            ids, looked[key] = lax.optimization_barrier((ids, looked[key]))
+    looked_sums[0] = near_sum(looked[0], looked[1])
+    mine, _, got = far_sum(looked_sums)
+    pieces = (mine + got).T.reshape(data_count, row_count, own_rows)
+    none, pieces = lax.optimization_barrier((jnp.minimum(data_rank, 0), pieces))
+    gate_error = lax.dynamic_slice_in_dim(gate_up_error[0], none, 1, 1)[:, 0]
+    up_error = lax.dynamic_slice_in_dim(gate_up_error[0], none + 1, 1, 1)[:, 0]
     embedded = lax.all_to_all(pieces, "dp", 0, 0).reshape(width, own_rows).T
 
     attend_cols = attend_error.shape[2]
     quarter = lax.dynamic_slice_in_dim(attend_weight, tensor_rank * attend_cols, attend_cols, 1)
+    queue_rows = queue_embed.shape[0] // tensor_count
+    queue_own = lax.dynamic_slice_in_dim(queue_embed, tensor_rank * queue_rows, queue_rows, 0)
+    joined = jnp.concatenate([quarter, gate_up[:, 0], gate_up[:, 1], down_weight], axis=1)
     joined = jnp.concatenate(
-        [quarter, gate_up[:, 0], gate_up[:, 1], down_weight], axis=1
-    ).astype(NARROW)
+        [joined.astype(NARROW), queue_own.reshape(row_count, -1)], axis=1
+    )
     joined_b = lax.all_gather(joined, "dp", axis=0, tiled=True)
-    quarter_b, ffn_b = joined_b[:, :attend_cols], joined_b
+    table_local, _ = lax.optimization_barrier((table_local, looked[tensor_count - 1]))
+    table_b = lax.all_gather(table_local, "dp", axis=0, tiled=True)
+
+    x_zero, x_zero_b = norm_forward(gains[:1], embedded)
+    side = (seq_lengths, mask_slots, mask_targets, positive_rows, doc_ids, false_pairs)
+    side = side + (queue_docs, factors, data_rank, token_ids, near)
+    errors = (gate_error, up_error)
+    x_zero_b, joined_b, side, errors = lax.optimization_barrier((x_zero_b, joined_b, side, errors))
+    gate_error, up_error = errors
+    seq_lengths, mask_slots, mask_targets, positive_rows, doc_ids, false_pairs = side[:6]
+    queue_docs, factors, data_rank, near_ids, near = side[6:]
+    x_blocks = spread_blocks(x_zero_b, "tensor")
+    quarter_b, queue_near = joined_b[:, :attend_cols], joined_b[:, 4 * attend_cols :]
     attend_near = picked_blocks(spread_blocks(quarter_b, "tensor"), near)
     attend_b = jnp.concatenate([attend_near[k] for k in range(tensor_count)], axis=1)
-    table_local, _ = lax.optimization_barrier((table_local, looked[tensor_count - 1]))
-    table_b = lax.all_gather(table_local, "dp", axis=0, tiled=True)
+    queue_near = normalize_keys(queue_near.reshape(data_count * queue_rows, width))
 
     every_rows = mask_slots + own_rows * jnp.arange(tensor_count)[None, :, None]
     every_len = seq_lengths[:, None, None]
@@ -1185,11 +1298,15 @@
         axis=1,
     )
     places = near[:, None] * own_rows + jnp.arange(own_rows)[None, :]
+    keep_own = (places[0] < my_length)[:, None]
     cosine, sine = rotary_tables(places.reshape(-1))
     cosines, sines = row_blocks(cosine, tensor_count), row_blocks(sine, tensor_count)
     bias = jnp.where(places < my_length, 0.0, NEGATIVE).astype(NARROW)
     biases = [jnp.broadcast_to(bias[k][:, None], (own_rows, PAIR)) for k in range(tensor_count)]
-    columns = jnp.arange(queue_docs.shape[0])
+    columns = jnp.arange(queue_docs.shape[0]).reshape(data_count, tensor_count, queue_rows)
+    columns = picked_blocks(jnp.swapaxes(columns, 0, 1), near).reshape(-1)
+    queue_docs = queue_docs.reshape(data_count, tensor_count, queue_rows)
+    queue_docs = picked_blocks(jnp.swapaxes(queue_docs, 0, 1), near).reshape(-1)
     pick = lambda array: lax.dynamic_slice_in_dim(array, data_rank, 1, 0)
     target_c = columns[None, :] == pick(positive_rows)[:, None]
     blocked = (queue_docs[None, :] == pick(doc_ids)[:, None]) | jnp.any(
@@ -1198,8 +1315,10 @@
     blocked = (blocked & jnp.logical_not(target_c)).astype(WIDE)
     target_c = target_c.astype(WIDE)
 
-    x_zero, x_zero_b = norm_forward(gains[:1], embedded)
-    x_blocks = spread_blocks(x_zero_b, "tensor")
+    factor_t = jnp.swapaxes(factors, 1, 2)
+    factor_near = spread_blocks(factor_t[0], "tensor")
+    error_p = partial_projections([attend_error[0]], [factor_t[0]])[0]
+
     queries, first_key, first_value = project(3, x_zero_b, attend_b, cosines[0], sines[0])
     keys, values = [first_key], [first_value]
     for k in range(1, tensor_count):
@@ -1207,34 +1326,20 @@
         keys.append(key)
         values.append(value)
     attended_t, log_total = attention_forward(queries, keys, values, biases)
-    queue_local, _ = lax.optimization_barrier((queue_embed, log_total))
-    queue_all = lax.all_gather(queue_local, "dp", axis=0, tiled=True)
-    keys_hat = normalize_keys(queue_all)
+    queue_near, _ = lax.optimization_barrier((queue_near, log_total))
+    keys_hat = jnp.concatenate(spread_blocks(queue_near, "tensor"), axis=0)
     weight_out = attend_b[:, 3 * width :]
     attended_b, pre_one, hidden_in, hidden_in_b = merge_branch(
         attended_t, weight_out, x_zero, gains[1:2]
     )
-    hidden_blocks = spread_blocks(hidden_in_b, "tensor")
-    half = max(1, tensor_count // 2)
-    hidden_parts = [
-        jnp.concatenate(hidden_blocks[at : at + half], axis=0)
-        for at in range(0, tensor_count, half)
-    ]
-    states = []
-    for part in hidden_parts:
-        if states:
-            part, _ = lax.optimization_barrier((part, states[-1][3]))
-        states.append(ffn_forward(part, ffn_b))
-    ffn_blocks = [block for state in states for block in row_blocks(state[3], half)]
-    ffn_mine, ffn_got = summed_pair(ffn_blocks, "tensor")
+    states, ffn_sums = paired(
+        hidden_in_b, lambda index, first, second: ffn_forward(first, second, joined_b, attend_cols)
+    )
+    ffn_mine, _, ffn_got = far_sum(ffn_sums)
     final, _ = norm_forward(gains[2:], hidden_in, ffn_mine, ffn_got)
 
-    factor_t = jnp.swapaxes(factors, 1, 2)
-    factor_near = spread_blocks(factor_t[0], "tensor")
-    error_p = partial_projections([attend_error[0]], [factor_t[0]])[0]
     ff_own = down_weight.shape[1]
 
-    keep_own = (places[0] < my_length)[:, None]
     pool_part = jnp.sum(jnp.where(keep_own, final, 0.0), axis=0)
     picked = jnp.take(final, own_slots[0], axis=0).astype(NARROW)
     rows_all = jnp.concatenate(spread_blocks(picked, "tensor"), axis=0)
@@ -1268,30 +1373,32 @@
     pre_grad, pre_grad_b, gain_two = last_back(
         own_length, own_slots, row_grad, pooled_grad, hidden_in, ffn_mine, ffn_got, gains[2:]
     )
-    grad_blocks = spread_blocks(pre_grad_b, "tensor")
-    grad_parts = [
-        jnp.concatenate(grad_blocks[at : at + half], axis=0) for at in range(0, tensor_count, half)
-    ]
-    backs = [
-        ffn_backward(part, state[0], state[1], ffn_b) for part, state in zip(grad_parts, states)
-    ]
-    hidden_sums = [block for back in backs for block in row_blocks(back[2], half)]
-    hidden_mine, hidden_got = summed_pair(hidden_sums, "tensor")
-    down_grad = sum(contract_rows(part, state[2]) for part, state in zip(grad_parts, states))
-    gate_w_grad = sum(contract_rows(part, back[0]) for part, back in zip(hidden_parts, backs))
-    up_w_grad = sum(contract_rows(part, back[1]) for part, back in zip(hidden_parts, backs))
+    backs, hidden_sums = paired(
+        pre_grad_b,
+        lambda index, first, second: ffn_backward(first, second, *states[index][:2], joined_b),
+    )
+    hidden_mine, hidden_sent, hidden_got = far_sum(hidden_sums)
+    late = [(back[2], state[2], state[3], back[0], back[1]) for back, state in zip(backs, states)]
+    late, _ = lax.optimization_barrier((late, hidden_sent))
+    down_grad = sum(contract_rows(part[0], part[1]) for part in late)
+    gate_w_grad = sum(contract_rows(part[2], part[3]) for part in late)
+    up_w_grad = sum(contract_rows(part[2], part[4]) for part in late)
     pre_one_grad, branch_grad, attended_grad, gain_one = branch_back(
         pre_grad, hidden_mine, hidden_got, pre_one, gains[1:2], weight_out
     )
     dq, dk, dv = attention_backward(
         queries, keys, values, biases, attended_grad, attended_t, log_total, cosines, sines
     )
-    weight_k, weight_v = attend_b[:, width : 2 * width], attend_b[:, 2 * width : 3 * width]
-    x_parts = [
-        (contract_cols(dk[k], weight_k) + contract_cols(dv[k], weight_v)).astype(NARROW)
-        for k in range(tensor_count)
-    ]
-    x_mine, x_got = summed_pair(x_parts, "tensor")
+    x_sums = {}
+    for key in reversed(range(0, tensor_count, 2)):
+        operands = (dk[key], dv[key], dk[key + 1], dv[key + 1])
+        if x_sums:
+            operands, _ = lax.optimization_barrier((operands, x_sums[key + 2]))
+        x_sums[key] = near_sum(*input_grads(*operands, attend_b))
+    x_mine, x_sent, x_got = far_sum(x_sums)
+    late = (dq, dk, dv, branch_grad)
+    late, _, x_mine = lax.optimization_barrier((late, x_sent, x_mine))
+    dq_late, dk, dv, branch_grad = late
     embedded_grad, gain_zero = first_back(
         pre_one_grad, dq, attend_b[:, :width], x_mine, x_got, embedded, gains[:1]
     )
@@ -1299,15 +1406,17 @@
     emb_all = jnp.dot(ordered.astype(NARROW), emb_all)
     attend_part = jnp.concatenate(
         [
-            contract_rows(x_zero_b, dq),
+            contract_rows(x_zero_b, dq_late),
             sum(contract_rows(x_blocks[k], dk[k]) for k in range(tensor_count)),
             sum(contract_rows(x_blocks[k], dv[k]) for k in range(tensor_count)),
             jnp.dot(attended_b, branch_grad, preferred_element_type=WIDE),
         ],
         axis=1,
     )
-    attend_blocks = jnp.moveaxis(attend_part.reshape(width, tensor_count, attend_cols), 1, 0)
-    attend_blocks = picked_blocks(attend_blocks, near)
+    attend_blocks = [
+        lax.dynamic_slice_in_dim(attend_part, near[k] * attend_cols, attend_cols, 1)
+        for k in range(tensor_count)
+    ]
     attend_p = partial_projections(
         [attend_blocks[k] for k in range(tensor_count)], factor_near
     )
@@ -1319,15 +1428,15 @@
         for key in sorted((k for k in attend_held if not k & bit), reverse=True):
             attend_held[key] = attend_held[key] + swap(attend_held.pop(key ^ bit), "tensor", bit)
     emb_all, attend_held[bits[-1]] = lax.optimization_barrier((emb_all, attend_held[bits[-1]]))
-    attend_grad = attend_held[0] + swap(attend_held[bits[-1]], "tensor", bits[-1])
+    attend_got = swap(attend_held[bits[-1]], "tensor", bits[-1])
 
     other_m, other_p = small_matrices(
         [gate_w_grad, up_w_grad, down_grad],
-        [gate_up_error[0, :, 0], gate_up_error[0, :, 1], down_error[0]],
+        [gate_error, up_error, down_error[0]],
         factor_t[1:4],
     )
     other_sum = summed_all(jnp.concatenate([other_p[k] for k in range(3)], axis=1), "dp")
-    cuts = [tiles * part // PARTS for part in range(PARTS + 1)]
+    cuts = sorted({0, (tiles + 1) // 2, tiles - 1, tiles})
     table_parts, table_sums = [], []
     for bounds in zip(cuts, cuts[1:]):
         found = table_matrix(
@@ -1342,7 +1451,8 @@
     parts = [table_sums[-1][:, -attend_cols:], other_sum] + table_sums[:-1]
     parts.append(table_sums[-1][:, :-attend_cols])
     sums = jnp.concatenate(parts, axis=1)
-    first_m = (attend_grad + attend_error[0])[None]
+    attend_got, _ = lax.optimization_barrier((attend_got, sums))
+    first_m = (attend_held[0] + attend_got + attend_error[0])[None]
     spans, start = [], 0
     for size in (attend_cols, ff_own, ff_own, ff_own, tiles * TILE):
         spans.append((start, size))

time: 786 us -> 717 us (0.912)
  Pallas kernels: 343 us -> 216 us
  local copies, waits for them, and re-layouts: 96.6 us -> 148 us
  waiting for transfers between devices: 123 us -> 157 us
  matrix products: 57.8 us -> 40.1 us
  other arithmetic: 69.5 us -> 61.4 us
    unnamed x203 -> x421, local copies, waits for them, and re-layouts: 40.7 us -> 119 us
    pallas_call x4, Pallas kernels: 52.4 us -> 24.7 us  [lookup(): pl.pallas_call(functools.partial(lookup_kernel, row_count), in_specs=[pl....]
    pallas_call x9 -> x10, Pallas kernels: 35.2 us -> 11.3 us  [whole_call(): pl.pallas_call(kernel, out_shape=[jax.ShapeDtypeStruct(shape, kind) for s...]
    dot_general x27 -> x19, matrix products: 46.6 us -> 30.2 us  [dot_in(): lax.dot_general(left, right, (axes, ((), ())), precision=precision, prefe...]
    ppermute x65 -> x68, waiting for transfers between devices: 102 us -> 117 us  [swap(): lax.ppermute(value, axis, [(index, index ^ bit) for index in range(size)])]
    all_gather x1, waiting for transfers between devices: 0.01 us -> 11.5 us  [per_device(): table_b = lax.all_gather(table_local, 'dp', axis=0, tiled=True)]
    pallas_call x4, Pallas kernels: 19.4 us -> 8.19 us  [project(): pl.pallas_call(functools.partial(project_kernel, count), grid=(1,), in_sp...]
    pallas_call x1, Pallas kernels: 20.6 us -> 11 us  [table_error(): pl.pallas_call(functools.partial(table_error_kernel, bounds), grid=(basis...]
  transfers between devices with their start and end apart: 70 -> 72, of which waited for: 22 -> 25; matrix products, arithmetic and copies ran while one was open for 24% -> 17% of each run, Pallas kernels for 44% -> 30%
where the time goes in v3:
time: 717 us; the launch traced here: 709 us
  Pallas kernels  216 us (30%)
  waiting for transfers between devices  157 us (22%)
  local copies, waits for them, and re-layouts  148 us (21%)
  other arithmetic  61.4 us (9%)
  starting transfers between devices  56 us (8%)
  matrix products  40.1 us (6%)
  between operations  31.5 us (4%)
    unnamed x421, local copies, waits for them, and re-layouts  119 us
    ppermute x68, waiting for transfers between devices, swap(): lax.ppermute(value, axis, [(index, index ^ bit) for index in range(size)])  117 us
    pallas_call x1, Pallas kernels, attention_backward(): pl.pallas_call(functools.partial(attend_back_kernel, count), grid=(pairs,...  46.3 us
    ppermute x68, starting transfers between devices, swap(): lax.ppermute(value, axis, [(index, index ^ bit) for index in range(size)])  45 us
    dot_general x19, matrix products, dot_in(): lax.dot_general(left, right, (axes, ((), ())), precision=precision, prefe...  30.2 us
    pallas_call x3, Pallas kernels, table_matrix(): pl.pallas_call(functools.partial(table_kernel, columns, first), grid=(til...  25.6 us
    pallas_call x4, Pallas kernels, lookup(): pl.pallas_call(functools.partial(lookup_kernel, row_count), in_specs=[pl....  24.7 us
    all_to_all x1, waiting for transfers between devices, per_device(): embedded = lax.all_to_all(pieces, 'dp', 0, 0).reshape(width, own_rows).T  24.1 us
  transfers between devices with their start and end apart: 72, of which 25 were waited for; matrix products, arithmetic and copies ran while one was open for 17% of the time, Pallas kernels for 30%

profile of v3, /device:TPU:0, one launch (start us, length us, event | category | flops | bytes accessed | tf_op | source)
XLA Modules:
  0.0 709.4 jit_solution(16734213287770450875)
XLA Ops:
  14.5 7.3 %all-to-all-start = ((s32[8,1,2048]{2,1,0:T(1,128)}), s32[8,1,2048]{2,1,0:T(1,128)S(1)}, u32[]{:S(2)}, u32[]{:S(2)}) async-start(s32[8,1,2048]{2,1,0:T(1,128)} %broadcast_in_dim.110), calls=%async_computation | async-start | bytes 131072 | tf_op jit(solution)/shard_map/all_to_all | solution.py:1222
  25.6 3.2 all-to-all-done
  31.2 6.2 shard_map.379
  39.7 6.2 shard_map.380
  45.8 6.2 shard_map.381
  56.4 6.2 shard_map.382
  62.6 9.6 %collective-permute-done.2 = bf16[512,768]{1,0:T(8,128)(2,1)S(1)} collective-permute-done((bf16[512,768]{1,0:T(8,128)(2,1)S(1)}, bf16[512,768]{1,0:T(8,128)(2,1)S(1)}, u32[]{:S(2)}, u32[]{:S(2)}) %collective-permute-start.2) | collective-permute-done | bytes 786464 | tf_op jit(solution)/shard_map/ppermute | solution.py:43
  73.7 3.7 all-to-all-start.1
  77.5 8.7 %constant_dynamic-slice_fusion.34 = (f32[1,768,1,768]{3,2,1,0:T(1,128)S(1)}, f32[1,768,1,768]{3,2,1,0:T(1,128)S(1)}) fusion(f32[1,768,2,768]{3,2,1,0:T(2,128)} %param.48, s32[]{:T(128)S(6)} %select_n.149, s32[]{:T(128)S(6)} %select_n.148), kind=kLoop, calls=%fused_computation.182 | loop fusion | bytes 9437192 | tf_op jit(solution)/shard_map/dynamic_slice | solution.py:1247
  88.6 24.1 %all-to-all-done.1 = bf16[8,96,512]{2,1,0:T(8,128)(2,1)S(1)} async-done(((bf16[8,96,512]{2,1,0:T(8,128)(2,1)}), bf16[8,96,512]{2,1,0:T(8,128)(2,1)S(1)}, u32[]{:S(2)}, u32[]{:S(2)}) %all-to-all-start.1) | async-done | bytes 786464 | tf_op jit(solution)/shard_map/all_to_all | solution.py:1248
  129.9 17.5 %collective-permute-done.4 = bf16[768,768]{1,0:T(8,128)(2,1)} collective-permute-done((bf16[768,768]{1,0:T(8,128)(2,1)}, bf16[768,768]{1,0:T(8,128)(2,1)}, u32[]{:S(2)}, u32[]{:S(2)}) %collective-permute-start.4) | collective-permute-done | bytes 1179680 | tf_op jit(solution)/shard_map/ppermute | solution.py:43
  147.4 3.7 multiply_sine_fusion
  152.1 11.3 %collective-permute-done.7.x_ref = bf16[512,768]{1,0:T(8,128)(2,1)} collective-permute-done((bf16[512,768]{1,0:T(8,128)(2,1)S(1)}, bf16[512,768]{1,0:T(8,128)(2,1)}, u32[]{:S(2)}, u32[]{:S(2)}) %collective-permute-start.7) | collective-permute-done | bytes 786464 | tf_op jit(solution)/shard_map/ppermute | solution.py:43
  175.8 23.2 %shard_map.388 = (f32[768,512]{1,0:T(8,128)S(1)}, f32[6,2,512]{2,1,0:T(2,128)S(1)}) custom-call(bf16[512,768]{1,0:T(8,128)(2,1)S(1)} %get-tuple-element.194.q_ref, bf16[512,768]{1,0:T(8,128)(2,1)S(1)} %get-tuple-element.198.refs_0_, bf16[512,768]{1,0:T(8,128)(2,1)S(1)} %get-tuple-element.199.refs_1_, bf16[512,768]{1,0:T(8,128)(2,1)S(1)} %get-tuple-element.200.refs_2_, ...), custom_call_target="tpu_custom_call" | custom-call | flops 3221225472 | bytes 9437184 | tf_op jit(solution)/shard_map/pallas_call | solution.py:789
  212.0 7.0 shard_map.390
  227.8 4.6 shard_map.391
  247.5 11.6 %collective-permute-done.14.refs_2_.got_ref = bf16[512,768]{1,0:T(8,128)(2,1)S(1)} collective-permute-done((bf16[512,768]{1,0:T(8,128)(2,1)}, bf16[512,768]{1,0:T(8,128)(2,1)S(1)}, u32[]{:S(2)}, u32[]{:S(2)}) %collective-permute-start.14) | collective-permute-done | bytes 786464 | tf_op jit(solution)/shard_map/ppermute | solution.py:43
  273.0 11.5 %all-gather.5.cloned.1.call-done.table_ref = bf16[768,7632]{1,0:T(8,128)(2,1)} async-done(((bf16[96,7632]{1,0:T(8,128)(2,1)}), bf16[768,7632]{1,0:T(8,128)(2,1)}) %all-gather.5.cloned.1.call-update) | async-done | bytes 11722768 | tf_op jit(solution)/shard_map/all_gather | solution.py:1260
  284.5 4.3 copy-done.9
  288.9 5.4 shard_map.393
  305.5 4.3 copy-done.10
  313.1 7.2 %shard_map.396 = (bf16[160,7680]{1,0:T(8,128)(2,1)S(1)}, f32[160,768]{1,0:T(8,128)S(1)}) custom-call(f32[160,7680]{1,0:T(8,128)S(1)} %copy-done.44, bf16[768,7632]{1,0:T(8,128)(2,1)S(1)} %copy-done.10, s32[160,1]{1,0:T(8,128)S(1)} %sub.77.targets_ref, f32[160,128]{1,0:T(8,128)S(1)} %slice.368.stats_ref, f32[160,1]{1,0:T(8,128)S(1)} %copy-done.117), custom_call_target="tpu_custom_call" | custom-call | flops 1875640320 | bytes 11722752 | tf_op jit(solution)/shard_map/pallas_call | solution.py:678
  332.1 6.4 shard_map.399
  342.9 6.9 collective-permute-done.28.first_ref
  359.5 6.8 shard_map.400
  368.9 5.2 convert_reduce_fusion
  385.8 9.7 %collective-permute-done.31.got_ref = bf16[512,768]{1,0:T(8,128)(2,1)S(1)} collective-permute-done((bf16[512,768]{1,0:T(8,128)(2,1)}, bf16[512,768]{1,0:T(8,128)(2,1)S(1)}, u32[]{:S(2)}, u32[]{:S(2)}) %collective-permute-start.31) | collective-permute-done | bytes 786464 | tf_op jit(solution)/shard_map/ppermute | solution.py:43
  405.6 46.3 %shard_map.402 = (bf16[512,768]{1,0:T(8,128)(2,1)S(1)}, bf16[512,768]{1,0:T(8,128)(2,1)S(1)}, bf16[512,768]{1,0:T(8,128)(2,1)S(1)}, bf16[512,768]{1,0:T(8,128)(2...) custom-call(bf16[512,768]{1,0:T(8,128)(2,1)S(1)} %copy-done.161, ...), custom_call_target="tpu_custom_call" | custom-call | flops 8053063680 | bytes 15728640 | tf_op jit(solution)/shard_map/pallas_call | solution.py:870
  452.0 3.5 shard_map.403
  456.8 3.5 fusion.93
  486.0 4.3 copy-done.168
  497.1 4.2 shard_map.409
  505.8 7.8 %collective-permute-done.37 = bf16[512,768]{1,0:T(8,128)(2,1)S(1)} collective-permute-done((bf16[512,768]{1,0:T(8,128)(2,1)S(1)}, bf16[512,768]{1,0:T(8,128)(2,1)S(1)}, u32[]{:S(2)}, u32[]{:S(2)}) %collective-permute-start.37) | collective-permute-done | bytes 786464 | tf_op jit(solution)/shard_map/ppermute | solution.py:43
  513.7 5.3 fusion.77
  522.0 7.9 %fusion.left_ref = bf16[2048,768]{1,0:T(8,128)(2,1)S(1)} fusion(s32[2048]{0:T(1024)S(1)} %copy-done.190, bf16[512,768]{1,0:T(8,128)(2,1)S(1)} %collective-permute-done.38, bf16[512,768]{1,0:T(8,128)(2,1)S(1)} %collective-permute-done.37, bf16[512,768]{1,0:T(8,128)(2,1)S(1)} %collective-permute-done.36, bf16[512,768]{1,0:T(8,128)(2,1)S(1)} %get-tuple-element.273), kind=kOutput, calls=%fused_computation.3 | convolution fusion | flops 6459228160 | bytes 6299648 | tf_op jit(solution)/shard_map/dot_general | solution.py:1406
  531.5 3.1 shard_map.406
  536.3 12.4 %shard_map.410 = (bf16[3840,768]{1,0:T(8,128)(2,1)S(1)}, bf16[3840,768]{1,0:T(8,128)(2,1)S(1)}, f32[8,3840]{1,0:T(8,128)S(1)}) custom-call(s32[13]{0:T(128)S(1)} %convert_reduce_fusion.1.starts_ref, bf16[2048,768]{1,0:T(8,128)(2,1)S(1)} %fusion.left_ref, s32[1,2048]{1,0:T(1,128)S(1)} %bitcast.258, bf16[160,768]{1,0:T(8,128)(2,1)S(1)} %pad_maximum_fusion.5.rows_ref, ...), custom_call_target="tpu_custom_call" | custom-call | flops 4105175040 | bytes 23592960 | tf_op jit(solution)/shard_map/pallas_call | solution.py:956
  557.8 10.1 %shard_map.411 = (bf16[3200,768]{1,0:T(8,128)(2,1)S(1)}, bf16[3200,768]{1,0:T(8,128)(2,1)S(1)}, f32[8,3200]{1,0:T(8,128)S(1)}) custom-call(s32[13]{0:T(128)S(1)} %convert_reduce_fusion.1.starts_ref, bf16[2048,768]{1,0:T(8,128)(2,1)S(1)} %fusion.left_ref, s32[1,2048]{1,0:T(1,128)S(1)} %bitcast.259, bf16[160,768]{1,0:T(8,128)(2,1)S(1)} %pad_maximum_fusion.5.rows_ref, ...), custom_call_target="tpu_custom_call" | custom-call | flops 3420979200 | bytes 19660800 | tf_op jit(solution)/shard_map/pallas_call | solution.py:956
  577.9 6.1 collective-permute-done.54
  587.1 7.4 %collective-permute-done.55 = f32[8,3840]{1,0:T(8,128)S(1)} collective-permute-done((f32[8,3840]{1,0:T(8,128)S(1)}, f32[8,3840]{1,0:T(8,128)S(1)}, u32[]{:S(2)}, u32[]{:S(2)}) %collective-permute-start.55) | collective-permute-done | bytes 122912 | tf_op jit(solution)/shard_map/ppermute | solution.py:43
  609.4 4.8 shard_map.415.refs_6_
  615.7 3.8 collective-permute-done.62
  620.2 8.9 %collective-permute-done.40 = f32[768,768]{1,0:T(8,128)} collective-permute-done((f32[768,768]{1,0:T(8,128)}, f32[768,768]{1,0:T(8,128)}, u32[]{:S(2)}, u32[]{:S(2)}) %collective-permute-start.40) | collective-permute-done | bytes 2359328 | tf_op jit(solution)/shard_map/ppermute | solution.py:43
  629.1 4.4 add_bitcast_fusion.m_ref
  646.9 9.0 %copy.157 = f32[1,768,2,768]{3,2,1,0:T(2,128)} copy(f32[1,768,2,768]{3,1,2,0:T(8,128)} %maximum_bitcast_fusion) | data formatting | bytes 9437184
  662.0 11.0 %shard_map.418 = f32[7632,768]{1,0:T(8,128)} custom-call(bf16[3840,768]{1,0:T(8,128)(2,1)S(1)} %bitcast.242, bf16[3200,768]{1,0:T(8,128)(2,1)S(1)} %copy-done.23, bf16[640,768]{1,0:T(8,128)(2,1)S(1)} %copy-done.47, bf16[3840,768]{1,0:T(8,128)(2,1)S(1)} %bitcast.244, bf16[3200,768]{1,0:T(8,128)(2,1)S(1)} %copy-done.26, bf16[640,768]{1,0:T(8,128)(2,1)S(1)} %copy-done.50, ...), custom_call_target="tpu_custom_call" | custom-call | flops 281346048 | bytes 46891008 | tf_op jit(solution)/shard_map/pallas_call | solution.py:1158
  678.5 3.3 collective-permute-done.66
  695.5 5.6 multiply_subtract_fusion
  (741 shorter events, 277.3 us)
Async XLA Ops:
  7.2 108.6 %all-gather.3.cloned.1.call-start = ((), (), s32[]{:S(2)}) async-start(), calls=%async_computation.2 | async-start | bytes 5750784 | tf_op jit(solution)/shard_map/all_gather | solution.py:1258
  14.5 14.3 %all-to-all-start = ((s32[8,1,2048]{2,1,0:T(1,128)}), s32[8,1,2048]{2,1,0:T(1,128)S(1)}, u32[]{:S(2)}, u32[]{:S(2)}) async-start(s32[8,1,2048]{2,1,0:T(1,128)} %broadcast_in_dim.110), calls=%async_computation | async-start | bytes 131072 | tf_op jit(solution)/shard_map/all_to_all | solution.py:1222
  21.8 262.7 %all-gather.5.cloned.1.call-start = ((), (), s32[]{:S(2)}) async-start(), calls=%async_computation.3 | async-start | bytes 13271040 | tf_op jit(solution)/shard_map/all_gather | solution.py:1260
  37.4 14.6 %collective-permute-start = (bf16[512,768]{1,0:T(8,128)(2,1)S(1)}, bf16[512,768]{1,0:T(8,128)(2,1)S(1)}, u32[]{:S(2)}, u32[]{:S(2)}) collective-permute-start(bf16[512,768]{1,0:T(8,128)(2,1)S(1)} %shard_map.379), channel_id=1, source_target_pairs={{0,1},{1,0},{2,3},{3,2},{4,5},{5,4},{6,7},{7,6},{8,9},{9,8},{10,11... | collective-permute-start | bytes 2359304 | tf_op jit(solution)/shard_map/ppermute | solution.py:43
  52.2 20.0 %collective-permute-start.2 = (bf16[512,768]{1,0:T(8,128)(2,1)S(1)}, bf16[512,768]{1,0:T(8,128)(2,1)S(1)}, u32[]{:S(2)}, u32[]{:S(2)}) collective-permute-start(bf16[512,768]{1,0:T(8,128)(2,1)S(1)} %add_convert_fusion.7), channel_id=1, source_target_pairs={{0,2},{1,3},{2,0},{3,1},{4,6},{5,7},{6,4},{7,5},{8,10},{9,11},{10,... | collective-permute-start | bytes 2359304 | tf_op jit(solution)/shard_map/ppermute | solution.py:43
  53.8 18.4 %collective-permute-start.1 = (bf16[512,768]{1,0:T(8,128)(2,1)S(1)}, bf16[512,768]{1,0:T(8,128)(2,1)S(1)}, u32[]{:S(2)}, u32[]{:S(2)}) collective-permute-start(bf16[512,768]{1,0:T(8,128)(2,1)S(1)} %shard_map.381), channel_id=1, source_target_pairs={{0,1},{1,0},{2,3},{3,2},{4,5},{5,4},{6,7},{7,6},{8,9},{9,8},{10,11... | collective-permute-start | bytes 2359304 | tf_op jit(solution)/shard_map/ppermute | solution.py:43
  73.7 39.0 %all-to-all-start.1 = ((bf16[8,96,512]{2,1,0:T(8,128)(2,1)}), bf16[8,96,512]{2,1,0:T(8,128)(2,1)S(1)}, u32[]{:S(2)}, u32[]{:S(2)}) async-start(bf16[8,96,512]{2,1,0:T(8,128)(2,1)} %bitcast.7), calls=%async_computation.1 | async-start | bytes 1572864 | tf_op jit(solution)/shard_map/all_to_all | solution.py:1248
  118.3 29.1 %collective-permute-start.4 = (bf16[768,768]{1,0:T(8,128)(2,1)}, bf16[768,768]{1,0:T(8,128)(2,1)}, u32[]{:S(2)}, u32[]{:S(2)}) collective-permute-start(bf16[768,768]{1,0:T(8,128)(2,1)} %get-tuple-element.435), channel_id=1, source_target_pairs={{0,2},{1,3},{2,0},{3,1},{4,6},{5,7},{6,4},{7,5},{8,10},{9,11},{10,... | collective-permute-start | bytes 3538952 | tf_op jit(solution)/shard_map/ppermute | solution.py:43
  119.8 43.6 %collective-permute-start.3 = (bf16[768,768]{1,0:T(8,128)(2,1)}, bf16[768,768]{1,0:T(8,128)(2,1)}, u32[]{:S(2)}, u32[]{:S(2)}) collective-permute-start(bf16[768,768]{1,0:T(8,128)(2,1)} %get-tuple-element.435), channel_id=1, source_target_pairs={{0,1},{1,0},{2,3},{3,2},{4,5},{5,4},{6,7},{7,6},{8,9},{9,8},{10,11... | collective-permute-start | bytes 3538952 | tf_op jit(solution)/shard_map/ppermute | solution.py:43
  125.5 44.3 %collective-permute-start.6 = (bf16[512,768]{1,0:T(8,128)(2,1)S(1)}, bf16[512,768]{1,0:T(8,128)(2,1)S(1)}, u32[]{:S(2)}, u32[]{:S(2)}) collective-permute-start(bf16[512,768]{1,0:T(8,128)(2,1)S(1)} %get-tuple-element.191.x_ref), channel_id=1, source_target_pairs={{0,1},{1,0},{2,3},{3,2},{4,5},{5,4},{6,7},{7,6},{8,9},{9,8},{10,11... | collective-permute-start | bytes 2359304 | tf_op jit(solution)/shard_map/ppermute | solution.py:43
  126.1 37.3 %collective-permute-start.7 = (bf16[512,768]{1,0:T(8,128)(2,1)S(1)}, bf16[512,768]{1,0:T(8,128)(2,1)}, u32[]{:S(2)}, u32[]{:S(2)}) collective-permute-start(bf16[512,768]{1,0:T(8,128)(2,1)S(1)} %get-tuple-element.191.x_ref), channel_id=1, source_target_pairs={{0,2},{1,3},{2,0},{3,1},{4,6},{5,7},{6,4},{7,5},{8,10},{9,11},{10,... | collective-permute-start | bytes 2359304 | tf_op jit(solution)/shard_map/ppermute | solution.py:43
  147.4 16.0 %collective-permute-start.5 = (bf16[768,768]{1,0:T(8,128)(2,1)}, bf16[768,768]{1,0:T(8,128)(2,1)S(1)}, u32[]{:S(2)}, u32[]{:S(2)}) collective-permute-start(bf16[768,768]{1,0:T(8,128)(2,1)} %collective-permute-done.4), channel_id=1, source_target_pairs={{0,1},{1,0},{2,3},{3,2},{4,5},{5,4},{6,7},{7,6},{8,9},{9,8},{10,11... | collective-permute-start | bytes 3538952 | tf_op jit(solution)/shard_map/ppermute | solution.py:43
  163.4 7.9 %collective-permute-start.8 = (bf16[512,768]{1,0:T(8,128)(2,1)}, bf16[512,768]{1,0:T(8,128)(2,1)S(1)}, u32[]{:S(2)}, u32[]{:S(2)}) collective-permute-start(bf16[512,768]{1,0:T(8,128)(2,1)} %collective-permute-done.7.x_ref), channel_id=1, source_target_pairs={{0,1},{1,0},{2,3},{3,2},{4,5},{5,4},{6,7},{7,6},{8,9},{9,8},{10,11... | collective-permute-start | bytes 2359304 | tf_op jit(solution)/shard_map/ppermute | solution.py:43
  205.0 20.6 %collective-permute-start.11 = (bf16[512,768]{1,0:T(8,128)(2,1)}, bf16[512,768]{1,0:T(8,128)(2,1)S(1)}, u32[]{:S(2)}, u32[]{:S(2)}) collective-permute-start(bf16[512,768]{1,0:T(8,128)(2,1)} %get-tuple-element.209.first_ref), channel_id=1, source_target_pairs={{0,2},{1,3},{2,0},{3,1},{4,6},{5,7},{6,4},{7,5},{8,10},{9,11},{10,... | collective-permute-start | bytes 2359304 | tf_op jit(solution)/shard_map/ppermute | solution.py:43
  237.8 8.1 %collective-permute-start.10 = (bf16[512,768]{1,0:T(8,128)(2,1)}, bf16[512,768]{1,0:T(8,128)(2,1)}, u32[]{:S(2)}, u32[]{:S(2)}) collective-permute-start(bf16[512,768]{1,0:T(8,128)(2,1)} %get-tuple-element.211), channel_id=1, source_target_pairs={{0,1},{1,0},{2,3},{3,2},{4,5},{5,4},{6,7},{7,6},{8,9},{9,8},{10,11... | collective-permute-start | bytes 2359304 | tf_op jit(solution)/shard_map/ppermute | solution.py:43
  239.4 19.7 %collective-permute-start.14 = (bf16[512,768]{1,0:T(8,128)(2,1)}, bf16[512,768]{1,0:T(8,128)(2,1)S(1)}, u32[]{:S(2)}, u32[]{:S(2)}) collective-permute-start(bf16[512,768]{1,0:T(8,128)(2,1)} %add_convert_fusion.4), channel_id=1, source_target_pairs={{0,2},{1,3},{2,0},{3,1},{4,6},{5,7},{6,4},{7,5},{8,10},{9,11},{10,... | collective-permute-start | bytes 2359304 | tf_op jit(solution)/shard_map/ppermute | solution.py:43
  267.8 32.7 %collective-permute-start.24 = (bf16[256,768]{1,0:T(8,128)(2,1)}, bf16[256,768]{1,0:T(8,128)(2,1)}, u32[]{:S(2)}, u32[]{:S(2)}) collective-permute-start(bf16[256,768]{1,0:T(8,128)(2,1)} %multiply_convert_fusion), channel_id=1, source_target_pairs={{0,2},{1,3},{2,0},{3,1},{4,6},{5,7},{6,4},{7,5},{8,10},{9,11},{10,... | collective-permute-start | bytes 1179656 | tf_op jit(solution)/shard_map/ppermute | solution.py:43
  300.5 20.0 %collective-permute-start.23 = (bf16[256,768]{1,0:T(8,128)(2,1)}, bf16[256,768]{1,0:T(8,128)(2,1)S(1)}, u32[]{:S(2)}, u32[]{:S(2)}) collective-permute-start(bf16[256,768]{1,0:T(8,128)(2,1)} %multiply_convert_fusion), channel_id=1, source_target_pairs={{0,1},{1,0},{2,3},{3,2},{4,5},{5,4},{6,7},{7,6},{8,9},{9,8},{10,11... | collective-permute-start | bytes 1179656 | tf_op jit(solution)/shard_map/ppermute | solution.py:43
  300.5 20.0 %collective-permute-start.25 = (bf16[256,768]{1,0:T(8,128)(2,1)}, bf16[256,768]{1,0:T(8,128)(2,1)S(1)}, u32[]{:S(2)}, u32[]{:S(2)}) collective-permute-start(bf16[256,768]{1,0:T(8,128)(2,1)} %collective-permute-done.24), channel_id=1, source_target_pairs={{0,1},{1,0},{2,3},{3,2},{4,5},{5,4},{6,7},{7,6},{8,9},{9,8},{10,11... | collective-permute-start | bytes 1179656 | tf_op jit(solution)/shard_map/ppermute | solution.py:43
  329.8 20.1 %collective-permute-start.28 = (bf16[512,768]{1,0:T(8,128)(2,1)S(1)}, bf16[512,768]{1,0:T(8,128)(2,1)}, u32[]{:S(2)}, u32[]{:S(2)}) collective-permute-start(bf16[512,768]{1,0:T(8,128)(2,1)S(1)} %get-tuple-element.229.first_ref), channel_id=1, source_target_pairs={{0,2},{1,3},{2,0},{3,1},{4,6},{5,7},{6,4},{7,5},{8,10},{9,11},{10,... | collective-permute-start | bytes 2359304 | tf_op jit(solution)/shard_map/ppermute | solution.py:43
  350.5 33.1 %collective-permute-start.42 = (f32[8,768]{1,0:T(8,128)S(1)}, f32[8,768]{1,0:T(8,128)S(1)}, u32[]{:S(2)}, u32[]{:S(2)}) collective-permute-start(f32[8,768]{1,0:T(8,128)S(1)} %get-tuple-element.465.refs_4_.refs_1_), channel_id=1, source_target_pairs={{0,2},{1,3},{2,0},{3,1},{4,6},{5,7},{6,4},{7,5},{8,10},{9,11},{10,... | collective-permute-start | bytes 73736 | tf_op jit(solution)/shard_map/ppermute | solution.py:43
  374.2 10.0 %collective-permute-start.27 = (bf16[512,768]{1,0:T(8,128)(2,1)}, bf16[512,768]{1,0:T(8,128)(2,1)}, u32[]{:S(2)}, u32[]{:S(2)}) collective-permute-start(bf16[512,768]{1,0:T(8,128)(2,1)} %get-tuple-element.233), channel_id=1, source_target_pairs={{0,1},{1,0},{2,3},{3,2},{4,5},{5,4},{6,7},{7,6},{8,9},{9,8},{10,11... | collective-permute-start | bytes 2359304 | tf_op jit(solution)/shard_map/ppermute | solution.py:43
  375.7 19.9 %collective-permute-start.31 = (bf16[512,768]{1,0:T(8,128)(2,1)}, bf16[512,768]{1,0:T(8,128)(2,1)S(1)}, u32[]{:S(2)}, u32[]{:S(2)}) collective-permute-start(bf16[512,768]{1,0:T(8,128)(2,1)} %add_convert_fusion.2), channel_id=1, source_target_pairs={{0,2},{1,3},{2,0},{3,1},{4,6},{5,7},{6,4},{7,5},{8,10},{9,11},{10,... | collective-permute-start | bytes 2359304 | tf_op jit(solution)/shard_map/ppermute | solution.py:43
  380.7 138.2 %collective-permute-start.41 = (f32[8,768]{1,0:T(8,128)S(1)}, f32[8,768]{1,0:T(8,128)S(1)}, u32[]{:S(2)}, u32[]{:S(2)}) collective-permute-start(f32[8,768]{1,0:T(8,128)S(1)} %get-tuple-element.465.refs_4_.refs_1_), channel_id=1, source_target_pairs={{0,1},{1,0},{2,3},{3,2},{4,5},{5,4},{6,7},{7,6},{8,9},{9,8},{10,11... | collective-permute-start | bytes 73736 | tf_op jit(solution)/shard_map/ppermute | solution.py:43
  383.6 135.4 %collective-permute-start.43 = (f32[8,768]{1,0:T(8,128)S(1)}, f32[8,768]{1,0:T(8,128)}, u32[]{:S(2)}, u32[]{:S(2)}) collective-permute-start(f32[8,768]{1,0:T(8,128)S(1)} %collective-permute-done.42.refs_6_), channel_id=1, source_target_pairs={{0,1},{1,0},{2,3},{3,2},{4,5},{5,4},{6,7},{7,6},{8,9},{9,8},{10,11... | collective-permute-start | bytes 73736 | tf_op jit(solution)/shard_map/ppermute | solution.py:43
  456.5 6.6 collective-permute-start.32
  471.2 21.2 %collective-permute-start.35 = (bf16[512,768]{1,0:T(8,128)(2,1)S(1)}, bf16[512,768]{1,0:T(8,128)(2,1)S(1)}, u32[]{:S(2)}, u32[]{:S(2)}) collective-permute-start(bf16[512,768]{1,0:T(8,128)(2,1)S(1)} %add_convert_fusion.1), channel_id=1, source_target_pairs={{0,2},{1,3},{2,0},{3,1},{4,6},{5,7},{6,4},{7,5},{8,10},{9,11},{10,... | collective-permute-start | bytes 2359304 | tf_op jit(solution)/shard_map/ppermute | solution.py:43
  490.4 23.3 %collective-permute-start.39 = (f32[768,768]{1,0:T(8,128)S(1)}, f32[768,768]{1,0:T(8,128)S(1)}, u32[]{:S(2)}, u32[]{:S(2)}) collective-permute-start(f32[768,768]{1,0:T(8,128)S(1)} %constant_dynamic-slice_fusion.8.refs_3_), channel_id=1, source_target_pairs={{0,1},{1,0},{2,3},{3,2},{4,5},{5,4},{6,7},{7,6},{8,9},{9,8},{10,11... | collective-permute-start | bytes 7077896 | tf_op jit(solution)/shard_map/ppermute | solution.py:43
  494.1 19.6 %collective-permute-start.37 = (bf16[512,768]{1,0:T(8,128)(2,1)S(1)}, bf16[512,768]{1,0:T(8,128)(2,1)S(1)}, u32[]{:S(2)}, u32[]{:S(2)}) collective-permute-start(bf16[512,768]{1,0:T(8,128)(2,1)S(1)} %get-tuple-element.273), channel_id=1, source_target_pairs={{0,2},{1,3},{2,0},{3,1},{4,6},{5,7},{6,4},{7,5},{8,10},{9,11},{10,... | collective-permute-start | bytes 2359304 | tf_op jit(solution)/shard_map/ppermute | solution.py:43
  505.8 16.2 %collective-permute-start.36 = (bf16[512,768]{1,0:T(8,128)(2,1)S(1)}, bf16[512,768]{1,0:T(8,128)(2,1)S(1)}, u32[]{:S(2)}, u32[]{:S(2)}) collective-permute-start(bf16[512,768]{1,0:T(8,128)(2,1)S(1)} %get-tuple-element.273), channel_id=1, source_target_pairs={{0,1},{1,0},{2,3},{3,2},{4,5},{5,4},{6,7},{7,6},{8,9},{9,8},{10,11... | collective-permute-start | bytes 2359304 | tf_op jit(solution)/shard_map/ppermute | solution.py:43
  513.6 8.4 %collective-permute-start.38 = (bf16[512,768]{1,0:T(8,128)(2,1)S(1)}, bf16[512,768]{1,0:T(8,128)(2,1)S(1)}, u32[]{:S(2)}, u32[]{:S(2)}) collective-permute-start(bf16[512,768]{1,0:T(8,128)(2,1)S(1)} %collective-permute-done.37), channel_id=1, source_target_pairs={{0,1},{1,0},{2,3},{3,2},{4,5},{5,4},{6,7},{7,6},{8,9},{9,8},{10,11... | collective-permute-start | bytes 2359304 | tf_op jit(solution)/shard_map/ppermute | solution.py:43
  513.6 60.2 %collective-permute-start.51 = (f32[8,2304]{1,0:T(8,128)S(1)}, f32[8,2304]{1,0:T(8,128)S(1)}, u32[]{:S(2)}, u32[]{:S(2)}) collective-permute-start(f32[8,2304]{1,0:T(8,128)S(1)} %fusion.75), channel_id=1, source_target_pairs={{0,8},{4,12},{8,0},{12,4},{16,24},{20,28},{24,16},{28,20},{1,9},{5... | collective-permute-start | bytes 221192 | tf_op jit(solution)/shard_map/ppermute | solution.py:43
  521.4 8.6 %collective-permute-start.45 = (f32[8,768]{1,0:T(8,128)S(1)}, f32[8,768]{1,0:T(8,128)S(1)}, u32[]{:S(2)}, u32[]{:S(2)}) collective-permute-start(f32[8,768]{1,0:T(8,128)S(1)} %get-tuple-element.467), channel_id=1, source_target_pairs={{0,1},{1,0},{2,3},{3,2},{4,5},{5,4},{6,7},{7,6},{8,9},{9,8},{10,11... | collective-permute-start | bytes 73736 | tf_op jit(solution)/shard_map/ppermute | solution.py:43
  535.7 19.6 %collective-permute-start.47 = (f32[8,1408]{1,0:T(8,128)S(1)}, f32[8,1408]{1,0:T(8,128)S(1)}, u32[]{:S(2)}, u32[]{:S(2)}) collective-permute-start(f32[8,1408]{1,0:T(8,128)S(1)} %pad_maximum_fusion.10), channel_id=1, source_target_pairs={{0,4},{4,0},{8,12},{12,8},{16,20},{20,16},{24,28},{28,24},{1,5},{5... | collective-permute-start | bytes 135176 | tf_op jit(solution)/shard_map/ppermute | solution.py:43
  553.8 21.9 %collective-permute-start.53 = (f32[8,3840]{1,0:T(8,128)S(1)}, f32[8,3840]{1,0:T(8,128)S(1)}, u32[]{:S(2)}, u32[]{:S(2)}) collective-permute-start(f32[8,3840]{1,0:T(8,128)S(1)} %get-tuple-element.302), channel_id=1, source_target_pairs={{0,4},{4,0},{8,12},{12,8},{16,20},{20,16},{24,28},{28,24},{1,5},{5... | collective-permute-start | bytes 368648 | tf_op jit(solution)/shard_map/ppermute | solution.py:43
  555.3 15.4 %collective-permute-start.48 = (f32[8,1408]{1,0:T(8,128)S(1)}, f32[8,1408]{1,0:T(8,128)S(1)}, u32[]{:S(2)}, u32[]{:S(2)}) collective-permute-start(f32[8,1408]{1,0:T(8,128)S(1)} %fusion.73), channel_id=1, source_target_pairs={{0,8},{4,12},{8,0},{12,4},{16,24},{20,28},{24,16},{28,20},{1,9},{5... | collective-permute-start | bytes 135176 | tf_op jit(solution)/shard_map/ppermute | solution.py:43
  573.9 11.4 %collective-permute-start.52 = (f32[8,2304]{1,0:T(8,128)S(1)}, f32[8,2304]{1,0:T(8,128)S(1)}, u32[]{:S(2)}, u32[]{:S(2)}) collective-permute-start(f32[8,2304]{1,0:T(8,128)S(1)} %add.400), channel_id=1, source_target_pairs={{0,16},{4,20},{8,24},{12,28},{16,0},{20,4},{24,8},{28,12},{1,17},{... | collective-permute-start | bytes 221192 | tf_op jit(solution)/shard_map/ppermute | solution.py:43
  575.1 54.0 %collective-permute-start.34 = (f32[768,768]{1,0:T(8,128)S(1)}, f32[768,768]{1,0:T(8,128)}, u32[]{:S(2)}, u32[]{:S(2)}) collective-permute-start(f32[768,768]{1,0:T(8,128)S(1)} %get-tuple-element.432.refs_1_), channel_id=1, source_target_pairs={{0,1},{1,0},{2,3},{3,2},{4,5},{5,4},{6,7},{7,6},{8,9},{9,8},{10,11... | collective-permute-start | bytes 7077896 | tf_op jit(solution)/shard_map/ppermute | solution.py:43
  575.1 54.0 %collective-permute-start.40 = (f32[768,768]{1,0:T(8,128)}, f32[768,768]{1,0:T(8,128)}, u32[]{:S(2)}, u32[]{:S(2)}) collective-permute-start(f32[768,768]{1,0:T(8,128)} %get-tuple-element.274), channel_id=1, source_target_pairs={{0,2},{1,3},{2,0},{3,1},{4,6},{5,7},{6,4},{7,5},{8,10},{9,11},{10,... | collective-permute-start | bytes 7077896 | tf_op jit(solution)/shard_map/ppermute | solution.py:43
  575.7 9.5 %collective-permute-start.57 = (f32[8,3200]{1,0:T(8,128)S(1)}, f32[8,3200]{1,0:T(8,128)S(1)}, u32[]{:S(2)}, u32[]{:S(2)}) collective-permute-start(f32[8,3200]{1,0:T(8,128)S(1)} %add.405), channel_id=1, source_target_pairs={{0,8},{4,12},{8,0},{12,4},{16,24},{20,28},{24,16},{28,20},{1,9},{5... | collective-permute-start | bytes 307208 | tf_op jit(solution)/shard_map/ppermute | solution.py:43
  576.1 7.9 %collective-permute-start.54 = (f32[8,3840]{1,0:T(8,128)S(1)}, f32[8,3840]{1,0:T(8,128)S(1)}, u32[]{:S(2)}, u32[]{:S(2)}) collective-permute-start(f32[8,3840]{1,0:T(8,128)S(1)} %add.402), channel_id=1, source_target_pairs={{0,8},{4,12},{8,0},{12,4},{16,24},{20,28},{24,16},{28,20},{1,9},{5... | collective-permute-start | bytes 368648 | tf_op jit(solution)/shard_map/ppermute | solution.py:43
  584.0 10.5 %collective-permute-start.55 = (f32[8,3840]{1,0:T(8,128)S(1)}, f32[8,3840]{1,0:T(8,128)S(1)}, u32[]{:S(2)}, u32[]{:S(2)}) collective-permute-start(f32[8,3840]{1,0:T(8,128)S(1)} %add.403), channel_id=1, source_target_pairs={{0,16},{4,20},{8,24},{12,28},{16,0},{20,4},{24,8},{28,12},{1,17},{... | collective-permute-start | bytes 368648 | tf_op jit(solution)/shard_map/ppermute | solution.py:43
  585.3 11.4 %collective-permute-start.58 = (f32[8,3200]{1,0:T(8,128)S(1)}, f32[8,3200]{1,0:T(8,128)S(1)}, u32[]{:S(2)}, u32[]{:S(2)}) collective-permute-start(f32[8,3200]{1,0:T(8,128)S(1)} %add.406), channel_id=1, source_target_pairs={{0,16},{4,20},{8,24},{12,28},{16,0},{20,4},{24,8},{28,12},{1,17},{... | collective-permute-start | bytes 307208 | tf_op jit(solution)/shard_map/ppermute | solution.py:43
  620.2 21.0 %collective-permute-start.63 = (f32[36,768]{1,0:T(8,128)}, f32[36,768]{1,0:T(8,128)}, u32[]{:S(2)}, u32[]{:S(2)}) collective-permute-start(f32[36,768]{1,0:T(8,128)} %add.414), channel_id=1, source_target_pairs={{0,8},{4,12},{8,0},{12,4},{16,24},{20,28},{24,16},{28,20},{1,9},{5... | collective-permute-start | bytes 331784 | tf_op jit(solution)/shard_map/ppermute | solution.py:43
  634.2 9.5 %collective-permute-start.59 = (f32[8,768]{1,0:T(8,128)S(1)}, f32[8,768]{1,0:T(8,128)S(1)}, u32[]{:S(2)}, u32[]{:S(2)}) collective-permute-start(f32[8,768]{1,0:T(8,128)S(1)} %bitcast.256), channel_id=1, source_target_pairs={{0,4},{4,0},{8,12},{12,8},{16,20},{20,16},{24,28},{28,24},{1,5},{5... | collective-permute-start | bytes 73736 | tf_op jit(solution)/shard_map/ppermute | solution.py:43
  642.2 30.9 %collective-permute-start.64 = (f32[36,768]{1,0:T(8,128)S(1)}, f32[36,768]{1,0:T(8,128)S(1)}, u32[]{:S(2)}, u32[]{:S(2)}) collective-permute-start(f32[36,768]{1,0:T(8,128)S(1)} %add.415), channel_id=1, source_target_pairs={{0,16},{4,20},{8,24},{12,28},{16,0},{20,4},{24,8},{28,12},{1,17},{... | collective-permute-start | bytes 331784 | tf_op jit(solution)/shard_map/ppermute | solution.py:43
  643.7 12.1 %collective-permute-start.60 = (f32[8,768]{1,0:T(8,128)S(1)}, f32[8,768]{1,0:T(8,128)S(1)}, u32[]{:S(2)}, u32[]{:S(2)}) collective-permute-start(f32[8,768]{1,0:T(8,128)S(1)} %bitcast_add_fusion), channel_id=1, source_target_pairs={{0,8},{4,12},{8,0},{12,4},{16,24},{20,28},{24,16},{28,20},{1,9},{5... | collective-permute-start | bytes 73736 | tf_op jit(solution)/shard_map/ppermute | solution.py:43
  655.8 19.2 %collective-permute-start.61 = (f32[8,768]{1,0:T(8,128)S(1)}, f32[8,768]{1,0:T(8,128)S(1)}, u32[]{:S(2)}, u32[]{:S(2)}) collective-permute-start(f32[8,768]{1,0:T(8,128)S(1)} %add.411), channel_id=1, source_target_pairs={{0,16},{4,20},{8,24},{12,28},{16,0},{20,4},{24,8},{28,12},{1,17},{... | collective-permute-start | bytes 73736 | tf_op jit(solution)/shard_map/ppermute | solution.py:43
  (228 other events, 1565.5 us)
Sparse Core Ops, SparseCore 0:
  14.0 101.8 all-gather.2
  118.6 165.8 all-gather.4

commit v4 on v3

--- a/solution.py
+++ b/solution.py
@@ -625,7 +625,7 @@
             jax.ShapeDtypeStruct((picks, 128), WIDE),
         ],
         scratch_shapes=[pltpu.VMEM((picks, 128), WIDE)] * 3,
-        compiler_params=params(14),
+        compiler_params=params(56),
         cost_estimate=pl.CostEstimate(
             flops=2 * picks * width * columns,
             bytes_accessed=2 * width * columns,
@@ -690,7 +690,7 @@
             jax.ShapeDtypeStruct(logits.shape, NARROW),
             jax.ShapeDtypeStruct((picks, width), WIDE),
         ],
-        compiler_params=params(14),
+        compiler_params=params(56),
         cost_estimate=pl.CostEstimate(
             flops=2 * picks * width * columns,
             bytes_accessed=2 * width * columns,
@@ -885,7 +885,7 @@
             pltpu.VMEM((length, PAIR), WIDE),
             pltpu.VMEM((PAIR, rows), WIDE),
         ],
-        compiler_params=params(24),
+        compiler_params=params(56),
         cost_estimate=pl.CostEstimate(
             flops=10 * rows * length * width,
             bytes_accessed=8 * length * width + 8 * rows * width,
@@ -1013,13 +1013,22 @@
 
 def small_matrices(grads, errors, factor_t):
     count, (width, columns) = len(grads), grads[0].shape
+    block = columns // 3
+    tall = pl.BlockSpec((width, block), lambda j: (0, j))
     return pl.pallas_call(
         functools.partial(small_kernel, count),
+        grid=(3,),
+        in_specs=[tall] * (2 * count)
+        + [pl.BlockSpec((count, RANK, width), lambda j: (0, 0, 0))],
+        out_specs=[
+            pl.BlockSpec((count, width, block), lambda j: (0, 0, j)),
+            pl.BlockSpec((count, RANK, block), lambda j: (0, 0, j)),
+        ],
         out_shape=[
             jax.ShapeDtypeStruct((count, width, columns), WIDE),
             jax.ShapeDtypeStruct((count, RANK, columns), WIDE),
         ],
-        compiler_params=params(36),
+        compiler_params=params(56),
         cost_estimate=pl.CostEstimate(
             flops=48 * count * width * columns,
             bytes_accessed=12 * count * width * columns,
@@ -1122,15 +1131,21 @@
 
 
 def small_error_kernel(m_ref, back_ref, basis_ref, *out_refs):
-    for index, out_ref in enumerate(out_refs):
-        out_ref[...] = m_ref[index] - expand(back_ref[index], basis_ref[index])
+    count = m_ref.shape[0]
+    for index in range(count):
+        error = m_ref[index] - expand(back_ref[index], basis_ref[index])
+        if count > 1 and index < 2:
+            out_refs[0][:, index, :] = error
+        else:
+            out_refs[-1][...] = error
 
 
 def small_errors(matrices, backs, basis):
     count, width, columns = matrices.shape
     return pl.pallas_call(
         small_error_kernel,
-        out_shape=[jax.ShapeDtypeStruct((width, columns), WIDE)] * count,
+        out_shape=[jax.ShapeDtypeStruct((width, 2, columns), WIDE)] * (count - 1 > 0)
+        + [jax.ShapeDtypeStruct((width, columns), WIDE)],
         compiler_params=params(32),
         cost_estimate=pl.CostEstimate(
             flops=48 * count * width * columns,
@@ -1242,7 +1257,20 @@
     looked_sums[0] = near_sum(looked[0], looked[1])
     mine, _, got = far_sum(looked_sums)
     pieces = (mine + got).T.reshape(data_count, row_count, own_rows)
-    none, pieces = lax.optimization_barrier((jnp.minimum(data_rank, 0), pieces))
+    soon = (jnp.minimum(data_rank, 0), token_ids, near)
+    (none, near_ids, near_soon), pieces = lax.optimization_barrier((soon, pieces))
+    near_tokens = picked_blocks(near_ids.reshape(tensor_count, own_rows), near_soon).reshape(1, -1)
+    shifted = near_tokens - vocab_start
+    tiles = -(-vocab_own // TILE)
+    index = jnp.arange(total_rows)
+    before = (shifted < shifted.T) | ((shifted == shifted.T) & (index[None, :] < index[:, None]))
+    ranks = jnp.sum(before.astype(jnp.int32), axis=1)
+    ordered = ranks[None, :] == index[:, None]
+    sorted_ids = jnp.sum(jnp.where(ordered, shifted, 0), axis=1)[None, :]
+    starts = jnp.sum(
+        (shifted < jnp.minimum(jnp.arange(tiles + 1) * TILE, vocab_own)[:, None]).astype(jnp.int32),
+        axis=1,
+    )
     gate_error = lax.dynamic_slice_in_dim(gate_up_error[0], none, 1, 1)[:, 0]
     up_error = lax.dynamic_slice_in_dim(gate_up_error[0], none + 1, 1, 1)[:, 0]
     embedded = lax.all_to_all(pieces, "dp", 0, 0).reshape(width, own_rows).T
@@ -1261,12 +1289,13 @@
 
     x_zero, x_zero_b = norm_forward(gains[:1], embedded)
     side = (seq_lengths, mask_slots, mask_targets, positive_rows, doc_ids, false_pairs)
-    side = side + (queue_docs, factors, data_rank, token_ids, near)
-    errors = (gate_error, up_error)
+    side = side + (queue_docs, factors, data_rank, near)
+    errors = (gate_error, up_error, ranks, sorted_ids, starts)
     x_zero_b, joined_b, side, errors = lax.optimization_barrier((x_zero_b, joined_b, side, errors))
-    gate_error, up_error = errors
+    gate_error, up_error, ranks, sorted_ids, starts = errors
+    ordered = ranks[None, :] == index[:, None]
     seq_lengths, mask_slots, mask_targets, positive_rows, doc_ids, false_pairs = side[:6]
-    queue_docs, factors, data_rank, near_ids, near = side[6:]
+    queue_docs, factors, data_rank, near = side[6:]
     x_blocks = spread_blocks(x_zero_b, "tensor")
     quarter_b, queue_near = joined_b[:, :attend_cols], joined_b[:, 4 * attend_cols :]
     attend_near = picked_blocks(spread_blocks(quarter_b, "tensor"), near)
@@ -1285,18 +1314,6 @@
     valid_rows = picked_blocks(group_valid, near).reshape(-1, 1).astype(WIDE)
     row_weight = valid_rows / count
     targets = picked_blocks(mask_targets[0], near).reshape(-1, 1) - vocab_start
-    near_tokens = picked_blocks(near_ids.reshape(tensor_count, own_rows), near).reshape(1, -1)
-    shifted = near_tokens - vocab_start
-    tiles = -(-vocab_own // TILE)
-    index = jnp.arange(total_rows)
-    before = (shifted < shifted.T) | ((shifted == shifted.T) & (index[None, :] < index[:, None]))
-    ranks = jnp.sum(before.astype(jnp.int32), axis=1)
-    ordered = ranks[None, :] == index[:, None]
-    sorted_ids = jnp.sum(jnp.where(ordered, shifted, 0), axis=1)[None, :]
-    starts = jnp.sum(
-        (shifted < jnp.minimum(jnp.arange(tiles + 1) * TILE, vocab_own)[:, None]).astype(jnp.int32),
-        axis=1,
-    )
     places = near[:, None] * own_rows + jnp.arange(own_rows)[None, :]
     keep_own = (places[0] < my_length)[:, None]
     cosine, sine = rotary_tables(places.reshape(-1))
@@ -1383,6 +1400,9 @@
     down_grad = sum(contract_rows(part[0], part[1]) for part in late)
     gate_w_grad = sum(contract_rows(part[2], part[3]) for part in late)
     up_w_grad = sum(contract_rows(part[2], part[4]) for part in late)
+    ffn_grads = (down_grad, gate_w_grad, up_w_grad)
+    ffn_grads, hidden_mine = lax.optimization_barrier((ffn_grads, hidden_mine))
+    down_grad, gate_w_grad, up_w_grad = ffn_grads
     pre_one_grad, branch_grad, attended_grad, gain_one = branch_back(
         pre_grad, hidden_mine, hidden_got, pre_one, gains[1:2], weight_out
     )
@@ -1399,11 +1419,6 @@
     late = (dq, dk, dv, branch_grad)
     late, _, x_mine = lax.optimization_barrier((late, x_sent, x_mine))
     dq_late, dk, dv, branch_grad = late
-    embedded_grad, gain_zero = first_back(
-        pre_one_grad, dq, attend_b[:, :width], x_mine, x_got, embedded, gains[:1]
-    )
-    emb_all = jnp.concatenate(spread_blocks(embedded_grad, "tensor"), axis=0)
-    emb_all = jnp.dot(ordered.astype(NARROW), emb_all)
     attend_part = jnp.concatenate(
         [
             contract_rows(x_zero_b, dq_late),
@@ -1413,6 +1428,29 @@
         ],
         axis=1,
     )
+    attend_part, x_mine = lax.optimization_barrier((attend_part, x_mine))
+    embedded_grad, gain_zero = first_back(
+        pre_one_grad, dq, attend_b[:, :width], x_mine, x_got, embedded, gains[:1]
+    )
+    other_m, other_p = small_matrices(
+        [gate_w_grad, up_w_grad, down_grad],
+        [gate_error, up_error, down_error[0]],
+        factor_t[1:4],
+    )
+    near_bit, *far_bits = axis_bits("tensor")
+    held = {0: embedded_grad}
+    for bit in reversed(far_bits):
+        for key in sorted(held):
+            held[key ^ bit] = swap(held[key], "tensor", bit)
+    emb_blocks = dict(held)
+    emb_blocks[1] = swap(held[0], "tensor", near_bit)
+    rest = {key: held[key] for key in held if key}
+    rest, other_p = lax.optimization_barrier((rest, other_p))
+    for key in rest:
+        emb_blocks[key] = rest[key]
+        emb_blocks[key + 1] = swap(rest[key], "tensor", near_bit)
+    emb_all = jnp.concatenate([emb_blocks[key] for key in range(tensor_count)], axis=0)
+    emb_all = jnp.dot(ordered.astype(NARROW), emb_all)
     attend_blocks = [
         lax.dynamic_slice_in_dim(attend_part, near[k] * attend_cols, attend_cols, 1)
         for k in range(tensor_count)
@@ -1428,21 +1466,23 @@
         for key in sorted((k for k in attend_held if not k & bit), reverse=True):
             attend_held[key] = attend_held[key] + swap(attend_held.pop(key ^ bit), "tensor", bit)
     emb_all, attend_held[bits[-1]] = lax.optimization_barrier((emb_all, attend_held[bits[-1]]))
-    attend_got = swap(attend_held[bits[-1]], "tensor", bits[-1])
-
-    other_m, other_p = small_matrices(
-        [gate_w_grad, up_w_grad, down_grad],
-        [gate_error, up_error, down_error[0]],
-        factor_t[1:4],
-    )
+    attend_got = [
+        swap(piece, "tensor", bits[-1]) for piece in row_blocks(attend_held[bits[-1]], 2)
+    ]
+
     other_sum = summed_all(jnp.concatenate([other_p[k] for k in range(3)], axis=1), "dp")
-    cuts = sorted({0, (tiles + 1) // 2, tiles - 1, tiles})
+    cuts = sorted({0, tiles * 5 // 12, tiles * 9 // 12, tiles})
     table_parts, table_sums = [], []
     for bounds in zip(cuts, cuts[1:]):
+        if table_parts:
+            emb_all, table_parts[-1][2] = lax.optimization_barrier((emb_all, table_parts[-1][2]))
+        if bounds[1] == tiles:
+            emb_all, attend_got[0] = lax.optimization_barrier((emb_all, attend_got[0]))
         found = table_matrix(
             bounds, starts, emb_all, sorted_ids, rows_all, dlogits, embed_error[0].T, factor_t[4]
         )
-        table_parts.append(found)
+        table_parts.append(list(found))
+    for bounds, found in zip(zip(cuts, cuts[1:]), table_parts):
         piece = found[2]
         if bounds[1] == tiles:
             piece = jnp.concatenate([piece, attend_p], axis=1)
@@ -1451,7 +1491,8 @@
     parts = [table_sums[-1][:, -attend_cols:], other_sum] + table_sums[:-1]
     parts.append(table_sums[-1][:, :-attend_cols])
     sums = jnp.concatenate(parts, axis=1)
-    attend_got, _ = lax.optimization_barrier((attend_got, sums))
+    attend_got[1], _ = lax.optimization_barrier((attend_got[1], sums))
+    attend_got = jnp.concatenate(attend_got, axis=0)
     first_m = (attend_held[0] + attend_got + attend_error[0])[None]
     spans, start = [], 0
     for size in (attend_cols, ff_own, ff_own, ff_own, tiles * TILE):
@@ -1530,8 +1571,8 @@
         new_gains,
         new_gains_moment,
         errors[0][None],
-        jnp.stack([errors[1], errors[2]], axis=1)[None],
-        errors[3][None],
+        errors[1][None],
+        errors[2][None],
         new_table_error[None],
         jnp.swapaxes(own_t, 1, 2),
         clip_norm,

time: 717 us -> 676 us (0.943)
  local copies, waits for them, and re-layouts: 148 us -> 108 us
  waiting for transfers between devices: 157 us -> 122 us
  Pallas kernels: 216 us -> 237 us
  between operations: 31.5 us -> 38.9 us
    unnamed x421 -> x324, local copies, waits for them, and re-layouts: 119 us -> 71.2 us
    ppermute x68 -> x69, waiting for transfers between devices: 117 us -> 99.7 us  [swap(): lax.ppermute(value, axis, [(index, index ^ bit) for index in range(size)])]
    all_to_all x1, waiting for transfers between devices: 24.1 us -> 11.6 us  [per_device(): embedded = lax.all_to_all(pieces, 'dp', 0, 0).reshape(width, own_rows).T]
    ppermute x68 -> x69, starting transfers between devices: 45 us -> 46.9 us  [swap(): lax.ppermute(value, axis, [(index, index ^ bit) for index in range(size)])]
  transfers between devices with their start and end apart: 72 -> 73, of which waited for: 25 -> 31; matrix products, arithmetic and copies ran while one was open for 17% -> 18% of each run, Pallas kernels for 30% -> 25%
where the time goes in v4:
time: 676 us; the launch traced here: 668 us
  Pallas kernels  237 us (35%)
  waiting for transfers between devices  122 us (18%)
  local copies, waits for them, and re-layouts  108 us (16%)
  other arithmetic  59.9 us (9%)
  starting transfers between devices  58.3 us (9%)
  matrix products  44.8 us (7%)
  between operations  38.9 us (6%)
    ppermute x69, waiting for transfers between devices, swap(): lax.ppermute(value, axis, [(index, index ^ bit) for index in range(size)])  99.7 us
    unnamed x324, local copies, waits for them, and re-layouts  71.2 us
    pallas_call x1, Pallas kernels, attention_backward(): pl.pallas_call(functools.partial(attend_back_kernel, count), grid=(pairs,...  47.7 us
    ppermute x69, starting transfers between devices, swap(): lax.ppermute(value, axis, [(index, index ^ bit) for index in range(size)])  46.9 us
    dot_general x19, matrix products, dot_in(): lax.dot_general(left, right, (axes, ((), ())), precision=precision, prefe...  33.3 us
    pallas_call x3, Pallas kernels, table_matrix(): pl.pallas_call(functools.partial(table_kernel, columns, first), grid=(til...  26.7 us
    pallas_call x4, Pallas kernels, lookup(): pl.pallas_call(functools.partial(lookup_kernel, row_count), in_specs=[pl....  24.7 us
    pallas_call x1, Pallas kernels, attention_forward(): pl.pallas_call(functools.partial(attend_kernel, count), grid=(pairs, 2),...  23.2 us
  transfers between devices with their start and end apart: 73, of which 31 were waited for; matrix products, arithmetic and copies ran while one was open for 18% of the time, Pallas kernels for 25%

profile of v4, /device:TPU:0, one launch (start us, length us, event | category | flops | bytes accessed | tf_op | source)
XLA Modules:
  0.0 668.3 jit_solution(14028537166415409636)
XLA Ops:
  14.5 7.3 %all-to-all-start = ((s32[8,1,2048]{2,1,0:T(1,128)}), s32[8,1,2048]{2,1,0:T(1,128)S(1)}, u32[]{:S(2)}, u32[]{:S(2)}) async-start(s32[8,1,2048]{2,1,0:T(1,128)} %broadcast_in_dim.112), calls=%async_computation | async-start | bytes 131072 | tf_op jit(solution)/shard_map/all_to_all | solution.py:1237
  25.6 3.2 all-to-all-done
  31.2 6.2 shard_map.379
  39.7 6.2 shard_map.380
  45.8 6.2 shard_map.381
  56.5 6.2 shard_map.382
  62.6 9.6 %collective-permute-done.2 = bf16[512,768]{1,0:T(8,128)(2,1)S(1)} collective-permute-done((bf16[512,768]{1,0:T(8,128)(2,1)S(1)}, bf16[512,768]{1,0:T(8,128)(2,1)S(1)}, u32[]{:S(2)}, u32[]{:S(2)}) %collective-permute-start.2) | collective-permute-done | bytes 786464 | tf_op jit(solution)/shard_map/ppermute | solution.py:43
  79.5 4.1 all-to-all-start.1
  87.4 8.6 %constant_dynamic-slice_fusion.34 = (f32[1,768,1,768]{3,2,1,0:T(1,128)S(1)}, f32[1,768,1,768]{3,2,1,0:T(1,128)S(1)}) fusion(f32[1,768,2,768]{3,2,1,0:T(2,128)} %param.48, s32[]{:T(128)S(6)} %select_n.157, s32[]{:T(128)S(6)} %select_n.156), kind=kLoop, calls=%fused_computation.184 | loop fusion | bytes 9437192 | tf_op jit(solution)/shard_map/dynamic_slice | solution.py:1275
  98.8 5.4 convert_reduce_fusion
  105.9 11.6 %all-to-all-done.1 = bf16[8,96,512]{2,1,0:T(8,128)(2,1)S(1)} async-done(((bf16[8,96,512]{2,1,0:T(8,128)(2,1)}), bf16[8,96,512]{2,1,0:T(8,128)(2,1)S(1)}, u32[]{:S(2)}, u32[]{:S(2)}) %all-to-all-start.1) | async-done | bytes 786464 | tf_op jit(solution)/shard_map/all_to_all | solution.py:1276
  133.7 17.5 %collective-permute-done.4 = bf16[768,768]{1,0:T(8,128)(2,1)} collective-permute-done((bf16[768,768]{1,0:T(8,128)(2,1)}, bf16[768,768]{1,0:T(8,128)(2,1)}, u32[]{:S(2)}, u32[]{:S(2)}) %collective-permute-start.4) | collective-permute-done | bytes 1179680 | tf_op jit(solution)/shard_map/ppermute | solution.py:43
  151.1 3.7 multiply_sine_fusion
  155.8 10.8 %collective-permute-done.7.x_ref = bf16[512,768]{1,0:T(8,128)(2,1)} collective-permute-done((bf16[512,768]{1,0:T(8,128)(2,1)S(1)}, bf16[512,768]{1,0:T(8,128)(2,1)}, u32[]{:S(2)}, u32[]{:S(2)}) %collective-permute-start.7) | collective-permute-done | bytes 786464 | tf_op jit(solution)/shard_map/ppermute | solution.py:43
  169.9 3.1 shard_map.386
  178.9 23.2 %shard_map.388 = (f32[768,512]{1,0:T(8,128)S(1)}, f32[6,2,512]{2,1,0:T(2,128)S(1)}) custom-call(bf16[512,768]{1,0:T(8,128)(2,1)S(1)} %get-tuple-element.213.q_ref, bf16[512,768]{1,0:T(8,128)(2,1)S(1)} %get-tuple-element.217.refs_0_, bf16[512,768]{1,0:T(8,128)(2,1)S(1)} %get-tuple-element.218.refs_1_, bf16[512,768]{1,0:T(8,128)(2,1)S(1)} %get-tuple-element.219.refs_2_, ...), custom_call_target="tpu_custom_call" | custom-call | flops 3221225472 | bytes 9437184 | tf_op jit(solution)/shard_map/pallas_call | solution.py:789
  215.1 7.0 %shard_map.390 = (f32[1024,768]{1,0:T(8,128)S(1)}, f32[1024,768]{1,0:T(8,128)S(1)}, bf16[1024,768]{1,0:T(8,128)(2,1)S(1)}, bf16[1024,768]{1,0:T(8,128)(2,1)S(1)}...) custom-call(bf16[512,768]{1,0:T(8,128)(2,1)} %get-tuple-element.228.first_ref, ...), custom_call_target="tpu_custom_call" | custom-call | flops 3623878656 | bytes 14548992 | tf_op jit(solution)/shard_map/pallas_call | solution.py:435
  231.0 4.6 shard_map.391
  251.6 10.8 %collective-permute-done.14.refs_2_.got_ref = bf16[512,768]{1,0:T(8,128)(2,1)S(1)} collective-permute-done((bf16[512,768]{1,0:T(8,128)(2,1)}, bf16[512,768]{1,0:T(8,128)(2,1)S(1)}, u32[]{:S(2)}, u32[]{:S(2)}) %collective-permute-start.14) | collective-permute-done | bytes 786464 | tf_op jit(solution)/shard_map/ppermute | solution.py:43
  276.9 7.4 %all-gather.5.cloned.1.call-done.table_ref = bf16[768,7632]{1,0:T(8,128)(2,1)} async-done(((bf16[96,7632]{1,0:T(8,128)(2,1)}), bf16[768,7632]{1,0:T(8,128)(2,1)}) %all-gather.5.cloned.1.call-update) | async-done | bytes 11722768 | tf_op jit(solution)/shard_map/all_gather | solution.py:1288
  284.3 9.7 %shard_map.393 = (f32[160,7680]{1,0:T(8,128)}, f32[160,128]{1,0:T(8,128)}) custom-call(bf16[160,768]{1,0:T(8,128)(2,1)} %pad_maximum_fusion.5.rows_ref, bf16[768,7632]{1,0:T(8,128)(2,1)} %all-gather.5.cloned.1.call-done.table_ref, s32[160,1]{1,0:T(8,128)} %sub.77.targets_ref), custom_call_target="tpu_custom_call" | custom-call | flops 1875640320 | bytes 11722752 | tf_op jit(solution)/shard_map/pallas_call | solution.py:614
  301.9 11.3 %shard_map.396 = (bf16[160,7680]{1,0:T(8,128)(2,1)}, f32[160,768]{1,0:T(8,128)}) custom-call(f32[160,7680]{1,0:T(8,128)} %get-tuple-element.237.logits_ref, bf16[768,7632]{1,0:T(8,128)(2,1)} %all-gather.5.cloned.1.call-done.table_ref, s32[160,1]{1,0:T(8,128)} %sub.77.targets_ref, f32[160,128]{1,0:T(8,128)} %slice.388.stats_ref, f32[160,1]{1,0:T(8,128)} %div.23.weight_ref), custom_call_target="tpu_custom_call" | custom-call | flops 1875640320 | bytes 11722752 | tf_op jit(solution)/shard_map/pallas_call | solution.py:678
  329.5 7.5 %shard_map.399 = (bf16[1024,768]{1,0:T(8,128)(2,1)S(1)}, bf16[1024,768]{1,0:T(8,128)(2,1)S(1)}, bf16[1024,768]{1,0:T(8,128)(2,1)S(1)}, bf16[512,768]{1,0:T(8,128)(2,1)S(1)}, bf16[512,768]{1,0:T(8,128)(2,1)}) custom-call(bf16[512,768]{1,0:T(8,128)(2,1)} %get-tuple-element.248.first_ref, bf16[512,768]{1,0:T(8,128)(2,1)S(1)} %copy-done.87, ...), custom_call_target="tpu_custom_call" | custom-call | flops 3623878656 | bytes 16121856 | tf_op jit(solution)/shard_map/pallas_call | solution.py:488
  341.3 3.8 collective-permute-done.27.first_ref
  348.5 6.0 shard_map.400
  361.9 2.9 convolution_add_fusion.1.refs_0_
  364.8 2.9 convolution_add_fusion.refs_1_
  372.6 4.1 collective-permute-done.31.got_ref
  381.4 47.7 %shard_map.402 = (bf16[512,768]{1,0:T(8,128)(2,1)}, bf16[512,768]{1,0:T(8,128)(2,1)}, bf16[512,768]{1,0:T(8,128)(2,1)}, bf16[512,768]{1,0:T(8,128)(2,1)}, bf16[5...) custom-call(bf16[512,768]{1,0:T(8,128)(2,1)} %copy-done.122, ...), custom_call_target="tpu_custom_call" | custom-call | flops 8053063680 | bytes 15728640 | tf_op jit(solution)/shard_map/pallas_call | solution.py:870
  457.0 4.6 pad_maximum_fusion
  466.3 3.3 constant_dynamic-slice_fusion.8.refs_3_
  470.2 9.6 %shard_map.406 = (f32[3,768,768]{2,1,0:T(8,128)}, f32[3,8,768]{2,1,0:T(8,128)}) custom-call(f32[768,768]{1,0:T(8,128)} %convolution_add_fusion.1.refs_0_, f32[768,768]{1,0:T(8,128)} %convolution_add_fusion.refs_1_, f32[768,768]{1,0:T(8,128)} %convolution_add_fusion.2.refs_2_, f32[768,768]{1,0:T(8,128)} %get-tuple-element.319.refs_3_, ...), custom_call_target="tpu_custom_call" | custom-call | flops 84934656 | bytes 21233664 | tf_op jit(solution)/shard_map/pallas_call | solution.py:1018
  480.4 3.7 collective-permute-done.37
  490.7 9.4 %fusion.2.left_ref = bf16[2048,768]{1,0:T(8,128)(2,1)S(1)} fusion(s32[2048]{0:T(1024)S(1)} %convert_reduce_fusion, bf16[512,768]{1,0:T(8,128)(2,1)} %collective-permute-done.38, bf16[512,768]{1,0:T(8,128)(2,1)} %collective-permute-done.37, bf16[512,768]{1,0:T(8,128)(2,1)} %collective-permute-done.36, bf16[512,768]{1,0:T(8,128)(2,1)} %get-tuple-element.315), kind=kOutput, calls=%fused_computation.8 | convolution fusion | flops 6459228160 | bytes 6299648 | tf_op jit(solution)/shard_map/dot_general | solution.py:1453
  500.1 6.0 fusion.79
  508.0 4.0 shard_map.410
  512.7 10.1 %shard_map.407 = (bf16[3200,768]{1,0:T(8,128)(2,1)S(1)}, bf16[3200,768]{1,0:T(8,128)(2,1)S(1)}, f32[8,3200]{1,0:T(8,128)S(1)}) custom-call(s32[13]{0:T(128)S(1)} %convert_reduce_fusion.1.starts_ref, bf16[2048,768]{1,0:T(8,128)(2,1)S(1)} %fusion.2.left_ref, s32[1,2048]{1,0:T(1,128)S(1)} %bitcast.249, bf16[160,768]{1,0:T(8,128)(2,1)S(1)} %copy-done.42, ...), custom_call_target="tpu_custom_call" | custom-call | flops 3420979200 | bytes 19660800 | tf_op jit(solution)/shard_map/pallas_call | solution.py:956
  525.2 9.5 %shard_map.408 = (bf16[2560,768]{1,0:T(8,128)(2,1)S(1)}, bf16[2560,768]{1,0:T(8,128)(2,1)S(1)}, f32[8,2560]{1,0:T(8,128)S(1)}) custom-call(s32[13]{0:T(128)S(1)} %convert_reduce_fusion.1.starts_ref, bf16[2048,768]{1,0:T(8,128)(2,1)S(1)} %fusion.2.left_ref, s32[1,2048]{1,0:T(1,128)S(1)} %bitcast.250, bf16[160,768]{1,0:T(8,128)(2,1)S(1)} %copy-done.42, ...), custom_call_target="tpu_custom_call" | custom-call | flops 2736783360 | bytes 15728640 | tf_op jit(solution)/shard_map/pallas_call | solution.py:956
  538.6 7.1 %shard_map.409 = (bf16[1920,768]{1,0:T(8,128)(2,1)S(1)}, bf16[1920,768]{1,0:T(8,128)(2,1)S(1)}, f32[8,1920]{1,0:T(8,128)S(1)}) custom-call(s32[13]{0:T(128)S(1)} %convert_reduce_fusion.1.starts_ref, bf16[2048,768]{1,0:T(8,128)(2,1)S(1)} %fusion.2.left_ref, s32[1,2048]{1,0:T(1,128)S(1)} %bitcast.251, bf16[160,768]{1,0:T(8,128)(2,1)S(1)} %copy-done.42, ...), custom_call_target="tpu_custom_call" | custom-call | flops 2052587520 | bytes 11796480 | tf_op jit(solution)/shard_map/pallas_call | solution.py:956
  565.1 4.3 collective-permute-done.50
  572.1 3.5 collective-permute-done.56
  583.4 4.6 shard_map.415.refs_6_
  593.1 4.4 fusion.13.m_ref
  604.1 3.0 copy-done.8
  607.1 4.6 shard_map.417
  620.7 11.2 %shard_map.418 = f32[7632,768]{1,0:T(8,128)} custom-call(bf16[3200,768]{1,0:T(8,128)(2,1)S(1)} %copy-done.14, bf16[2560,768]{1,0:T(8,128)(2,1)S(1)} %copy-done.20, bf16[1920,768]{1,0:T(8,128)(2,1)S(1)} %copy-done.27, bf16[3200,768]{1,0:T(8,128)(2,1)S(1)} %copy-done.17, bf16[2560,768]{1,0:T(8,128)(2,1)S(1)} %copy-done.23, bf16[1920,768]{1,0:T(8,128)(2,1)S(1)} %copy-done.29, ...), custom_call_target="tpu_custom_call" | custom-call | flops 281346048 | bytes 46891008 | tf_op jit(solution)/shard_map/pallas_call | solution.py:1173
  637.2 3.3 collective-permute-done.67
  653.7 6.4 multiply_subtract_fusion
  (644 shorter events, 258.7 us)
Async XLA Ops:
  7.2 112.2 %all-gather.3.cloned.1.call-start = ((), (), s32[]{:S(2)}) async-start(), calls=%async_computation.2 | async-start | bytes 5750784 | tf_op jit(solution)/shard_map/all_gather | solution.py:1286
  14.5 14.3 %all-to-all-start = ((s32[8,1,2048]{2,1,0:T(1,128)}), s32[8,1,2048]{2,1,0:T(1,128)S(1)}, u32[]{:S(2)}, u32[]{:S(2)}) async-start(s32[8,1,2048]{2,1,0:T(1,128)} %broadcast_in_dim.112), calls=%async_computation | async-start | bytes 131072 | tf_op jit(solution)/shard_map/all_to_all | solution.py:1237
  21.8 262.6 %all-gather.5.cloned.1.call-start = ((), (), s32[]{:S(2)}) async-start(), calls=%async_computation.3 | async-start | bytes 13271040 | tf_op jit(solution)/shard_map/all_gather | solution.py:1288
  37.4 14.6 %collective-permute-start = (bf16[512,768]{1,0:T(8,128)(2,1)S(1)}, bf16[512,768]{1,0:T(8,128)(2,1)S(1)}, u32[]{:S(2)}, u32[]{:S(2)}) collective-permute-start(bf16[512,768]{1,0:T(8,128)(2,1)S(1)} %shard_map.379), channel_id=1, source_target_pairs={{0,1},{1,0},{2,3},{3,2},{4,5},{5,4},{6,7},{7,6},{8,9},{9,8},{10,11... | collective-permute-start | bytes 2359304 | tf_op jit(solution)/shard_map/ppermute | solution.py:43
  52.2 20.0 %collective-permute-start.2 = (bf16[512,768]{1,0:T(8,128)(2,1)S(1)}, bf16[512,768]{1,0:T(8,128)(2,1)S(1)}, u32[]{:S(2)}, u32[]{:S(2)}) collective-permute-start(bf16[512,768]{1,0:T(8,128)(2,1)S(1)} %add_convert_fusion.7), channel_id=1, source_target_pairs={{0,2},{1,3},{2,0},{3,1},{4,6},{5,7},{6,4},{7,5},{8,10},{9,11},{10,... | collective-permute-start | bytes 2359304 | tf_op jit(solution)/shard_map/ppermute | solution.py:43
  53.8 18.4 %collective-permute-start.1 = (bf16[512,768]{1,0:T(8,128)(2,1)S(1)}, bf16[512,768]{1,0:T(8,128)(2,1)S(1)}, u32[]{:S(2)}, u32[]{:S(2)}) collective-permute-start(bf16[512,768]{1,0:T(8,128)(2,1)S(1)} %shard_map.381), channel_id=1, source_target_pairs={{0,1},{1,0},{2,3},{3,2},{4,5},{5,4},{6,7},{7,6},{8,9},{9,8},{10,11... | collective-permute-start | bytes 2359304 | tf_op jit(solution)/shard_map/ppermute | solution.py:43
  79.5 38.0 %all-to-all-start.1 = ((bf16[8,96,512]{2,1,0:T(8,128)(2,1)}), bf16[8,96,512]{2,1,0:T(8,128)(2,1)S(1)}, u32[]{:S(2)}, u32[]{:S(2)}) async-start(bf16[8,96,512]{2,1,0:T(8,128)(2,1)} %bitcast.7), calls=%async_computation.1 | async-start | bytes 1572864 | tf_op jit(solution)/shard_map/all_to_all | solution.py:1276
  121.9 29.2 %collective-permute-start.4 = (bf16[768,768]{1,0:T(8,128)(2,1)}, bf16[768,768]{1,0:T(8,128)(2,1)}, u32[]{:S(2)}, u32[]{:S(2)}) collective-permute-start(bf16[768,768]{1,0:T(8,128)(2,1)} %get-tuple-element.469), channel_id=1, source_target_pairs={{0,2},{1,3},{2,0},{3,1},{4,6},{5,7},{6,4},{7,5},{8,10},{9,11},{10,... | collective-permute-start | bytes 3538952 | tf_op jit(solution)/shard_map/ppermute | solution.py:43
  123.4 43.2 %collective-permute-start.3 = (bf16[768,768]{1,0:T(8,128)(2,1)}, bf16[768,768]{1,0:T(8,128)(2,1)}, u32[]{:S(2)}, u32[]{:S(2)}) collective-permute-start(bf16[768,768]{1,0:T(8,128)(2,1)} %get-tuple-element.469), channel_id=1, source_target_pairs={{0,1},{1,0},{2,3},{3,2},{4,5},{5,4},{6,7},{7,6},{8,9},{9,8},{10,11... | collective-permute-start | bytes 3538952 | tf_op jit(solution)/shard_map/ppermute | solution.py:43
  129.3 43.7 %collective-permute-start.6 = (bf16[512,768]{1,0:T(8,128)(2,1)S(1)}, bf16[512,768]{1,0:T(8,128)(2,1)S(1)}, u32[]{:S(2)}, u32[]{:S(2)}) collective-permute-start(bf16[512,768]{1,0:T(8,128)(2,1)S(1)} %get-tuple-element.210.x_ref), channel_id=1, source_target_pairs={{0,1},{1,0},{2,3},{3,2},{4,5},{5,4},{6,7},{7,6},{8,9},{9,8},{10,11... | collective-permute-start | bytes 2359304 | tf_op jit(solution)/shard_map/ppermute | solution.py:43
  129.9 36.7 %collective-permute-start.7 = (bf16[512,768]{1,0:T(8,128)(2,1)S(1)}, bf16[512,768]{1,0:T(8,128)(2,1)}, u32[]{:S(2)}, u32[]{:S(2)}) collective-permute-start(bf16[512,768]{1,0:T(8,128)(2,1)S(1)} %get-tuple-element.210.x_ref), channel_id=1, source_target_pairs={{0,2},{1,3},{2,0},{3,1},{4,6},{5,7},{6,4},{7,5},{8,10},{9,11},{10,... | collective-permute-start | bytes 2359304 | tf_op jit(solution)/shard_map/ppermute | solution.py:43
  151.1 15.5 %collective-permute-start.5 = (bf16[768,768]{1,0:T(8,128)(2,1)}, bf16[768,768]{1,0:T(8,128)(2,1)S(1)}, u32[]{:S(2)}, u32[]{:S(2)}) collective-permute-start(bf16[768,768]{1,0:T(8,128)(2,1)} %collective-permute-done.4), channel_id=1, source_target_pairs={{0,1},{1,0},{2,3},{3,2},{4,5},{5,4},{6,7},{7,6},{8,9},{9,8},{10,11... | collective-permute-start | bytes 3538952 | tf_op jit(solution)/shard_map/ppermute | solution.py:43
  166.6 7.9 %collective-permute-start.8 = (bf16[512,768]{1,0:T(8,128)(2,1)}, bf16[512,768]{1,0:T(8,128)(2,1)S(1)}, u32[]{:S(2)}, u32[]{:S(2)}) collective-permute-start(bf16[512,768]{1,0:T(8,128)(2,1)} %collective-permute-done.7.x_ref), channel_id=1, source_target_pairs={{0,1},{1,0},{2,3},{3,2},{4,5},{5,4},{6,7},{7,6},{8,9},{9,8},{10,11... | collective-permute-start | bytes 2359304 | tf_op jit(solution)/shard_map/ppermute | solution.py:43
  208.0 20.7 %collective-permute-start.11 = (bf16[512,768]{1,0:T(8,128)(2,1)}, bf16[512,768]{1,0:T(8,128)(2,1)S(1)}, u32[]{:S(2)}, u32[]{:S(2)}) collective-permute-start(bf16[512,768]{1,0:T(8,128)(2,1)} %get-tuple-element.228.first_ref), channel_id=1, source_target_pairs={{0,2},{1,3},{2,0},{3,1},{4,6},{5,7},{6,4},{7,5},{8,10},{9,11},{10,... | collective-permute-start | bytes 2359304 | tf_op jit(solution)/shard_map/ppermute | solution.py:43
  241.1 8.8 %collective-permute-start.10 = (bf16[512,768]{1,0:T(8,128)(2,1)}, bf16[512,768]{1,0:T(8,128)(2,1)}, u32[]{:S(2)}, u32[]{:S(2)}) collective-permute-start(bf16[512,768]{1,0:T(8,128)(2,1)} %get-tuple-element.230), channel_id=1, source_target_pairs={{0,1},{1,0},{2,3},{3,2},{4,5},{5,4},{6,7},{7,6},{8,9},{9,8},{10,11... | collective-permute-start | bytes 2359304 | tf_op jit(solution)/shard_map/ppermute | solution.py:43
  242.7 19.7 %collective-permute-start.14 = (bf16[512,768]{1,0:T(8,128)(2,1)}, bf16[512,768]{1,0:T(8,128)(2,1)S(1)}, u32[]{:S(2)}, u32[]{:S(2)}) collective-permute-start(bf16[512,768]{1,0:T(8,128)(2,1)} %add_convert_fusion.4), channel_id=1, source_target_pairs={{0,2},{1,3},{2,0},{3,1},{4,6},{5,7},{6,4},{7,5},{8,10},{9,11},{10,... | collective-permute-start | bytes 2359304 | tf_op jit(solution)/shard_map/ppermute | solution.py:43
  271.1 27.7 %collective-permute-start.24 = (bf16[256,768]{1,0:T(8,128)(2,1)}, bf16[256,768]{1,0:T(8,128)(2,1)}, u32[]{:S(2)}, u32[]{:S(2)}) collective-permute-start(bf16[256,768]{1,0:T(8,128)(2,1)} %multiply_convert_fusion), channel_id=1, source_target_pairs={{0,2},{1,3},{2,0},{3,1},{4,6},{5,7},{6,4},{7,5},{8,10},{9,11},{10,... | collective-permute-start | bytes 1179656 | tf_op jit(solution)/shard_map/ppermute | solution.py:43
  298.8 15.8 %collective-permute-start.23 = (bf16[256,768]{1,0:T(8,128)(2,1)}, bf16[256,768]{1,0:T(8,128)(2,1)S(1)}, u32[]{:S(2)}, u32[]{:S(2)}) collective-permute-start(bf16[256,768]{1,0:T(8,128)(2,1)} %multiply_convert_fusion), channel_id=1, source_target_pairs={{0,1},{1,0},{2,3},{3,2},{4,5},{5,4},{6,7},{7,6},{8,9},{9,8},{10,11... | collective-permute-start | bytes 1179656 | tf_op jit(solution)/shard_map/ppermute | solution.py:43
  298.8 15.8 %collective-permute-start.25 = (bf16[256,768]{1,0:T(8,128)(2,1)}, bf16[256,768]{1,0:T(8,128)(2,1)}, u32[]{:S(2)}, u32[]{:S(2)}) collective-permute-start(bf16[256,768]{1,0:T(8,128)(2,1)} %collective-permute-done.24), channel_id=1, source_target_pairs={{0,1},{1,0},{2,3},{3,2},{4,5},{5,4},{6,7},{7,6},{8,9},{9,8},{10,11... | collective-permute-start | bytes 1179656 | tf_op jit(solution)/shard_map/ppermute | solution.py:43
  324.9 20.2 %collective-permute-start.27 = (bf16[512,768]{1,0:T(8,128)(2,1)}, bf16[512,768]{1,0:T(8,128)(2,1)S(1)}, u32[]{:S(2)}, u32[]{:S(2)}) collective-permute-start(bf16[512,768]{1,0:T(8,128)(2,1)} %get-tuple-element.248.first_ref), channel_id=1, source_target_pairs={{0,2},{1,3},{2,0},{3,1},{4,6},{5,7},{6,4},{7,5},{8,10},{9,11},{10,... | collective-permute-start | bytes 2359304 | tf_op jit(solution)/shard_map/ppermute | solution.py:43
  345.1 9.5 %collective-permute-start.30 = (bf16[512,768]{1,0:T(8,128)(2,1)}, bf16[512,768]{1,0:T(8,128)(2,1)S(1)}, u32[]{:S(2)}, u32[]{:S(2)}) collective-permute-start(bf16[512,768]{1,0:T(8,128)(2,1)} %get-tuple-element.256), channel_id=1, source_target_pairs={{0,1},{1,0},{2,3},{3,2},{4,5},{5,4},{6,7},{7,6},{8,9},{9,8},{10,11... | collective-permute-start | bytes 2359304 | tf_op jit(solution)/shard_map/ppermute | solution.py:43
  357.0 19.6 %collective-permute-start.31 = (bf16[512,768]{1,0:T(8,128)(2,1)S(1)}, bf16[512,768]{1,0:T(8,128)(2,1)S(1)}, u32[]{:S(2)}, u32[]{:S(2)}) collective-permute-start(bf16[512,768]{1,0:T(8,128)(2,1)S(1)} %add_convert_fusion.3), channel_id=1, source_target_pairs={{0,2},{1,3},{2,0},{3,1},{4,6},{5,7},{6,4},{7,5},{8,10},{9,11},{10,... | collective-permute-start | bytes 2359304 | tf_op jit(solution)/shard_map/ppermute | solution.py:43
  441.8 19.8 %collective-permute-start.35 = (bf16[512,768]{1,0:T(8,128)(2,1)S(1)}, bf16[512,768]{1,0:T(8,128)(2,1)S(1)}, u32[]{:S(2)}, u32[]{:S(2)}) collective-permute-start(bf16[512,768]{1,0:T(8,128)(2,1)S(1)} %add_convert_fusion.1), channel_id=1, source_target_pairs={{0,2},{1,3},{2,0},{3,1},{4,6},{5,7},{6,4},{7,5},{8,10},{9,11},{10,... | collective-permute-start | bytes 2359304 | tf_op jit(solution)/shard_map/ppermute | solution.py:43
  464.1 19.9 %collective-permute-start.37 = (bf16[512,768]{1,0:T(8,128)(2,1)}, bf16[512,768]{1,0:T(8,128)(2,1)}, u32[]{:S(2)}, u32[]{:S(2)}) collective-permute-start(bf16[512,768]{1,0:T(8,128)(2,1)} %get-tuple-element.315), channel_id=1, source_target_pairs={{0,2},{1,3},{2,0},{3,1},{4,6},{5,7},{6,4},{7,5},{8,10},{9,11},{10,... | collective-permute-start | bytes 2359304 | tf_op jit(solution)/shard_map/ppermute | solution.py:43
  469.5 30.6 %collective-permute-start.39 = (f32[768,768]{1,0:T(8,128)}, f32[768,768]{1,0:T(8,128)}, u32[]{:S(2)}, u32[]{:S(2)}) collective-permute-start(f32[768,768]{1,0:T(8,128)} %constant_dynamic-slice_fusion.8.refs_3_), channel_id=1, source_target_pairs={{0,1},{1,0},{2,3},{3,2},{4,5},{5,4},{6,7},{7,6},{8,9},{9,8},{10,11... | collective-permute-start | bytes 7077896 | tf_op jit(solution)/shard_map/ppermute | solution.py:43
  479.8 10.9 %collective-permute-start.36 = (bf16[512,768]{1,0:T(8,128)(2,1)}, bf16[512,768]{1,0:T(8,128)(2,1)}, u32[]{:S(2)}, u32[]{:S(2)}) collective-permute-start(bf16[512,768]{1,0:T(8,128)(2,1)} %get-tuple-element.315), channel_id=1, source_target_pairs={{0,1},{1,0},{2,3},{3,2},{4,5},{5,4},{6,7},{7,6},{8,9},{9,8},{10,11... | collective-permute-start | bytes 2359304 | tf_op jit(solution)/shard_map/ppermute | solution.py:43
  484.0 6.6 collective-permute-start.38
  488.7 19.3 %collective-permute-start.42 = (f32[8,768]{1,0:T(8,128)S(1)}, f32[8,768]{1,0:T(8,128)S(1)}, u32[]{:S(2)}, u32[]{:S(2)}) collective-permute-start(f32[8,768]{1,0:T(8,128)S(1)} %get-tuple-element.501.refs_4_.refs_1_), channel_id=1, source_target_pairs={{0,1},{1,0},{2,3},{3,2},{4,5},{5,4},{6,7},{7,6},{8,9},{9,8},{10,11... | collective-permute-start | bytes 73736 | tf_op jit(solution)/shard_map/ppermute | solution.py:43
  489.5 18.5 %collective-permute-start.44 = (f32[8,768]{1,0:T(8,128)S(1)}, f32[8,768]{1,0:T(8,128)S(1)}, u32[]{:S(2)}, u32[]{:S(2)}) collective-permute-start(f32[8,768]{1,0:T(8,128)S(1)} %collective-permute-done.43.refs_6_), channel_id=1, source_target_pairs={{0,1},{1,0},{2,3},{3,2},{4,5},{5,4},{6,7},{7,6},{8,9},{9,8},{10,11... | collective-permute-start | bytes 73736 | tf_op jit(solution)/shard_map/ppermute | solution.py:43
  507.4 31.1 %collective-permute-start.40 = (f32[384,768]{1,0:T(8,128)S(1)}, f32[384,768]{1,0:T(8,128)S(1)}, u32[]{:S(2)}, u32[]{:S(2)}) collective-permute-start(f32[384,768]{1,0:T(8,128)S(1)} %get-tuple-element.477), channel_id=1, source_target_pairs={{0,2},{1,3},{2,0},{3,1},{4,6},{5,7},{6,4},{7,5},{8,10},{9,11},{10,... | collective-permute-start | bytes 3538952 | tf_op jit(solution)/shard_map/ppermute | solution.py:43
  512.1 10.7 %collective-permute-start.46 = (f32[8,768]{1,0:T(8,128)S(1)}, f32[8,768]{1,0:T(8,128)S(1)}, u32[]{:S(2)}, u32[]{:S(2)}) collective-permute-start(f32[8,768]{1,0:T(8,128)S(1)} %get-tuple-element.503), channel_id=1, source_target_pairs={{0,1},{1,0},{2,3},{3,2},{4,5},{5,4},{6,7},{7,6},{8,9},{9,8},{10,11... | collective-permute-start | bytes 73736 | tf_op jit(solution)/shard_map/ppermute | solution.py:43
  512.2 26.4 %collective-permute-start.45 = (f32[8,768]{1,0:T(8,128)S(1)}, f32[8,768]{1,0:T(8,128)S(1)}, u32[]{:S(2)}, u32[]{:S(2)}) collective-permute-start(f32[8,768]{1,0:T(8,128)S(1)} %get-tuple-element.502), channel_id=1, source_target_pairs={{0,1},{1,0},{2,3},{3,2},{4,5},{5,4},{6,7},{7,6},{8,9},{9,8},{10,11... | collective-permute-start | bytes 73736 | tf_op jit(solution)/shard_map/ppermute | solution.py:43
  522.8 15.8 %collective-permute-start.47 = (f32[8,768]{1,0:T(8,128)S(1)}, f32[8,768]{1,0:T(8,128)S(1)}, u32[]{:S(2)}, u32[]{:S(2)}) collective-permute-start(f32[8,768]{1,0:T(8,128)S(1)} %fusion.32), channel_id=1, source_target_pairs={{0,2},{1,3},{2,0},{3,1},{4,6},{5,7},{6,4},{7,5},{8,10},{9,11},{10,... | collective-permute-start | bytes 73736 | tf_op jit(solution)/shard_map/ppermute | solution.py:43
  546.4 6.4 collective-permute-start.51
  547.9 7.8 %collective-permute-start.54 = (f32[8,3200]{1,0:T(8,128)S(1)}, f32[8,3200]{1,0:T(8,128)S(1)}, u32[]{:S(2)}, u32[]{:S(2)}) collective-permute-start(f32[8,3200]{1,0:T(8,128)S(1)} %get-tuple-element.337), channel_id=1, source_target_pairs={{0,4},{4,0},{8,12},{12,8},{16,20},{20,16},{24,28},{28,24},{1,5},{5... | collective-permute-start | bytes 307208 | tf_op jit(solution)/shard_map/ppermute | solution.py:43
  548.5 7.2 %collective-permute-start.57 = (f32[8,2560]{1,0:T(8,128)S(1)}, f32[8,2560]{1,0:T(8,128)S(1)}, u32[]{:S(2)}, u32[]{:S(2)}) collective-permute-start(f32[8,2560]{1,0:T(8,128)S(1)} %get-tuple-element.338), channel_id=1, source_target_pairs={{0,4},{4,0},{8,12},{12,8},{16,20},{20,16},{24,28},{28,24},{1,5},{5... | collective-permute-start | bytes 245768 | tf_op jit(solution)/shard_map/ppermute | solution.py:43
  551.3 6.5 collective-permute-start.49
  552.9 8.3 %collective-permute-start.52 = (f32[8,2304]{1,0:T(8,128)S(1)}, f32[8,2304]{1,0:T(8,128)S(1)}, u32[]{:S(2)}, u32[]{:S(2)}) collective-permute-start(f32[8,2304]{1,0:T(8,128)S(1)} %fusion.77), channel_id=1, source_target_pairs={{0,8},{4,12},{8,0},{12,4},{16,24},{20,28},{24,16},{28,20},{1,9},{5... | collective-permute-start | bytes 221192 | tf_op jit(solution)/shard_map/ppermute | solution.py:43
  555.6 6.7 collective-permute-start.58
  555.7 7.4 %collective-permute-start.55 = (f32[8,3200]{1,0:T(8,128)S(1)}, f32[8,3200]{1,0:T(8,128)S(1)}, u32[]{:S(2)}, u32[]{:S(2)}) collective-permute-start(f32[8,3200]{1,0:T(8,128)S(1)} %add.414), channel_id=1, source_target_pairs={{0,8},{4,12},{8,0},{12,4},{16,24},{20,28},{24,16},{28,20},{1,9},{5... | collective-permute-start | bytes 307208 | tf_op jit(solution)/shard_map/ppermute | solution.py:43
  557.8 11.6 %collective-permute-start.50 = (f32[8,2688]{1,0:T(8,128)S(1)}, f32[8,2688]{1,0:T(8,128)S(1)}, u32[]{:S(2)}, u32[]{:S(2)}) collective-permute-start(f32[8,2688]{1,0:T(8,128)S(1)} %add.409), channel_id=1, source_target_pairs={{0,16},{4,20},{8,24},{12,28},{16,0},{20,4},{24,8},{28,12},{1,17},{... | collective-permute-start | bytes 258056 | tf_op jit(solution)/shard_map/ppermute | solution.py:43
  561.2 10.9 %collective-permute-start.53 = (f32[8,2304]{1,0:T(8,128)S(1)}, f32[8,2304]{1,0:T(8,128)S(1)}, u32[]{:S(2)}, u32[]{:S(2)}) collective-permute-start(f32[8,2304]{1,0:T(8,128)S(1)} %add.412), channel_id=1, source_target_pairs={{0,16},{4,20},{8,24},{12,28},{16,0},{20,4},{24,8},{28,12},{1,17},{... | collective-permute-start | bytes 221192 | tf_op jit(solution)/shard_map/ppermute | solution.py:43
  562.3 30.9 %collective-permute-start.34 = (f32[768,768]{1,0:T(8,128)}, f32[768,768]{1,0:T(8,128)}, u32[]{:S(2)}, u32[]{:S(2)}) collective-permute-start(f32[768,768]{1,0:T(8,128)} %get-tuple-element.466.refs_1_), channel_id=1, source_target_pairs={{0,1},{1,0},{2,3},{3,2},{4,5},{5,4},{6,7},{7,6},{8,9},{9,8},{10,11... | collective-permute-start | bytes 7077896 | tf_op jit(solution)/shard_map/ppermute | solution.py:43
  562.3 28.7 %collective-permute-start.41 = (f32[384,768]{1,0:T(8,128)}, f32[384,768]{1,0:T(8,128)}, u32[]{:S(2)}, u32[]{:S(2)}) collective-permute-start(f32[384,768]{1,0:T(8,128)} %get-tuple-element.476), channel_id=1, source_target_pairs={{0,2},{1,3},{2,0},{3,1},{4,6},{5,7},{6,4},{7,5},{8,10},{9,11},{10,... | collective-permute-start | bytes 3538952 | tf_op jit(solution)/shard_map/ppermute | solution.py:43
  563.1 12.5 %collective-permute-start.59 = (f32[8,2560]{1,0:T(8,128)S(1)}, f32[8,2560]{1,0:T(8,128)S(1)}, u32[]{:S(2)}, u32[]{:S(2)}) collective-permute-start(f32[8,2560]{1,0:T(8,128)S(1)} %add.418), channel_id=1, source_target_pairs={{0,16},{4,20},{8,24},{12,28},{16,0},{20,4},{24,8},{28,12},{1,17},{... | collective-permute-start | bytes 245768 | tf_op jit(solution)/shard_map/ppermute | solution.py:43
  599.2 32.8 %collective-permute-start.65 = (f32[36,768]{1,0:T(8,128)S(1)}, f32[36,768]{1,0:T(8,128)S(1)}, u32[]{:S(2)}, u32[]{:S(2)}) collective-permute-start(f32[36,768]{1,0:T(8,128)S(1)} %add.427), channel_id=1, source_target_pairs={{0,16},{4,20},{8,24},{12,28},{16,0},{20,4},{24,8},{28,12},{1,17},{... | collective-permute-start | bytes 331784 | tf_op jit(solution)/shard_map/ppermute | solution.py:43
  602.1 9.7 %collective-permute-start.61 = (f32[8,768]{1,0:T(8,128)S(1)}, f32[8,768]{1,0:T(8,128)S(1)}, u32[]{:S(2)}, u32[]{:S(2)}) collective-permute-start(f32[8,768]{1,0:T(8,128)S(1)} %bitcast_add_fusion), channel_id=1, source_target_pairs={{0,8},{4,12},{8,0},{12,4},{16,24},{20,28},{24,16},{28,20},{1,9},{5... | collective-permute-start | bytes 73736 | tf_op jit(solution)/shard_map/ppermute | solution.py:43
  611.8 22.2 %collective-permute-start.62 = (f32[8,768]{1,0:T(8,128)S(1)}, f32[8,768]{1,0:T(8,128)S(1)}, u32[]{:S(2)}, u32[]{:S(2)}) collective-permute-start(f32[8,768]{1,0:T(8,128)S(1)} %add.423), channel_id=1, source_target_pairs={{0,16},{4,20},{8,24},{12,28},{16,0},{20,4},{24,8},{28,12},{1,17},{... | collective-permute-start | bytes 73736 | tf_op jit(solution)/shard_map/ppermute | solution.py:43
  (181 other events, 1361.3 us)
Sparse Core Ops, SparseCore 0:
  14.0 102.8 all-gather.2
  119.7 164.6 all-gather.4

commit v5 on v4

--- a/solution.py
+++ b/solution.py
@@ -813,7 +813,7 @@
     k_refs, v_refs, bias_refs, cos_refs, sin_refs = groups
     rest = refs[5 * count :]
     dq_ref, dk_refs, dv_refs = rest[0], rest[1 : 1 + count], rest[1 + count : 1 + 2 * count]
-    dk_sum, dv_sum, dq_sum = rest[1 + 2 * count :]
+    dk_sum, dv_sum, dq_sum, key_all, value_all = rest[1 + 2 * count :]
     head = pl.program_id(1)
     mine, spare = head_lanes(head)
     step, scale = k_refs[0].shape[0], HEAD_DIM ** (-0.5)
@@ -824,30 +824,32 @@
     grad = grad_wide.astype(NARROW)
     delta = jnp.sum(grad_wide.T * out_ref[...], axis=0, keepdims=True)
     log_total = log_ref[0, pl.ds(head, 1), :]
-    dq = None
     for k in range(count):
         rows = pl.ds(k * step, step)
-        key_block = k_refs[k][...]
-        key = jnp.where(spare, bias_refs[k][...].astype(WIDE), key_block.astype(WIDE))
-        scores = contract_cols(key.astype(NARROW), asked)
-        probs = jnp.exp(scores - log_total)
-        dprobs = contract_cols(v_refs[k][...], grad)
-        dv = jnp.dot(probs.astype(NARROW), grad, preferred_element_type=WIDE)
-        dscores = (probs * (dprobs - delta)).astype(NARROW)
-        dk = jnp.dot(dscores, query, preferred_element_type=WIDE)
-        part = contract_rows(key_block, dscores)
-        dq = part if dq is None else dq + part
-
-        @pl.when(head == 0)
-        def _():
-            dk_sum[rows, :] = dk
-            dv_sum[rows, :] = dv
-
-        @pl.when(head == 1)
-        def _():
-            total = dk_sum[rows, :] + dk
-            dk_refs[k][...] = turn(total, cos_refs[k][...], -sin_refs[k][...]).astype(NARROW)
-            dv_refs[k][...] = (dv_sum[rows, :] + dv).astype(NARROW)
+        key = jnp.where(spare, bias_refs[k][...].astype(WIDE), k_refs[k][...].astype(WIDE))
+        key_all[rows, :] = key.astype(NARROW)
+        value_all[rows, :] = v_refs[k][...]
+    keys = key_all[...]
+    probs = jnp.exp(contract_cols(keys, asked) - log_total)
+    dprobs = contract_cols(value_all[...], grad)
+    dv = jnp.dot(probs.astype(NARROW), grad, preferred_element_type=WIDE)
+    dscores = (probs * (dprobs - delta)).astype(NARROW)
+    dk = jnp.dot(dscores, query, preferred_element_type=WIDE)
+    dq = contract_rows(keys, dscores)
+
+    @pl.when(head == 0)
+    def _():
+        dk_sum[...] = dk
+        dv_sum[...] = dv
+
+    @pl.when(head == 1)
+    def _():
+        key_grad, value_grad = dk_sum[...] + dk, dv_sum[...] + dv
+        for k in range(count):
+            rows = slice(k * step, (k + 1) * step)
+            piece = turn(key_grad[rows], cos_refs[k][...], -sin_refs[k][...])
+            dk_refs[k][...] = piece.astype(NARROW)
+            dv_refs[k][...] = value_grad[rows].astype(NARROW)
 
     @pl.when(head == 0)
     def _():
@@ -884,6 +886,8 @@
             pltpu.VMEM((length, PAIR), WIDE),
             pltpu.VMEM((length, PAIR), WIDE),
             pltpu.VMEM((PAIR, rows), WIDE),
+            pltpu.VMEM((length, PAIR), NARROW),
+            pltpu.VMEM((length, PAIR), NARROW),
         ],
         compiler_params=params(56),
         cost_estimate=pl.CostEstimate(

time: 676 us -> 673 us (level)
  transfers between devices with their start and end apart: 73 -> 73, of which waited for: 31 -> 31; matrix products, arithmetic and copies ran while one was open for 18% -> 18% of each run, Pallas kernels for 25% -> 26%
where the time goes in v5:
time: 673 us; the launch traced here: 665 us
  Pallas kernels  234 us (35%)
  waiting for transfers between devices  122 us (18%)
  local copies, waits for them, and re-layouts  108 us (16%)
  other arithmetic  59.9 us (9%)
  starting transfers between devices  57.8 us (9%)
  matrix products  44.8 us (7%)
  between operations  38.9 us (6%)
    ppermute x69, waiting for transfers between devices, swap(): lax.ppermute(value, axis, [(index, index ^ bit) for index in range(size)])  99.4 us
    unnamed x324, local copies, waits for them, and re-layouts  71.2 us
    ppermute x69, starting transfers between devices, swap(): lax.ppermute(value, axis, [(index, index ^ bit) for index in range(size)])  46.4 us
    pallas_call x1, Pallas kernels, attention_backward(): pl.pallas_call(functools.partial(attend_back_kernel, count), grid=(pairs,...  44.2 us
    dot_general x19, matrix products, dot_in(): lax.dot_general(left, right, (axes, ((), ())), precision=precision, prefe...  33.3 us
    pallas_call x3, Pallas kernels, table_matrix(): pl.pallas_call(functools.partial(table_kernel, columns, first), grid=(til...  27.6 us
    pallas_call x4, Pallas kernels, lookup(): pl.pallas_call(functools.partial(lookup_kernel, row_count), in_specs=[pl....  24.7 us
    pallas_call x1, Pallas kernels, attention_forward(): pl.pallas_call(functools.partial(attend_kernel, count), grid=(pairs, 2),...  23.2 us
  transfers between devices with their start and end apart: 73, of which 31 were waited for; matrix products, arithmetic and copies ran while one was open for 18% of the time, Pallas kernels for 26%

profile of v5, /device:TPU:0, one launch (start us, length us, event | category | flops | bytes accessed | tf_op | source)
XLA Modules:
  0.0 665.0 jit_solution(3042727305343732871)
XLA Ops:
  14.5 7.3 %all-to-all-start = ((s32[8,1,2048]{2,1,0:T(1,128)}), s32[8,1,2048]{2,1,0:T(1,128)S(1)}, u32[]{:S(2)}, u32[]{:S(2)}) async-start(s32[8,1,2048]{2,1,0:T(1,128)} %broadcast_in_dim.112), calls=%async_computation | async-start | bytes 131072 | tf_op jit(solution)/shard_map/all_to_all | solution.py:1241
  25.6 3.2 all-to-all-done
  31.2 6.2 shard_map.379
  39.7 6.2 shard_map.380
  45.8 6.2 shard_map.381
  56.5 6.2 shard_map.382
  62.6 9.6 %collective-permute-done.2 = bf16[512,768]{1,0:T(8,128)(2,1)S(1)} collective-permute-done((bf16[512,768]{1,0:T(8,128)(2,1)S(1)}, bf16[512,768]{1,0:T(8,128)(2,1)S(1)}, u32[]{:S(2)}, u32[]{:S(2)}) %collective-permute-start.2) | collective-permute-done | bytes 786464 | tf_op jit(solution)/shard_map/ppermute | solution.py:43
  79.5 4.1 all-to-all-start.1
  87.4 8.6 %constant_dynamic-slice_fusion.34 = (f32[1,768,1,768]{3,2,1,0:T(1,128)S(1)}, f32[1,768,1,768]{3,2,1,0:T(1,128)S(1)}) fusion(f32[1,768,2,768]{3,2,1,0:T(2,128)} %param.48, s32[]{:T(128)S(6)} %select_n.157, s32[]{:T(128)S(6)} %select_n.156), kind=kLoop, calls=%fused_computation.184 | loop fusion | bytes 9437192 | tf_op jit(solution)/shard_map/dynamic_slice | solution.py:1279
  98.8 5.4 convert_reduce_fusion
  105.9 11.6 %all-to-all-done.1 = bf16[8,96,512]{2,1,0:T(8,128)(2,1)S(1)} async-done(((bf16[8,96,512]{2,1,0:T(8,128)(2,1)}), bf16[8,96,512]{2,1,0:T(8,128)(2,1)S(1)}, u32[]{:S(2)}, u32[]{:S(2)}) %all-to-all-start.1) | async-done | bytes 786464 | tf_op jit(solution)/shard_map/all_to_all | solution.py:1280
  133.7 17.5 %collective-permute-done.4 = bf16[768,768]{1,0:T(8,128)(2,1)} collective-permute-done((bf16[768,768]{1,0:T(8,128)(2,1)}, bf16[768,768]{1,0:T(8,128)(2,1)}, u32[]{:S(2)}, u32[]{:S(2)}) %collective-permute-start.4) | collective-permute-done | bytes 1179680 | tf_op jit(solution)/shard_map/ppermute | solution.py:43
  151.1 3.7 multiply_sine_fusion
  155.8 10.8 %collective-permute-done.7.x_ref = bf16[512,768]{1,0:T(8,128)(2,1)} collective-permute-done((bf16[512,768]{1,0:T(8,128)(2,1)S(1)}, bf16[512,768]{1,0:T(8,128)(2,1)}, u32[]{:S(2)}, u32[]{:S(2)}) %collective-permute-start.7) | collective-permute-done | bytes 786464 | tf_op jit(solution)/shard_map/ppermute | solution.py:43
  169.9 3.1 shard_map.386
  178.9 23.2 %shard_map.388 = (f32[768,512]{1,0:T(8,128)S(1)}, f32[6,2,512]{2,1,0:T(2,128)S(1)}) custom-call(bf16[512,768]{1,0:T(8,128)(2,1)S(1)} %get-tuple-element.213.q_ref, bf16[512,768]{1,0:T(8,128)(2,1)S(1)} %get-tuple-element.217.refs_0_, bf16[512,768]{1,0:T(8,128)(2,1)S(1)} %get-tuple-element.218.refs_1_, bf16[512,768]{1,0:T(8,128)(2,1)S(1)} %get-tuple-element.219.refs_2_, ...), custom_call_target="tpu_custom_call" | custom-call | flops 3221225472 | bytes 9437184 | tf_op jit(solution)/shard_map/pallas_call | solution.py:789
  215.1 7.0 %shard_map.390 = (f32[1024,768]{1,0:T(8,128)S(1)}, f32[1024,768]{1,0:T(8,128)S(1)}, bf16[1024,768]{1,0:T(8,128)(2,1)S(1)}, bf16[1024,768]{1,0:T(8,128)(2,1)S(1)}...) custom-call(bf16[512,768]{1,0:T(8,128)(2,1)} %get-tuple-element.228.first_ref, ...), custom_call_target="tpu_custom_call" | custom-call | flops 3623878656 | bytes 14548992 | tf_op jit(solution)/shard_map/pallas_call | solution.py:435
  231.0 4.6 shard_map.391
  251.6 10.8 %collective-permute-done.14.refs_2_.got_ref = bf16[512,768]{1,0:T(8,128)(2,1)S(1)} collective-permute-done((bf16[512,768]{1,0:T(8,128)(2,1)}, bf16[512,768]{1,0:T(8,128)(2,1)S(1)}, u32[]{:S(2)}, u32[]{:S(2)}) %collective-permute-start.14) | collective-permute-done | bytes 786464 | tf_op jit(solution)/shard_map/ppermute | solution.py:43
  276.9 7.4 %all-gather.5.cloned.1.call-done.table_ref = bf16[768,7632]{1,0:T(8,128)(2,1)} async-done(((bf16[96,7632]{1,0:T(8,128)(2,1)}), bf16[768,7632]{1,0:T(8,128)(2,1)}) %all-gather.5.cloned.1.call-update) | async-done | bytes 11722768 | tf_op jit(solution)/shard_map/all_gather | solution.py:1292
  284.3 9.7 %shard_map.393 = (f32[160,7680]{1,0:T(8,128)}, f32[160,128]{1,0:T(8,128)}) custom-call(bf16[160,768]{1,0:T(8,128)(2,1)} %pad_maximum_fusion.5.rows_ref, bf16[768,7632]{1,0:T(8,128)(2,1)} %all-gather.5.cloned.1.call-done.table_ref, s32[160,1]{1,0:T(8,128)} %sub.77.targets_ref), custom_call_target="tpu_custom_call" | custom-call | flops 1875640320 | bytes 11722752 | tf_op jit(solution)/shard_map/pallas_call | solution.py:614
  301.9 11.3 %shard_map.396 = (bf16[160,7680]{1,0:T(8,128)(2,1)}, f32[160,768]{1,0:T(8,128)}) custom-call(f32[160,7680]{1,0:T(8,128)} %get-tuple-element.237.logits_ref, bf16[768,7632]{1,0:T(8,128)(2,1)} %all-gather.5.cloned.1.call-done.table_ref, s32[160,1]{1,0:T(8,128)} %sub.77.targets_ref, f32[160,128]{1,0:T(8,128)} %slice.388.stats_ref, f32[160,1]{1,0:T(8,128)} %div.23.weight_ref), custom_call_target="tpu_custom_call" | custom-call | flops 1875640320 | bytes 11722752 | tf_op jit(solution)/shard_map/pallas_call | solution.py:678
  329.5 7.5 %shard_map.399 = (bf16[1024,768]{1,0:T(8,128)(2,1)S(1)}, bf16[1024,768]{1,0:T(8,128)(2,1)S(1)}, bf16[1024,768]{1,0:T(8,128)(2,1)S(1)}, bf16[512,768]{1,0:T(8,128)(2,1)S(1)}, bf16[512,768]{1,0:T(8,128)(2,1)}) custom-call(bf16[512,768]{1,0:T(8,128)(2,1)} %get-tuple-element.248.first_ref, bf16[512,768]{1,0:T(8,128)(2,1)S(1)} %copy-done.87, ...), custom_call_target="tpu_custom_call" | custom-call | flops 3623878656 | bytes 16121856 | tf_op jit(solution)/shard_map/pallas_call | solution.py:488
  341.3 3.8 collective-permute-done.27.first_ref
  348.5 6.0 shard_map.400
  361.9 2.9 convolution_add_fusion.1.refs_0_
  364.8 2.9 convolution_add_fusion.refs_1_
  372.6 4.1 collective-permute-done.31.got_ref
  381.4 44.2 %shard_map.402 = (bf16[512,768]{1,0:T(8,128)(2,1)}, bf16[512,768]{1,0:T(8,128)(2,1)}, bf16[512,768]{1,0:T(8,128)(2,1)}, bf16[512,768]{1,0:T(8,128)(2,1)}, bf16[5...) custom-call(bf16[512,768]{1,0:T(8,128)(2,1)} %copy-done.122, ...), custom_call_target="tpu_custom_call" | custom-call | flops 8053063680 | bytes 15728640 | tf_op jit(solution)/shard_map/pallas_call | solution.py:872
  453.5 4.6 pad_maximum_fusion
  462.8 3.3 constant_dynamic-slice_fusion.8.refs_3_
  466.7 9.6 %shard_map.406 = (f32[3,768,768]{2,1,0:T(8,128)}, f32[3,8,768]{2,1,0:T(8,128)}) custom-call(f32[768,768]{1,0:T(8,128)} %convolution_add_fusion.1.refs_0_, f32[768,768]{1,0:T(8,128)} %convolution_add_fusion.refs_1_, f32[768,768]{1,0:T(8,128)} %convolution_add_fusion.2.refs_2_, f32[768,768]{1,0:T(8,128)} %get-tuple-element.319.refs_3_, ...), custom_call_target="tpu_custom_call" | custom-call | flops 84934656 | bytes 21233664 | tf_op jit(solution)/shard_map/pallas_call | solution.py:1022
  476.9 3.7 collective-permute-done.37
  487.2 9.4 %fusion.2.left_ref = bf16[2048,768]{1,0:T(8,128)(2,1)S(1)} fusion(s32[2048]{0:T(1024)S(1)} %convert_reduce_fusion, bf16[512,768]{1,0:T(8,128)(2,1)} %collective-permute-done.38, bf16[512,768]{1,0:T(8,128)(2,1)} %collective-permute-done.37, bf16[512,768]{1,0:T(8,128)(2,1)} %collective-permute-done.36, bf16[512,768]{1,0:T(8,128)(2,1)} %get-tuple-element.315), kind=kOutput, calls=%fused_computation.8 | convolution fusion | flops 6459228160 | bytes 6299648 | tf_op jit(solution)/shard_map/dot_general | solution.py:1457
  496.6 6.0 fusion.79
  504.5 4.0 shard_map.410
  509.2 10.1 %shard_map.407 = (bf16[3200,768]{1,0:T(8,128)(2,1)S(1)}, bf16[3200,768]{1,0:T(8,128)(2,1)S(1)}, f32[8,3200]{1,0:T(8,128)S(1)}) custom-call(s32[13]{0:T(128)S(1)} %convert_reduce_fusion.1.starts_ref, bf16[2048,768]{1,0:T(8,128)(2,1)S(1)} %fusion.2.left_ref, s32[1,2048]{1,0:T(1,128)S(1)} %bitcast.249, bf16[160,768]{1,0:T(8,128)(2,1)S(1)} %copy-done.42, ...), custom_call_target="tpu_custom_call" | custom-call | flops 3420979200 | bytes 19660800 | tf_op jit(solution)/shard_map/pallas_call | solution.py:960
  521.2 10.0 %shard_map.408 = (bf16[2560,768]{1,0:T(8,128)(2,1)S(1)}, bf16[2560,768]{1,0:T(8,128)(2,1)S(1)}, f32[8,2560]{1,0:T(8,128)S(1)}) custom-call(s32[13]{0:T(128)S(1)} %convert_reduce_fusion.1.starts_ref, bf16[2048,768]{1,0:T(8,128)(2,1)S(1)} %fusion.2.left_ref, s32[1,2048]{1,0:T(1,128)S(1)} %bitcast.250, bf16[160,768]{1,0:T(8,128)(2,1)S(1)} %copy-done.42, ...), custom_call_target="tpu_custom_call" | custom-call | flops 2736783360 | bytes 15728640 | tf_op jit(solution)/shard_map/pallas_call | solution.py:960
  535.1 7.6 %shard_map.409 = (bf16[1920,768]{1,0:T(8,128)(2,1)S(1)}, bf16[1920,768]{1,0:T(8,128)(2,1)S(1)}, f32[8,1920]{1,0:T(8,128)S(1)}) custom-call(s32[13]{0:T(128)S(1)} %convert_reduce_fusion.1.starts_ref, bf16[2048,768]{1,0:T(8,128)(2,1)S(1)} %fusion.2.left_ref, s32[1,2048]{1,0:T(1,128)S(1)} %bitcast.251, bf16[160,768]{1,0:T(8,128)(2,1)S(1)} %copy-done.42, ...), custom_call_target="tpu_custom_call" | custom-call | flops 2052587520 | bytes 11796480 | tf_op jit(solution)/shard_map/pallas_call | solution.py:960
  561.5 4.9 collective-permute-done.50
  569.1 3.0 collective-permute-done.56
  579.9 4.6 shard_map.415.refs_6_
  589.6 4.4 fusion.13.m_ref
  600.6 3.0 copy-done.8
  603.6 4.6 shard_map.417
  617.4 11.2 %shard_map.418 = f32[7632,768]{1,0:T(8,128)} custom-call(bf16[3200,768]{1,0:T(8,128)(2,1)S(1)} %copy-done.14, bf16[2560,768]{1,0:T(8,128)(2,1)S(1)} %copy-done.20, bf16[1920,768]{1,0:T(8,128)(2,1)S(1)} %copy-done.27, bf16[3200,768]{1,0:T(8,128)(2,1)S(1)} %copy-done.17, bf16[2560,768]{1,0:T(8,128)(2,1)S(1)} %copy-done.23, bf16[1920,768]{1,0:T(8,128)(2,1)S(1)} %copy-done.29, ...), custom_call_target="tpu_custom_call" | custom-call | flops 281346048 | bytes 46891008 | tf_op jit(solution)/shard_map/pallas_call | solution.py:1177
  633.9 3.1 collective-permute-done.67
  650.4 6.4 multiply_subtract_fusion
  (644 shorter events, 257.9 us)
Async XLA Ops:
  7.2 112.2 %all-gather.3.cloned.1.call-start = ((), (), s32[]{:S(2)}) async-start(), calls=%async_computation.2 | async-start | bytes 5750784 | tf_op jit(solution)/shard_map/all_gather | solution.py:1290
  14.5 14.3 %all-to-all-start = ((s32[8,1,2048]{2,1,0:T(1,128)}), s32[8,1,2048]{2,1,0:T(1,128)S(1)}, u32[]{:S(2)}, u32[]{:S(2)}) async-start(s32[8,1,2048]{2,1,0:T(1,128)} %broadcast_in_dim.112), calls=%async_computation | async-start | bytes 131072 | tf_op jit(solution)/shard_map/all_to_all | solution.py:1241
  21.8 262.6 %all-gather.5.cloned.1.call-start = ((), (), s32[]{:S(2)}) async-start(), calls=%async_computation.3 | async-start | bytes 13271040 | tf_op jit(solution)/shard_map/all_gather | solution.py:1292
  37.4 14.6 %collective-permute-start = (bf16[512,768]{1,0:T(8,128)(2,1)S(1)}, bf16[512,768]{1,0:T(8,128)(2,1)S(1)}, u32[]{:S(2)}, u32[]{:S(2)}) collective-permute-start(bf16[512,768]{1,0:T(8,128)(2,1)S(1)} %shard_map.379), channel_id=1, source_target_pairs={{0,1},{1,0},{2,3},{3,2},{4,5},{5,4},{6,7},{7,6},{8,9},{9,8},{10,11... | collective-permute-start | bytes 2359304 | tf_op jit(solution)/shard_map/ppermute | solution.py:43
  52.2 20.0 %collective-permute-start.2 = (bf16[512,768]{1,0:T(8,128)(2,1)S(1)}, bf16[512,768]{1,0:T(8,128)(2,1)S(1)}, u32[]{:S(2)}, u32[]{:S(2)}) collective-permute-start(bf16[512,768]{1,0:T(8,128)(2,1)S(1)} %add_convert_fusion.7), channel_id=1, source_target_pairs={{0,2},{1,3},{2,0},{3,1},{4,6},{5,7},{6,4},{7,5},{8,10},{9,11},{10,... | collective-permute-start | bytes 2359304 | tf_op jit(solution)/shard_map/ppermute | solution.py:43
  53.8 18.4 %collective-permute-start.1 = (bf16[512,768]{1,0:T(8,128)(2,1)S(1)}, bf16[512,768]{1,0:T(8,128)(2,1)S(1)}, u32[]{:S(2)}, u32[]{:S(2)}) collective-permute-start(bf16[512,768]{1,0:T(8,128)(2,1)S(1)} %shard_map.381), channel_id=1, source_target_pairs={{0,1},{1,0},{2,3},{3,2},{4,5},{5,4},{6,7},{7,6},{8,9},{9,8},{10,11... | collective-permute-start | bytes 2359304 | tf_op jit(solution)/shard_map/ppermute | solution.py:43
  79.5 38.0 %all-to-all-start.1 = ((bf16[8,96,512]{2,1,0:T(8,128)(2,1)}), bf16[8,96,512]{2,1,0:T(8,128)(2,1)S(1)}, u32[]{:S(2)}, u32[]{:S(2)}) async-start(bf16[8,96,512]{2,1,0:T(8,128)(2,1)} %bitcast.7), calls=%async_computation.1 | async-start | bytes 1572864 | tf_op jit(solution)/shard_map/all_to_all | solution.py:1280
  121.9 29.2 %collective-permute-start.4 = (bf16[768,768]{1,0:T(8,128)(2,1)}, bf16[768,768]{1,0:T(8,128)(2,1)}, u32[]{:S(2)}, u32[]{:S(2)}) collective-permute-start(bf16[768,768]{1,0:T(8,128)(2,1)} %get-tuple-element.469), channel_id=1, source_target_pairs={{0,2},{1,3},{2,0},{3,1},{4,6},{5,7},{6,4},{7,5},{8,10},{9,11},{10,... | collective-permute-start | bytes 3538952 | tf_op jit(solution)/shard_map/ppermute | solution.py:43
  123.4 43.2 %collective-permute-start.3 = (bf16[768,768]{1,0:T(8,128)(2,1)}, bf16[768,768]{1,0:T(8,128)(2,1)}, u32[]{:S(2)}, u32[]{:S(2)}) collective-permute-start(bf16[768,768]{1,0:T(8,128)(2,1)} %get-tuple-element.469), channel_id=1, source_target_pairs={{0,1},{1,0},{2,3},{3,2},{4,5},{5,4},{6,7},{7,6},{8,9},{9,8},{10,11... | collective-permute-start | bytes 3538952 | tf_op jit(solution)/shard_map/ppermute | solution.py:43
  129.3 43.7 %collective-permute-start.6 = (bf16[512,768]{1,0:T(8,128)(2,1)S(1)}, bf16[512,768]{1,0:T(8,128)(2,1)S(1)}, u32[]{:S(2)}, u32[]{:S(2)}) collective-permute-start(bf16[512,768]{1,0:T(8,128)(2,1)S(1)} %get-tuple-element.210.x_ref), channel_id=1, source_target_pairs={{0,1},{1,0},{2,3},{3,2},{4,5},{5,4},{6,7},{7,6},{8,9},{9,8},{10,11... | collective-permute-start | bytes 2359304 | tf_op jit(solution)/shard_map/ppermute | solution.py:43
  129.9 36.7 %collective-permute-start.7 = (bf16[512,768]{1,0:T(8,128)(2,1)S(1)}, bf16[512,768]{1,0:T(8,128)(2,1)}, u32[]{:S(2)}, u32[]{:S(2)}) collective-permute-start(bf16[512,768]{1,0:T(8,128)(2,1)S(1)} %get-tuple-element.210.x_ref), channel_id=1, source_target_pairs={{0,2},{1,3},{2,0},{3,1},{4,6},{5,7},{6,4},{7,5},{8,10},{9,11},{10,... | collective-permute-start | bytes 2359304 | tf_op jit(solution)/shard_map/ppermute | solution.py:43
  151.1 15.5 %collective-permute-start.5 = (bf16[768,768]{1,0:T(8,128)(2,1)}, bf16[768,768]{1,0:T(8,128)(2,1)S(1)}, u32[]{:S(2)}, u32[]{:S(2)}) collective-permute-start(bf16[768,768]{1,0:T(8,128)(2,1)} %collective-permute-done.4), channel_id=1, source_target_pairs={{0,1},{1,0},{2,3},{3,2},{4,5},{5,4},{6,7},{7,6},{8,9},{9,8},{10,11... | collective-permute-start | bytes 3538952 | tf_op jit(solution)/shard_map/ppermute | solution.py:43
  166.6 7.9 %collective-permute-start.8 = (bf16[512,768]{1,0:T(8,128)(2,1)}, bf16[512,768]{1,0:T(8,128)(2,1)S(1)}, u32[]{:S(2)}, u32[]{:S(2)}) collective-permute-start(bf16[512,768]{1,0:T(8,128)(2,1)} %collective-permute-done.7.x_ref), channel_id=1, source_target_pairs={{0,1},{1,0},{2,3},{3,2},{4,5},{5,4},{6,7},{7,6},{8,9},{9,8},{10,11... | collective-permute-start | bytes 2359304 | tf_op jit(solution)/shard_map/ppermute | solution.py:43
  208.0 20.7 %collective-permute-start.11 = (bf16[512,768]{1,0:T(8,128)(2,1)}, bf16[512,768]{1,0:T(8,128)(2,1)S(1)}, u32[]{:S(2)}, u32[]{:S(2)}) collective-permute-start(bf16[512,768]{1,0:T(8,128)(2,1)} %get-tuple-element.228.first_ref), channel_id=1, source_target_pairs={{0,2},{1,3},{2,0},{3,1},{4,6},{5,7},{6,4},{7,5},{8,10},{9,11},{10,... | collective-permute-start | bytes 2359304 | tf_op jit(solution)/shard_map/ppermute | solution.py:43
  241.1 8.8 %collective-permute-start.10 = (bf16[512,768]{1,0:T(8,128)(2,1)}, bf16[512,768]{1,0:T(8,128)(2,1)}, u32[]{:S(2)}, u32[]{:S(2)}) collective-permute-start(bf16[512,768]{1,0:T(8,128)(2,1)} %get-tuple-element.230), channel_id=1, source_target_pairs={{0,1},{1,0},{2,3},{3,2},{4,5},{5,4},{6,7},{7,6},{8,9},{9,8},{10,11... | collective-permute-start | bytes 2359304 | tf_op jit(solution)/shard_map/ppermute | solution.py:43
  242.7 19.7 %collective-permute-start.14 = (bf16[512,768]{1,0:T(8,128)(2,1)}, bf16[512,768]{1,0:T(8,128)(2,1)S(1)}, u32[]{:S(2)}, u32[]{:S(2)}) collective-permute-start(bf16[512,768]{1,0:T(8,128)(2,1)} %add_convert_fusion.4), channel_id=1, source_target_pairs={{0,2},{1,3},{2,0},{3,1},{4,6},{5,7},{6,4},{7,5},{8,10},{9,11},{10,... | collective-permute-start | bytes 2359304 | tf_op jit(solution)/shard_map/ppermute | solution.py:43
  271.1 27.7 %collective-permute-start.24 = (bf16[256,768]{1,0:T(8,128)(2,1)}, bf16[256,768]{1,0:T(8,128)(2,1)}, u32[]{:S(2)}, u32[]{:S(2)}) collective-permute-start(bf16[256,768]{1,0:T(8,128)(2,1)} %multiply_convert_fusion), channel_id=1, source_target_pairs={{0,2},{1,3},{2,0},{3,1},{4,6},{5,7},{6,4},{7,5},{8,10},{9,11},{10,... | collective-permute-start | bytes 1179656 | tf_op jit(solution)/shard_map/ppermute | solution.py:43
  298.8 15.8 %collective-permute-start.23 = (bf16[256,768]{1,0:T(8,128)(2,1)}, bf16[256,768]{1,0:T(8,128)(2,1)S(1)}, u32[]{:S(2)}, u32[]{:S(2)}) collective-permute-start(bf16[256,768]{1,0:T(8,128)(2,1)} %multiply_convert_fusion), channel_id=1, source_target_pairs={{0,1},{1,0},{2,3},{3,2},{4,5},{5,4},{6,7},{7,6},{8,9},{9,8},{10,11... | collective-permute-start | bytes 1179656 | tf_op jit(solution)/shard_map/ppermute | solution.py:43
  298.8 15.8 %collective-permute-start.25 = (bf16[256,768]{1,0:T(8,128)(2,1)}, bf16[256,768]{1,0:T(8,128)(2,1)}, u32[]{:S(2)}, u32[]{:S(2)}) collective-permute-start(bf16[256,768]{1,0:T(8,128)(2,1)} %collective-permute-done.24), channel_id=1, source_target_pairs={{0,1},{1,0},{2,3},{3,2},{4,5},{5,4},{6,7},{7,6},{8,9},{9,8},{10,11... | collective-permute-start | bytes 1179656 | tf_op jit(solution)/shard_map/ppermute | solution.py:43
  324.9 20.2 %collective-permute-start.27 = (bf16[512,768]{1,0:T(8,128)(2,1)}, bf16[512,768]{1,0:T(8,128)(2,1)S(1)}, u32[]{:S(2)}, u32[]{:S(2)}) collective-permute-start(bf16[512,768]{1,0:T(8,128)(2,1)} %get-tuple-element.248.first_ref), channel_id=1, source_target_pairs={{0,2},{1,3},{2,0},{3,1},{4,6},{5,7},{6,4},{7,5},{8,10},{9,11},{10,... | collective-permute-start | bytes 2359304 | tf_op jit(solution)/shard_map/ppermute | solution.py:43
  345.1 9.5 %collective-permute-start.30 = (bf16[512,768]{1,0:T(8,128)(2,1)}, bf16[512,768]{1,0:T(8,128)(2,1)S(1)}, u32[]{:S(2)}, u32[]{:S(2)}) collective-permute-start(bf16[512,768]{1,0:T(8,128)(2,1)} %get-tuple-element.256), channel_id=1, source_target_pairs={{0,1},{1,0},{2,3},{3,2},{4,5},{5,4},{6,7},{7,6},{8,9},{9,8},{10,11... | collective-permute-start | bytes 2359304 | tf_op jit(solution)/shard_map/ppermute | solution.py:43
  357.0 19.6 %collective-permute-start.31 = (bf16[512,768]{1,0:T(8,128)(2,1)S(1)}, bf16[512,768]{1,0:T(8,128)(2,1)S(1)}, u32[]{:S(2)}, u32[]{:S(2)}) collective-permute-start(bf16[512,768]{1,0:T(8,128)(2,1)S(1)} %add_convert_fusion.3), channel_id=1, source_target_pairs={{0,2},{1,3},{2,0},{3,1},{4,6},{5,7},{6,4},{7,5},{8,10},{9,11},{10,... | collective-permute-start | bytes 2359304 | tf_op jit(solution)/shard_map/ppermute | solution.py:43
  438.3 19.8 %collective-permute-start.35 = (bf16[512,768]{1,0:T(8,128)(2,1)S(1)}, bf16[512,768]{1,0:T(8,128)(2,1)S(1)}, u32[]{:S(2)}, u32[]{:S(2)}) collective-permute-start(bf16[512,768]{1,0:T(8,128)(2,1)S(1)} %add_convert_fusion.1), channel_id=1, source_target_pairs={{0,2},{1,3},{2,0},{3,1},{4,6},{5,7},{6,4},{7,5},{8,10},{9,11},{10,... | collective-permute-start | bytes 2359304 | tf_op jit(solution)/shard_map/ppermute | solution.py:43
  460.6 19.9 %collective-permute-start.37 = (bf16[512,768]{1,0:T(8,128)(2,1)}, bf16[512,768]{1,0:T(8,128)(2,1)}, u32[]{:S(2)}, u32[]{:S(2)}) collective-permute-start(bf16[512,768]{1,0:T(8,128)(2,1)} %get-tuple-element.315), channel_id=1, source_target_pairs={{0,2},{1,3},{2,0},{3,1},{4,6},{5,7},{6,4},{7,5},{8,10},{9,11},{10,... | collective-permute-start | bytes 2359304 | tf_op jit(solution)/shard_map/ppermute | solution.py:43
  466.0 30.6 %collective-permute-start.39 = (f32[768,768]{1,0:T(8,128)}, f32[768,768]{1,0:T(8,128)}, u32[]{:S(2)}, u32[]{:S(2)}) collective-permute-start(f32[768,768]{1,0:T(8,128)} %constant_dynamic-slice_fusion.8.refs_3_), channel_id=1, source_target_pairs={{0,1},{1,0},{2,3},{3,2},{4,5},{5,4},{6,7},{7,6},{8,9},{9,8},{10,11... | collective-permute-start | bytes 7077896 | tf_op jit(solution)/shard_map/ppermute | solution.py:43
  476.3 10.9 %collective-permute-start.36 = (bf16[512,768]{1,0:T(8,128)(2,1)}, bf16[512,768]{1,0:T(8,128)(2,1)}, u32[]{:S(2)}, u32[]{:S(2)}) collective-permute-start(bf16[512,768]{1,0:T(8,128)(2,1)} %get-tuple-element.315), channel_id=1, source_target_pairs={{0,1},{1,0},{2,3},{3,2},{4,5},{5,4},{6,7},{7,6},{8,9},{9,8},{10,11... | collective-permute-start | bytes 2359304 | tf_op jit(solution)/shard_map/ppermute | solution.py:43
  480.5 6.6 collective-permute-start.38
  485.2 19.3 %collective-permute-start.42 = (f32[8,768]{1,0:T(8,128)S(1)}, f32[8,768]{1,0:T(8,128)S(1)}, u32[]{:S(2)}, u32[]{:S(2)}) collective-permute-start(f32[8,768]{1,0:T(8,128)S(1)} %get-tuple-element.501.refs_4_.refs_1_), channel_id=1, source_target_pairs={{0,1},{1,0},{2,3},{3,2},{4,5},{5,4},{6,7},{7,6},{8,9},{9,8},{10,11... | collective-permute-start | bytes 73736 | tf_op jit(solution)/shard_map/ppermute | solution.py:43
  486.0 18.5 %collective-permute-start.44 = (f32[8,768]{1,0:T(8,128)S(1)}, f32[8,768]{1,0:T(8,128)S(1)}, u32[]{:S(2)}, u32[]{:S(2)}) collective-permute-start(f32[8,768]{1,0:T(8,128)S(1)} %collective-permute-done.43.refs_6_), channel_id=1, source_target_pairs={{0,1},{1,0},{2,3},{3,2},{4,5},{5,4},{6,7},{7,6},{8,9},{9,8},{10,11... | collective-permute-start | bytes 73736 | tf_op jit(solution)/shard_map/ppermute | solution.py:43
  503.9 31.2 %collective-permute-start.40 = (f32[384,768]{1,0:T(8,128)S(1)}, f32[384,768]{1,0:T(8,128)S(1)}, u32[]{:S(2)}, u32[]{:S(2)}) collective-permute-start(f32[384,768]{1,0:T(8,128)S(1)} %get-tuple-element.477), channel_id=1, source_target_pairs={{0,2},{1,3},{2,0},{3,1},{4,6},{5,7},{6,4},{7,5},{8,10},{9,11},{10,... | collective-permute-start | bytes 3538952 | tf_op jit(solution)/shard_map/ppermute | solution.py:43
  508.6 10.7 %collective-permute-start.46 = (f32[8,768]{1,0:T(8,128)S(1)}, f32[8,768]{1,0:T(8,128)S(1)}, u32[]{:S(2)}, u32[]{:S(2)}) collective-permute-start(f32[8,768]{1,0:T(8,128)S(1)} %get-tuple-element.503), channel_id=1, source_target_pairs={{0,1},{1,0},{2,3},{3,2},{4,5},{5,4},{6,7},{7,6},{8,9},{9,8},{10,11... | collective-permute-start | bytes 73736 | tf_op jit(solution)/shard_map/ppermute | solution.py:43
  508.7 26.4 %collective-permute-start.45 = (f32[8,768]{1,0:T(8,128)S(1)}, f32[8,768]{1,0:T(8,128)S(1)}, u32[]{:S(2)}, u32[]{:S(2)}) collective-permute-start(f32[8,768]{1,0:T(8,128)S(1)} %get-tuple-element.502), channel_id=1, source_target_pairs={{0,1},{1,0},{2,3},{3,2},{4,5},{5,4},{6,7},{7,6},{8,9},{9,8},{10,11... | collective-permute-start | bytes 73736 | tf_op jit(solution)/shard_map/ppermute | solution.py:43
  519.3 15.8 %collective-permute-start.47 = (f32[8,768]{1,0:T(8,128)S(1)}, f32[8,768]{1,0:T(8,128)S(1)}, u32[]{:S(2)}, u32[]{:S(2)}) collective-permute-start(f32[8,768]{1,0:T(8,128)S(1)} %fusion.32), channel_id=1, source_target_pairs={{0,2},{1,3},{2,0},{3,1},{4,6},{5,7},{6,4},{7,5},{8,10},{9,11},{10,... | collective-permute-start | bytes 73736 | tf_op jit(solution)/shard_map/ppermute | solution.py:43
  543.4 6.5 collective-permute-start.51
  544.8 7.8 %collective-permute-start.54 = (f32[8,3200]{1,0:T(8,128)S(1)}, f32[8,3200]{1,0:T(8,128)S(1)}, u32[]{:S(2)}, u32[]{:S(2)}) collective-permute-start(f32[8,3200]{1,0:T(8,128)S(1)} %get-tuple-element.337), channel_id=1, source_target_pairs={{0,4},{4,0},{8,12},{12,8},{16,20},{20,16},{24,28},{28,24},{1,5},{5... | collective-permute-start | bytes 307208 | tf_op jit(solution)/shard_map/ppermute | solution.py:43
  545.4 7.1 %collective-permute-start.57 = (f32[8,2560]{1,0:T(8,128)S(1)}, f32[8,2560]{1,0:T(8,128)S(1)}, u32[]{:S(2)}, u32[]{:S(2)}) collective-permute-start(f32[8,2560]{1,0:T(8,128)S(1)} %get-tuple-element.338), channel_id=1, source_target_pairs={{0,4},{4,0},{8,12},{12,8},{16,20},{20,16},{24,28},{28,24},{1,5},{5... | collective-permute-start | bytes 245768 | tf_op jit(solution)/shard_map/ppermute | solution.py:43
  548.2 6.5 collective-permute-start.49
  549.8 7.9 %collective-permute-start.52 = (f32[8,2304]{1,0:T(8,128)S(1)}, f32[8,2304]{1,0:T(8,128)S(1)}, u32[]{:S(2)}, u32[]{:S(2)}) collective-permute-start(f32[8,2304]{1,0:T(8,128)S(1)} %fusion.77), channel_id=1, source_target_pairs={{0,8},{4,12},{8,0},{12,4},{16,24},{20,28},{24,16},{28,20},{1,9},{5... | collective-permute-start | bytes 221192 | tf_op jit(solution)/shard_map/ppermute | solution.py:43
  552.5 6.7 %collective-permute-start.58 = (f32[8,2560]{1,0:T(8,128)S(1)}, f32[8,2560]{1,0:T(8,128)S(1)}, u32[]{:S(2)}, u32[]{:S(2)}) collective-permute-start(f32[8,2560]{1,0:T(8,128)S(1)} %add.417), channel_id=1, source_target_pairs={{0,8},{4,12},{8,0},{12,4},{16,24},{20,28},{24,16},{28,20},{1,9},{5... | collective-permute-start | bytes 245768 | tf_op jit(solution)/shard_map/ppermute | solution.py:43
  552.6 7.0 %collective-permute-start.55 = (f32[8,3200]{1,0:T(8,128)S(1)}, f32[8,3200]{1,0:T(8,128)S(1)}, u32[]{:S(2)}, u32[]{:S(2)}) collective-permute-start(f32[8,3200]{1,0:T(8,128)S(1)} %add.414), channel_id=1, source_target_pairs={{0,8},{4,12},{8,0},{12,4},{16,24},{20,28},{24,16},{28,20},{1,9},{5... | collective-permute-start | bytes 307208 | tf_op jit(solution)/shard_map/ppermute | solution.py:43
  554.7 11.7 %collective-permute-start.50 = (f32[8,2688]{1,0:T(8,128)S(1)}, f32[8,2688]{1,0:T(8,128)S(1)}, u32[]{:S(2)}, u32[]{:S(2)}) collective-permute-start(f32[8,2688]{1,0:T(8,128)S(1)} %add.409), channel_id=1, source_target_pairs={{0,16},{4,20},{8,24},{12,28},{16,0},{20,4},{24,8},{28,12},{1,17},{... | collective-permute-start | bytes 258056 | tf_op jit(solution)/shard_map/ppermute | solution.py:43
  557.7 11.4 %collective-permute-start.53 = (f32[8,2304]{1,0:T(8,128)S(1)}, f32[8,2304]{1,0:T(8,128)S(1)}, u32[]{:S(2)}, u32[]{:S(2)}) collective-permute-start(f32[8,2304]{1,0:T(8,128)S(1)} %add.412), channel_id=1, source_target_pairs={{0,16},{4,20},{8,24},{12,28},{16,0},{20,4},{24,8},{28,12},{1,17},{... | collective-permute-start | bytes 221192 | tf_op jit(solution)/shard_map/ppermute | solution.py:43
  559.2 30.5 %collective-permute-start.34 = (f32[768,768]{1,0:T(8,128)}, f32[768,768]{1,0:T(8,128)}, u32[]{:S(2)}, u32[]{:S(2)}) collective-permute-start(f32[768,768]{1,0:T(8,128)} %get-tuple-element.466.refs_1_), channel_id=1, source_target_pairs={{0,1},{1,0},{2,3},{3,2},{4,5},{5,4},{6,7},{7,6},{8,9},{9,8},{10,11... | collective-permute-start | bytes 7077896 | tf_op jit(solution)/shard_map/ppermute | solution.py:43
  559.2 28.7 %collective-permute-start.41 = (f32[384,768]{1,0:T(8,128)}, f32[384,768]{1,0:T(8,128)}, u32[]{:S(2)}, u32[]{:S(2)}) collective-permute-start(f32[384,768]{1,0:T(8,128)} %get-tuple-element.476), channel_id=1, source_target_pairs={{0,2},{1,3},{2,0},{3,1},{4,6},{5,7},{6,4},{7,5},{8,10},{9,11},{10,... | collective-permute-start | bytes 3538952 | tf_op jit(solution)/shard_map/ppermute | solution.py:43
  559.6 12.5 %collective-permute-start.59 = (f32[8,2560]{1,0:T(8,128)S(1)}, f32[8,2560]{1,0:T(8,128)S(1)}, u32[]{:S(2)}, u32[]{:S(2)}) collective-permute-start(f32[8,2560]{1,0:T(8,128)S(1)} %add.418), channel_id=1, source_target_pairs={{0,16},{4,20},{8,24},{12,28},{16,0},{20,4},{24,8},{28,12},{1,17},{... | collective-permute-start | bytes 245768 | tf_op jit(solution)/shard_map/ppermute | solution.py:43
  595.7 33.0 %collective-permute-start.65 = (f32[36,768]{1,0:T(8,128)S(1)}, f32[36,768]{1,0:T(8,128)S(1)}, u32[]{:S(2)}, u32[]{:S(2)}) collective-permute-start(f32[36,768]{1,0:T(8,128)S(1)} %add.427), channel_id=1, source_target_pairs={{0,16},{4,20},{8,24},{12,28},{16,0},{20,4},{24,8},{28,12},{1,17},{... | collective-permute-start | bytes 331784 | tf_op jit(solution)/shard_map/ppermute | solution.py:43
  598.6 9.7 %collective-permute-start.61 = (f32[8,768]{1,0:T(8,128)S(1)}, f32[8,768]{1,0:T(8,128)S(1)}, u32[]{:S(2)}, u32[]{:S(2)}) collective-permute-start(f32[8,768]{1,0:T(8,128)S(1)} %bitcast_add_fusion), channel_id=1, source_target_pairs={{0,8},{4,12},{8,0},{12,4},{16,24},{20,28},{24,16},{28,20},{1,9},{5... | collective-permute-start | bytes 73736 | tf_op jit(solution)/shard_map/ppermute | solution.py:43
  608.2 22.4 %collective-permute-start.62 = (f32[8,768]{1,0:T(8,128)S(1)}, f32[8,768]{1,0:T(8,128)S(1)}, u32[]{:S(2)}, u32[]{:S(2)}) collective-permute-start(f32[8,768]{1,0:T(8,128)S(1)} %add.423), channel_id=1, source_target_pairs={{0,16},{4,20},{8,24},{12,28},{16,0},{20,4},{24,8},{28,12},{1,17},{... | collective-permute-start | bytes 73736 | tf_op jit(solution)/shard_map/ppermute | solution.py:43
  (181 other events, 1353.6 us)
Sparse Core Ops, SparseCore 0:
  14.0 102.8 all-gather.2
  119.7 164.6 all-gather.4

commit v6 on v5

--- a/solution.py
+++ b/solution.py
@@ -211,6 +211,40 @@
     return whole_call(
         turn_table_kernel, [((columns // 8 * 8 + 8, lanes), WIDE)], 8 * table.size, table
     )[0]
+
+
+def pack_kernel(rank_ref, attend_ref, gate_ref, down_ref, queue_ref, out_ref):
+    at = 0
+    for part in (attend_ref[...], gate_ref[:, 0, :], gate_ref[:, 1, :], down_ref[...]):
+        out_ref[:, at : at + part.shape[1]] = part.astype(NARROW)
+        at += part.shape[1]
+    out_ref[:, at:] = queue_ref[...]
+
+
+def packed_weights(rank, attend, gate_up, down, queue, columns):
+    rows, hidden = down.shape
+    span = queue.shape[1]
+    still = lambda i, rank_ref: (0, 0)
+    total = columns + 3 * hidden + span
+    return pl.pallas_call(
+        pack_kernel,
+        grid_spec=pltpu.PrefetchScalarGridSpec(
+            num_scalar_prefetch=1,
+            grid=(1,),
+            in_specs=[
+                pl.BlockSpec((rows, columns), lambda i, rank_ref: (0, rank_ref[0])),
+                pl.BlockSpec((rows, 2, hidden), lambda i, rank_ref: (0, 0, 0)),
+                pl.BlockSpec((rows, hidden), still),
+                pl.BlockSpec((rows, span), still),
+            ],
+            out_specs=pl.BlockSpec((rows, total), still),
+        ),
+        out_shape=jax.ShapeDtypeStruct((rows, total), NARROW),
+        compiler_params=params(12),
+        cost_estimate=pl.CostEstimate(
+            flops=rows * total, bytes_accessed=6 * rows * total, transcendentals=0
+        ),
+    )(rank, attend, gate_up, down, queue)
 
 
 def lookup_kernel(row_count, start_ref, ids_ref, table_ref, out_ref, held):
@@ -1280,12 +1314,15 @@
     embedded = lax.all_to_all(pieces, "dp", 0, 0).reshape(width, own_rows).T
 
     attend_cols = attend_error.shape[2]
-    quarter = lax.dynamic_slice_in_dim(attend_weight, tensor_rank * attend_cols, attend_cols, 1)
     queue_rows = queue_embed.shape[0] // tensor_count
     queue_own = lax.dynamic_slice_in_dim(queue_embed, tensor_rank * queue_rows, queue_rows, 0)
-    joined = jnp.concatenate([quarter, gate_up[:, 0], gate_up[:, 1], down_weight], axis=1)
-    joined = jnp.concatenate(
-        [joined.astype(NARROW), queue_own.reshape(row_count, -1)], axis=1
+    joined = packed_weights(
+        tensor_rank.astype(jnp.int32).reshape(1),
+        attend_weight,
+        gate_up,
+        down_weight,
+        queue_own.reshape(row_count, -1),
+        attend_cols,
     )
     joined_b = lax.all_gather(joined, "dp", axis=0, tiled=True)
     table_local, _ = lax.optimization_barrier((table_local, looked[tensor_count - 1]))
@@ -1475,7 +1512,7 @@
     ]
 
     other_sum = summed_all(jnp.concatenate([other_p[k] for k in range(3)], axis=1), "dp")
-    cuts = sorted({0, tiles * 5 // 12, tiles * 9 // 12, tiles})
+    cuts = sorted({0, tiles * 6 // 12, tiles * 10 // 12, tiles})
     table_parts, table_sums = [], []
     for bounds in zip(cuts, cuts[1:]):
         if table_parts:

time: 673 us -> 673 us (level)
    unnamed x324 -> x310, local copies, waits for them, and re-layouts: 71.2 us -> 73.7 us
  transfers between devices with their start and end apart: 73 -> 73, of which waited for: 31 -> 29; matrix products, arithmetic and copies ran while one was open for 18% -> 18% of each run, Pallas kernels for 26% -> 27%
where the time goes in v6:
time: 673 us; the launch traced here: 665 us
  Pallas kernels  236 us (35%)
  waiting for transfers between devices  119 us (18%)
  local copies, waits for them, and re-layouts  109 us (16%)
  starting transfers between devices  60.6 us (9%)
  other arithmetic  59.6 us (9%)
  matrix products  42.5 us (6%)
  between operations  38.8 us (6%)
    ppermute x69, waiting for transfers between devices, swap(): lax.ppermute(value, axis, [(index, index ^ bit) for index in range(size)])  96.6 us
    unnamed x310, local copies, waits for them, and re-layouts  73.7 us
    ppermute x69, starting transfers between devices, swap(): lax.ppermute(value, axis, [(index, index ^ bit) for index in range(size)])  49.2 us
    pallas_call x1, Pallas kernels, attention_backward(): pl.pallas_call(functools.partial(attend_back_kernel, count), grid=(pairs,...  44.2 us
    dot_general x19, matrix products, dot_in(): lax.dot_general(left, right, (axes, ((), ())), precision=precision, prefe...  31.1 us
    pallas_call x3, Pallas kernels, table_matrix(): pl.pallas_call(functools.partial(table_kernel, columns, first), grid=(til...  28.2 us
    pallas_call x4, Pallas kernels, lookup(): pl.pallas_call(functools.partial(lookup_kernel, row_count), in_specs=[pl....  24.7 us
    pallas_call x1, Pallas kernels, attention_forward(): pl.pallas_call(functools.partial(attend_kernel, count), grid=(pairs, 2),...  23.2 us
  transfers between devices with their start and end apart: 73, of which 29 were waited for; matrix products, arithmetic and copies ran while one was open for 18% of the time, Pallas kernels for 27%

profile of v6, /device:TPU:0, one launch (start us, length us, event | category | flops | bytes accessed | tf_op | source)
XLA Modules:
  0.0 664.5 jit_solution(4698478188739476269)
XLA Ops:
  13.6 7.3 %all-to-all-start = ((s32[8,1,2048]{2,1,0:T(1,128)}), s32[8,1,2048]{2,1,0:T(1,128)S(1)}, u32[]{:S(2)}, u32[]{:S(2)}) async-start(s32[8,1,2048]{2,1,0:T(1,128)} %broadcast_in_dim.112), calls=%async_computation | async-start | bytes 131072 | tf_op jit(solution)/shard_map/all_to_all | solution.py:1275
  24.7 3.2 all-to-all-done
  30.3 6.2 shard_map.379
  38.8 6.2 shard_map.380
  44.9 6.2 shard_map.381
  55.6 6.2 shard_map.382
  61.7 9.6 %collective-permute-done.2 = bf16[512,768]{1,0:T(8,128)(2,1)S(1)} collective-permute-done((bf16[512,768]{1,0:T(8,128)(2,1)S(1)}, bf16[512,768]{1,0:T(8,128)(2,1)S(1)}, u32[]{:S(2)}, u32[]{:S(2)}) %collective-permute-start.2) | collective-permute-done | bytes 786464 | tf_op jit(solution)/shard_map/ppermute | solution.py:43
  78.6 4.1 all-to-all-start.1
  86.5 8.6 %constant_dynamic-slice_fusion.34 = (f32[1,768,1,768]{3,2,1,0:T(1,128)S(1)}, f32[1,768,1,768]{3,2,1,0:T(1,128)S(1)}) fusion(f32[1,768,2,768]{3,2,1,0:T(2,128)} %param.48, s32[]{:T(128)S(6)} %select_n.153, s32[]{:T(128)S(6)} %select_n.152), kind=kLoop, calls=%fused_computation.175 | loop fusion | bytes 9437192 | tf_op jit(solution)/shard_map/dynamic_slice | solution.py:1313
  97.9 5.4 convert_reduce_fusion
  105.0 11.6 %all-to-all-done.1 = bf16[8,96,512]{2,1,0:T(8,128)(2,1)S(1)} async-done(((bf16[8,96,512]{2,1,0:T(8,128)(2,1)}), bf16[8,96,512]{2,1,0:T(8,128)(2,1)S(1)}, u32[]{:S(2)}, u32[]{:S(2)}) %all-to-all-start.1) | async-done | bytes 786464 | tf_op jit(solution)/shard_map/all_to_all | solution.py:1314
  132.8 17.4 %collective-permute-done.4 = bf16[768,768]{1,0:T(8,128)(2,1)} collective-permute-done((bf16[768,768]{1,0:T(8,128)(2,1)}, bf16[768,768]{1,0:T(8,128)(2,1)}, u32[]{:S(2)}, u32[]{:S(2)}) %collective-permute-start.4) | collective-permute-done | bytes 1179680 | tf_op jit(solution)/shard_map/ppermute | solution.py:43
  150.2 3.7 multiply_sine_fusion
  154.9 10.8 %collective-permute-done.7.x_ref = bf16[512,768]{1,0:T(8,128)(2,1)} collective-permute-done((bf16[512,768]{1,0:T(8,128)(2,1)S(1)}, bf16[512,768]{1,0:T(8,128)(2,1)}, u32[]{:S(2)}, u32[]{:S(2)}) %collective-permute-start.7) | collective-permute-done | bytes 786464 | tf_op jit(solution)/shard_map/ppermute | solution.py:43
  169.0 3.1 shard_map.387
  178.0 23.2 %shard_map.389 = (f32[768,512]{1,0:T(8,128)S(1)}, f32[6,2,512]{2,1,0:T(2,128)S(1)}) custom-call(bf16[512,768]{1,0:T(8,128)(2,1)S(1)} %get-tuple-element.213.q_ref, bf16[512,768]{1,0:T(8,128)(2,1)S(1)} %get-tuple-element.217.refs_0_, bf16[512,768]{1,0:T(8,128)(2,1)S(1)} %get-tuple-element.218.refs_1_, bf16[512,768]{1,0:T(8,128)(2,1)S(1)} %get-tuple-element.219.refs_2_, ...), custom_call_target="tpu_custom_call" | custom-call | flops 3221225472 | bytes 9437184 | tf_op jit(solution)/shard_map/pallas_call | solution.py:823
  214.3 7.0 %shard_map.391 = (f32[1024,768]{1,0:T(8,128)S(1)}, f32[1024,768]{1,0:T(8,128)S(1)}, bf16[1024,768]{1,0:T(8,128)(2,1)S(1)}, bf16[1024,768]{1,0:T(8,128)(2,1)S(1)}...) custom-call(bf16[512,768]{1,0:T(8,128)(2,1)} %get-tuple-element.228.first_ref, ...), custom_call_target="tpu_custom_call" | custom-call | flops 3623878656 | bytes 14548992 | tf_op jit(solution)/shard_map/pallas_call | solution.py:469
  230.2 4.6 shard_map.392
  250.8 10.8 %collective-permute-done.14.refs_2_.got_ref = bf16[512,768]{1,0:T(8,128)(2,1)S(1)} collective-permute-done((bf16[512,768]{1,0:T(8,128)(2,1)}, bf16[512,768]{1,0:T(8,128)(2,1)S(1)}, u32[]{:S(2)}, u32[]{:S(2)}) %collective-permute-start.14) | collective-permute-done | bytes 786464 | tf_op jit(solution)/shard_map/ppermute | solution.py:43
  276.1 7.4 %all-gather.5.cloned.1.call-done.table_ref = bf16[768,7632]{1,0:T(8,128)(2,1)} async-done(((bf16[96,7632]{1,0:T(8,128)(2,1)}), bf16[768,7632]{1,0:T(8,128)(2,1)}) %all-gather.5.cloned.1.call-update) | async-done | bytes 11722768 | tf_op jit(solution)/shard_map/all_gather | solution.py:1329
  283.4 9.7 %shard_map.394 = (f32[160,7680]{1,0:T(8,128)}, f32[160,128]{1,0:T(8,128)}) custom-call(bf16[160,768]{1,0:T(8,128)(2,1)} %pad_maximum_fusion.5.rows_ref, bf16[768,7632]{1,0:T(8,128)(2,1)} %all-gather.5.cloned.1.call-done.table_ref, s32[160,1]{1,0:T(8,128)} %sub.77.targets_ref), custom_call_target="tpu_custom_call" | custom-call | flops 1875640320 | bytes 11722752 | tf_op jit(solution)/shard_map/pallas_call | solution.py:648
  301.0 11.3 %shard_map.397 = (bf16[160,7680]{1,0:T(8,128)(2,1)}, f32[160,768]{1,0:T(8,128)}) custom-call(f32[160,7680]{1,0:T(8,128)} %get-tuple-element.237.logits_ref, bf16[768,7632]{1,0:T(8,128)(2,1)} %all-gather.5.cloned.1.call-done.table_ref, s32[160,1]{1,0:T(8,128)} %sub.77.targets_ref, f32[160,128]{1,0:T(8,128)} %slice.376.stats_ref, f32[160,1]{1,0:T(8,128)} %div.23.weight_ref), custom_call_target="tpu_custom_call" | custom-call | flops 1875640320 | bytes 11722752 | tf_op jit(solution)/shard_map/pallas_call | solution.py:712
  328.6 7.5 %shard_map.400 = (bf16[1024,768]{1,0:T(8,128)(2,1)S(1)}, bf16[1024,768]{1,0:T(8,128)(2,1)S(1)}, bf16[1024,768]{1,0:T(8,128)(2,1)S(1)}, bf16[512,768]{1,0:T(8,128)(2,1)S(1)}, bf16[512,768]{1,0:T(8,128)(2,1)}) custom-call(bf16[512,768]{1,0:T(8,128)(2,1)} %get-tuple-element.248.first_ref, bf16[512,768]{1,0:T(8,128)(2,1)S(1)} %copy-done.90, ...), custom_call_target="tpu_custom_call" | custom-call | flops 3623878656 | bytes 16121856 | tf_op jit(solution)/shard_map/pallas_call | solution.py:522
  340.4 3.8 collective-permute-done.27.first_ref
  347.6 6.0 shard_map.401
  361.0 2.9 convolution_add_fusion.1.refs_0_
  363.9 2.9 convolution_add_fusion.refs_1_
  371.7 4.1 collective-permute-done.31.got_ref
  380.5 44.2 %shard_map.403 = (bf16[512,768]{1,0:T(8,128)(2,1)}, bf16[512,768]{1,0:T(8,128)(2,1)}, bf16[512,768]{1,0:T(8,128)(2,1)}, bf16[512,768]{1,0:T(8,128)(2,1)}, bf16[5...) custom-call(bf16[512,768]{1,0:T(8,128)(2,1)} %copy-done.124, ...), custom_call_target="tpu_custom_call" | custom-call | flops 8053063680 | bytes 15728640 | tf_op jit(solution)/shard_map/pallas_call | solution.py:906
  452.6 4.6 pad_maximum_fusion
  461.8 3.3 constant_dynamic-slice_fusion.8.refs_3_
  465.7 9.6 %shard_map.407 = (f32[3,768,768]{2,1,0:T(8,128)}, f32[3,8,768]{2,1,0:T(8,128)}) custom-call(f32[768,768]{1,0:T(8,128)} %convolution_add_fusion.1.refs_0_, f32[768,768]{1,0:T(8,128)} %convolution_add_fusion.refs_1_, f32[768,768]{1,0:T(8,128)} %convolution_add_fusion.2.refs_2_, f32[768,768]{1,0:T(8,128)} %get-tuple-element.319.refs_3_, ...), custom_call_target="tpu_custom_call" | custom-call | flops 84934656 | bytes 21233664 | tf_op jit(solution)/shard_map/pallas_call | solution.py:1056
  475.9 3.7 collective-permute-done.37
  485.7 9.4 %fusion.2.left_ref = bf16[2048,768]{1,0:T(8,128)(2,1)S(1)} fusion(s32[2048]{0:T(1024)S(1)} %convert_reduce_fusion, bf16[512,768]{1,0:T(8,128)(2,1)} %collective-permute-done.38, bf16[512,768]{1,0:T(8,128)(2,1)} %collective-permute-done.37, bf16[512,768]{1,0:T(8,128)(2,1)} %collective-permute-done.36, bf16[512,768]{1,0:T(8,128)(2,1)} %get-tuple-element.315), kind=kOutput, calls=%fused_computation.8 | convolution fusion | flops 6459228160 | bytes 6299648 | tf_op jit(solution)/shard_map/dot_general | solution.py:1494
  495.1 6.1 fusion.76
  503.6 4.1 shard_map.411
  508.3 12.2 %shard_map.408 = (bf16[3840,768]{1,0:T(8,128)(2,1)S(1)}, bf16[3840,768]{1,0:T(8,128)(2,1)S(1)}, f32[8,3840]{1,0:T(8,128)S(1)}) custom-call(s32[13]{0:T(128)S(1)} %convert_reduce_fusion.1.starts_ref, bf16[2048,768]{1,0:T(8,128)(2,1)S(1)} %fusion.2.left_ref, s32[1,2048]{1,0:T(1,128)S(1)} %bitcast.242, bf16[160,768]{1,0:T(8,128)(2,1)S(1)} %copy-done.42, ...), custom_call_target="tpu_custom_call" | custom-call | flops 4105175040 | bytes 23592960 | tf_op jit(solution)/shard_map/pallas_call | solution.py:994
  522.1 9.9 %shard_map.409 = (bf16[2560,768]{1,0:T(8,128)(2,1)S(1)}, bf16[2560,768]{1,0:T(8,128)(2,1)S(1)}, f32[8,2560]{1,0:T(8,128)S(1)}) custom-call(s32[13]{0:T(128)S(1)} %convert_reduce_fusion.1.starts_ref, bf16[2048,768]{1,0:T(8,128)(2,1)S(1)} %fusion.2.left_ref, s32[1,2048]{1,0:T(1,128)S(1)} %bitcast.243, bf16[160,768]{1,0:T(8,128)(2,1)S(1)} %copy-done.42, ...), custom_call_target="tpu_custom_call" | custom-call | flops 2736783360 | bytes 15728640 | tf_op jit(solution)/shard_map/pallas_call | solution.py:994
  538.7 6.1 shard_map.410
  563.9 4.2 collective-permute-done.53
  568.1 4.3 collective-permute-done.56
  578.3 4.6 shard_map.416.refs_6_
  583.9 4.2 collective-permute-done.41
  588.6 4.4 fusion.13.m_ref
  599.4 3.0 copy-done.8
  602.4 4.6 shard_map.418
  617.2 11.3 %shard_map.419 = f32[7632,768]{1,0:T(8,128)} custom-call(bf16[3840,768]{1,0:T(8,128)(2,1)S(1)} %copy-done.12, bf16[2560,768]{1,0:T(8,128)(2,1)S(1)} %copy-done.20, bf16[1280,768]{1,0:T(8,128)(2,1)S(1)} %copy-done.30, bf16[3840,768]{1,0:T(8,128)(2,1)S(1)} %copy-done.14, bf16[2560,768]{1,0:T(8,128)(2,1)S(1)} %copy-done.23, bf16[1280,768]{1,0:T(8,128)(2,1)S(1)} %copy-done.32, ...), custom_call_target="tpu_custom_call" | custom-call | flops 281346048 | bytes 46891008 | tf_op jit(solution)/shard_map/pallas_call | solution.py:1211
  650.7 5.6 multiply_subtract_fusion
  (629 shorter events, 256.0 us)
Async XLA Ops:
  7.2 111.4 %all-gather.3.cloned.1.call-start = ((), (), s32[]{:S(2)}) async-start(), calls=%async_computation.2 | async-start | bytes 5750784 | tf_op jit(solution)/shard_map/all_gather | solution.py:1327
  13.6 14.3 %all-to-all-start = ((s32[8,1,2048]{2,1,0:T(1,128)}), s32[8,1,2048]{2,1,0:T(1,128)S(1)}, u32[]{:S(2)}, u32[]{:S(2)}) async-start(s32[8,1,2048]{2,1,0:T(1,128)} %broadcast_in_dim.112), calls=%async_computation | async-start | bytes 131072 | tf_op jit(solution)/shard_map/all_to_all | solution.py:1275
  20.9 262.6 %all-gather.5.cloned.1.call-start = ((), (), s32[]{:S(2)}) async-start(), calls=%async_computation.3 | async-start | bytes 13271040 | tf_op jit(solution)/shard_map/all_gather | solution.py:1329
  36.5 14.6 %collective-permute-start = (bf16[512,768]{1,0:T(8,128)(2,1)S(1)}, bf16[512,768]{1,0:T(8,128)(2,1)S(1)}, u32[]{:S(2)}, u32[]{:S(2)}) collective-permute-start(bf16[512,768]{1,0:T(8,128)(2,1)S(1)} %shard_map.379), channel_id=1, source_target_pairs={{0,1},{1,0},{2,3},{3,2},{4,5},{5,4},{6,7},{7,6},{8,9},{9,8},{10,11... | collective-permute-start | bytes 2359304 | tf_op jit(solution)/shard_map/ppermute | solution.py:43
  51.3 20.0 %collective-permute-start.2 = (bf16[512,768]{1,0:T(8,128)(2,1)S(1)}, bf16[512,768]{1,0:T(8,128)(2,1)S(1)}, u32[]{:S(2)}, u32[]{:S(2)}) collective-permute-start(bf16[512,768]{1,0:T(8,128)(2,1)S(1)} %add_convert_fusion.7), channel_id=1, source_target_pairs={{0,2},{1,3},{2,0},{3,1},{4,6},{5,7},{6,4},{7,5},{8,10},{9,11},{10,... | collective-permute-start | bytes 2359304 | tf_op jit(solution)/shard_map/ppermute | solution.py:43
  52.9 18.4 %collective-permute-start.1 = (bf16[512,768]{1,0:T(8,128)(2,1)S(1)}, bf16[512,768]{1,0:T(8,128)(2,1)S(1)}, u32[]{:S(2)}, u32[]{:S(2)}) collective-permute-start(bf16[512,768]{1,0:T(8,128)(2,1)S(1)} %shard_map.381), channel_id=1, source_target_pairs={{0,1},{1,0},{2,3},{3,2},{4,5},{5,4},{6,7},{7,6},{8,9},{9,8},{10,11... | collective-permute-start | bytes 2359304 | tf_op jit(solution)/shard_map/ppermute | solution.py:43
  78.6 38.0 %all-to-all-start.1 = ((bf16[8,96,512]{2,1,0:T(8,128)(2,1)}), bf16[8,96,512]{2,1,0:T(8,128)(2,1)S(1)}, u32[]{:S(2)}, u32[]{:S(2)}) async-start(bf16[8,96,512]{2,1,0:T(8,128)(2,1)} %bitcast.7), calls=%async_computation.1 | async-start | bytes 1572864 | tf_op jit(solution)/shard_map/all_to_all | solution.py:1314
  121.0 29.2 %collective-permute-start.4 = (bf16[768,768]{1,0:T(8,128)(2,1)}, bf16[768,768]{1,0:T(8,128)(2,1)}, u32[]{:S(2)}, u32[]{:S(2)}) collective-permute-start(bf16[768,768]{1,0:T(8,128)(2,1)} %get-tuple-element.469), channel_id=1, source_target_pairs={{0,2},{1,3},{2,0},{3,1},{4,6},{5,7},{6,4},{7,5},{8,10},{9,11},{10,... | collective-permute-start | bytes 3538952 | tf_op jit(solution)/shard_map/ppermute | solution.py:43
  122.5 43.2 %collective-permute-start.3 = (bf16[768,768]{1,0:T(8,128)(2,1)}, bf16[768,768]{1,0:T(8,128)(2,1)}, u32[]{:S(2)}, u32[]{:S(2)}) collective-permute-start(bf16[768,768]{1,0:T(8,128)(2,1)} %get-tuple-element.469), channel_id=1, source_target_pairs={{0,1},{1,0},{2,3},{3,2},{4,5},{5,4},{6,7},{7,6},{8,9},{9,8},{10,11... | collective-permute-start | bytes 3538952 | tf_op jit(solution)/shard_map/ppermute | solution.py:43
  128.4 43.7 %collective-permute-start.6 = (bf16[512,768]{1,0:T(8,128)(2,1)S(1)}, bf16[512,768]{1,0:T(8,128)(2,1)S(1)}, u32[]{:S(2)}, u32[]{:S(2)}) collective-permute-start(bf16[512,768]{1,0:T(8,128)(2,1)S(1)} %get-tuple-element.210.x_ref), channel_id=1, source_target_pairs={{0,1},{1,0},{2,3},{3,2},{4,5},{5,4},{6,7},{7,6},{8,9},{9,8},{10,11... | collective-permute-start | bytes 2359304 | tf_op jit(solution)/shard_map/ppermute | solution.py:43
  129.0 36.7 %collective-permute-start.7 = (bf16[512,768]{1,0:T(8,128)(2,1)S(1)}, bf16[512,768]{1,0:T(8,128)(2,1)}, u32[]{:S(2)}, u32[]{:S(2)}) collective-permute-start(bf16[512,768]{1,0:T(8,128)(2,1)S(1)} %get-tuple-element.210.x_ref), channel_id=1, source_target_pairs={{0,2},{1,3},{2,0},{3,1},{4,6},{5,7},{6,4},{7,5},{8,10},{9,11},{10,... | collective-permute-start | bytes 2359304 | tf_op jit(solution)/shard_map/ppermute | solution.py:43
  150.2 15.5 %collective-permute-start.5 = (bf16[768,768]{1,0:T(8,128)(2,1)}, bf16[768,768]{1,0:T(8,128)(2,1)S(1)}, u32[]{:S(2)}, u32[]{:S(2)}) collective-permute-start(bf16[768,768]{1,0:T(8,128)(2,1)} %collective-permute-done.4), channel_id=1, source_target_pairs={{0,1},{1,0},{2,3},{3,2},{4,5},{5,4},{6,7},{7,6},{8,9},{9,8},{10,11... | collective-permute-start | bytes 3538952 | tf_op jit(solution)/shard_map/ppermute | solution.py:43
  165.7 7.9 %collective-permute-start.8 = (bf16[512,768]{1,0:T(8,128)(2,1)}, bf16[512,768]{1,0:T(8,128)(2,1)S(1)}, u32[]{:S(2)}, u32[]{:S(2)}) collective-permute-start(bf16[512,768]{1,0:T(8,128)(2,1)} %collective-permute-done.7.x_ref), channel_id=1, source_target_pairs={{0,1},{1,0},{2,3},{3,2},{4,5},{5,4},{6,7},{7,6},{8,9},{9,8},{10,11... | collective-permute-start | bytes 2359304 | tf_op jit(solution)/shard_map/ppermute | solution.py:43
  207.2 20.7 %collective-permute-start.11 = (bf16[512,768]{1,0:T(8,128)(2,1)}, bf16[512,768]{1,0:T(8,128)(2,1)S(1)}, u32[]{:S(2)}, u32[]{:S(2)}) collective-permute-start(bf16[512,768]{1,0:T(8,128)(2,1)} %get-tuple-element.228.first_ref), channel_id=1, source_target_pairs={{0,2},{1,3},{2,0},{3,1},{4,6},{5,7},{6,4},{7,5},{8,10},{9,11},{10,... | collective-permute-start | bytes 2359304 | tf_op jit(solution)/shard_map/ppermute | solution.py:43
  240.3 8.8 %collective-permute-start.10 = (bf16[512,768]{1,0:T(8,128)(2,1)}, bf16[512,768]{1,0:T(8,128)(2,1)}, u32[]{:S(2)}, u32[]{:S(2)}) collective-permute-start(bf16[512,768]{1,0:T(8,128)(2,1)} %get-tuple-element.230), channel_id=1, source_target_pairs={{0,1},{1,0},{2,3},{3,2},{4,5},{5,4},{6,7},{7,6},{8,9},{9,8},{10,11... | collective-permute-start | bytes 2359304 | tf_op jit(solution)/shard_map/ppermute | solution.py:43
  241.8 19.7 %collective-permute-start.14 = (bf16[512,768]{1,0:T(8,128)(2,1)}, bf16[512,768]{1,0:T(8,128)(2,1)S(1)}, u32[]{:S(2)}, u32[]{:S(2)}) collective-permute-start(bf16[512,768]{1,0:T(8,128)(2,1)} %add_convert_fusion.4), channel_id=1, source_target_pairs={{0,2},{1,3},{2,0},{3,1},{4,6},{5,7},{6,4},{7,5},{8,10},{9,11},{10,... | collective-permute-start | bytes 2359304 | tf_op jit(solution)/shard_map/ppermute | solution.py:43
  270.2 27.7 %collective-permute-start.24 = (bf16[256,768]{1,0:T(8,128)(2,1)}, bf16[256,768]{1,0:T(8,128)(2,1)}, u32[]{:S(2)}, u32[]{:S(2)}) collective-permute-start(bf16[256,768]{1,0:T(8,128)(2,1)} %multiply_convert_fusion), channel_id=1, source_target_pairs={{0,2},{1,3},{2,0},{3,1},{4,6},{5,7},{6,4},{7,5},{8,10},{9,11},{10,... | collective-permute-start | bytes 1179656 | tf_op jit(solution)/shard_map/ppermute | solution.py:43
  297.9 15.8 %collective-permute-start.23 = (bf16[256,768]{1,0:T(8,128)(2,1)}, bf16[256,768]{1,0:T(8,128)(2,1)S(1)}, u32[]{:S(2)}, u32[]{:S(2)}) collective-permute-start(bf16[256,768]{1,0:T(8,128)(2,1)} %multiply_convert_fusion), channel_id=1, source_target_pairs={{0,1},{1,0},{2,3},{3,2},{4,5},{5,4},{6,7},{7,6},{8,9},{9,8},{10,11... | collective-permute-start | bytes 1179656 | tf_op jit(solution)/shard_map/ppermute | solution.py:43
  297.9 15.8 %collective-permute-start.25 = (bf16[256,768]{1,0:T(8,128)(2,1)}, bf16[256,768]{1,0:T(8,128)(2,1)}, u32[]{:S(2)}, u32[]{:S(2)}) collective-permute-start(bf16[256,768]{1,0:T(8,128)(2,1)} %collective-permute-done.24), channel_id=1, source_target_pairs={{0,1},{1,0},{2,3},{3,2},{4,5},{5,4},{6,7},{7,6},{8,9},{9,8},{10,11... | collective-permute-start | bytes 1179656 | tf_op jit(solution)/shard_map/ppermute | solution.py:43
  324.0 20.2 %collective-permute-start.27 = (bf16[512,768]{1,0:T(8,128)(2,1)}, bf16[512,768]{1,0:T(8,128)(2,1)S(1)}, u32[]{:S(2)}, u32[]{:S(2)}) collective-permute-start(bf16[512,768]{1,0:T(8,128)(2,1)} %get-tuple-element.248.first_ref), channel_id=1, source_target_pairs={{0,2},{1,3},{2,0},{3,1},{4,6},{5,7},{6,4},{7,5},{8,10},{9,11},{10,... | collective-permute-start | bytes 2359304 | tf_op jit(solution)/shard_map/ppermute | solution.py:43
  344.2 9.5 %collective-permute-start.30 = (bf16[512,768]{1,0:T(8,128)(2,1)}, bf16[512,768]{1,0:T(8,128)(2,1)S(1)}, u32[]{:S(2)}, u32[]{:S(2)}) collective-permute-start(bf16[512,768]{1,0:T(8,128)(2,1)} %get-tuple-element.256), channel_id=1, source_target_pairs={{0,1},{1,0},{2,3},{3,2},{4,5},{5,4},{6,7},{7,6},{8,9},{9,8},{10,11... | collective-permute-start | bytes 2359304 | tf_op jit(solution)/shard_map/ppermute | solution.py:43
  356.1 19.6 %collective-permute-start.31 = (bf16[512,768]{1,0:T(8,128)(2,1)S(1)}, bf16[512,768]{1,0:T(8,128)(2,1)S(1)}, u32[]{:S(2)}, u32[]{:S(2)}) collective-permute-start(bf16[512,768]{1,0:T(8,128)(2,1)S(1)} %add_convert_fusion.3), channel_id=1, source_target_pairs={{0,2},{1,3},{2,0},{3,1},{4,6},{5,7},{6,4},{7,5},{8,10},{9,11},{10,... | collective-permute-start | bytes 2359304 | tf_op jit(solution)/shard_map/ppermute | solution.py:43
  437.3 19.8 %collective-permute-start.35 = (bf16[512,768]{1,0:T(8,128)(2,1)S(1)}, bf16[512,768]{1,0:T(8,128)(2,1)S(1)}, u32[]{:S(2)}, u32[]{:S(2)}) collective-permute-start(bf16[512,768]{1,0:T(8,128)(2,1)S(1)} %add_convert_fusion.1), channel_id=1, source_target_pairs={{0,2},{1,3},{2,0},{3,1},{4,6},{5,7},{6,4},{7,5},{8,10},{9,11},{10,... | collective-permute-start | bytes 2359304 | tf_op jit(solution)/shard_map/ppermute | solution.py:43
  459.7 19.9 %collective-permute-start.37 = (bf16[512,768]{1,0:T(8,128)(2,1)}, bf16[512,768]{1,0:T(8,128)(2,1)}, u32[]{:S(2)}, u32[]{:S(2)}) collective-permute-start(bf16[512,768]{1,0:T(8,128)(2,1)} %get-tuple-element.315), channel_id=1, source_target_pairs={{0,2},{1,3},{2,0},{3,1},{4,6},{5,7},{6,4},{7,5},{8,10},{9,11},{10,... | collective-permute-start | bytes 2359304 | tf_op jit(solution)/shard_map/ppermute | solution.py:43
  465.1 30.0 %collective-permute-start.39 = (f32[768,768]{1,0:T(8,128)}, f32[768,768]{1,0:T(8,128)}, u32[]{:S(2)}, u32[]{:S(2)}) collective-permute-start(f32[768,768]{1,0:T(8,128)} %constant_dynamic-slice_fusion.8.refs_3_), channel_id=1, source_target_pairs={{0,1},{1,0},{2,3},{3,2},{4,5},{5,4},{6,7},{7,6},{8,9},{9,8},{10,11... | collective-permute-start | bytes 7077896 | tf_op jit(solution)/shard_map/ppermute | solution.py:43
  475.3 10.4 %collective-permute-start.36 = (bf16[512,768]{1,0:T(8,128)(2,1)}, bf16[512,768]{1,0:T(8,128)(2,1)}, u32[]{:S(2)}, u32[]{:S(2)}) collective-permute-start(bf16[512,768]{1,0:T(8,128)(2,1)} %get-tuple-element.315), channel_id=1, source_target_pairs={{0,1},{1,0},{2,3},{3,2},{4,5},{5,4},{6,7},{7,6},{8,9},{9,8},{10,11... | collective-permute-start | bytes 2359304 | tf_op jit(solution)/shard_map/ppermute | solution.py:43
  479.6 6.1 collective-permute-start.38
  483.7 19.8 %collective-permute-start.42 = (f32[8,768]{1,0:T(8,128)S(1)}, f32[8,768]{1,0:T(8,128)S(1)}, u32[]{:S(2)}, u32[]{:S(2)}) collective-permute-start(f32[8,768]{1,0:T(8,128)S(1)} %get-tuple-element.501.refs_4_.refs_1_), channel_id=1, source_target_pairs={{0,1},{1,0},{2,3},{3,2},{4,5},{5,4},{6,7},{7,6},{8,9},{9,8},{10,11... | collective-permute-start | bytes 73736 | tf_op jit(solution)/shard_map/ppermute | solution.py:43
  484.4 19.1 %collective-permute-start.44 = (f32[8,768]{1,0:T(8,128)S(1)}, f32[8,768]{1,0:T(8,128)S(1)}, u32[]{:S(2)}, u32[]{:S(2)}) collective-permute-start(f32[8,768]{1,0:T(8,128)S(1)} %collective-permute-done.43.refs_6_), channel_id=1, source_target_pairs={{0,1},{1,0},{2,3},{3,2},{4,5},{5,4},{6,7},{7,6},{8,9},{9,8},{10,11... | collective-permute-start | bytes 73736 | tf_op jit(solution)/shard_map/ppermute | solution.py:43
  503.0 33.8 %collective-permute-start.40 = (f32[384,768]{1,0:T(8,128)}, f32[384,768]{1,0:T(8,128)}, u32[]{:S(2)}, u32[]{:S(2)}) collective-permute-start(f32[384,768]{1,0:T(8,128)} %get-tuple-element.477), channel_id=1, source_target_pairs={{0,2},{1,3},{2,0},{3,1},{4,6},{5,7},{6,4},{7,5},{8,10},{9,11},{10,... | collective-permute-start | bytes 3538952 | tf_op jit(solution)/shard_map/ppermute | solution.py:43
  507.7 12.8 %collective-permute-start.46 = (f32[8,768]{1,0:T(8,128)S(1)}, f32[8,768]{1,0:T(8,128)S(1)}, u32[]{:S(2)}, u32[]{:S(2)}) collective-permute-start(f32[8,768]{1,0:T(8,128)S(1)} %get-tuple-element.503), channel_id=1, source_target_pairs={{0,1},{1,0},{2,3},{3,2},{4,5},{5,4},{6,7},{7,6},{8,9},{9,8},{10,11... | collective-permute-start | bytes 73736 | tf_op jit(solution)/shard_map/ppermute | solution.py:43
  507.8 29.0 %collective-permute-start.45 = (f32[8,768]{1,0:T(8,128)S(1)}, f32[8,768]{1,0:T(8,128)S(1)}, u32[]{:S(2)}, u32[]{:S(2)}) collective-permute-start(f32[8,768]{1,0:T(8,128)S(1)} %get-tuple-element.502), channel_id=1, source_target_pairs={{0,1},{1,0},{2,3},{3,2},{4,5},{5,4},{6,7},{7,6},{8,9},{9,8},{10,11... | collective-permute-start | bytes 73736 | tf_op jit(solution)/shard_map/ppermute | solution.py:43
  520.5 16.2 %collective-permute-start.47 = (f32[8,768]{1,0:T(8,128)S(1)}, f32[8,768]{1,0:T(8,128)S(1)}, u32[]{:S(2)}, u32[]{:S(2)}) collective-permute-start(f32[8,768]{1,0:T(8,128)S(1)} %fusion.29), channel_id=1, source_target_pairs={{0,2},{1,3},{2,0},{3,1},{4,6},{5,7},{6,4},{7,5},{8,10},{9,11},{10,... | collective-permute-start | bytes 73736 | tf_op jit(solution)/shard_map/ppermute | solution.py:43
  535.8 11.7 %collective-permute-start.54 = (f32[8,3840]{1,0:T(8,128)S(1)}, f32[8,3840]{1,0:T(8,128)S(1)}, u32[]{:S(2)}, u32[]{:S(2)}) collective-permute-start(f32[8,3840]{1,0:T(8,128)S(1)} %get-tuple-element.337), channel_id=1, source_target_pairs={{0,4},{4,0},{8,12},{12,8},{16,20},{20,16},{24,28},{28,24},{1,5},{5... | collective-permute-start | bytes 368648 | tf_op jit(solution)/shard_map/ppermute | solution.py:43
  545.5 5.4 collective-permute-start.51
  547.5 13.2 %collective-permute-start.55 = (f32[8,3840]{1,0:T(8,128)S(1)}, f32[8,3840]{1,0:T(8,128)S(1)}, u32[]{:S(2)}, u32[]{:S(2)}) collective-permute-start(f32[8,3840]{1,0:T(8,128)S(1)} %add.410), channel_id=1, source_target_pairs={{0,8},{4,12},{8,0},{12,4},{16,24},{20,28},{24,16},{28,20},{1,9},{5... | collective-permute-start | bytes 368648 | tf_op jit(solution)/shard_map/ppermute | solution.py:43
  551.0 6.6 collective-permute-start.52
  552.0 7.4 %collective-permute-start.58 = (f32[8,2560]{1,0:T(8,128)S(1)}, f32[8,2560]{1,0:T(8,128)S(1)}, u32[]{:S(2)}, u32[]{:S(2)}) collective-permute-start(f32[8,2560]{1,0:T(8,128)S(1)} %add.413), channel_id=1, source_target_pairs={{0,8},{4,12},{8,0},{12,4},{16,24},{20,28},{24,16},{28,20},{1,9},{5... | collective-permute-start | bytes 245768 | tf_op jit(solution)/shard_map/ppermute | solution.py:43
  555.0 7.2 %collective-permute-start.50 = (f32[8,2048]{1,0:T(8,128)S(1)}, f32[8,2048]{1,0:T(8,128)S(1)}, u32[]{:S(2)}, u32[]{:S(2)}) collective-permute-start(f32[8,2048]{1,0:T(8,128)S(1)} %add.405), channel_id=1, source_target_pairs={{0,16},{4,20},{8,24},{12,28},{16,0},{20,4},{24,8},{28,12},{1,17},{... | collective-permute-start | bytes 196616 | tf_op jit(solution)/shard_map/ppermute | solution.py:43
  557.6 10.5 %collective-permute-start.53 = (f32[8,2304]{1,0:T(8,128)S(1)}, f32[8,2304]{1,0:T(8,128)S(1)}, u32[]{:S(2)}, u32[]{:S(2)}) collective-permute-start(f32[8,2304]{1,0:T(8,128)S(1)} %add.408), channel_id=1, source_target_pairs={{0,16},{4,20},{8,24},{12,28},{16,0},{20,4},{24,8},{28,12},{1,17},{... | collective-permute-start | bytes 221192 | tf_op jit(solution)/shard_map/ppermute | solution.py:43
  559.4 29.1 %collective-permute-start.34 = (f32[768,768]{1,0:T(8,128)}, f32[768,768]{1,0:T(8,128)}, u32[]{:S(2)}, u32[]{:S(2)}) collective-permute-start(f32[768,768]{1,0:T(8,128)} %get-tuple-element.466.refs_1_), channel_id=1, source_target_pairs={{0,1},{1,0},{2,3},{3,2},{4,5},{5,4},{6,7},{7,6},{8,9},{9,8},{10,11... | collective-permute-start | bytes 7077896 | tf_op jit(solution)/shard_map/ppermute | solution.py:43
  559.4 28.7 %collective-permute-start.41 = (f32[384,768]{1,0:T(8,128)}, f32[384,768]{1,0:T(8,128)}, u32[]{:S(2)}, u32[]{:S(2)}) collective-permute-start(f32[384,768]{1,0:T(8,128)} %get-tuple-element.476), channel_id=1, source_target_pairs={{0,2},{1,3},{2,0},{3,1},{4,6},{5,7},{6,4},{7,5},{8,10},{9,11},{10,... | collective-permute-start | bytes 3538952 | tf_op jit(solution)/shard_map/ppermute | solution.py:43
  560.8 11.7 %collective-permute-start.59 = (f32[8,2560]{1,0:T(8,128)S(1)}, f32[8,2560]{1,0:T(8,128)S(1)}, u32[]{:S(2)}, u32[]{:S(2)}) collective-permute-start(f32[8,2560]{1,0:T(8,128)S(1)} %add.414), channel_id=1, source_target_pairs={{0,16},{4,20},{8,24},{12,28},{16,0},{20,4},{24,8},{28,12},{1,17},{... | collective-permute-start | bytes 245768 | tf_op jit(solution)/shard_map/ppermute | solution.py:43
  562.2 10.2 %collective-permute-start.56 = (f32[8,3840]{1,0:T(8,128)S(1)}, f32[8,3840]{1,0:T(8,128)S(1)}, u32[]{:S(2)}, u32[]{:S(2)}) collective-permute-start(f32[8,3840]{1,0:T(8,128)S(1)} %add.411), channel_id=1, source_target_pairs={{0,16},{4,20},{8,24},{12,28},{16,0},{20,4},{24,8},{28,12},{1,17},{... | collective-permute-start | bytes 368648 | tf_op jit(solution)/shard_map/ppermute | solution.py:43
  588.4 7.0 %collective-permute-start.64 = (f32[36,768]{1,0:T(8,128)S(1)}, f32[36,768]{1,0:T(8,128)S(1)}, u32[]{:S(2)}, u32[]{:S(2)}) collective-permute-start(f32[36,768]{1,0:T(8,128)S(1)} %add.422), channel_id=1, source_target_pairs={{0,8},{4,12},{8,0},{12,4},{16,24},{20,28},{24,16},{28,20},{1,9},{5... | collective-permute-start | bytes 331784 | tf_op jit(solution)/shard_map/ppermute | solution.py:43
  595.4 33.1 %collective-permute-start.65 = (f32[36,768]{1,0:T(8,128)S(1)}, f32[36,768]{1,0:T(8,128)S(1)}, u32[]{:S(2)}, u32[]{:S(2)}) collective-permute-start(f32[36,768]{1,0:T(8,128)S(1)} %add.423), channel_id=1, source_target_pairs={{0,16},{4,20},{8,24},{12,28},{16,0},{20,4},{24,8},{28,12},{1,17},{... | collective-permute-start | bytes 331784 | tf_op jit(solution)/shard_map/ppermute | solution.py:43
  598.1 9.0 %collective-permute-start.61 = (f32[8,768]{1,0:T(8,128)S(1)}, f32[8,768]{1,0:T(8,128)S(1)}, u32[]{:S(2)}, u32[]{:S(2)}) collective-permute-start(f32[8,768]{1,0:T(8,128)S(1)} %bitcast_add_fusion), channel_id=1, source_target_pairs={{0,8},{4,12},{8,0},{12,4},{16,24},{20,28},{24,16},{28,20},{1,9},{5... | collective-permute-start | bytes 73736 | tf_op jit(solution)/shard_map/ppermute | solution.py:43
  607.1 23.3 %collective-permute-start.62 = (f32[8,768]{1,0:T(8,128)S(1)}, f32[8,768]{1,0:T(8,128)S(1)}, u32[]{:S(2)}, u32[]{:S(2)}) collective-permute-start(f32[8,768]{1,0:T(8,128)S(1)} %add.419), channel_id=1, source_target_pairs={{0,16},{4,20},{8,24},{12,28},{16,0},{20,4},{24,8},{28,12},{1,17},{... | collective-permute-start | bytes 73736 | tf_op jit(solution)/shard_map/ppermute | solution.py:43
  (176 other events, 1337.6 us)
Sparse Core Ops, SparseCore 0:
  13.1 102.8 all-gather.2
  118.8 164.6 all-gather.4
